TPU v7x, 512 devices: a whole 4x4x16 slice. The times are simulated.
512 devices in a mesh: peer: 64 (over z, x), head: 8 (over y, core).
Axes of the slice: x: 4, y: 4, z: 16, core: 2. Of those that a mesh axis runs over, the one named last changes fastest.
Arguments:
- queries: bfloat16 [16384, 4096], P('peer', 'head'), parts along dimension 1, may hold values from -128 to 128
- keys: bfloat16 [16384, 1024], P('peer', 'head'), parts along dimension 1, may hold values from -24 to 24
- values: bfloat16 [16384, 1024], P('peer', 'head'), parts along dimension 1, may hold values from -6 to 6
- grad_out: bfloat16 [16384, 4096], P('peer', 'head'), parts along dimension 1, may hold values from -6 to 6
- doc_lengths: int32 [32], replicated, may hold values from 1 to 2048, 16384 in all
Outputs:
- attended: bfloat16 [16384, 4096], P('peer', 'head'), parts along dimension 1
- query_grad: float32 [16384, 4096], P('peer', 'head'), parts along dimension 1
- key_grad: float32 [16384, 1024], P('peer', 'head'), parts along dimension 1
- value_grad: float32 [16384, 1024], P('peer', 'head'), parts along dimension 1
There are 8 independent parts, one for each index of `head`. A program takes and returns all parts, laid end to end along the dimension named above; an argument that names none is the same for every part. Nothing has to cross between parts.
Inputs may be any that keep to these rules, and one draw needn't show every extreme that they name: `doc_lengths`: the lengths sum to 16384; the largest is exactly 2048.
All inputs are finite; a program needn't handle non-finite values.
Results may differ from a plain program's by a relative error of at most 0.02.
Values may be sent and summed in bfloat16 or wider, within the bound.
No kernel may reach another device: no remote copies, remote signals or barrier semaphores. Data moves between devices by JAX's collectives and lax.ppermute only.
A program may use at most 64 MiB of HBM per device.

v0:
```python
import jax
import jax.numpy as jnp
from jax import lax
from jax.sharding import PartitionSpec as P

SPAN = 8


masked_score = -1e30


def from_behind(block, axis, distance):
    devices = range(lax.axis_size(axis))
    route = [(i - distance, i) for i in devices if i - distance in devices]
    return lax.ppermute(block, axis, route)


def doc_index(positions, doc_lengths):
    starts = jnp.cumsum(doc_lengths) - doc_lengths
    hits = (starts[None, :] <= positions[:, None]).astype(jnp.int32)
    return jnp.sum(hits, axis=1) - 1


def partial_forward(query, key_block, value_block, visible):
    scale = query.shape[2] ** (-0.5)
    score = jnp.einsum("qhd,kd->hqk", query, key_block, preferred_element_type=jnp.float32) * scale
    score = jnp.where(visible[None], score, masked_score)
    peak = jnp.max(score, axis=2)
    weight = jnp.where(visible[None], jnp.exp(score - peak[:, :, None]), 0.0)
    total = jnp.sum(weight, axis=2)
    accum = jnp.einsum(
        "hqk,kd->qhd", weight.astype(jnp.bfloat16), value_block, preferred_element_type=jnp.float32
    )
    return (peak, total, accum)


def empty_partial(rows, heads, width):
    return (
        jnp.full((heads, rows), masked_score, jnp.float32),
        jnp.zeros((heads, rows), jnp.float32),
        jnp.zeros((rows, heads, width), jnp.float32),
    )


def merge_partial(first, second):
    peak = jnp.maximum(first[0], second[0])
    left = jnp.exp(first[0] - peak)
    right = jnp.exp(second[0] - peak)
    total = left * first[1] + right * second[1]
    accum = first[2] * left.T[:, :, None] + second[2] * right.T[:, :, None]
    return (peak, total, accum)


def partial_backward(query, grad, log_total, row_dot, key_block, value_block, visible):
    scale = query.shape[2] ** (-0.5)
    score = jnp.einsum("qhd,kd->hqk", query, key_block, preferred_element_type=jnp.float32) * scale
    prob = jnp.where(visible[None], jnp.exp(score - log_total[:, :, None]), 0.0)
    dprob = jnp.einsum("qhd,kd->hqk", grad, value_block, preferred_element_type=jnp.float32)
    dscore = (prob * (dprob - row_dot[:, :, None]) * scale).astype(jnp.bfloat16)
    query_part = jnp.einsum("hqk,kd->qhd", dscore, key_block, preferred_element_type=jnp.float32)
    key_part = jnp.einsum("hqk,qhd->kd", dscore, query, preferred_element_type=jnp.float32)
    value_part = jnp.einsum(
        "hqk,qhd->kd", prob.astype(jnp.bfloat16), grad, preferred_element_type=jnp.float32
    )
    return (query_part, key_part, value_part)


def empty_grads(rows, heads, width):
    return (
        jnp.zeros((rows, heads, width), jnp.float32),
        jnp.zeros((rows, width), jnp.float32),
        jnp.zeros((rows, width), jnp.float32),
    )


def return_key_grads(key_part, value_part, distance):
    return from_behind((key_part, value_part), "peer", -distance)


def body(queries, keys, values, grad_out, doc_lengths):
    rows = keys.shape[0]
    width = keys.shape[1]
    heads = queries.shape[1] // width
    place = lax.axis_index("peer")
    local = jnp.arange(rows, dtype=jnp.int32)
    query = queries.reshape(rows, heads, width)
    grad = grad_out.reshape(rows, heads, width)

    def docs_at(peer):
        return doc_index(peer * rows + local, doc_lengths)

    own_docs = docs_at(place)
    home_mask = (own_docs[:, None] == own_docs[None, :]) & (local[None, :] <= local[:, None])
    nothing = empty_partial(rows, heads, width)
    state = partial_forward(query, keys, values, home_mask)
    remotes = {}
    carried = (keys, values)
    for distance in range(1, SPAN + 1):
        carried = from_behind((carried[0], carried[1]), "peer", 1)
        remotes[distance] = carried
        key_docs = docs_at(place - distance)
        valid = (place >= distance) & (key_docs[rows - 1] == own_docs[0])
        remote_keys, remote_values = remotes[distance]
        visible = own_docs[:, None] == key_docs[None, :]
        partial_value = lax.cond(
            valid,
            lambda: partial_forward(query, remote_keys, remote_values, visible),
            lambda: nothing,
        )
        state = merge_partial(state, partial_value)
    peak, total, accum = state
    attended = (accum / total.T[:, :, None]).astype(jnp.bfloat16)
    log_total = peak + jnp.log(total)
    row_dot = jnp.sum(grad.astype(jnp.float32) * attended.astype(jnp.float32), axis=2).T
    query_grad, key_grad, value_grad = partial_backward(
        query, grad, log_total, row_dot, keys, values, home_mask
    )
    zeros = empty_grads(rows, heads, width)
    for distance in range(1, SPAN + 1):
        remote_keys, remote_values = remotes[distance]
        key_docs = docs_at(place - distance)
        valid = (place >= distance) & (key_docs[rows - 1] == own_docs[0])
        visible = own_docs[:, None] == key_docs[None, :]
        parts = lax.cond(
            valid,
            lambda: partial_backward(
                query, grad, log_total, row_dot, remote_keys, remote_values, visible
            ),
            lambda: zeros,
        )
        query_grad = query_grad + parts[0]
        back_keys, back_values = return_key_grads(parts[1], parts[2], distance)
        key_grad = key_grad + back_keys
        value_grad = value_grad + back_values
    return (
        attended.reshape(rows, heads * width),
        query_grad.reshape(rows, heads * width),
        key_grad,
        value_grad,
    )


def solution(mesh):
    placed = (P("peer", "head"), P("peer", "head"), P("peer", "head"), P("peer", "head"), P())
    return jax.shard_map(
        body,
        mesh=mesh,
        in_specs=placed,
        out_specs=(P("peer", "head"), P("peer", "head"), P("peer", "head"), P("peer", "head")),
        check_vma=False,
    )
```

profile of v0, /device:TPU:128, one launch (start us, length us, event | category | flops | bytes accessed | tf_op | source)
XLA Modules:
  0.0 244.3 jit_solution(5060549187573347502)
XLA Ops:
  0.6 3.4 %collective-permute-start = (bf16[256,128]{1,0:T(8,128)(2,1)}, bf16[256,128]{1,0:T(8,128)(2,1)S(1)}, u32[]{:S(2)}, u32[]{:S(2)}) collective-permute-start(bf16[256,128]{1,0:T(8,128)(2,1)} %param.38), channel_id=1, source_target_pairs={{0,8},{8,16},{16,24},{24,32},{32,40},{40,48},{48,56},{56,64},{64,7... | collective-permute-start | bytes 196616 | tf_op jit(solution)/shard_map/ppermute | solution.py:15
  4.0 3.4 %collective-permute-start.1 = (bf16[256,128]{1,0:T(8,128)(2,1)}, bf16[256,128]{1,0:T(8,128)(2,1)S(1)}, u32[]{:S(2)}, u32[]{:S(2)}) collective-permute-start(bf16[256,128]{1,0:T(8,128)(2,1)} %param.39), channel_id=1, source_target_pairs={{0,8},{8,16},{16,24},{24,32},{32,40},{40,48},{48,56},{56,64},{64,7... | collective-permute-start | bytes 196616 | tf_op jit(solution)/shard_map/ppermute | solution.py:15
  15.7 4.1 %collective-permute-done.2 = bf16[256,128]{1,0:T(8,128)(2,1)S(1)} collective-permute-done((bf16[256,128]{1,0:T(8,128)(2,1)S(1)}, bf16[256,128]{1,0:T(8,128)(2,1)S(1)}, u32[]{:S(2)}, u32[]{:S(2)}) %collective-permute-start.2) | collective-permute-done | bytes 65568 | tf_op jit(solution)/shard_map/ppermute | solution.py:15
  25.1 4.5 %collective-permute-done.4 = bf16[256,128]{1,0:T(8,128)(2,1)S(1)} collective-permute-done((bf16[256,128]{1,0:T(8,128)(2,1)S(1)}, bf16[256,128]{1,0:T(8,128)(2,1)S(1)}, u32[]{:S(2)}, u32[]{:S(2)}) %collective-permute-start.4) | collective-permute-done | bytes 65568 | tf_op jit(solution)/shard_map/ppermute | solution.py:15
  34.6 4.5 %collective-permute-done.6 = bf16[256,128]{1,0:T(8,128)(2,1)S(1)} collective-permute-done((bf16[256,128]{1,0:T(8,128)(2,1)S(1)}, bf16[256,128]{1,0:T(8,128)(2,1)S(1)}, u32[]{:S(2)}, u32[]{:S(2)}) %collective-permute-start.6) | collective-permute-done | bytes 65568 | tf_op jit(solution)/shard_map/ppermute | solution.py:15
  44.4 4.2 %collective-permute-done.8 = bf16[256,128]{1,0:T(8,128)(2,1)S(1)} collective-permute-done((bf16[256,128]{1,0:T(8,128)(2,1)S(1)}, bf16[256,128]{1,0:T(8,128)(2,1)S(1)}, u32[]{:S(2)}, u32[]{:S(2)}) %collective-permute-start.8) | collective-permute-done | bytes 65568 | tf_op jit(solution)/shard_map/ppermute | solution.py:15
  55.1 3.0 %collective-permute-done.10 = bf16[256,128]{1,0:T(8,128)(2,1)S(1)} collective-permute-done((bf16[256,128]{1,0:T(8,128)(2,1)S(1)}, bf16[256,128]{1,0:T(8,128)(2,1)S(1)}, u32[]{:S(2)}, u32[]{:S(2)}) %collective-permute-start.10) | collective-permute-done | bytes 65568 | tf_op jit(solution)/shard_map/ppermute | solution.py:15
  63.7 4.1 %collective-permute-done.12 = bf16[256,128]{1,0:T(8,128)(2,1)} collective-permute-done((bf16[256,128]{1,0:T(8,128)(2,1)S(1)}, bf16[256,128]{1,0:T(8,128)(2,1)}, u32[]{:S(2)}, u32[]{:S(2)}) %collective-permute-start.12) | collective-permute-done | bytes 65568 | tf_op jit(solution)/shard_map/ppermute | solution.py:15
  90.5 2.0 conditional.16
  93.1 3.4 %conditional.17 = (f32[4,256]{1,0:T(4,128)S(1)}, f32[4,256]{1,0:T(4,128)S(1)}, f32[256,4,128]{0,2,1:T(8,128)S(1)}) conditional(s32[]{:T(128)} %convert_element_type.162, () %tuple.138, (pred[256,256]{0,1:T(8,128)(4,1)S(1)}, bf16[256,128]{1,0:T(8,128)(2,1)S(1)}, bf16[256,4,128]{0,2,1:T(8,128)(2,1)S(1)}, bf16[256,128]{1,0:T(8,128)(2,1)}) %tuple.398), branch_computations={%region_9.10_spmd, %region_10.13_spmd} | conditional | flops 136574976 | bytes 5881992 | solution.py:105
  97.1 4.5 %conditional.18 = (f32[4,256]{1,0:T(4,128)S(1)}, f32[4,256]{1,0:T(4,128)S(1)}, f32[256,4,128]{0,2,1:T(8,128)S(1)}) conditional(s32[]{:T(128)} %convert_element_type.164, () %tuple.140, (pred[256,256]{0,1:T(8,128)(4,1)S(1)}, bf16[256,128]{1,0:T(8,128)(2,1)}, bf16[256,4,128]{0,2,1:T(8,128)(2,1)S(1)}, bf16[256,128]{1,0:T(8,128)(2,1)}) %tuple.396), branch_computations={%region_14.15_spmd, %region_15.18_spmd} | conditional | flops 136574976 | bytes 5619820 | solution.py:105
  111.6 2.4 multiply_reduce_fusion
  117.5 3.1 %conditional.24 = (f32[256,128]{1,0:T(8,128)}, f32[256,128]{1,0:T(8,128)}, f32[256,4,128]{0,2,1:T(8,128)S(1)}) conditional(s32[]{:T(128)} %convert_element_type.160, () %tuple.152, (pred[256,256]{0,1:T(8,128)(4,1)S(1)}, bf16[256,128]{1,0:T(8,128)(2,1)S(1)}, bf16[256,4,128]{0,2,1:T(8,128)(2,1)S(1)}, f32[4,256]{1,0:T(4,128)S(1)}, ...), branch_computations={%region_45.46_spmd, %region_46.47_spmd} | conditional | flops 337641472 | bytes 7872536 | solution.py:124
  120.6 2.8 %collective-permute-start.16 = (f32[256,128]{1,0:T(8,128)}, f32[256,128]{1,0:T(8,128)}, u32[]{:S(2)}, u32[]{:S(2)}) collective-permute-start(f32[256,128]{1,0:T(8,128)} %get-tuple-element.348), channel_id=1, source_target_pairs={{8,0},{16,8},{24,16},{32,24},{40,32},{48,40},{56,48},{64,56},{72,6... | collective-permute-start | bytes 393224 | tf_op jit(solution)/shard_map/ppermute | solution.py:15
  123.4 1.9 collective-permute-start.24
  125.4 5.0 %conditional.25 = (f32[256,128]{1,0:T(8,128)}, f32[256,128]{1,0:T(8,128)}, f32[256,4,128]{0,2,1:T(8,128)S(1)}) conditional(s32[]{:T(128)} %convert_element_type.162, () %tuple.154, (pred[256,256]{0,1:T(8,128)(4,1)S(1)}, bf16[256,128]{1,0:T(8,128)(2,1)S(1)}, bf16[256,4,128]{0,2,1:T(8,128)(2,1)S(1)}, f32[4,256]{1,0:T(4,128)S(1)}, ...), branch_computations={%region_47.48_spmd, %region_48.49_spmd} | conditional | flops 337641472 | bytes 8134708 | solution.py:124
  130.3 1.9 collective-permute-start.17
  132.3 1.9 collective-permute-start.25
  134.3 4.0 %conditional.26 = (f32[256,128]{1,0:T(8,128)}, f32[256,128]{1,0:T(8,128)}, f32[256,4,128]{0,2,1:T(8,128)}) conditional(s32[]{:T(128)} %convert_element_type.164, () %tuple.156, (pred[256,256]{0,1:T(8,128)(4,1)S(1)}, bf16[256,128]{1,0:T(8,128)(2,1)S(1)}, bf16[256,4,128]{0,2,1:T(8,128)(2,1)S(1)}, f32[4,256]{1,0:T(4,128)S(1)}, ...), branch_computations={%region_49.50_spmd, %region_50.51_spmd} | conditional | flops 337641472 | bytes 8134708 | solution.py:124
  138.2 14.2 %collective-permute-start.18 = (f32[256,128]{1,0:T(8,128)}, f32[256,128]{1,0:T(8,128)}, u32[]{:S(2)}, u32[]{:S(2)}) collective-permute-start(f32[256,128]{1,0:T(8,128)} %get-tuple-element.350), channel_id=1, source_target_pairs={{24,0},{32,8},{40,16},{48,24},{56,32},{64,40},{72,48},{80,56},{88,... | collective-permute-start | bytes 393224 | tf_op jit(solution)/shard_map/ppermute | solution.py:15
  154.6 2.1 conditional.28
  157.7 2.2 conditional.30
  162.2 2.3 add_add_fusion
  165.5 2.0 collective-permute-start.26
  167.9 1.9 collective-permute-start.19
  169.9 16.8 %collective-permute-start.20 = (f32[256,128]{1,0:T(8,128)}, f32[256,128]{1,0:T(8,128)S(1)}, u32[]{:S(2)}, u32[]{:S(2)}) collective-permute-start(f32[256,128]{1,0:T(8,128)} %get-tuple-element.352), channel_id=1, source_target_pairs={{40,0},{48,8},{56,16},{64,24},{72,32},{80,40},{88,48},{96,56},{104... | collective-permute-start | bytes 393224 | tf_op jit(solution)/shard_map/ppermute | solution.py:15
  186.7 2.8 %collective-permute-start.21 = (f32[256,128]{1,0:T(8,128)S(1)}, f32[256,128]{1,0:T(8,128)S(1)}, u32[]{:S(2)}, u32[]{:S(2)}) collective-permute-start(f32[256,128]{1,0:T(8,128)S(1)} %get-tuple-element.353), channel_id=1, source_target_pairs={{48,0},{56,8},{64,16},{72,24},{80,32},{88,40},{96,48},{104,56},{11... | collective-permute-start | bytes 393224 | tf_op jit(solution)/shard_map/ppermute | solution.py:15
  195.7 11.2 %collective-permute-done.20 = f32[256,128]{1,0:T(8,128)S(1)} collective-permute-done((f32[256,128]{1,0:T(8,128)}, f32[256,128]{1,0:T(8,128)S(1)}, u32[]{:S(2)}, u32[]{:S(2)}) %collective-permute-start.20) | collective-permute-done | bytes 131104 | tf_op jit(solution)/shard_map/ppermute | solution.py:15
  208.8 2.2 collective-permute-start.29
  211.0 4.7 %collective-permute-start.30 = (f32[256,128]{1,0:T(8,128)}, f32[256,128]{1,0:T(8,128)S(1)}, u32[]{:S(2)}, u32[]{:S(2)}) collective-permute-start(f32[256,128]{1,0:T(8,128)} %get-tuple-element.362), channel_id=1, source_target_pairs={{56,0},{64,8},{72,16},{80,24},{88,32},{96,40},{104,48},{112,56},{1... | collective-permute-start | bytes 393224 | tf_op jit(solution)/shard_map/ppermute | solution.py:15
  215.7 11.6 %collective-permute-done.23 = f32[256,128]{1,0:T(8,128)S(1)} collective-permute-done((f32[256,128]{1,0:T(8,128)}, f32[256,128]{1,0:T(8,128)S(1)}, u32[]{:S(2)}, u32[]{:S(2)}) %collective-permute-start.23) | collective-permute-done | bytes 131104 | tf_op jit(solution)/shard_map/ppermute | solution.py:15
  231.1 11.6 %collective-permute-done.31 = f32[256,128]{1,0:T(8,128)S(1)} collective-permute-done((f32[256,128]{1,0:T(8,128)}, f32[256,128]{1,0:T(8,128)S(1)}, u32[]{:S(2)}, u32[]{:S(2)}) %collective-permute-start.31) | collective-permute-done | bytes 131104 | tf_op jit(solution)/shard_map/ppermute | solution.py:15
  (306 shorter events, 116.2 us)
Async XLA Ops:
  0.6 9.7 %collective-permute-start = (bf16[256,128]{1,0:T(8,128)(2,1)}, bf16[256,128]{1,0:T(8,128)(2,1)S(1)}, u32[]{:S(2)}, u32[]{:S(2)}) collective-permute-start(bf16[256,128]{1,0:T(8,128)(2,1)} %param.38), channel_id=1, source_target_pairs={{0,8},{8,16},{16,24},{24,32},{32,40},{40,48},{48,56},{56,64},{64,7... | collective-permute-start | bytes 196616 | tf_op jit(solution)/shard_map/ppermute | solution.py:15
  4.0 9.7 %collective-permute-start.1 = (bf16[256,128]{1,0:T(8,128)(2,1)}, bf16[256,128]{1,0:T(8,128)(2,1)S(1)}, u32[]{:S(2)}, u32[]{:S(2)}) collective-permute-start(bf16[256,128]{1,0:T(8,128)(2,1)} %param.39), channel_id=1, source_target_pairs={{0,8},{8,16},{16,24},{24,32},{32,40},{40,48},{48,56},{56,64},{64,7... | collective-permute-start | bytes 196616 | tf_op jit(solution)/shard_map/ppermute | solution.py:15
  10.3 9.5 %collective-permute-start.2 = (bf16[256,128]{1,0:T(8,128)(2,1)S(1)}, bf16[256,128]{1,0:T(8,128)(2,1)S(1)}, u32[]{:S(2)}, u32[]{:S(2)}) collective-permute-start(bf16[256,128]{1,0:T(8,128)(2,1)S(1)} %collective-permute-done), channel_id=1, source_target_pairs={{0,8},{8,16},{16,24},{24,32},{32,40},{40,48},{48,56},{56,64},{64,7... | collective-permute-start | bytes 196616 | tf_op jit(solution)/shard_map/ppermute | solution.py:15
  13.7 9.5 %collective-permute-start.3 = (bf16[256,128]{1,0:T(8,128)(2,1)S(1)}, bf16[256,128]{1,0:T(8,128)(2,1)S(1)}, u32[]{:S(2)}, u32[]{:S(2)}) collective-permute-start(bf16[256,128]{1,0:T(8,128)(2,1)S(1)} %collective-permute-done.1), channel_id=1, source_target_pairs={{0,8},{8,16},{16,24},{24,32},{32,40},{40,48},{48,56},{56,64},{64,7... | collective-permute-start | bytes 196616 | tf_op jit(solution)/shard_map/ppermute | solution.py:15
  19.8 9.9 %collective-permute-start.4 = (bf16[256,128]{1,0:T(8,128)(2,1)S(1)}, bf16[256,128]{1,0:T(8,128)(2,1)S(1)}, u32[]{:S(2)}, u32[]{:S(2)}) collective-permute-start(bf16[256,128]{1,0:T(8,128)(2,1)S(1)} %collective-permute-done.2), channel_id=1, source_target_pairs={{0,8},{8,16},{16,24},{24,32},{32,40},{40,48},{48,56},{56,64},{64,7... | collective-permute-start | bytes 196616 | tf_op jit(solution)/shard_map/ppermute | solution.py:15
  23.2 9.5 %collective-permute-start.5 = (bf16[256,128]{1,0:T(8,128)(2,1)S(1)}, bf16[256,128]{1,0:T(8,128)(2,1)S(1)}, u32[]{:S(2)}, u32[]{:S(2)}) collective-permute-start(bf16[256,128]{1,0:T(8,128)(2,1)S(1)} %collective-permute-done.3), channel_id=1, source_target_pairs={{0,8},{8,16},{16,24},{24,32},{32,40},{40,48},{48,56},{56,64},{64,7... | collective-permute-start | bytes 196616 | tf_op jit(solution)/shard_map/ppermute | solution.py:15
  29.7 9.5 %collective-permute-start.6 = (bf16[256,128]{1,0:T(8,128)(2,1)S(1)}, bf16[256,128]{1,0:T(8,128)(2,1)S(1)}, u32[]{:S(2)}, u32[]{:S(2)}) collective-permute-start(bf16[256,128]{1,0:T(8,128)(2,1)S(1)} %collective-permute-done.4), channel_id=1, source_target_pairs={{0,8},{8,16},{16,24},{24,32},{32,40},{40,48},{48,56},{56,64},{64,7... | collective-permute-start | bytes 196616 | tf_op jit(solution)/shard_map/ppermute | solution.py:15
  32.7 9.8 %collective-permute-start.7 = (bf16[256,128]{1,0:T(8,128)(2,1)S(1)}, bf16[256,128]{1,0:T(8,128)(2,1)S(1)}, u32[]{:S(2)}, u32[]{:S(2)}) collective-permute-start(bf16[256,128]{1,0:T(8,128)(2,1)S(1)} %collective-permute-done.5), channel_id=1, source_target_pairs={{0,8},{8,16},{16,24},{24,32},{32,40},{40,48},{48,56},{56,64},{64,7... | collective-permute-start | bytes 196616 | tf_op jit(solution)/shard_map/ppermute | solution.py:15
  39.1 9.5 %collective-permute-start.8 = (bf16[256,128]{1,0:T(8,128)(2,1)S(1)}, bf16[256,128]{1,0:T(8,128)(2,1)S(1)}, u32[]{:S(2)}, u32[]{:S(2)}) collective-permute-start(bf16[256,128]{1,0:T(8,128)(2,1)S(1)} %collective-permute-done.6), channel_id=1, source_target_pairs={{0,8},{8,16},{16,24},{24,32},{32,40},{40,48},{48,56},{56,64},{64,7... | collective-permute-start | bytes 196616 | tf_op jit(solution)/shard_map/ppermute | solution.py:15
  42.5 9.5 %collective-permute-start.9 = (bf16[256,128]{1,0:T(8,128)(2,1)S(1)}, bf16[256,128]{1,0:T(8,128)(2,1)S(1)}, u32[]{:S(2)}, u32[]{:S(2)}) collective-permute-start(bf16[256,128]{1,0:T(8,128)(2,1)S(1)} %collective-permute-done.7), channel_id=1, source_target_pairs={{0,8},{8,16},{16,24},{24,32},{32,40},{40,48},{48,56},{56,64},{64,7... | collective-permute-start | bytes 196616 | tf_op jit(solution)/shard_map/ppermute | solution.py:15
  48.6 9.5 %collective-permute-start.10 = (bf16[256,128]{1,0:T(8,128)(2,1)S(1)}, bf16[256,128]{1,0:T(8,128)(2,1)S(1)}, u32[]{:S(2)}, u32[]{:S(2)}) collective-permute-start(bf16[256,128]{1,0:T(8,128)(2,1)S(1)} %collective-permute-done.8), channel_id=1, source_target_pairs={{0,8},{8,16},{16,24},{24,32},{32,40},{40,48},{48,56},{56,64},{64,7... | collective-permute-start | bytes 196616 | tf_op jit(solution)/shard_map/ppermute | solution.py:15
  52.0 9.5 %collective-permute-start.11 = (bf16[256,128]{1,0:T(8,128)(2,1)S(1)}, bf16[256,128]{1,0:T(8,128)(2,1)S(1)}, u32[]{:S(2)}, u32[]{:S(2)}) collective-permute-start(bf16[256,128]{1,0:T(8,128)(2,1)S(1)} %collective-permute-done.9), channel_id=1, source_target_pairs={{0,8},{8,16},{16,24},{24,32},{32,40},{40,48},{48,56},{56,64},{64,7... | collective-permute-start | bytes 196616 | tf_op jit(solution)/shard_map/ppermute | solution.py:15
  58.1 9.8 %collective-permute-start.12 = (bf16[256,128]{1,0:T(8,128)(2,1)S(1)}, bf16[256,128]{1,0:T(8,128)(2,1)}, u32[]{:S(2)}, u32[]{:S(2)}) collective-permute-start(bf16[256,128]{1,0:T(8,128)(2,1)S(1)} %collective-permute-done.10), channel_id=1, source_target_pairs={{0,8},{8,16},{16,24},{24,32},{32,40},{40,48},{48,56},{56,64},{64,7... | collective-permute-start | bytes 196616 | tf_op jit(solution)/shard_map/ppermute | solution.py:15
  61.5 9.7 %collective-permute-start.13 = (bf16[256,128]{1,0:T(8,128)(2,1)S(1)}, bf16[256,128]{1,0:T(8,128)(2,1)}, u32[]{:S(2)}, u32[]{:S(2)}) collective-permute-start(bf16[256,128]{1,0:T(8,128)(2,1)S(1)} %collective-permute-done.11), channel_id=1, source_target_pairs={{0,8},{8,16},{16,24},{24,32},{32,40},{40,48},{48,56},{56,64},{64,7... | collective-permute-start | bytes 196616 | tf_op jit(solution)/shard_map/ppermute | solution.py:15
  67.8 39.6 %collective-permute-start.14 = (bf16[256,128]{1,0:T(8,128)(2,1)}, bf16[256,128]{1,0:T(8,128)(2,1)}, u32[]{:S(2)}, u32[]{:S(2)}) collective-permute-start(bf16[256,128]{1,0:T(8,128)(2,1)} %collective-permute-done.12), channel_id=1, source_target_pairs={{0,8},{8,16},{16,24},{24,32},{32,40},{40,48},{48,56},{56,64},{64,7... | collective-permute-start | bytes 196616 | tf_op jit(solution)/shard_map/ppermute | solution.py:15
  71.1 36.3 %collective-permute-start.15 = (bf16[256,128]{1,0:T(8,128)(2,1)}, bf16[256,128]{1,0:T(8,128)(2,1)}, u32[]{:S(2)}, u32[]{:S(2)}) collective-permute-start(bf16[256,128]{1,0:T(8,128)(2,1)} %collective-permute-done.13), channel_id=1, source_target_pairs={{0,8},{8,16},{16,24},{24,32},{32,40},{40,48},{48,56},{56,64},{64,7... | collective-permute-start | bytes 196616 | tf_op jit(solution)/shard_map/ppermute | solution.py:15
  120.6 44.9 %collective-permute-start.16 = (f32[256,128]{1,0:T(8,128)}, f32[256,128]{1,0:T(8,128)}, u32[]{:S(2)}, u32[]{:S(2)}) collective-permute-start(f32[256,128]{1,0:T(8,128)} %get-tuple-element.348), channel_id=1, source_target_pairs={{8,0},{16,8},{24,16},{32,24},{40,32},{48,40},{56,48},{64,56},{72,6... | collective-permute-start | bytes 393224 | tf_op jit(solution)/shard_map/ppermute | solution.py:15
  123.4 44.5 %collective-permute-start.24 = (f32[256,128]{1,0:T(8,128)}, f32[256,128]{1,0:T(8,128)}, u32[]{:S(2)}, u32[]{:S(2)}) collective-permute-start(f32[256,128]{1,0:T(8,128)} %get-tuple-element.356), channel_id=1, source_target_pairs={{8,0},{16,8},{24,16},{32,24},{40,32},{48,40},{56,48},{64,56},{72,6... | collective-permute-start | bytes 393224 | tf_op jit(solution)/shard_map/ppermute | solution.py:15
  130.3 39.5 %collective-permute-start.17 = (f32[256,128]{1,0:T(8,128)}, f32[256,128]{1,0:T(8,128)}, u32[]{:S(2)}, u32[]{:S(2)}) collective-permute-start(f32[256,128]{1,0:T(8,128)} %get-tuple-element.349), channel_id=1, source_target_pairs={{16,0},{24,8},{32,16},{40,24},{48,32},{56,40},{64,48},{72,56},{80,... | collective-permute-start | bytes 393224 | tf_op jit(solution)/shard_map/ppermute | solution.py:15
  132.3 54.4 %collective-permute-start.25 = (f32[256,128]{1,0:T(8,128)}, f32[256,128]{1,0:T(8,128)}, u32[]{:S(2)}, u32[]{:S(2)}) collective-permute-start(f32[256,128]{1,0:T(8,128)} %get-tuple-element.357), channel_id=1, source_target_pairs={{16,0},{24,8},{32,16},{40,24},{48,32},{56,40},{64,48},{72,56},{80,... | collective-permute-start | bytes 393224 | tf_op jit(solution)/shard_map/ppermute | solution.py:15
  138.2 51.3 %collective-permute-start.18 = (f32[256,128]{1,0:T(8,128)}, f32[256,128]{1,0:T(8,128)}, u32[]{:S(2)}, u32[]{:S(2)}) collective-permute-start(f32[256,128]{1,0:T(8,128)} %get-tuple-element.350), channel_id=1, source_target_pairs={{24,0},{32,8},{40,16},{48,24},{56,32},{64,40},{72,48},{80,56},{88,... | collective-permute-start | bytes 393224 | tf_op jit(solution)/shard_map/ppermute | solution.py:15
  165.5 26.0 %collective-permute-start.26 = (f32[256,128]{1,0:T(8,128)}, f32[256,128]{1,0:T(8,128)S(1)}, u32[]{:S(2)}, u32[]{:S(2)}) collective-permute-start(f32[256,128]{1,0:T(8,128)} %get-tuple-element.358), channel_id=1, source_target_pairs={{24,0},{32,8},{40,16},{48,24},{56,32},{64,40},{72,48},{80,56},{88,... | collective-permute-start | bytes 393224 | tf_op jit(solution)/shard_map/ppermute | solution.py:15
  167.9 25.8 %collective-permute-start.19 = (f32[256,128]{1,0:T(8,128)}, f32[256,128]{1,0:T(8,128)S(1)}, u32[]{:S(2)}, u32[]{:S(2)}) collective-permute-start(f32[256,128]{1,0:T(8,128)} %get-tuple-element.351), channel_id=1, source_target_pairs={{32,0},{40,8},{48,16},{56,24},{64,32},{72,40},{80,48},{88,56},{96,... | collective-permute-start | bytes 393224 | tf_op jit(solution)/shard_map/ppermute | solution.py:15
  169.9 37.0 %collective-permute-start.20 = (f32[256,128]{1,0:T(8,128)}, f32[256,128]{1,0:T(8,128)S(1)}, u32[]{:S(2)}, u32[]{:S(2)}) collective-permute-start(f32[256,128]{1,0:T(8,128)} %get-tuple-element.352), channel_id=1, source_target_pairs={{40,0},{48,8},{56,16},{64,24},{72,32},{80,40},{88,48},{96,56},{104... | collective-permute-start | bytes 393224 | tf_op jit(solution)/shard_map/ppermute | solution.py:15
  186.7 22.1 %collective-permute-start.21 = (f32[256,128]{1,0:T(8,128)S(1)}, f32[256,128]{1,0:T(8,128)S(1)}, u32[]{:S(2)}, u32[]{:S(2)}) collective-permute-start(f32[256,128]{1,0:T(8,128)S(1)} %get-tuple-element.353), channel_id=1, source_target_pairs={{48,0},{56,8},{64,16},{72,24},{80,32},{88,40},{96,48},{104,56},{11... | collective-permute-start | bytes 393224 | tf_op jit(solution)/shard_map/ppermute | solution.py:15
  189.6 21.5 %collective-permute-start.22 = (f32[256,128]{1,0:T(8,128)}, f32[256,128]{1,0:T(8,128)S(1)}, u32[]{:S(2)}, u32[]{:S(2)}) collective-permute-start(f32[256,128]{1,0:T(8,128)} %get-tuple-element.354), channel_id=1, source_target_pairs={{56,0},{64,8},{72,16},{80,24},{88,32},{96,40},{104,48},{112,56},{1... | collective-permute-start | bytes 393224 | tf_op jit(solution)/shard_map/ppermute | solution.py:15
  191.5 35.9 %collective-permute-start.23 = (f32[256,128]{1,0:T(8,128)}, f32[256,128]{1,0:T(8,128)S(1)}, u32[]{:S(2)}, u32[]{:S(2)}) collective-permute-start(f32[256,128]{1,0:T(8,128)} %get-tuple-element.355), channel_id=1, source_target_pairs={{64,0},{72,8},{80,16},{88,24},{96,32},{104,40},{112,48},{120,56},{... | collective-permute-start | bytes 393224 | tf_op jit(solution)/shard_map/ppermute | solution.py:15
  193.8 37.3 %collective-permute-start.27 = (f32[256,128]{1,0:T(8,128)}, f32[256,128]{1,0:T(8,128)S(1)}, u32[]{:S(2)}, u32[]{:S(2)}) collective-permute-start(f32[256,128]{1,0:T(8,128)} %get-tuple-element.359), channel_id=1, source_target_pairs={{32,0},{40,8},{48,16},{56,24},{64,32},{72,40},{80,48},{88,56},{96,... | collective-permute-start | bytes 393224 | tf_op jit(solution)/shard_map/ppermute | solution.py:15
  206.9 24.2 %collective-permute-start.28 = (f32[256,128]{1,0:T(8,128)}, f32[256,128]{1,0:T(8,128)S(1)}, u32[]{:S(2)}, u32[]{:S(2)}) collective-permute-start(f32[256,128]{1,0:T(8,128)} %get-tuple-element.360), channel_id=1, source_target_pairs={{40,0},{48,8},{56,16},{64,24},{72,32},{80,40},{88,48},{96,56},{104... | collective-permute-start | bytes 393224 | tf_op jit(solution)/shard_map/ppermute | solution.py:15
  208.8 22.2 %collective-permute-start.29 = (f32[256,128]{1,0:T(8,128)S(1)}, f32[256,128]{1,0:T(8,128)S(1)}, u32[]{:S(2)}, u32[]{:S(2)}) collective-permute-start(f32[256,128]{1,0:T(8,128)S(1)} %get-tuple-element.361), channel_id=1, source_target_pairs={{48,0},{56,8},{64,16},{72,24},{80,32},{88,40},{96,48},{104,56},{11... | collective-permute-start | bytes 393224 | tf_op jit(solution)/shard_map/ppermute | solution.py:15
  211.0 20.0 %collective-permute-start.30 = (f32[256,128]{1,0:T(8,128)}, f32[256,128]{1,0:T(8,128)S(1)}, u32[]{:S(2)}, u32[]{:S(2)}) collective-permute-start(f32[256,128]{1,0:T(8,128)} %get-tuple-element.362), channel_id=1, source_target_pairs={{56,0},{64,8},{72,16},{80,24},{88,32},{96,40},{104,48},{112,56},{1... | collective-permute-start | bytes 393224 | tf_op jit(solution)/shard_map/ppermute | solution.py:15
  227.4 15.3 %collective-permute-start.31 = (f32[256,128]{1,0:T(8,128)}, f32[256,128]{1,0:T(8,128)S(1)}, u32[]{:S(2)}, u32[]{:S(2)}) collective-permute-start(f32[256,128]{1,0:T(8,128)} %get-tuple-element.363), channel_id=1, source_target_pairs={{64,0},{72,8},{80,16},{88,24},{96,32},{104,40},{112,48},{120,56},{... | collective-permute-start | bytes 393224 | tf_op jit(solution)/shard_map/ppermute | solution.py:15
  (76 other events, 757.4 us)
where the time goes:
time: 247 us; the launch traced here: 244 us
  starting transfers between devices  96.3 us (39%)
  waiting for transfers between devices  70.4 us (29%)
  local copies, waits for them, and re-layouts  36.3 us (15%)
  matrix products  16.1 us (7%)
  other arithmetic  12.6 us (5%)
  between operations  12 us (5%)
    ppermute x32, starting transfers between devices, from_behind(): return lax.ppermute(block, axis, route)  96.3 us
    ppermute x32, waiting for transfers between devices, from_behind(): return lax.ppermute(block, axis, route)  70.4 us
    unnamed x134, local copies, waits for them, and re-layouts  11.9 us
    another operation x21, local copies, waits for them, and re-layouts  11.4 us
    slice x9, local copies, waits for them, and re-layouts, body(): valid = (place >= distance) & (key_docs[rows - 1] == own_docs[0])  5.45 us
  transfers between devices with their start and end apart: 32, of which 17 were waited for; matrix products, arithmetic and copies ran while one was open for 17% of the time, Pallas kernels for 0%

commit v1 on v0

v1 whole, which is shorter than its diff:
```python
import functools
import math

import jax
import jax.numpy as jnp
from jax import lax
from jax.experimental import pallas as pl
from jax.experimental.pallas import tpu as pltpu
from jax.sharding import PartitionSpec as P

T = 256
D = 128
H = 4
ROW = 4
F32 = jnp.float32
BF16 = jnp.bfloat16
NEG = -1e30
SCALE = D**-0.5
TO_EXP2 = SCALE * math.log2(math.e)
LONG = (((1,), (1,)), ((), ()))
PLAIN = (((1,), (0,)), ((), ()))
VM = pl.BlockSpec(memory_space=pltpu.VMEM)
SM = pl.BlockSpec(memory_space=pltpu.SMEM)


def dot(a, b, dims):
    return lax.dot_general(a, b, dims, preferred_element_type=F32)


def head(ref, h):
    return ref[:, h * D : (h + 1) * D]


def doc_starts(lengths_ref, first):
    place = first + lax.broadcasted_iota(jnp.int32, (1, T), 1)
    start = jnp.int32(0)
    own = jnp.zeros((1, T), jnp.int32)
    for i in range(lengths_ref.shape[0]):
        own = jnp.where(place >= start, start, own)
        start = start + lengths_ref[i]
    return own


def scores(q_ref, g_ref, key, value, hidden, index, p_ref, dp_ref, m_ref, t_ref, r_ref):
    for h in range(H):
        s = dot(key, head(q_ref, h), LONG)
        dp = dot(value, head(g_ref, h), LONG)
        s = jnp.where(hidden, NEG, s)
        m = jnp.max(s, axis=0, keepdims=True)
        p = jnp.exp2((s - m) * TO_EXP2)
        p_ref[index, h] = p
        dp_ref[index, h] = dp
        m_ref[index, h : h + 1] = m
        t_ref[index, h : h + 1] = jnp.sum(p, axis=0, keepdims=True)
        r_ref[index, h : h + 1] = jnp.sum(p * dp, axis=0, keepdims=True)


def near_kernel(lengths_ref, q_ref, g_ref, k_ref, v_ref, z1_ref, z2_ref, p_ref, dp_ref, m_ref, t_ref, r_ref):
    first = lax.axis_index("peer") * T
    starts = doc_starts(lengths_ref, first)
    rows = lax.broadcasted_iota(jnp.int32, (T, 1), 0)
    out = (p_ref, dp_ref, m_ref, t_ref, r_ref)
    ahead = rows > lax.broadcasted_iota(jnp.int32, (1, T), 1)
    hidden = ((rows + first) < starts) | ahead
    scores(q_ref, g_ref, k_ref[...], v_ref[...], hidden, 0, *out)
    for i, ref in ((1, z1_ref), (2, z2_ref)):
        hidden = (rows + (first - i * ROW * T)) < starts
        scores(q_ref, g_ref, ref[:, :D], ref[:, D:], hidden, i, *out)


def slot(i, x):
    column = lax.rem(x + 1 + i // 2, ROW)
    kind = lax.rem(i, 2)
    behind = x - column + jnp.where(kind == 1, ROW, jnp.where(column < x, 0, 2 * ROW))
    return column, kind, behind


def far_kernel(
    lengths_ref, q_ref, g_ref, far_ref, m_in, t_in, r_in,
    back_ref, pb_ref, ds_ref, w_ref, rd_ref,
    p_ref, dp_ref, m_ref, t_ref, r_ref,
):
    peer = lax.axis_index("peer")
    x = lax.rem(peer, ROW)
    first = peer * T
    starts = doc_starts(lengths_ref, first)
    rows = lax.broadcasted_iota(jnp.int32, (T, 1), 0)

    @pl.loop(0, 6)
    def _(i):
        column, kind, behind = slot(i, x)
        hidden = (rows + (first - behind * T)) < starts
        key, value = far_ref[column, kind, :, :D], far_ref[column, kind, :, D:]
        scores(q_ref, g_ref, key, value, hidden, i, p_ref, dp_ref, m_ref, t_ref, r_ref)

    peaks = [m_in[b] for b in range(3)] + [m_ref[b] for b in range(6)]
    totals = [t_in[b] for b in range(3)] + [t_ref[b] for b in range(6)]
    dots = [r_in[b] for b in range(3)] + [r_ref[b] for b in range(6)]
    peak = functools.reduce(jnp.maximum, peaks)
    factors = [jnp.exp2((m - peak) * TO_EXP2) for m in peaks]
    over = 1.0 / sum(f * t for f, t in zip(factors, totals))
    rd_ref[...] = sum(f * r for f, r in zip(factors, dots)) * over
    for b in range(9):
        w_ref[b] = factors[b] * over

    @pl.loop(0, 6)
    def _(i):
        column, kind, _ = slot(i, x)
        dk = jnp.zeros((T, D), F32)
        dv = jnp.zeros((T, D), F32)
        for h in range(H):
            pn = p_ref[i, h] * w_ref[3 + i, h : h + 1]
            ds = (pn * (dp_ref[i, h] - rd_ref[h : h + 1])).astype(BF16)
            pb = pn.astype(BF16)
            pb_ref[i, h] = pb
            ds_ref[i, h] = ds
            dk += dot(ds, head(q_ref, h), PLAIN)
            dv += dot(pb, head(g_ref, h), PLAIN)
        back_ref[column, kind, :, :D] = (dk * SCALE).astype(BF16)
        back_ref[column, kind, :, D:] = dv.astype(BF16)

    back_ref[x] = jnp.zeros((2, T, 2 * D), BF16)


def rest_kernel(
    q_ref, g_ref, k_ref, v_ref, z1_ref, z2_ref, far_ref, p_ref, dp_ref, pb_ref, ds_ref, w_ref, rd_ref,
    out_ref, dq_ref, near_ref, o_acc, dq_acc,
):
    x = lax.rem(lax.axis_index("peer"), ROW)
    for b in range(3):
        key = (k_ref[...], z1_ref[:, :D], z2_ref[:, :D])[b]
        value = (v_ref[...], z1_ref[:, D:], z2_ref[:, D:])[b]
        kt, vt = key.T, value.T
        dk = jnp.zeros((T, D), F32)
        dv = jnp.zeros((T, D), F32)
        for h in range(H):
            pn = p_ref[b, h] * w_ref[b, h : h + 1]
            ds = (pn * (dp_ref[b, h] - rd_ref[h : h + 1])).astype(BF16)
            pb = pn.astype(BF16)
            dk += dot(ds, head(q_ref, h), PLAIN)
            dv += dot(pb, head(g_ref, h), PLAIN)
            o, dq = dot(vt, pb, PLAIN), dot(kt, ds, PLAIN)
            o_acc[h] = o if b == 0 else o_acc[h] + o
            dq_acc[h] = dq if b == 0 else dq_acc[h] + dq
        near_ref[b, :, :D] = dk * SCALE
        near_ref[b, :, D:] = dv

    @pl.loop(0, 6)
    def _(i):
        column, kind, _ = slot(i, x)
        kt, vt = far_ref[column, kind, :, :D].T, far_ref[column, kind, :, D:].T
        for h in range(H):
            o_acc[h] += dot(vt, pb_ref[i, h], PLAIN)
            dq_acc[h] += dot(kt, ds_ref[i, h], PLAIN)

    for h in range(H):
        out_ref[:, h * D : (h + 1) * D] = o_acc[h].T.astype(BF16)
        dq_ref[:, h * D : (h + 1) * D] = dq_acc[h].T * SCALE


def gather_kernel(got_ref, near_ref, own_ref, one_ref, two_ref):
    x = lax.rem(lax.axis_index("peer"), ROW)
    own, one, two = near_ref[0], near_ref[1], near_ref[2]
    for s in range(ROW):
        a, b = got_ref[s, 0].astype(F32), got_ref[s, 1].astype(F32)
        own += jnp.where(s > x, a, 0.0)
        two += jnp.where(s < x, a, 0.0)
        one += jnp.where(s != x, b, 0.0)
    own_ref[...] = own
    one_ref[...] = one.astype(BF16)
    two_ref[...] = two.astype(BF16)


def along_z(block, rows, peers):
    far = rows * ROW
    return lax.ppermute(block, "peer", [(i, i + far) for i in range(peers) if 0 <= i + far < peers])


def call(kernel, out, specs, scratch=(), blocks=0, limit=24):
    return pl.pallas_call(
        kernel,
        out_shape=out,
        in_specs=specs,
        out_specs=tuple(VM for _ in out),
        scratch_shapes=list(scratch),
        compiler_params=pltpu.CompilerParams(vmem_limit_bytes=limit << 20),
        cost_estimate=pl.CostEstimate(
            flops=blocks * H * T * T * D * 4, bytes_accessed=4 << 20, transcendentals=blocks * H * T * T
        ),
    )


def body(queries, keys, values, grad_out, doc_lengths):
    peers = lax.axis_size("peer")
    x = lax.rem(lax.axis_index("peer"), ROW)
    groups = [[z * ROW + i for i in range(ROW)] for z in range(peers // ROW)]
    array = jax.ShapeDtypeStruct
    both = jnp.concatenate([keys, values], axis=1)
    z1 = along_z(both, 1, peers)
    z2 = along_z(both, 2, peers)
    sent = jnp.stack([jnp.stack([jnp.where(t > x, both, z2), z1]) for t in range(ROW)])
    far = lax.all_to_all(sent, "peer", 0, 0, axis_index_groups=groups)
    stats = (H, T)
    p, dp, m, t, r = call(
        near_kernel,
        (array((3, H, T, T), F32),) * 2 + (array((3, *stats), F32),) * 3,
        [SM] + [VM] * 6,
        blocks=3,
        limit=16,
    )(doc_lengths, queries, grad_out, keys, values, z1, z2)
    back, pb, ds, w, rd = call(
        far_kernel,
        (
            array((ROW, 2, T, 2 * D), BF16),
            array((6, H, T, T), BF16),
            array((6, H, T, T), BF16),
            array((9, *stats), F32),
            array(stats, F32),
        ),
        [SM] + [VM] * 6,
        [pltpu.VMEM((6, H, T, T), F32)] * 2 + [pltpu.VMEM((6, *stats), F32)] * 3,
        blocks=6,
        limit=32,
    )(doc_lengths, queries, grad_out, far, m, t, r)
    got = lax.all_to_all(back, "peer", 0, 0, axis_index_groups=groups)
    attended, query_grad, near = call(
        rest_kernel,
        (array((T, H * D), BF16), array((T, H * D), F32), array((3, T, 2 * D), F32)),
        [VM] * 13,
        [pltpu.VMEM((H, D, T), F32)] * 2,
        blocks=9,
        limit=32,
    )(queries, grad_out, keys, values, z1, z2, far, p, dp, pb, ds, w, rd)
    own, one, two = call(
        gather_kernel,
        (array((T, 2 * D), F32), array((T, 2 * D), BF16), array((T, 2 * D), BF16)),
        [VM] * 2,
        limit=8,
    )(got, near)
    total = own + along_z(one, -1, peers).astype(F32) + along_z(two, -2, peers).astype(F32)
    return attended, query_grad, total[:, :D], total[:, D:]


def solution(mesh):
    tokens = P("peer", "head")
    return jax.shard_map(
        body,
        mesh=mesh,
        in_specs=(tokens, tokens, tokens, tokens, P()),
        out_specs=(tokens, tokens, tokens, tokens),
        check_vma=False,
    )
```

time: 247 us -> 83.6 us (0.34)
  the two profiles are of different devices: /device:TPU:128 before, /device:TPU:122 now
where the time goes in v1:
time: 83.6 us; the launch traced here: 82.9 us
  starting transfers between devices  23.8 us (28%)
  waiting for transfers between devices  23.5 us (28%)
  local copies, waits for them, and re-layouts  19 us (23%)
  Pallas kernels  14.6 us (17%)
  other arithmetic  1.26 us (2%)
    unnamed x33, local copies, waits for them, and re-layouts  17.5 us
    ppermute x4, waiting for transfers between devices, along_z(): lax.ppermute(block, 'peer', [(i, i + far) for i in range(peers) if 0 <= i...  15.7 us
    ppermute x4, starting transfers between devices, along_z(): lax.ppermute(block, 'peer', [(i, i + far) for i in range(peers) if 0 <= i...  14.1 us
    all_to_all x1, waiting for transfers between devices, body(): far = lax.all_to_all(sent, 'peer', 0, 0, axis_index_groups=groups)  7.78 us
    pallas_call x1, Pallas kernels, body(): call(far_kernel, (array((ROW, 2, T, 2 * D), BF16), array((6, H, T, T), BF...  7.71 us
    all_to_all x1, starting transfers between devices, body(): got = lax.all_to_all(back, 'peer', 0, 0, axis_index_groups=groups)  4.95 us
    all_to_all x1, starting transfers between devices, body(): far = lax.all_to_all(sent, 'peer', 0, 0, axis_index_groups=groups)  4.82 us
    pallas_call x1, Pallas kernels, body(): call(rest_kernel, (array((T, H * D), BF16), array((T, H * D), F32), array...  4.68 us
  transfers between devices with their start and end apart: 6, of which 5 were waited for; matrix products, arithmetic and copies ran while one was open for 0% of the time, Pallas kernels for 8%

profile of v1, /device:TPU:122, one launch (start us, length us, event | category | flops | bytes accessed | tf_op | source)
XLA Modules:
  0.0 82.9 jit_solution(7360143609136906190)
XLA Ops:
  0.6 0.9 %constant_dynamic-update-slice_fusion.1 = bf16[256,256]{1,0:T(8,128)(2,1)S(1)} fusion(bf16[256,128]{1,0:T(8,128)(2,1)} %k_ref.3), kind=kLoop, calls=%fused_computation.15 | loop fusion | bytes 131072
  1.5 0.9 %constant_dynamic-update-slice_fusion = bf16[256,256]{1,0:T(8,128)(2,1)S(1)} fusion(bf16[256,256]{1,0:T(8,128)(2,1)S(1)} %constant_dynamic-update-slice_fusion.1, bf16[256,128]{1,0:T(8,128)(2,1)} %v_ref.3), kind=kLoop, calls=%fused_computation.14 | loop fusion | bytes 131072 | tf_op jit(solution)/shard_map/concatenate | solution.py:198
  2.3 6.4 %collective-permute-start.1 = (bf16[256,256]{1,0:T(8,128)(2,1)S(1)}, bf16[256,256]{1,0:T(8,128)(2,1)S(1)}, u32[]{:S(2)}, u32[]{:S(2)}) collective-permute-start(bf16[256,256]{1,0:T(8,128)(2,1)S(1)} %constant_dynamic-update-slice_fusion), channel_id=1, source_target_pairs={{0,64},{8,72},{16,80},{24,88},{32,96},{40,104},{48,112},{56,120},{... | collective-permute-start | bytes 393224 | tf_op jit(solution)/shard_map/ppermute | solution.py:176
  8.7 3.8 %collective-permute-start = (bf16[256,256]{1,0:T(8,128)(2,1)S(1)}, bf16[256,256]{1,0:T(8,128)(2,1)S(1)}, u32[]{:S(2)}, u32[]{:S(2)}) collective-permute-start(bf16[256,256]{1,0:T(8,128)(2,1)S(1)} %constant_dynamic-update-slice_fusion), channel_id=1, source_target_pairs={{0,32},{8,40},{16,48},{24,56},{32,64},{40,72},{48,80},{56,88},{64,... | collective-permute-start | bytes 393224 | tf_op jit(solution)/shard_map/ppermute | solution.py:176
  12.6 0.3 collective-permute-done.1.z2_ref
  12.9 0.0 copy-start.11
  13.0 4.6 %collective-permute-done.z1_ref = bf16[256,256]{1,0:T(8,128)(2,1)S(1)} collective-permute-done((bf16[256,256]{1,0:T(8,128)(2,1)S(1)}, bf16[256,256]{1,0:T(8,128)(2,1)S(1)}, u32[]{:S(2)}, u32[]{:S(2)}) %collective-permute-start) | collective-permute-done | bytes 131104 | tf_op jit(solution)/shard_map/ppermute | solution.py:176
  17.6 0.1 fusion
  17.7 1.1 %pad_maximum_fusion = bf16[4,2,256,256]{3,2,1,0:T(8,128)(2,1)} fusion(bf16[1,2,256,256]{3,2,1,0:T(8,128)(2,1)S(1)} %get-tuple-element.45, bf16[1,2,256,256]{3,2,1,0:T(8,128)(2,1)S(1)} %get-tuple-element.44, bf16[1,2,256,256]{3,2,1,0:T(8,128)(2,1)S(1)} %get-tuple-element.43, bf16[1,2,256,256]{3,2,1,0:T(8,128)(2,1)S(1)} %get-tuple-element.42), kind=kLoop, calls=%fused_computation | loop fusion | flops 1572864 | bytes 2097152 | tf_op jit(solution)/shard_map/stack | solution.py:201
  18.8 4.8 %all-to-all-start = ((bf16[4,2,256,256]{3,2,1,0:T(8,128)(2,1)}), bf16[4,2,256,256]{3,2,1,0:T(8,128)(2,1)S(1)}, u32[]{:S(2)}, u32[]{:S(2)}) async-start(bf16[4,2,256,256]{3,2,1,0:T(8,128)(2,1)} %pad_maximum_fusion), calls=%async_computation | async-start | bytes 2097152 | tf_op jit(solution)/shard_map/all_to_all | solution.py:202
  23.6 1.9 %shard_map.84 = (f32[3,4,256,256]{3,2,1,0:T(8,128)S(1)}, f32[3,4,256,256]{3,2,1,0:T(8,128)S(1)}, f32[3,4,256]{2,1,0:T(4,128)S(1)}, f32[3,4,256]{2,1,0:T(4,128)S(1)}, f32[3,4,256]{2,1,0:T(4,128)S(1)}) custom-call(s32[32]{0:T(128)S(1)} %copy-done.15, bf16[256,512]{1,0:T(8,128)(2,1)S(1)} %copy-done.8, bf16[256,512]{1,0:T(8,128)(2,1)S(1)} %copy-done.9, ...), custom_call_target="tpu_custom_call" | custom-call | flops 402653184 | bytes 4194304 | tf_op jit(solution)/shard_map/pallas_call | solution.py:204
  25.6 1.6 %copy-done = f32[3,4,256,256]{3,2,1,0:T(8,128)} copy-done((f32[3,4,256,256]{3,2,1,0:T(8,128)}, f32[3,4,256,256]{3,2,1,0:T(8,128)S(1)}, u32[]{:S(2)}) %copy-start) | copy-done | bytes 3145752
  27.2 1.7 %copy-done.2 = f32[3,4,256,256]{3,2,1,0:T(8,128)} copy-done((f32[3,4,256,256]{3,2,1,0:T(8,128)}, f32[3,4,256,256]{3,2,1,0:T(8,128)S(1)}, u32[]{:S(2)}) %copy-start.2) | copy-done | bytes 3145752
  28.8 7.8 %all-to-all-done.far_ref = bf16[4,2,256,256]{3,2,1,0:T(8,128)(2,1)S(1)} async-done(((bf16[4,2,256,256]{3,2,1,0:T(8,128)(2,1)}), bf16[4,2,256,256]{3,2,1,0:T(8,128)(2,1)S(1)}, u32[]{:S(2)}, u32[]{:S(2)}) %all-to-all-start) | async-done | bytes 1048608 | tf_op jit(solution)/shard_map/all_to_all | solution.py:202
  36.6 7.7 %shard_map.85 = (bf16[4,2,256,256]{3,2,1,0:T(8,128)(2,1)}, bf16[6,4,256,256]{3,2,1,0:T(8,128)(2,1)S(1)}, bf16[6,4,256,256]{3,2,1,0:T(8,128)(2,1)S(1)}, f32[9,4,256]{2,1,0:T(4,128)S(1)}, f32[4,256]{1,0:T(4,128)S(1)}) custom-call(s32[32]{0:T(128)S(1)} %copy-done.15, bf16[256,512]{1,0:T(8,128)(2,1)S(1)} %copy-done.8, bf16[256,512]{1,0:T(8,128)(2,1)S(1)} %copy-done.9, ...), custom_call_target="tpu_custom_call" | custom-call | flops 805306368 | bytes 4194304 | tf_op jit(solution)/shard_map/pallas_call | solution.py:211
  44.3 1.7 %copy-done.4 = bf16[6,4,256,256]{3,2,1,0:T(8,128)(2,1)} copy-done((bf16[6,4,256,256]{3,2,1,0:T(8,128)(2,1)}, bf16[6,4,256,256]{3,2,1,0:T(8,128)(2,1)S(1)}, u32[]{:S(2)}) %copy-start.4) | copy-done | bytes 3145752
  46.0 1.7 %copy-done.6 = bf16[6,4,256,256]{3,2,1,0:T(8,128)(2,1)} copy-done((bf16[6,4,256,256]{3,2,1,0:T(8,128)(2,1)}, bf16[6,4,256,256]{3,2,1,0:T(8,128)(2,1)S(1)}, u32[]{:S(2)}) %copy-start.6) | copy-done | bytes 3145752
  47.7 0.6 copy-done.13
  48.3 4.9 %all-to-all-start.1 = ((bf16[4,2,256,256]{3,2,1,0:T(8,128)(2,1)}), bf16[4,2,256,256]{3,2,1,0:T(8,128)(2,1)S(1)}, u32[]{:S(2)}, u32[]{:S(2)}) async-start(bf16[4,2,256,256]{3,2,1,0:T(8,128)(2,1)} %get-tuple-element.31), calls=%async_computation.1 | async-start | bytes 2097152 | tf_op jit(solution)/shard_map/all_to_all | solution.py:225
  53.3 1.9 %copy-done.1 = f32[3,4,256,256]{3,2,1,0:T(8,128)S(1)} copy-done((f32[3,4,256,256]{3,2,1,0:T(8,128)S(1)}, f32[3,4,256,256]{3,2,1,0:T(8,128)}, u32[]{:S(2)}) %copy-start.1) | copy-done | bytes 3145752
  55.2 1.9 %copy-done.3 = f32[3,4,256,256]{3,2,1,0:T(8,128)S(1)} copy-done((f32[3,4,256,256]{3,2,1,0:T(8,128)S(1)}, f32[3,4,256,256]{3,2,1,0:T(8,128)}, u32[]{:S(2)}) %copy-start.3) | copy-done | bytes 3145752
  57.1 1.9 %copy-done.5 = bf16[6,4,256,256]{3,2,1,0:T(8,128)(2,1)S(1)} copy-done((bf16[6,4,256,256]{3,2,1,0:T(8,128)(2,1)S(1)}, bf16[6,4,256,256]{3,2,1,0:T(8,128)(2,1)}, u32[]{:S(2)}) %copy-start.5) | copy-done | bytes 3145752
  59.0 1.9 %copy-done.7 = bf16[6,4,256,256]{3,2,1,0:T(8,128)(2,1)S(1)} copy-done((bf16[6,4,256,256]{3,2,1,0:T(8,128)(2,1)S(1)}, bf16[6,4,256,256]{3,2,1,0:T(8,128)(2,1)}, u32[]{:S(2)}) %copy-start.7) | copy-done | bytes 3145752
  60.9 0.9 %copy-done.10 = bf16[256,512]{1,0:T(8,128)(2,1)S(1)} copy-done((bf16[256,512]{1,0:T(8,128)(2,1)S(1)}, bf16[256,512]{1,0:T(8,128)(2,1)}, u32[]{:S(2)}) %copy-start.10) | copy-done | bytes 262168
  61.8 0.8 copy-done.14
  62.6 4.7 %shard_map.86 = (bf16[256,512]{1,0:T(8,128)(2,1)}, f32[256,512]{1,0:T(8,128)}, f32[3,256,256]{2,1,0:T(8,128)S(1)}) custom-call(bf16[256,512]{1,0:T(8,128)(2,1)S(1)} %copy-done.8, bf16[256,512]{1,0:T(8,128)(2,1)S(1)} %copy-done.10, bf16[256,128]{1,0:T(8,128)(2,1)S(1)} %copy-done.11, bf16[256,128]{1,0:T(8,128)(2,1)S(1)} %copy-done.12, ...), custom_call_target="tpu_custom_call" | custom-call | flops 1207959552 | bytes 4194304 | tf_op jit(solution)/shard_map/pallas_call | solution.py:226
  67.3 0.3 shard_map.87
  67.6 1.9 %collective-permute-start.2 = (bf16[256,256]{1,0:T(8,128)(2,1)S(1)}, bf16[256,256]{1,0:T(8,128)(2,1)S(1)}, u32[]{:S(2)}, u32[]{:S(2)}) collective-permute-start(bf16[256,256]{1,0:T(8,128)(2,1)S(1)} %get-tuple-element.34), channel_id=1, source_target_pairs={{32,0},{40,8},{48,16},{56,24},{64,32},{72,40},{80,48},{88,56},{96,... | collective-permute-start | bytes 393224 | tf_op jit(solution)/shard_map/ppermute | solution.py:176
  69.5 1.9 %collective-permute-start.3 = (bf16[256,256]{1,0:T(8,128)(2,1)S(1)}, bf16[256,256]{1,0:T(8,128)(2,1)S(1)}, u32[]{:S(2)}, u32[]{:S(2)}) collective-permute-start(bf16[256,256]{1,0:T(8,128)(2,1)S(1)} %get-tuple-element.35), channel_id=1, source_target_pairs={{64,0},{72,8},{80,16},{88,24},{96,32},{104,40},{112,48},{120,56},{... | collective-permute-start | bytes 393224 | tf_op jit(solution)/shard_map/ppermute | solution.py:176
  71.4 6.6 %collective-permute-done.2 = bf16[256,256]{1,0:T(8,128)(2,1)S(1)} collective-permute-done((bf16[256,256]{1,0:T(8,128)(2,1)S(1)}, bf16[256,256]{1,0:T(8,128)(2,1)S(1)}, u32[]{:S(2)}, u32[]{:S(2)}) %collective-permute-start.2) | collective-permute-done | bytes 131104 | tf_op jit(solution)/shard_map/ppermute | solution.py:176
  78.0 4.2 %collective-permute-done.3 = bf16[256,256]{1,0:T(8,128)(2,1)S(1)} collective-permute-done((bf16[256,256]{1,0:T(8,128)(2,1)S(1)}, bf16[256,256]{1,0:T(8,128)(2,1)S(1)}, u32[]{:S(2)}, u32[]{:S(2)}) %collective-permute-start.3) | collective-permute-done | bytes 131104 | tf_op jit(solution)/shard_map/ppermute | solution.py:176
  82.2 0.7 fusion.4
  (23 shorter events, 0.1 us)
Async XLA Ops:
  2.3 10.5 %collective-permute-start.1 = (bf16[256,256]{1,0:T(8,128)(2,1)S(1)}, bf16[256,256]{1,0:T(8,128)(2,1)S(1)}, u32[]{:S(2)}, u32[]{:S(2)}) collective-permute-start(bf16[256,256]{1,0:T(8,128)(2,1)S(1)} %constant_dynamic-update-slice_fusion), channel_id=1, source_target_pairs={{0,64},{8,72},{16,80},{24,88},{32,96},{40,104},{48,112},{56,120},{... | collective-permute-start | bytes 393224 | tf_op jit(solution)/shard_map/ppermute | solution.py:176
  8.7 8.9 %collective-permute-start = (bf16[256,256]{1,0:T(8,128)(2,1)S(1)}, bf16[256,256]{1,0:T(8,128)(2,1)S(1)}, u32[]{:S(2)}, u32[]{:S(2)}) collective-permute-start(bf16[256,256]{1,0:T(8,128)(2,1)S(1)} %constant_dynamic-update-slice_fusion), channel_id=1, source_target_pairs={{0,32},{8,40},{16,48},{24,56},{32,64},{40,72},{48,80},{56,88},{64,... | collective-permute-start | bytes 393224 | tf_op jit(solution)/shard_map/ppermute | solution.py:176
  12.9 10.7 %copy-start.8 = (bf16[256,512]{1,0:T(8,128)(2,1)S(1)}, bf16[256,512]{1,0:T(8,128)(2,1)}, u32[]{:S(2)}) copy-start(bf16[256,512]{1,0:T(8,128)(2,1)} %q_ref.5) | copy-start | bytes 786436
  12.9 10.7 %copy-start.9 = (bf16[256,512]{1,0:T(8,128)(2,1)S(1)}, bf16[256,512]{1,0:T(8,128)(2,1)}, u32[]{:S(2)}) copy-start(bf16[256,512]{1,0:T(8,128)(2,1)} %g_ref.5) | copy-start | bytes 786436
  12.9 10.7 %copy-start.11 = (bf16[256,128]{1,0:T(8,128)(2,1)S(1)}, bf16[256,128]{1,0:T(8,128)(2,1)}, u32[]{:S(2)}) copy-start(bf16[256,128]{1,0:T(8,128)(2,1)} %k_ref.3) | copy-start | bytes 196612
  13.0 10.7 %copy-start.12 = (bf16[256,128]{1,0:T(8,128)(2,1)S(1)}, bf16[256,128]{1,0:T(8,128)(2,1)}, u32[]{:S(2)}) copy-start(bf16[256,128]{1,0:T(8,128)(2,1)} %v_ref.3) | copy-start | bytes 196612
  13.0 10.7 %copy-start.15 = (s32[32]{0:T(128)S(1)}, s32[32]{0:T(128)}, u32[]{:S(2)}) copy-start(s32[32]{0:T(128)} %lengths_ref.3) | copy-start | bytes 388
  18.8 17.8 %all-to-all-start = ((bf16[4,2,256,256]{3,2,1,0:T(8,128)(2,1)}), bf16[4,2,256,256]{3,2,1,0:T(8,128)(2,1)S(1)}, u32[]{:S(2)}, u32[]{:S(2)}) async-start(bf16[4,2,256,256]{3,2,1,0:T(8,128)(2,1)} %pad_maximum_fusion), calls=%async_computation | async-start | bytes 2097152 | tf_op jit(solution)/shard_map/all_to_all | solution.py:202
  25.5 1.6 %copy-start = (f32[3,4,256,256]{3,2,1,0:T(8,128)}, f32[3,4,256,256]{3,2,1,0:T(8,128)S(1)}, u32[]{:S(2)}) copy-start(f32[3,4,256,256]{3,2,1,0:T(8,128)S(1)} %get-tuple-element.20.p_ref) | copy-start | bytes 9437188
  27.2 1.7 %copy-start.2 = (f32[3,4,256,256]{3,2,1,0:T(8,128)}, f32[3,4,256,256]{3,2,1,0:T(8,128)S(1)}, u32[]{:S(2)}) copy-start(f32[3,4,256,256]{3,2,1,0:T(8,128)S(1)} %get-tuple-element.21.dp_ref) | copy-start | bytes 9437188
  44.3 1.7 %copy-start.4 = (bf16[6,4,256,256]{3,2,1,0:T(8,128)(2,1)}, bf16[6,4,256,256]{3,2,1,0:T(8,128)(2,1)S(1)}, u32[]{:S(2)}) copy-start(bf16[6,4,256,256]{3,2,1,0:T(8,128)(2,1)S(1)} %get-tuple-element.25.pb_ref) | copy-start | bytes 9437188
  46.0 1.7 %copy-start.6 = (bf16[6,4,256,256]{3,2,1,0:T(8,128)(2,1)}, bf16[6,4,256,256]{3,2,1,0:T(8,128)(2,1)S(1)}, u32[]{:S(2)}) copy-start(bf16[6,4,256,256]{3,2,1,0:T(8,128)(2,1)S(1)} %get-tuple-element.26.ds_ref) | copy-start | bytes 9437188
  47.7 0.6 copy-start.13
  48.3 18.9 %all-to-all-start.1 = ((bf16[4,2,256,256]{3,2,1,0:T(8,128)(2,1)}), bf16[4,2,256,256]{3,2,1,0:T(8,128)(2,1)S(1)}, u32[]{:S(2)}, u32[]{:S(2)}) async-start(bf16[4,2,256,256]{3,2,1,0:T(8,128)(2,1)} %get-tuple-element.31), calls=%async_computation.1 | async-start | bytes 2097152 | tf_op jit(solution)/shard_map/all_to_all | solution.py:225
  53.3 1.9 %copy-start.1 = (f32[3,4,256,256]{3,2,1,0:T(8,128)S(1)}, f32[3,4,256,256]{3,2,1,0:T(8,128)}, u32[]{:S(2)}) copy-start(f32[3,4,256,256]{3,2,1,0:T(8,128)} %copy-done) | copy-start | bytes 9437188
  55.2 1.9 %copy-start.3 = (f32[3,4,256,256]{3,2,1,0:T(8,128)S(1)}, f32[3,4,256,256]{3,2,1,0:T(8,128)}, u32[]{:S(2)}) copy-start(f32[3,4,256,256]{3,2,1,0:T(8,128)} %copy-done.2) | copy-start | bytes 9437188
  57.1 1.9 %copy-start.5 = (bf16[6,4,256,256]{3,2,1,0:T(8,128)(2,1)S(1)}, bf16[6,4,256,256]{3,2,1,0:T(8,128)(2,1)}, u32[]{:S(2)}) copy-start(bf16[6,4,256,256]{3,2,1,0:T(8,128)(2,1)} %copy-done.4) | copy-start | bytes 9437188
  59.0 1.9 %copy-start.7 = (bf16[6,4,256,256]{3,2,1,0:T(8,128)(2,1)S(1)}, bf16[6,4,256,256]{3,2,1,0:T(8,128)(2,1)}, u32[]{:S(2)}) copy-start(bf16[6,4,256,256]{3,2,1,0:T(8,128)(2,1)} %copy-done.6) | copy-start | bytes 9437188
  60.9 0.9 %copy-start.10 = (bf16[256,512]{1,0:T(8,128)(2,1)S(1)}, bf16[256,512]{1,0:T(8,128)(2,1)}, u32[]{:S(2)}) copy-start(bf16[256,512]{1,0:T(8,128)(2,1)} %g_ref.5) | copy-start | bytes 786436
  61.8 0.8 copy-start.14
  67.6 10.4 %collective-permute-start.2 = (bf16[256,256]{1,0:T(8,128)(2,1)S(1)}, bf16[256,256]{1,0:T(8,128)(2,1)S(1)}, u32[]{:S(2)}, u32[]{:S(2)}) collective-permute-start(bf16[256,256]{1,0:T(8,128)(2,1)S(1)} %get-tuple-element.34), channel_id=1, source_target_pairs={{32,0},{40,8},{48,16},{56,24},{64,32},{72,40},{80,48},{88,56},{96,... | collective-permute-start | bytes 393224 | tf_op jit(solution)/shard_map/ppermute | solution.py:176
  69.5 12.7 %collective-permute-start.3 = (bf16[256,256]{1,0:T(8,128)(2,1)S(1)}, bf16[256,256]{1,0:T(8,128)(2,1)S(1)}, u32[]{:S(2)}, u32[]{:S(2)}) collective-permute-start(bf16[256,256]{1,0:T(8,128)(2,1)S(1)} %get-tuple-element.35), channel_id=1, source_target_pairs={{64,0},{72,8},{80,16},{88,24},{96,32},{104,40},{112,48},{120,56},{... | collective-permute-start | bytes 393224 | tf_op jit(solution)/shard_map/ppermute | solution.py:176

commit v2 on v1

v2 whole, which is shorter than its diff:
```python
import functools
import math

import jax
import jax.numpy as jnp
from jax import lax
from jax.experimental import pallas as pl
from jax.experimental.pallas import tpu as pltpu
from jax.sharding import PartitionSpec as P

T = 256
D = 128
H = 4
ROW = 4
F32 = jnp.float32
BF16 = jnp.bfloat16
NEG = -1e30
SCALE = D**-0.5
TO_EXP2 = SCALE * math.log2(math.e)
LONG = (((1,), (1,)), ((), ()))
PLAIN = (((1,), (0,)), ((), ()))
VM = pl.BlockSpec(memory_space=pltpu.VMEM)
SM = pl.BlockSpec(memory_space=pltpu.SMEM)


def dot(a, b, dims):
    return lax.dot_general(a, b, dims, preferred_element_type=F32)


def head(ref, h):
    return ref[:, h * D : (h + 1) * D]


def doc_starts(lengths_ref, first):
    place = first + lax.broadcasted_iota(jnp.int32, (1, T), 1)
    start = jnp.int32(0)
    own = jnp.zeros((1, T), jnp.int32)
    for i in range(lengths_ref.shape[0]):
        own = jnp.where(place >= start, start, own)
        start = start + lengths_ref[i]
    return own


def scores(q_ref, g_ref, key, value, hidden, index, m_ref, t_ref, r_ref, p_ref=None, dp_ref=None):
    for h in range(H):
        s = dot(key, head(q_ref, h), LONG)
        dp = dot(value, head(g_ref, h), LONG)
        s = jnp.where(hidden, NEG, s)
        m = jnp.max(s, axis=0, keepdims=True)
        p = jnp.exp2((s - m) * TO_EXP2)
        if p_ref is not None:
            p_ref[index, h] = p
            dp_ref[index, h] = dp
        m_ref[index, h : h + 1] = m
        t_ref[index, h : h + 1] = jnp.sum(p, axis=0, keepdims=True)
        r_ref[index, h : h + 1] = jnp.sum(p * dp, axis=0, keepdims=True)


def pair_kernel(k_ref, v_ref, out_ref):
    out_ref[0] = k_ref[...]
    out_ref[1] = v_ref[...]


def pack_kernel(own_ref, z1_ref, z2_ref, out_ref, sem):
    x = lax.rem(lax.axis_index("peer"), ROW)

    def fill(t, kind, ref):
        return pltpu.make_async_copy(ref, out_ref.at[t, kind], sem.at[t, kind])

    for t in range(ROW):
        fill(t, 1, z1_ref).start()

        @pl.when(t > x)
        def _(t=t):
            fill(t, 0, own_ref).start()

        @pl.when(t <= x)
        def _(t=t):
            fill(t, 0, z2_ref).start()

    for t in range(ROW):
        for kind in range(2):
            fill(t, kind, z1_ref).wait()


def near_hidden(first, starts, block):
    rows = lax.broadcasted_iota(jnp.int32, (T, 1), 0)
    hidden = (rows + (first - block * ROW * T)) < starts
    if block == 0:
        hidden = hidden | (rows > lax.broadcasted_iota(jnp.int32, (1, T), 1))
    return hidden


def far_hidden(first, starts, behind):
    rows = lax.broadcasted_iota(jnp.int32, (T, 1), 0)
    return (rows + (first - behind * T)) < starts


def near_kernel(lengths_ref, q_ref, g_ref, own_ref, z1_ref, z2_ref, m_ref, t_ref, r_ref):
    first = lax.axis_index("peer") * T
    starts = doc_starts(lengths_ref, first)
    for i, ref in enumerate((own_ref, z1_ref, z2_ref)):
        scores(q_ref, g_ref, ref[0], ref[1], near_hidden(first, starts, i), i, m_ref, t_ref, r_ref)


def slot(i, x):
    column = lax.rem(x + 1 + i // 2, ROW)
    kind = lax.rem(i, 2)
    behind = x - column + jnp.where(kind == 1, ROW, jnp.where(column < x, 0, 2 * ROW))
    return column, kind, behind


def far_kernel(
    lengths_ref, q_ref, g_ref, far_ref, m_in, t_in, r_in,
    back_ref, peak_ref, over_ref, rd_ref,
    p_ref, dp_ref, m_ref, t_ref, r_ref, w_ref,
):
    peer = lax.axis_index("peer")
    x = lax.rem(peer, ROW)
    first = peer * T
    starts = doc_starts(lengths_ref, first)

    @pl.loop(0, 6)
    def _(i):
        column, kind, behind = slot(i, x)
        hidden = far_hidden(first, starts, behind)
        key, value = far_ref[column, kind, 0], far_ref[column, kind, 1]
        scores(q_ref, g_ref, key, value, hidden, i, m_ref, t_ref, r_ref, p_ref, dp_ref)

    peaks = [m_in[b] for b in range(3)] + [m_ref[b] for b in range(6)]
    totals = [t_in[b] for b in range(3)] + [t_ref[b] for b in range(6)]
    dots = [r_in[b] for b in range(3)] + [r_ref[b] for b in range(6)]
    peak = functools.reduce(jnp.maximum, peaks)
    factors = [jnp.exp2((m - peak) * TO_EXP2) for m in peaks]
    over = 1.0 / sum(f * t for f, t in zip(factors, totals))
    peak_ref[...] = peak
    over_ref[...] = over
    rd_ref[...] = sum(f * r for f, r in zip(factors, dots)) * over
    for b in range(6):
        w_ref[b] = factors[3 + b] * over

    @pl.loop(0, 6)
    def _(i):
        column, kind, _ = slot(i, x)
        dk = jnp.zeros((T, D), F32)
        dv = jnp.zeros((T, D), F32)
        for h in range(H):
            pn = p_ref[i, h] * w_ref[i, h : h + 1]
            ds = (pn * (dp_ref[i, h] - rd_ref[h : h + 1])).astype(BF16)
            dk += dot(ds, head(q_ref, h), PLAIN)
            dv += dot(pn.astype(BF16), head(g_ref, h), PLAIN)
        back_ref[column, kind, 0] = (dk * SCALE).astype(BF16)
        back_ref[column, kind, 1] = dv.astype(BF16)

    back_ref[x] = jnp.zeros((2, 2, T, D), BF16)


def rest_kernel(
    lengths_ref, q_ref, g_ref, own_ref, z1_ref, z2_ref, far_ref, peak_ref, over_ref, rd_ref,
    out_ref, dq_ref, near_ref, o_acc, dq_acc,
):
    peer = lax.axis_index("peer")
    x = lax.rem(peer, ROW)
    first = peer * T
    starts = doc_starts(lengths_ref, first)

    def weights(key, value, hidden, h):
        s = dot(key, head(q_ref, h), LONG)
        dp = dot(value, head(g_ref, h), LONG)
        s = jnp.where(hidden, NEG, s)
        pn = jnp.exp2((s - peak_ref[h : h + 1]) * TO_EXP2) * over_ref[h : h + 1]
        ds = pn * (dp - rd_ref[h : h + 1])
        return pn.astype(BF16), ds.astype(BF16)

    for b, ref in enumerate((own_ref, z1_ref, z2_ref)):
        key, value = ref[0], ref[1]
        hidden = near_hidden(first, starts, b)
        kt, vt = key.T, value.T
        dk = jnp.zeros((T, D), F32)
        dv = jnp.zeros((T, D), F32)
        for h in range(H):
            pb, ds = weights(key, value, hidden, h)
            dk += dot(ds, head(q_ref, h), PLAIN)
            dv += dot(pb, head(g_ref, h), PLAIN)
            o, dq = dot(vt, pb, PLAIN), dot(kt, ds, PLAIN)
            o_acc[h] = o if b == 0 else o_acc[h] + o
            dq_acc[h] = dq if b == 0 else dq_acc[h] + dq
        near_ref[b, 0] = dk * SCALE
        near_ref[b, 1] = dv

    @pl.loop(0, 6)
    def _(i):
        column, kind, behind = slot(i, x)
        hidden = far_hidden(first, starts, behind)
        key, value = far_ref[column, kind, 0], far_ref[column, kind, 1]
        kt, vt = key.T, value.T
        for h in range(H):
            pb, ds = weights(key, value, hidden, h)
            o_acc[h] += dot(vt, pb, PLAIN)
            dq_acc[h] += dot(kt, ds, PLAIN)

    for h in range(H):
        out_ref[:, h * D : (h + 1) * D] = o_acc[h].T.astype(BF16)
        dq_ref[:, h * D : (h + 1) * D] = dq_acc[h].T * SCALE


def gather_kernel(got_ref, near_ref, own_ref, one_ref, two_ref):
    x = lax.rem(lax.axis_index("peer"), ROW)
    own, one, two = near_ref[0], near_ref[1], near_ref[2]
    for s in range(ROW):
        a, b = got_ref[s, 0].astype(F32), got_ref[s, 1].astype(F32)
        own += jnp.where(s > x, a, 0.0)
        two += jnp.where(s < x, a, 0.0)
        one += jnp.where(s != x, b, 0.0)
    own_ref[...] = own
    one_ref[...] = one.astype(BF16)
    two_ref[...] = two.astype(BF16)


def final_kernel(own_ref, one_ref, two_ref, dk_ref, dv_ref):
    dk_ref[...] = own_ref[0] + one_ref[0].astype(F32) + two_ref[0].astype(F32)
    dv_ref[...] = own_ref[1] + one_ref[1].astype(F32) + two_ref[1].astype(F32)


def along_z(block, rows, peers):
    far = rows * ROW
    return lax.ppermute(block, "peer", [(i, i + far) for i in range(peers) if 0 <= i + far < peers])


def call(kernel, out, specs, scratch=(), blocks=0, limit=24, space=VM):
    return pl.pallas_call(
        kernel,
        out_shape=out,
        in_specs=specs,
        out_specs=tuple(space for _ in out),
        scratch_shapes=list(scratch),
        compiler_params=pltpu.CompilerParams(vmem_limit_bytes=limit << 20),
        cost_estimate=pl.CostEstimate(
            flops=blocks * H * T * T * D * 4, bytes_accessed=1 << 20, transcendentals=blocks * H * T * T
        ),
    )


def body(queries, keys, values, grad_out, doc_lengths):
    peers = lax.axis_size("peer")
    groups = [[z * ROW + i for i in range(ROW)] for z in range(peers // ROW)]
    array = jax.ShapeDtypeStruct
    block, sums, stats = (2, T, D), array((2, T, D), F32), (H, T)
    (own,) = call(pair_kernel, (array(block, BF16),), [VM] * 2, limit=4)(keys, values)
    z1 = along_z(own, 1, peers)
    z2 = along_z(own, 2, peers)
    (sent,) = call(
        pack_kernel,
        (array((ROW, 2, *block), BF16),),
        [VM] * 3,
        [pltpu.SemaphoreType.DMA((ROW, 2))],
        limit=4,
        space=pl.BlockSpec(memory_space=pl.ANY),
    )(own, z1, z2)
    far = lax.all_to_all(sent, "peer", 0, 0, axis_index_groups=groups)
    m, t, r = call(near_kernel, (array((3, *stats), F32),) * 3, [SM] + [VM] * 5, blocks=3, limit=8)(
        doc_lengths, queries, grad_out, own, z1, z2
    )
    back, peak, over, rd = call(
        far_kernel,
        (array((ROW, 2, *block), BF16),) + (array(stats, F32),) * 3,
        [SM] + [VM] * 6,
        [pltpu.VMEM((6, H, T, T), F32)] * 2 + [pltpu.VMEM((6, *stats), F32)] * 4,
        blocks=6,
        limit=24,
    )(doc_lengths, queries, grad_out, far, m, t, r)
    got = lax.all_to_all(back, "peer", 0, 0, axis_index_groups=groups)
    attended, query_grad, near = call(
        rest_kernel,
        (array((T, H * D), BF16), array((T, H * D), F32), array((3, *block), F32)),
        [SM] + [VM] * 9,
        [pltpu.VMEM((H, D, T), F32)] * 2,
        blocks=9,
        limit=16,
    )(doc_lengths, queries, grad_out, own, z1, z2, far, peak, over, rd)
    mine, one, two = call(
        gather_kernel, (sums, array(block, BF16), array(block, BF16)), [VM] * 2, limit=8
    )(got, near)
    key_grad, value_grad = call(final_kernel, (array((T, D), F32),) * 2, [VM] * 3, limit=4)(
        mine, along_z(one, -1, peers), along_z(two, -2, peers)
    )
    return attended, query_grad, key_grad, value_grad


def solution(mesh):
    tokens = P("peer", "head")
    return jax.shard_map(
        body,
        mesh=mesh,
        in_specs=(tokens, tokens, tokens, tokens, P()),
        out_specs=(tokens, tokens, tokens, tokens),
        check_vma=False,
    )
```

time: 83.6 us -> 78.4 us (0.938)
  the two profiles are of different devices: /device:TPU:122 before, /device:TPU:120 now
where the time goes in v2:
time: 78.4 us; the launch traced here: 77.9 us
  waiting for transfers between devices  29 us (37%)
  Pallas kernels  23.5 us (30%)
  starting transfers between devices  22 us (28%)
  local copies, waits for them, and re-layouts  2.64 us (3%)
    ppermute x4, waiting for transfers between devices, along_z(): lax.ppermute(block, 'peer', [(i, i + far) for i in range(peers) if 0 <= i...  15.9 us
    ppermute x4, starting transfers between devices, along_z(): lax.ppermute(block, 'peer', [(i, i + far) for i in range(peers) if 0 <= i...  14.1 us
    all_to_all x1, waiting for transfers between devices, body(): far = lax.all_to_all(sent, 'peer', 0, 0, axis_index_groups=groups)  12.7 us
    pallas_call x1, Pallas kernels, body(): call(rest_kernel, (array((T, H * D), BF16), array((T, H * D), F32), array...  12 us
    pallas_call x1, Pallas kernels, body(): call(far_kernel, (array((ROW, 2, *block), BF16),) + (array(stats, F32),)...  7.56 us
    all_to_all x1, starting transfers between devices, body(): far = lax.all_to_all(sent, 'peer', 0, 0, axis_index_groups=groups)  4.44 us
    all_to_all x1, starting transfers between devices, body(): got = lax.all_to_all(back, 'peer', 0, 0, axis_index_groups=groups)  3.51 us
    unnamed x12, local copies, waits for them, and re-layouts  2.64 us
  transfers between devices with their start and end apart: 6, of which 6 were waited for; matrix products, arithmetic and copies ran while one was open for 0% of the time, Pallas kernels for 18%

profile of v2, /device:TPU:120, one launch (start us, length us, event | category | flops | bytes accessed | tf_op | source)
XLA Modules:
  0.0 77.9 jit_solution(635691206757593645)
XLA Ops:
  0.6 0.0 copy-start
  0.6 0.8 %copy-done = bf16[256,128]{1,0:T(8,128)(2,1)S(1)} copy-done((bf16[256,128]{1,0:T(8,128)(2,1)S(1)}, bf16[256,128]{1,0:T(8,128)(2,1)}, u32[]{:S(2)}) %copy-start) | copy-done | bytes 65560
  1.5 0.0 copy-start.1
  1.5 0.8 %copy-done.1 = bf16[256,128]{1,0:T(8,128)(2,1)S(1)} copy-done((bf16[256,128]{1,0:T(8,128)(2,1)S(1)}, bf16[256,128]{1,0:T(8,128)(2,1)}, u32[]{:S(2)}) %copy-start.1) | copy-done | bytes 65560
  2.3 6.4 %collective-permute-start.1 = (bf16[2,256,128]{2,1,0:T(8,128)(2,1)S(1)}, bf16[2,256,128]{2,1,0:T(8,128)(2,1)S(1)}, u32[]{:S(2)}, u32[]{:S(2)}) collective-permute-start(bf16[2,256,128]{2,1,0:T(8,128)(2,1)S(1)} %shard_map.84.own_ref), channel_id=1, source_target_pairs={{0,64},{8,72},{16,80},{24,88},{32,96},{40,104},{48,112},{56,120},{... | collective-permute-start | bytes 393224 | tf_op jit(solution)/shard_map/ppermute | solution.py:227
  8.7 3.8 %collective-permute-start = (bf16[2,256,128]{2,1,0:T(8,128)(2,1)S(1)}, bf16[2,256,128]{2,1,0:T(8,128)(2,1)S(1)}, u32[]{:S(2)}, u32[]{:S(2)}) collective-permute-start(bf16[2,256,128]{2,1,0:T(8,128)(2,1)S(1)} %shard_map.84.own_ref), channel_id=1, source_target_pairs={{0,32},{8,40},{16,48},{24,56},{32,64},{40,72},{48,80},{56,88},{64,... | collective-permute-start | bytes 393224 | tf_op jit(solution)/shard_map/ppermute | solution.py:227
  12.6 0.3 collective-permute-done.1.z2_ref
  12.8 4.7 %collective-permute-done.z1_ref = bf16[2,256,128]{2,1,0:T(8,128)(2,1)S(1)} collective-permute-done((bf16[2,256,128]{2,1,0:T(8,128)(2,1)S(1)}, bf16[2,256,128]{2,1,0:T(8,128)(2,1)S(1)}, u32[]{:S(2)}, u32[]{:S(2)}) %collective-permute-start) | collective-permute-done | bytes 131104 | tf_op jit(solution)/shard_map/ppermute | solution.py:227
  17.6 1.1 %shard_map.85 = bf16[4,2,2,256,128]{4,3,2,1,0:T(8,128)(2,1)} custom-call(bf16[2,256,128]{2,1,0:T(8,128)(2,1)S(1)} %shard_map.84.own_ref, bf16[2,256,128]{2,1,0:T(8,128)(2,1)S(1)} %collective-permute-done.z1_ref, bf16[2,256,128]{2,1,0:T(8,128)(2,1)S(1)} %collective-permute-done.1.z2_ref), custom_call_target="tpu_custom_call" | custom-call | bytes 1048576 | tf_op jit(solution)/shard_map/pallas_call | solution.py:252
  18.7 0.0 copy-start.2
  18.7 0.0 copy-start.3
  18.7 0.0 copy-start.5
  18.7 4.4 %all-to-all-start = ((bf16[4,2,2,256,128]{4,3,2,1,0:T(8,128)(2,1)}), bf16[4,2,2,256,128]{4,3,2,1,0:T(8,128)(2,1)S(1)}, u32[]{:S(2)}, u32[]{:S(2)}) async-start(bf16[4,2,2,256,128]{4,3,2,1,0:T(8,128)(2,1)} %shard_map.85), calls=%async_computation | async-start | bytes 2097152 | tf_op jit(solution)/shard_map/all_to_all | solution.py:260
  23.1 0.0 copy-done.2
  23.1 0.0 copy-done.3
  23.1 0.0 copy-done.5
  23.1 1.8 %shard_map.86 = (f32[3,4,256]{2,1,0:T(4,128)S(1)}, f32[3,4,256]{2,1,0:T(4,128)S(1)}, f32[3,4,256]{2,1,0:T(4,128)S(1)}) custom-call(s32[32]{0:T(128)S(1)} %copy-done.5, bf16[256,512]{1,0:T(8,128)(2,1)S(1)} %copy-done.2, bf16[256,512]{1,0:T(8,128)(2,1)S(1)} %copy-done.3, bf16[2,256,128]{2,1,0:T(8,128)(2,1)S(1)} %shard_map.84.own_ref, ...), custom_call_target="tpu_custom_call" | custom-call | flops 402653184 | bytes 1048576 | tf_op jit(solution)/shard_map/pallas_call | solution.py:261
  24.9 12.7 %all-to-all-done.far_ref = bf16[4,2,2,256,128]{4,3,2,1,0:T(8,128)(2,1)S(1)} async-done(((bf16[4,2,2,256,128]{4,3,2,1,0:T(8,128)(2,1)}), bf16[4,2,2,256,128]{4,3,2,1,0:T(8,128)(2,1)S(1)}, u32[]{:S(2)}, u32[]{:S(2)}) %all-to-all-start) | async-done | bytes 1048608 | tf_op jit(solution)/shard_map/all_to_all | solution.py:260
  37.6 7.6 %shard_map.87 = (bf16[4,2,2,256,128]{4,3,2,1,0:T(8,128)(2,1)}, f32[4,256]{1,0:T(4,128)S(1)}, f32[4,256]{1,0:T(4,128)S(1)}, f32[4,256]{1,0:T(4,128)S(1)}) custom-call(s32[32]{0:T(128)S(1)} %copy-done.5, bf16[256,512]{1,0:T(8,128)(2,1)S(1)} %copy-done.2, bf16[256,512]{1,0:T(8,128)(2,1)S(1)} %copy-done.3, ...), custom_call_target="tpu_custom_call" | custom-call | flops 805306368 | bytes 1048576 | tf_op jit(solution)/shard_map/pallas_call | solution.py:264
  45.2 3.5 %all-to-all-start.1 = ((bf16[4,2,2,256,128]{4,3,2,1,0:T(8,128)(2,1)}), bf16[4,2,2,256,128]{4,3,2,1,0:T(8,128)(2,1)S(1)}, u32[]{:S(2)}, u32[]{:S(2)}) async-start(bf16[4,2,2,256,128]{4,3,2,1,0:T(8,128)(2,1)} %get-tuple-element.27), calls=%async_computation.1 | async-start | bytes 2097152 | tf_op jit(solution)/shard_map/all_to_all | solution.py:272
  48.7 0.0 copy-start.4
  48.7 0.9 %copy-done.4 = bf16[256,512]{1,0:T(8,128)(2,1)S(1)} copy-done((bf16[256,512]{1,0:T(8,128)(2,1)S(1)}, bf16[256,512]{1,0:T(8,128)(2,1)}, u32[]{:S(2)}) %copy-start.4) | copy-done | bytes 262168
  49.6 12.0 %shard_map.88 = (bf16[256,512]{1,0:T(8,128)(2,1)}, f32[256,512]{1,0:T(8,128)}, f32[3,2,256,128]{3,2,1,0:T(8,128)S(1)}) custom-call(s32[32]{0:T(128)S(1)} %copy-done.5, bf16[256,512]{1,0:T(8,128)(2,1)S(1)} %copy-done.2, bf16[256,512]{1,0:T(8,128)(2,1)S(1)} %copy-done.4, bf16[2,256,128]{2,1,0:T(8,128)(2,1)S(1)} %shard_map.84.own_ref, ...), custom_call_target="tpu_custom_call" | custom-call | flops 1207959552 | bytes 1048576 | tf_op jit(solution)/shard_map/pallas_call | solution.py:273
  61.7 0.5 all-to-all-done.1.got_ref
  62.2 0.3 shard_map.89
  62.5 1.9 %collective-permute-start.2 = (bf16[2,256,128]{2,1,0:T(8,128)(2,1)S(1)}, bf16[2,256,128]{2,1,0:T(8,128)(2,1)S(1)}, u32[]{:S(2)}, u32[]{:S(2)}) collective-permute-start(bf16[2,256,128]{2,1,0:T(8,128)(2,1)S(1)} %get-tuple-element.30), channel_id=1, source_target_pairs={{32,0},{40,8},{48,16},{56,24},{64,32},{72,40},{80,48},{88,56},{96,... | collective-permute-start | bytes 393224 | tf_op jit(solution)/shard_map/ppermute | solution.py:227
  64.4 1.9 %collective-permute-start.3 = (bf16[2,256,128]{2,1,0:T(8,128)(2,1)S(1)}, bf16[2,256,128]{2,1,0:T(8,128)(2,1)S(1)}, u32[]{:S(2)}, u32[]{:S(2)}) collective-permute-start(bf16[2,256,128]{2,1,0:T(8,128)(2,1)S(1)} %get-tuple-element.31), channel_id=1, source_target_pairs={{64,0},{72,8},{80,16},{88,24},{96,32},{104,40},{112,48},{120,56},{... | collective-permute-start | bytes 393224 | tf_op jit(solution)/shard_map/ppermute | solution.py:227
  66.4 6.8 %collective-permute-done.2.one_ref = bf16[2,256,128]{2,1,0:T(8,128)(2,1)S(1)} collective-permute-done((bf16[2,256,128]{2,1,0:T(8,128)(2,1)S(1)}, bf16[2,256,128]{2,1,0:T(8,128)(2,1)S(1)}, u32[]{:S(2)}, u32[]{:S(2)}) %collective-permute-start.2) | collective-permute-done | bytes 131104 | tf_op jit(solution)/shard_map/ppermute | solution.py:227
  73.1 4.1 %collective-permute-done.3.two_ref = bf16[2,256,128]{2,1,0:T(8,128)(2,1)S(1)} collective-permute-done((bf16[2,256,128]{2,1,0:T(8,128)(2,1)S(1)}, bf16[2,256,128]{2,1,0:T(8,128)(2,1)S(1)}, u32[]{:S(2)}, u32[]{:S(2)}) %collective-permute-start.3) | collective-permute-done | bytes 131104 | tf_op jit(solution)/shard_map/ppermute | solution.py:227
  77.2 0.7 shard_map.90
  (1 shorter events, 0.0 us)
Async XLA Ops:
  0.6 0.8 %copy-start = (bf16[256,128]{1,0:T(8,128)(2,1)S(1)}, bf16[256,128]{1,0:T(8,128)(2,1)}, u32[]{:S(2)}) copy-start(bf16[256,128]{1,0:T(8,128)(2,1)} %k_ref.1) | copy-start | bytes 196612
  1.5 0.8 %copy-start.1 = (bf16[256,128]{1,0:T(8,128)(2,1)S(1)}, bf16[256,128]{1,0:T(8,128)(2,1)}, u32[]{:S(2)}) copy-start(bf16[256,128]{1,0:T(8,128)(2,1)} %v_ref.1) | copy-start | bytes 196612
  2.3 10.5 %collective-permute-start.1 = (bf16[2,256,128]{2,1,0:T(8,128)(2,1)S(1)}, bf16[2,256,128]{2,1,0:T(8,128)(2,1)S(1)}, u32[]{:S(2)}, u32[]{:S(2)}) collective-permute-start(bf16[2,256,128]{2,1,0:T(8,128)(2,1)S(1)} %shard_map.84.own_ref), channel_id=1, source_target_pairs={{0,64},{8,72},{16,80},{24,88},{32,96},{40,104},{48,112},{56,120},{... | collective-permute-start | bytes 393224 | tf_op jit(solution)/shard_map/ppermute | solution.py:227
  8.7 8.9 %collective-permute-start = (bf16[2,256,128]{2,1,0:T(8,128)(2,1)S(1)}, bf16[2,256,128]{2,1,0:T(8,128)(2,1)S(1)}, u32[]{:S(2)}, u32[]{:S(2)}) collective-permute-start(bf16[2,256,128]{2,1,0:T(8,128)(2,1)S(1)} %shard_map.84.own_ref), channel_id=1, source_target_pairs={{0,32},{8,40},{16,48},{24,56},{32,64},{40,72},{48,80},{56,88},{64,... | collective-permute-start | bytes 393224 | tf_op jit(solution)/shard_map/ppermute | solution.py:227
  18.7 4.5 %copy-start.2 = (bf16[256,512]{1,0:T(8,128)(2,1)S(1)}, bf16[256,512]{1,0:T(8,128)(2,1)}, u32[]{:S(2)}) copy-start(bf16[256,512]{1,0:T(8,128)(2,1)} %q_ref.5) | copy-start | bytes 786436
  18.7 4.5 %copy-start.3 = (bf16[256,512]{1,0:T(8,128)(2,1)S(1)}, bf16[256,512]{1,0:T(8,128)(2,1)}, u32[]{:S(2)}) copy-start(bf16[256,512]{1,0:T(8,128)(2,1)} %g_ref.5) | copy-start | bytes 786436
  18.7 4.5 %copy-start.5 = (s32[32]{0:T(128)S(1)}, s32[32]{0:T(128)}, u32[]{:S(2)}) copy-start(s32[32]{0:T(128)} %lengths_ref.5) | copy-start | bytes 388
  18.7 18.9 %all-to-all-start = ((bf16[4,2,2,256,128]{4,3,2,1,0:T(8,128)(2,1)}), bf16[4,2,2,256,128]{4,3,2,1,0:T(8,128)(2,1)S(1)}, u32[]{:S(2)}, u32[]{:S(2)}) async-start(bf16[4,2,2,256,128]{4,3,2,1,0:T(8,128)(2,1)} %shard_map.85), calls=%async_computation | async-start | bytes 2097152 | tf_op jit(solution)/shard_map/all_to_all | solution.py:260
  45.2 17.0 %all-to-all-start.1 = ((bf16[4,2,2,256,128]{4,3,2,1,0:T(8,128)(2,1)}), bf16[4,2,2,256,128]{4,3,2,1,0:T(8,128)(2,1)S(1)}, u32[]{:S(2)}, u32[]{:S(2)}) async-start(bf16[4,2,2,256,128]{4,3,2,1,0:T(8,128)(2,1)} %get-tuple-element.27), calls=%async_computation.1 | async-start | bytes 2097152 | tf_op jit(solution)/shard_map/all_to_all | solution.py:272
  48.7 1.0 %copy-start.4 = (bf16[256,512]{1,0:T(8,128)(2,1)S(1)}, bf16[256,512]{1,0:T(8,128)(2,1)}, u32[]{:S(2)}) copy-start(bf16[256,512]{1,0:T(8,128)(2,1)} %g_ref.5) | copy-start | bytes 786436
  62.5 10.6 %collective-permute-start.2 = (bf16[2,256,128]{2,1,0:T(8,128)(2,1)S(1)}, bf16[2,256,128]{2,1,0:T(8,128)(2,1)S(1)}, u32[]{:S(2)}, u32[]{:S(2)}) collective-permute-start(bf16[2,256,128]{2,1,0:T(8,128)(2,1)S(1)} %get-tuple-element.30), channel_id=1, source_target_pairs={{32,0},{40,8},{48,16},{56,24},{64,32},{72,40},{80,48},{88,56},{96,... | collective-permute-start | bytes 393224 | tf_op jit(solution)/shard_map/ppermute | solution.py:227
  64.4 12.8 %collective-permute-start.3 = (bf16[2,256,128]{2,1,0:T(8,128)(2,1)S(1)}, bf16[2,256,128]{2,1,0:T(8,128)(2,1)S(1)}, u32[]{:S(2)}, u32[]{:S(2)}) collective-permute-start(bf16[2,256,128]{2,1,0:T(8,128)(2,1)S(1)} %get-tuple-element.31), channel_id=1, source_target_pairs={{64,0},{72,8},{80,16},{88,24},{96,32},{104,40},{112,48},{120,56},{... | collective-permute-start | bytes 393224 | tf_op jit(solution)/shard_map/ppermute | solution.py:227

commit v3 on v2

--- a/solution.py
+++ b/solution.py
@@ -20,6 +20,7 @@
 LONG = (((1,), (1,)), ((), ()))
 PLAIN = (((1,), (0,)), ((), ()))
 VM = pl.BlockSpec(memory_space=pltpu.VMEM)
+ANY = pl.BlockSpec(memory_space=pl.ANY)
 SM = pl.BlockSpec(memory_space=pltpu.SMEM)
 
 
@@ -56,31 +57,42 @@
         r_ref[index, h : h + 1] = jnp.sum(p * dp, axis=0, keepdims=True)
 
 
-def pair_kernel(k_ref, v_ref, out_ref):
-    out_ref[0] = k_ref[...]
-    out_ref[1] = v_ref[...]
-
-
-def pack_kernel(own_ref, z1_ref, z2_ref, out_ref, sem):
+def pair_kernel(k_ref, v_ref, out_ref, sem):
+    copies = [pltpu.make_async_copy(r, out_ref.at[i], sem.at[i]) for i, r in enumerate((k_ref, v_ref))]
+    for copy in copies:
+        copy.start()
+    for copy in copies:
+        copy.wait()
+
+
+def filler(out_ref, sem):
     x = lax.rem(lax.axis_index("peer"), ROW)
 
-    def fill(t, kind, ref):
-        return pltpu.make_async_copy(ref, out_ref.at[t, kind], sem.at[t, kind])
-
-    for t in range(ROW):
-        fill(t, 1, z1_ref).start()
-
-        @pl.when(t > x)
-        def _(t=t):
-            fill(t, 0, own_ref).start()
-
-        @pl.when(t <= x)
-        def _(t=t):
-            fill(t, 0, z2_ref).start()
-
-    for t in range(ROW):
-        for kind in range(2):
-            fill(t, kind, z1_ref).wait()
+    def fill(i, kind, ref):
+        return pltpu.make_async_copy(ref, out_ref.at[lax.rem(x + i, ROW), kind], sem.at[i - 1, kind])
+
+    return x, fill
+
+
+def pack_own_kernel(own_ref, out_ref, sem):
+    x, fill = filler(out_ref, sem)
+    for act in ("start", "wait"):
+        for i in range(1, ROW):
+
+            @pl.when(x + i < ROW)
+            def _(i=i, act=act):
+                getattr(fill(i, 0, own_ref), act)()
+
+
+def pack_rows_kernel(z1_ref, z2_ref, _, out_ref, sem):
+    x, fill = filler(out_ref, sem)
+    for act in ("start", "wait"):
+        for i in range(1, ROW):
+            getattr(fill(i, 1, z1_ref), act)()
+
+            @pl.when(x + i >= ROW)
+            def _(i=i, act=act):
+                getattr(fill(i, 0, z2_ref), act)()
 
 
 def near_hidden(first, starts, block):
@@ -105,23 +117,27 @@
 
 def slot(i, x):
     column = lax.rem(x + 1 + i // 2, ROW)
-    kind = lax.rem(i, 2)
-    behind = x - column + jnp.where(kind == 1, ROW, jnp.where(column < x, 0, 2 * ROW))
+    kind = i % 2
+    behind = x - column + (ROW if kind else jnp.where(column < x, 0, 2 * ROW))
     return column, kind, behind
+
+
+def key_side(q_ref, g_ref, pb_ref, ds_ref):
+    dk = sum(dot(ds_ref[h], head(q_ref, h), PLAIN) for h in range(H))
+    dv = sum(dot(pb_ref[h], head(g_ref, h), PLAIN) for h in range(H))
+    return dk * SCALE, dv
 
 
 def far_kernel(
     lengths_ref, q_ref, g_ref, far_ref, m_in, t_in, r_in,
     back_ref, peak_ref, over_ref, rd_ref,
-    p_ref, dp_ref, m_ref, t_ref, r_ref, w_ref,
+    p_ref, dp_ref, m_ref, t_ref, r_ref, w_ref, pb_ref, ds_ref, ready_ref, sem,
 ):
     peer = lax.axis_index("peer")
     x = lax.rem(peer, ROW)
     first = peer * T
     starts = doc_starts(lengths_ref, first)
-
-    @pl.loop(0, 6)
-    def _(i):
+    for i in range(6):
         column, kind, behind = slot(i, x)
         hidden = far_hidden(first, starts, behind)
         key, value = far_ref[column, kind, 0], far_ref[column, kind, 1]
@@ -139,65 +155,54 @@
     for b in range(6):
         w_ref[b] = factors[3 + b] * over
 
-    @pl.loop(0, 6)
-    def _(i):
+    copies = []
+    for i in range(6):
         column, kind, _ = slot(i, x)
-        dk = jnp.zeros((T, D), F32)
-        dv = jnp.zeros((T, D), F32)
         for h in range(H):
             pn = p_ref[i, h] * w_ref[i, h : h + 1]
-            ds = (pn * (dp_ref[i, h] - rd_ref[h : h + 1])).astype(BF16)
-            dk += dot(ds, head(q_ref, h), PLAIN)
-            dv += dot(pn.astype(BF16), head(g_ref, h), PLAIN)
-        back_ref[column, kind, 0] = (dk * SCALE).astype(BF16)
-        back_ref[column, kind, 1] = dv.astype(BF16)
-
-    back_ref[x] = jnp.zeros((2, 2, T, D), BF16)
+            pb_ref[i % 2, h] = pn.astype(BF16)
+            ds_ref[i % 2, h] = (pn * (dp_ref[i, h] - rd_ref[h : h + 1])).astype(BF16)
+        dk, dv = key_side(q_ref, g_ref, pb_ref.at[i % 2], ds_ref.at[i % 2])
+        ready_ref[i, 0] = dk.astype(BF16)
+        ready_ref[i, 1] = dv.astype(BF16)
+        copies.append(pltpu.make_async_copy(ready_ref.at[i], back_ref.at[column, kind], sem.at[i]))
+        copies[-1].start()
+    for copy in copies:
+        copy.wait()
 
 
 def rest_kernel(
     lengths_ref, q_ref, g_ref, own_ref, z1_ref, z2_ref, far_ref, peak_ref, over_ref, rd_ref,
-    out_ref, dq_ref, near_ref, o_acc, dq_acc,
+    out_ref, dq_ref, near_ref, o_acc, dq_acc, pb_ref, ds_ref,
 ):
     peer = lax.axis_index("peer")
     x = lax.rem(peer, ROW)
     first = peer * T
     starts = doc_starts(lengths_ref, first)
-
-    def weights(key, value, hidden, h):
-        s = dot(key, head(q_ref, h), LONG)
-        dp = dot(value, head(g_ref, h), LONG)
-        s = jnp.where(hidden, NEG, s)
-        pn = jnp.exp2((s - peak_ref[h : h + 1]) * TO_EXP2) * over_ref[h : h + 1]
-        ds = pn * (dp - rd_ref[h : h + 1])
-        return pn.astype(BF16), ds.astype(BF16)
-
-    for b, ref in enumerate((own_ref, z1_ref, z2_ref)):
-        key, value = ref[0], ref[1]
-        hidden = near_hidden(first, starts, b)
+    near = (own_ref, z1_ref, z2_ref)
+    for b in range(9):
+        if b < 3:
+            key, value = near[b][0], near[b][1]
+            hidden = near_hidden(first, starts, b)
+        else:
+            column, kind, behind = slot(b - 3, x)
+            key, value = far_ref[column, kind, 0], far_ref[column, kind, 1]
+            hidden = far_hidden(first, starts, behind)
+        pb, ds = pb_ref.at[b % 2], ds_ref.at[b % 2]
+        for h in range(H):
+            s = dot(key, head(q_ref, h), LONG)
+            dp = dot(value, head(g_ref, h), LONG)
+            s = jnp.where(hidden, NEG, s)
+            pn = jnp.exp2((s - peak_ref[h : h + 1]) * TO_EXP2) * over_ref[h : h + 1]
+            pb[h] = pn.astype(BF16)
+            ds[h] = (pn * (dp - rd_ref[h : h + 1])).astype(BF16)
         kt, vt = key.T, value.T
-        dk = jnp.zeros((T, D), F32)
-        dv = jnp.zeros((T, D), F32)
         for h in range(H):
-            pb, ds = weights(key, value, hidden, h)
-            dk += dot(ds, head(q_ref, h), PLAIN)
-            dv += dot(pb, head(g_ref, h), PLAIN)
-            o, dq = dot(vt, pb, PLAIN), dot(kt, ds, PLAIN)
+            o, dq = dot(vt, pb[h], PLAIN), dot(kt, ds[h], PLAIN)
             o_acc[h] = o if b == 0 else o_acc[h] + o
             dq_acc[h] = dq if b == 0 else dq_acc[h] + dq
-        near_ref[b, 0] = dk * SCALE
-        near_ref[b, 1] = dv
-
-    @pl.loop(0, 6)
-    def _(i):
-        column, kind, behind = slot(i, x)
-        hidden = far_hidden(first, starts, behind)
-        key, value = far_ref[column, kind, 0], far_ref[column, kind, 1]
-        kt, vt = key.T, value.T
-        for h in range(H):
-            pb, ds = weights(key, value, hidden, h)
-            o_acc[h] += dot(vt, pb, PLAIN)
-            dq_acc[h] += dot(kt, ds, PLAIN)
+        if b < 3:
+            near_ref[b, 0], near_ref[b, 1] = key_side(q_ref, g_ref, pb, ds)
 
     for h in range(H):
         out_ref[:, h * D : (h + 1) * D] = o_acc[h].T.astype(BF16)
@@ -227,13 +232,14 @@
     return lax.ppermute(block, "peer", [(i, i + far) for i in range(peers) if 0 <= i + far < peers])
 
 
-def call(kernel, out, specs, scratch=(), blocks=0, limit=24, space=VM):
+def call(kernel, out, specs, scratch=(), blocks=0, limit=24, first=VM, alias={}):
     return pl.pallas_call(
         kernel,
         out_shape=out,
         in_specs=specs,
-        out_specs=tuple(space for _ in out),
+        out_specs=(first,) + tuple(VM for _ in out[1:]),
         scratch_shapes=list(scratch),
+        input_output_aliases=alias,
         compiler_params=pltpu.CompilerParams(vmem_limit_bytes=limit << 20),
         cost_estimate=pl.CostEstimate(
             flops=blocks * H * T * T * D * 4, bytes_accessed=1 << 20, transcendentals=blocks * H * T * T
@@ -246,17 +252,15 @@
     groups = [[z * ROW + i for i in range(ROW)] for z in range(peers // ROW)]
     array = jax.ShapeDtypeStruct
     block, sums, stats = (2, T, D), array((2, T, D), F32), (H, T)
-    (own,) = call(pair_kernel, (array(block, BF16),), [VM] * 2, limit=4)(keys, values)
+    (own,) = call(pair_kernel, (array(block, BF16),), [ANY] * 2, [pltpu.SemaphoreType.DMA((2,))], limit=60)(
+        keys, values
+    )
     z1 = along_z(own, 1, peers)
     z2 = along_z(own, 2, peers)
-    (sent,) = call(
-        pack_kernel,
-        (array((ROW, 2, *block), BF16),),
-        [VM] * 3,
-        [pltpu.SemaphoreType.DMA((ROW, 2))],
-        limit=4,
-        space=pl.BlockSpec(memory_space=pl.ANY),
-    )(own, z1, z2)
+    slots = [pltpu.SemaphoreType.DMA((ROW - 1, 2))]
+    packed = (array((ROW, 2, *block), BF16),)
+    (sent,) = call(pack_own_kernel, packed, [ANY], slots, limit=4, first=ANY)(own)
+    (sent,) = call(pack_rows_kernel, packed, [VM, VM, ANY], slots, limit=4, first=ANY, alias={2: 0})(z1, z2, sent)
     far = lax.all_to_all(sent, "peer", 0, 0, axis_index_groups=groups)
     m, t, r = call(near_kernel, (array((3, *stats), F32),) * 3, [SM] + [VM] * 5, blocks=3, limit=8)(
         doc_lengths, queries, grad_out, own, z1, z2
@@ -265,16 +269,20 @@
         far_kernel,
         (array((ROW, 2, *block), BF16),) + (array(stats, F32),) * 3,
         [SM] + [VM] * 6,
-        [pltpu.VMEM((6, H, T, T), F32)] * 2 + [pltpu.VMEM((6, *stats), F32)] * 4,
+        [pltpu.VMEM((6, H, T, T), F32)] * 2
+        + [pltpu.VMEM((6, *stats), F32)] * 4
+        + [pltpu.VMEM((2, H, T, T), BF16)] * 2
+        + [pltpu.VMEM((6, *block), BF16), pltpu.SemaphoreType.DMA((6,))],
         blocks=6,
         limit=24,
+        first=ANY,
     )(doc_lengths, queries, grad_out, far, m, t, r)
     got = lax.all_to_all(back, "peer", 0, 0, axis_index_groups=groups)
     attended, query_grad, near = call(
         rest_kernel,
         (array((T, H * D), BF16), array((T, H * D), F32), array((3, *block), F32)),
         [SM] + [VM] * 9,
-        [pltpu.VMEM((H, D, T), F32)] * 2,
+        [pltpu.VMEM((H, D, T), F32)] * 2 + [pltpu.VMEM((2, H, T, T), BF16)] * 2,
         blocks=9,
         limit=16,
     )(doc_lengths, queries, grad_out, own, z1, z2, far, peak, over, rd)

time: 78.4 us -> 77.3 us (0.986)
  the two profiles are of different devices: /device:TPU:120 before, /device:TPU:72 now
where the time goes in v3:
time: 77.3 us; the launch traced here: 76.9 us
  waiting for transfers between devices  32.5 us (42%)
  starting transfers between devices  22.3 us (29%)
  Pallas kernels  19.4 us (25%)
  local copies, waits for them, and re-layouts  1.88 us (2%)
  between operations  0.78 us (1%)
    ppermute x4, waiting for transfers between devices, along_z(): lax.ppermute(block, 'peer', [(i, i + far) for i in range(peers) if 0 <= i...  14.4 us
    ppermute x4, starting transfers between devices, along_z(): lax.ppermute(block, 'peer', [(i, i + far) for i in range(peers) if 0 <= i...  14.1 us
    all_to_all x1, waiting for transfers between devices, body(): far = lax.all_to_all(sent, 'peer', 0, 0, axis_index_groups=groups)  12.6 us
    pallas_call x1, Pallas kernels, body(): call(rest_kernel, (array((T, H * D), BF16), array((T, H * D), F32), array...  6.86 us
    pallas_call x1, Pallas kernels, body(): call(far_kernel, (array((ROW, 2, *block), BF16),) + (array(stats, F32),)...  6.53 us
    all_to_all x1, waiting for transfers between devices, body(): got = lax.all_to_all(back, 'peer', 0, 0, axis_index_groups=groups)  5.52 us
    all_to_all x1, starting transfers between devices, body(): far = lax.all_to_all(sent, 'peer', 0, 0, axis_index_groups=groups)  4.5 us
    all_to_all x1, starting transfers between devices, body(): got = lax.all_to_all(back, 'peer', 0, 0, axis_index_groups=groups)  3.71 us
  transfers between devices with their start and end apart: 6, of which 6 were waited for; matrix products, arithmetic and copies ran while one was open for 0% of the time, Pallas kernels for 12%

profile of v3, /device:TPU:72, one launch (start us, length us, event | category | flops | bytes accessed | tf_op | source)
XLA Modules:
  0.0 76.9 jit_solution(6923708400437330619)
XLA Ops:
  0.6 1.5 %shard_map.84.own_ref = bf16[2,256,128]{2,1,0:T(8,128)(2,1)} custom-call(bf16[256,128]{1,0:T(8,128)(2,1)} %k_ref.1, bf16[256,128]{1,0:T(8,128)(2,1)} %v_ref.1), custom_call_target="tpu_custom_call" | custom-call | bytes 1048576 | tf_op jit(solution)/shard_map/pallas_call | solution.py:255
  2.2 6.4 %collective-permute-start.1 = (bf16[2,256,128]{2,1,0:T(8,128)(2,1)}, bf16[2,256,128]{2,1,0:T(8,128)(2,1)S(1)}, u32[]{:S(2)}, u32[]{:S(2)}) collective-permute-start(bf16[2,256,128]{2,1,0:T(8,128)(2,1)} %shard_map.84.own_ref), channel_id=1, source_target_pairs={{0,64},{8,72},{16,80},{24,88},{32,96},{40,104},{48,112},{56,120},{... | collective-permute-start | bytes 393224 | tf_op jit(solution)/shard_map/ppermute | solution.py:232
  8.6 3.8 %collective-permute-start = (bf16[2,256,128]{2,1,0:T(8,128)(2,1)}, bf16[2,256,128]{2,1,0:T(8,128)(2,1)S(1)}, u32[]{:S(2)}, u32[]{:S(2)}) collective-permute-start(bf16[2,256,128]{2,1,0:T(8,128)(2,1)} %shard_map.84.own_ref), channel_id=1, source_target_pairs={{0,32},{8,40},{16,48},{24,56},{32,64},{40,72},{48,80},{56,88},{64,... | collective-permute-start | bytes 393224 | tf_op jit(solution)/shard_map/ppermute | solution.py:232
  12.4 0.0 copy-start
  12.4 0.9 %copy-done = bf16[2,256,128]{2,1,0:T(8,128)(2,1)S(1)} copy-done((bf16[2,256,128]{2,1,0:T(8,128)(2,1)S(1)}, bf16[2,256,128]{2,1,0:T(8,128)(2,1)}, u32[]{:S(2)}) %copy-start) | copy-done | bytes 131096
  13.3 0.8 %shard_map.85._ = bf16[4,2,2,256,128]{4,3,2,1,0:T(8,128)(2,1)} custom-call(bf16[2,256,128]{2,1,0:T(8,128)(2,1)S(1)} %copy-done), custom_call_target="tpu_custom_call" | custom-call | bytes 1048576 | tf_op jit(solution)/shard_map/pallas_call | solution.py:262
  14.2 1.1 %collective-permute-done.1.z2_ref = bf16[2,256,128]{2,1,0:T(8,128)(2,1)S(1)} collective-permute-done((bf16[2,256,128]{2,1,0:T(8,128)(2,1)}, bf16[2,256,128]{2,1,0:T(8,128)(2,1)S(1)}, u32[]{:S(2)}, u32[]{:S(2)}) %collective-permute-start.1) | collective-permute-done | bytes 131104 | tf_op jit(solution)/shard_map/ppermute | solution.py:232
  15.3 1.9 %collective-permute-done.z1_ref = bf16[2,256,128]{2,1,0:T(8,128)(2,1)S(1)} collective-permute-done((bf16[2,256,128]{2,1,0:T(8,128)(2,1)}, bf16[2,256,128]{2,1,0:T(8,128)(2,1)S(1)}, u32[]{:S(2)}, u32[]{:S(2)}) %collective-permute-start) | collective-permute-done | bytes 131104 | tf_op jit(solution)/shard_map/ppermute | solution.py:232
  17.2 0.8 %shard_map.86 = bf16[4,2,2,256,128]{4,3,2,1,0:T(8,128)(2,1)} custom-call(bf16[2,256,128]{2,1,0:T(8,128)(2,1)S(1)} %collective-permute-done.z1_ref, bf16[2,256,128]{2,1,0:T(8,128)(2,1)S(1)} %collective-permute-done.1.z2_ref, bf16[4,2,2,256,128]{4,3,2,1,0:T(8,128)(2,1)} %shard_map.85._), custom_call_target="tpu_custom_call", output_to_operand_aliasing={{}: (2, {})} | custom-call | bytes 1048576 | tf_op jit(solution)/shard_map/pallas_call | solution.py:263
  18.0 0.0 copy-start.1
  18.0 0.0 copy-start.2
  18.1 0.0 copy-start.3
  18.1 0.0 copy-start.5
  18.1 4.5 %all-to-all-start = ((bf16[4,2,2,256,128]{4,3,2,1,0:T(8,128)(2,1)}), bf16[4,2,2,256,128]{4,3,2,1,0:T(8,128)(2,1)S(1)}, u32[]{:S(2)}, u32[]{:S(2)}) async-start(bf16[4,2,2,256,128]{4,3,2,1,0:T(8,128)(2,1)} %shard_map.86), calls=%async_computation | async-start | bytes 2097152 | tf_op jit(solution)/shard_map/all_to_all | solution.py:264
  22.6 0.0 copy-done.1
  22.6 0.0 copy-done.2
  22.6 0.0 copy-done.3
  22.6 0.0 copy-done.5
  22.6 1.8 %shard_map.87 = (f32[3,4,256]{2,1,0:T(4,128)S(1)}, f32[3,4,256]{2,1,0:T(4,128)S(1)}, f32[3,4,256]{2,1,0:T(4,128)S(1)}) custom-call(s32[32]{0:T(128)S(1)} %copy-done.5, bf16[256,512]{1,0:T(8,128)(2,1)S(1)} %copy-done.2, bf16[256,512]{1,0:T(8,128)(2,1)S(1)} %copy-done.3, bf16[2,256,128]{2,1,0:T(8,128)(2,1)S(1)} %copy-done.1, ...), custom_call_target="tpu_custom_call" | custom-call | flops 402653184 | bytes 1048576 | tf_op jit(solution)/shard_map/pallas_call | solution.py:265
  24.4 12.6 %all-to-all-done.far_ref = bf16[4,2,2,256,128]{4,3,2,1,0:T(8,128)(2,1)S(1)} async-done(((bf16[4,2,2,256,128]{4,3,2,1,0:T(8,128)(2,1)}), bf16[4,2,2,256,128]{4,3,2,1,0:T(8,128)(2,1)S(1)}, u32[]{:S(2)}, u32[]{:S(2)}) %all-to-all-start) | async-done | bytes 1048608 | tf_op jit(solution)/shard_map/all_to_all | solution.py:264
  37.1 6.5 %shard_map.88 = (bf16[4,2,2,256,128]{4,3,2,1,0:T(8,128)(2,1)}, f32[4,256]{1,0:T(4,128)S(1)}, f32[4,256]{1,0:T(4,128)S(1)}, f32[4,256]{1,0:T(4,128)S(1)}) custom-call(s32[32]{0:T(128)S(1)} %copy-done.5, bf16[256,512]{1,0:T(8,128)(2,1)S(1)} %copy-done.2, bf16[256,512]{1,0:T(8,128)(2,1)S(1)} %copy-done.3, ...), custom_call_target="tpu_custom_call" | custom-call | flops 805306368 | bytes 1048576 | tf_op jit(solution)/shard_map/pallas_call | solution.py:268
  43.6 3.7 %all-to-all-start.1 = ((bf16[4,2,2,256,128]{4,3,2,1,0:T(8,128)(2,1)}), bf16[4,2,2,256,128]{4,3,2,1,0:T(8,128)(2,1)S(1)}, u32[]{:S(2)}, u32[]{:S(2)}) async-start(bf16[4,2,2,256,128]{4,3,2,1,0:T(8,128)(2,1)} %get-tuple-element.27), calls=%async_computation.1 | async-start | bytes 2097152 | tf_op jit(solution)/shard_map/all_to_all | solution.py:280
  47.3 0.0 copy-start.4
  47.3 0.9 %copy-done.4 = bf16[256,512]{1,0:T(8,128)(2,1)S(1)} copy-done((bf16[256,512]{1,0:T(8,128)(2,1)S(1)}, bf16[256,512]{1,0:T(8,128)(2,1)}, u32[]{:S(2)}) %copy-start.4) | copy-done | bytes 262168
  48.3 6.9 %shard_map.89 = (bf16[256,512]{1,0:T(8,128)(2,1)}, f32[256,512]{1,0:T(8,128)}, f32[3,2,256,128]{3,2,1,0:T(8,128)S(1)}) custom-call(s32[32]{0:T(128)S(1)} %copy-done.5, bf16[256,512]{1,0:T(8,128)(2,1)S(1)} %copy-done.2, bf16[256,512]{1,0:T(8,128)(2,1)S(1)} %copy-done.4, bf16[2,256,128]{2,1,0:T(8,128)(2,1)S(1)} %copy-done.1, ...), custom_call_target="tpu_custom_call" | custom-call | flops 1207959552 | bytes 1048576 | tf_op jit(solution)/shard_map/pallas_call | solution.py:281
  55.1 5.5 %all-to-all-done.1.got_ref = bf16[4,2,2,256,128]{4,3,2,1,0:T(8,128)(2,1)S(1)} async-done(((bf16[4,2,2,256,128]{4,3,2,1,0:T(8,128)(2,1)}), bf16[4,2,2,256,128]{4,3,2,1,0:T(8,128)(2,1)S(1)}, u32[]{:S(2)}, u32[]{:S(2)}) %all-to-all-start.1) | async-done | bytes 1048608 | tf_op jit(solution)/shard_map/all_to_all | solution.py:280
  60.6 0.3 shard_map.90
  61.0 1.9 %collective-permute-start.2 = (bf16[2,256,128]{2,1,0:T(8,128)(2,1)S(1)}, bf16[2,256,128]{2,1,0:T(8,128)(2,1)S(1)}, u32[]{:S(2)}, u32[]{:S(2)}) collective-permute-start(bf16[2,256,128]{2,1,0:T(8,128)(2,1)S(1)} %get-tuple-element.30), channel_id=1, source_target_pairs={{32,0},{40,8},{48,16},{56,24},{64,32},{72,40},{80,48},{88,56},{96,... | collective-permute-start | bytes 393224 | tf_op jit(solution)/shard_map/ppermute | solution.py:232
  62.9 1.9 %collective-permute-start.3 = (bf16[2,256,128]{2,1,0:T(8,128)(2,1)S(1)}, bf16[2,256,128]{2,1,0:T(8,128)(2,1)S(1)}, u32[]{:S(2)}, u32[]{:S(2)}) collective-permute-start(bf16[2,256,128]{2,1,0:T(8,128)(2,1)S(1)} %get-tuple-element.31), channel_id=1, source_target_pairs={{64,0},{72,8},{80,16},{88,24},{96,32},{104,40},{112,48},{120,56},{... | collective-permute-start | bytes 393224 | tf_op jit(solution)/shard_map/ppermute | solution.py:232
  64.8 3.4 %collective-permute-done.2.one_ref = bf16[2,256,128]{2,1,0:T(8,128)(2,1)S(1)} collective-permute-done((bf16[2,256,128]{2,1,0:T(8,128)(2,1)S(1)}, bf16[2,256,128]{2,1,0:T(8,128)(2,1)S(1)}, u32[]{:S(2)}, u32[]{:S(2)}) %collective-permute-start.2) | collective-permute-done | bytes 131104 | tf_op jit(solution)/shard_map/ppermute | solution.py:232
  68.2 8.0 %collective-permute-done.3.two_ref = bf16[2,256,128]{2,1,0:T(8,128)(2,1)S(1)} collective-permute-done((bf16[2,256,128]{2,1,0:T(8,128)(2,1)S(1)}, bf16[2,256,128]{2,1,0:T(8,128)(2,1)S(1)}, u32[]{:S(2)}, u32[]{:S(2)}) %collective-permute-start.3) | collective-permute-done | bytes 131104 | tf_op jit(solution)/shard_map/ppermute | solution.py:232
  76.1 0.7 shard_map.91
Async XLA Ops:
  2.2 13.1 %collective-permute-start.1 = (bf16[2,256,128]{2,1,0:T(8,128)(2,1)}, bf16[2,256,128]{2,1,0:T(8,128)(2,1)S(1)}, u32[]{:S(2)}, u32[]{:S(2)}) collective-permute-start(bf16[2,256,128]{2,1,0:T(8,128)(2,1)} %shard_map.84.own_ref), channel_id=1, source_target_pairs={{0,64},{8,72},{16,80},{24,88},{32,96},{40,104},{48,112},{56,120},{... | collective-permute-start | bytes 393224 | tf_op jit(solution)/shard_map/ppermute | solution.py:232
  8.6 8.6 %collective-permute-start = (bf16[2,256,128]{2,1,0:T(8,128)(2,1)}, bf16[2,256,128]{2,1,0:T(8,128)(2,1)S(1)}, u32[]{:S(2)}, u32[]{:S(2)}) collective-permute-start(bf16[2,256,128]{2,1,0:T(8,128)(2,1)} %shard_map.84.own_ref), channel_id=1, source_target_pairs={{0,32},{8,40},{16,48},{24,56},{32,64},{40,72},{48,80},{56,88},{64,... | collective-permute-start | bytes 393224 | tf_op jit(solution)/shard_map/ppermute | solution.py:232
  12.4 0.9 %copy-start = (bf16[2,256,128]{2,1,0:T(8,128)(2,1)S(1)}, bf16[2,256,128]{2,1,0:T(8,128)(2,1)}, u32[]{:S(2)}) copy-start(bf16[2,256,128]{2,1,0:T(8,128)(2,1)} %shard_map.84.own_ref) | copy-start | bytes 393220
  18.0 4.6 %copy-start.1 = (bf16[2,256,128]{2,1,0:T(8,128)(2,1)S(1)}, bf16[2,256,128]{2,1,0:T(8,128)(2,1)}, u32[]{:S(2)}) copy-start(bf16[2,256,128]{2,1,0:T(8,128)(2,1)} %shard_map.84.own_ref) | copy-start | bytes 393220
  18.0 4.5 %copy-start.2 = (bf16[256,512]{1,0:T(8,128)(2,1)S(1)}, bf16[256,512]{1,0:T(8,128)(2,1)}, u32[]{:S(2)}) copy-start(bf16[256,512]{1,0:T(8,128)(2,1)} %q_ref.5) | copy-start | bytes 786436
  18.1 4.5 %copy-start.3 = (bf16[256,512]{1,0:T(8,128)(2,1)S(1)}, bf16[256,512]{1,0:T(8,128)(2,1)}, u32[]{:S(2)}) copy-start(bf16[256,512]{1,0:T(8,128)(2,1)} %g_ref.5) | copy-start | bytes 786436
  18.1 4.5 %copy-start.5 = (s32[32]{0:T(128)S(1)}, s32[32]{0:T(128)}, u32[]{:S(2)}) copy-start(s32[32]{0:T(128)} %lengths_ref.5) | copy-start | bytes 388
  18.1 19.0 %all-to-all-start = ((bf16[4,2,2,256,128]{4,3,2,1,0:T(8,128)(2,1)}), bf16[4,2,2,256,128]{4,3,2,1,0:T(8,128)(2,1)S(1)}, u32[]{:S(2)}, u32[]{:S(2)}) async-start(bf16[4,2,2,256,128]{4,3,2,1,0:T(8,128)(2,1)} %shard_map.86), calls=%async_computation | async-start | bytes 2097152 | tf_op jit(solution)/shard_map/all_to_all | solution.py:264
  43.6 17.0 %all-to-all-start.1 = ((bf16[4,2,2,256,128]{4,3,2,1,0:T(8,128)(2,1)}), bf16[4,2,2,256,128]{4,3,2,1,0:T(8,128)(2,1)S(1)}, u32[]{:S(2)}, u32[]{:S(2)}) async-start(bf16[4,2,2,256,128]{4,3,2,1,0:T(8,128)(2,1)} %get-tuple-element.27), calls=%async_computation.1 | async-start | bytes 2097152 | tf_op jit(solution)/shard_map/all_to_all | solution.py:280
  47.3 1.0 %copy-start.4 = (bf16[256,512]{1,0:T(8,128)(2,1)S(1)}, bf16[256,512]{1,0:T(8,128)(2,1)}, u32[]{:S(2)}) copy-start(bf16[256,512]{1,0:T(8,128)(2,1)} %g_ref.5) | copy-start | bytes 786436
  61.0 7.2 %collective-permute-start.2 = (bf16[2,256,128]{2,1,0:T(8,128)(2,1)S(1)}, bf16[2,256,128]{2,1,0:T(8,128)(2,1)S(1)}, u32[]{:S(2)}, u32[]{:S(2)}) collective-permute-start(bf16[2,256,128]{2,1,0:T(8,128)(2,1)S(1)} %get-tuple-element.30), channel_id=1, source_target_pairs={{32,0},{40,8},{48,16},{56,24},{64,32},{72,40},{80,48},{88,56},{96,... | collective-permute-start | bytes 393224 | tf_op jit(solution)/shard_map/ppermute | solution.py:232
  62.9 13.3 %collective-permute-start.3 = (bf16[2,256,128]{2,1,0:T(8,128)(2,1)S(1)}, bf16[2,256,128]{2,1,0:T(8,128)(2,1)S(1)}, u32[]{:S(2)}, u32[]{:S(2)}) collective-permute-start(bf16[2,256,128]{2,1,0:T(8,128)(2,1)S(1)} %get-tuple-element.31), channel_id=1, source_target_pairs={{64,0},{72,8},{80,16},{88,24},{96,32},{104,40},{112,48},{120,56},{... | collective-permute-start | bytes 393224 | tf_op jit(solution)/shard_map/ppermute | solution.py:232

commit v4 on v3

v4 whole, which is shorter than its diff:
```python
import functools
import math

import jax
import jax.numpy as jnp
from jax import lax
from jax.experimental import pallas as pl
from jax.experimental.pallas import tpu as pltpu
from jax.sharding import PartitionSpec as P

T = 256
D = 128
H = 4
ROW = 4
F32 = jnp.float32
BF16 = jnp.bfloat16
NEG = -1e30
SCALE = D**-0.5
TO_EXP2 = SCALE * math.log2(math.e)
LONG = (((1,), (1,)), ((), ()))
PLAIN = (((1,), (0,)), ((), ()))
VM = pl.BlockSpec(memory_space=pltpu.VMEM)
ANY = pl.BlockSpec(memory_space=pl.ANY)
SM = pl.BlockSpec(memory_space=pltpu.SMEM)


def dot(a, b, dims):
    return lax.dot_general(a, b, dims, preferred_element_type=F32)


def head(ref, h):
    return ref[:, h * D : (h + 1) * D]


def doc_starts(lengths_ref, first):
    place = first + lax.broadcasted_iota(jnp.int32, (1, T), 1)
    start = jnp.int32(0)
    own = jnp.zeros((1, T), jnp.int32)
    for i in range(lengths_ref.shape[0]):
        own = jnp.where(place >= start, start, own)
        start = start + lengths_ref[i]
    return own


def scores(q_ref, g_ref, key, value, hidden, index, m_ref, t_ref, r_ref, p_ref=None, dp_ref=None):
    for h in range(H):
        s = dot(key, head(q_ref, h), LONG)
        dp = dot(value, head(g_ref, h), LONG)
        s = jnp.where(hidden, NEG, s)
        m = jnp.max(s, axis=0, keepdims=True)
        p = jnp.exp2((s - m) * TO_EXP2)
        if p_ref is not None:
            p_ref[index, h] = p
            dp_ref[index, h] = dp
        m_ref[index, h : h + 1] = m
        t_ref[index, h : h + 1] = jnp.sum(p, axis=0, keepdims=True)
        r_ref[index, h : h + 1] = jnp.sum(p * dp, axis=0, keepdims=True)


def pair_kernel(k_ref, v_ref, out_ref, sem):
    copies = [pltpu.make_async_copy(r, out_ref.at[i], sem.at[i]) for i, r in enumerate((k_ref, v_ref))]
    for copy in copies:
        copy.start()
    for copy in copies:
        copy.wait()


def pack_kernel(own_ref, z1_ref, z2_ref, *out_refs):
    x = lax.rem(lax.axis_index("peer"), ROW)
    for d, ref in enumerate(out_refs, 1):

        @pl.when(x + d < ROW)
        def _(ref=ref):
            ref[0] = own_ref[...]

        @pl.when(x + d >= ROW)
        def _(ref=ref):
            ref[0] = z2_ref[...]

        ref[1] = z1_ref[...]


def near_hidden(first, starts, block):
    rows = lax.broadcasted_iota(jnp.int32, (T, 1), 0)
    hidden = (rows + (first - block * ROW * T)) < starts
    if block == 0:
        hidden = hidden | (rows > lax.broadcasted_iota(jnp.int32, (1, T), 1))
    return hidden


def far_hidden(first, starts, behind):
    rows = lax.broadcasted_iota(jnp.int32, (T, 1), 0)
    return (rows + (first - behind * T)) < starts


def hold_kernel(own_ref, held_ref):
    held_ref[...] = own_ref[...]


def near_kernel(lengths_ref, q_ref, g_ref, own_ref, z1_ref, z2_ref, m_ref, t_ref, r_ref):
    first = lax.axis_index("peer") * T
    starts = doc_starts(lengths_ref, first)
    for i, ref in enumerate((own_ref, z1_ref, z2_ref)):
        scores(q_ref, g_ref, ref[0], ref[1], near_hidden(first, starts, i), i, m_ref, t_ref, r_ref)


def behind(d, kind, x):
    return jnp.where((x >= d) ^ (kind == 1), d, ROW + d)


def key_side(q_ref, g_ref, pb_ref, ds_ref):
    dk = sum(dot(ds_ref[h], head(q_ref, h), PLAIN) for h in range(H))
    dv = sum(dot(pb_ref[h], head(g_ref, h), PLAIN) for h in range(H))
    return dk * SCALE, dv


def far_scores(d, lengths_ref, q_ref, g_ref, far_ref, p_ref, dp_ref, m_ref, t_ref, r_ref):
    peer = lax.axis_index("peer")
    first = peer * T
    starts = doc_starts(lengths_ref, first)
    for i in range(2):
        hidden = far_hidden(first, starts, behind(d, i, lax.rem(peer, ROW)))
        scores(q_ref, g_ref, far_ref[i, 0], far_ref[i, 1], hidden, i, m_ref, t_ref, r_ref, p_ref, dp_ref)


def far_back(p_ref, dp_ref, w_ref, rd_ref, q_ref, g_ref, back_ref, pb_ref, ds_ref):
    for i in range(2):
        for h in range(H):
            pn = p_ref[i, h] * w_ref[i, h : h + 1]
            pb_ref[i, h] = pn.astype(BF16)
            ds_ref[i, h] = (pn * (dp_ref[i, h] - rd_ref[h : h + 1])).astype(BF16)
        dk, dv = key_side(q_ref, g_ref, pb_ref.at[i], ds_ref.at[i])
        back_ref[i, 0] = dk.astype(BF16)
        back_ref[i, 1] = dv.astype(BF16)


def last_kernel(
    d, lengths_ref, q_ref, g_ref, far_ref, mn, tn, rn, m1, t1, r1, m3, t3, r3,
    back_ref, peak_ref, over_ref, rd_ref, w1_ref, w3_ref,
    p_ref, dp_ref, m_ref, t_ref, r_ref, w_ref, pb_ref, ds_ref,
):
    far_scores(d, lengths_ref, q_ref, g_ref, far_ref, p_ref, dp_ref, m_ref, t_ref, r_ref)

    def each(near, *pairs):
        return [near[b] for b in range(3)] + [ref[b] for ref in pairs for b in range(2)]

    peaks, totals, dots = each(mn, m1, m3, m_ref), each(tn, t1, t3, t_ref), each(rn, r1, r3, r_ref)
    peak = functools.reduce(jnp.maximum, peaks)
    factors = [jnp.exp2((m - peak) * TO_EXP2) for m in peaks]
    over = 1.0 / sum(f * t for f, t in zip(factors, totals))
    peak_ref[...] = peak
    over_ref[...] = over
    rd_ref[...] = sum(f * r for f, r in zip(factors, dots)) * over
    for n, ref in enumerate((w1_ref, w3_ref, w_ref)):
        for b in range(2):
            ref[b] = factors[3 + 2 * n + b] * over
    far_back(p_ref, dp_ref, w_ref, rd_ref, q_ref, g_ref, back_ref, pb_ref, ds_ref)


def rest_kernel(
    lengths_ref, q_ref, g_ref, own_ref, z1_ref, z2_ref, f1_ref, f2_ref, f3_ref, peak_ref, over_ref, rd_ref,
    out_ref, dq_ref, near_ref, o_acc, dq_acc, pb_ref, ds_ref,
):
    peer = lax.axis_index("peer")
    x = lax.rem(peer, ROW)
    first = peer * T
    starts = doc_starts(lengths_ref, first)
    near = (own_ref, z1_ref, z2_ref)
    for b in range(9):
        if b < 3:
            key, value = near[b][0], near[b][1]
            hidden = near_hidden(first, starts, b)
        else:
            d, kind = (b - 3) // 2 + 1, (b - 3) % 2
            ref = (f1_ref, f2_ref, f3_ref)[d - 1]
            key, value = ref[kind, 0], ref[kind, 1]
            hidden = far_hidden(first, starts, behind(d, kind, x))
        pb, ds = pb_ref.at[b % 2], ds_ref.at[b % 2]
        for h in range(H):
            s = dot(key, head(q_ref, h), LONG)
            dp = dot(value, head(g_ref, h), LONG)
            s = jnp.where(hidden, NEG, s)
            pn = jnp.exp2((s - peak_ref[h : h + 1]) * TO_EXP2) * over_ref[h : h + 1]
            pb[h] = pn.astype(BF16)
            ds[h] = (pn * (dp - rd_ref[h : h + 1])).astype(BF16)
        kt, vt = key.T, value.T
        for h in range(H):
            o, dq = dot(vt, pb[h], PLAIN), dot(kt, ds[h], PLAIN)
            o_acc[h] = o if b == 0 else o_acc[h] + o
            dq_acc[h] = dq if b == 0 else dq_acc[h] + dq
        if b < 3:
            near_ref[b, 0], near_ref[b, 1] = key_side(q_ref, g_ref, pb, ds)

    for h in range(H):
        out_ref[:, h * D : (h + 1) * D] = o_acc[h].T.astype(BF16)
        dq_ref[:, h * D : (h + 1) * D] = dq_acc[h].T * SCALE


def gather_kernel(near_ref, g1_ref, g2_ref, g3_ref, own_ref, one_ref, two_ref):
    x = lax.rem(lax.axis_index("peer"), ROW)
    own, one, two = near_ref[0], near_ref[1], near_ref[2]
    for d, ref in enumerate((g1_ref, g2_ref, g3_ref), 1):
        a, b = ref[0].astype(F32), ref[1].astype(F32)
        same = x + d < ROW
        own += jnp.where(same, a, 0.0)
        two += jnp.where(same, 0.0, a)
        one += b
    own_ref[...] = own
    one_ref[...] = one.astype(BF16)
    two_ref[...] = two.astype(BF16)


def final_kernel(own_ref, one_ref, two_ref, dk_ref, dv_ref):
    dk_ref[...] = own_ref[0] + one_ref[0].astype(F32) + two_ref[0].astype(F32)
    dv_ref[...] = own_ref[1] + one_ref[1].astype(F32) + two_ref[1].astype(F32)


def along_z(block, rows, peers):
    far = rows * ROW
    return lax.ppermute(block, "peer", [(i, i + far) for i in range(peers) if 0 <= i + far < peers])


def along_x(block, columns, peers):
    return lax.ppermute(block, "peer", [(i, i - i % ROW + (i + columns) % ROW) for i in range(peers)])


def call(kernel, out, specs, scratch=(), blocks=0, limit=24, first=VM):
    return pl.pallas_call(
        kernel,
        out_shape=out,
        in_specs=specs,
        out_specs=(first,) + tuple(VM for _ in out[1:]),
        scratch_shapes=list(scratch),
        compiler_params=pltpu.CompilerParams(vmem_limit_bytes=limit << 20),
        cost_estimate=pl.CostEstimate(
            flops=blocks * H * T * T * D * 4, bytes_accessed=1 << 20, transcendentals=blocks * H * T * T
        ),
    )


def body(queries, keys, values, grad_out, doc_lengths):
    peers = lax.axis_size("peer")
    array = jax.ShapeDtypeStruct
    block, stats = (2, T, D), (H, T)
    pair = array((2, *block), BF16)
    tiles, sums = (array((2, H, T, T), F32),) * 2, (array((2, *stats), F32),) * 3
    staged = [pltpu.VMEM((2, H, T, T), BF16)] * 2
    (own,) = call(
        pair_kernel, (array(block, BF16),), [ANY] * 2, [pltpu.SemaphoreType.DMA((2,))], limit=60, first=ANY
    )(keys, values)
    z1 = along_z(own, 1, peers)
    z2 = along_z(own, 2, peers)
    wanted = (doc_lengths, queries, grad_out)
    (own,) = call(hold_kernel, (array(block, BF16),), [VM], limit=4)(own)
    packed = call(pack_kernel, (pair,) * 3, [VM] * 3, limit=4)(own, z1, z2)
    f1, f2, f3 = (along_x(p, d, peers) for d, p in enumerate(packed, 1))
    near = call(near_kernel, (array((3, *stats), F32),) * 3, [SM] + [VM] * 5, blocks=3, limit=8)(*wanted, own, z1, z2)
    tiles1, sums1, tiles3, sums3 = [], [], [], []
    for d, f, t, u in ((1, f1, tiles1, sums1), (3, f3, tiles3, sums3)):
        got = call(functools.partial(far_scores, d), tiles + sums, [SM] + [VM] * 3, blocks=2, limit=8)(*wanted, f)
        t.extend(got[:2])
        u.extend(got[2:])
    b2, peak, over, rd, w1, w3 = call(
        functools.partial(last_kernel, 2),
        (pair,) + (array(stats, F32),) * 3 + (array((2, *stats), F32),) * 2,
        [SM] + [VM] * 12,
        [pltpu.VMEM((2, H, T, T), F32)] * 2 + [pltpu.VMEM((2, *stats), F32)] * 4 + staged,
        blocks=4,
        limit=16,
    )(*wanted, f2, *near, *sums1, *sums3)
    r2 = along_x(b2, -2, peers)
    back = functools.partial(call, far_back, (pair,), [VM] * 6, staged, blocks=2, limit=8)
    (b3,) = back()(*tiles3, w3, rd, queries, grad_out)
    r3 = along_x(b3, -3, peers)
    (b1,) = back()(*tiles1, w1, rd, queries, grad_out)
    r1 = along_x(b1, -1, peers)
    attended, query_grad, mine = call(
        rest_kernel,
        (array((T, H * D), BF16), array((T, H * D), F32), array((3, *block), F32)),
        [SM] + [VM] * 11,
        [pltpu.VMEM((H, D, T), F32)] * 2 + staged,
        blocks=9,
        limit=16,
    )(*wanted, own, z1, z2, f1, f2, f3, peak, over, rd)
    mine, one, two = call(
        gather_kernel, (array(block, F32), array(block, BF16), array(block, BF16)), [VM] * 4, limit=8
    )(mine, r1, r2, r3)
    key_grad, value_grad = call(final_kernel, (array((T, D), F32),) * 2, [VM] * 3, limit=4)(
        mine, along_z(one, -1, peers), along_z(two, -2, peers)
    )
    return attended, query_grad, key_grad, value_grad


def solution(mesh):
    tokens = P("peer", "head")
    return jax.shard_map(
        body,
        mesh=mesh,
        in_specs=(tokens, tokens, tokens, tokens, P()),
        out_specs=(tokens, tokens, tokens, tokens),
        check_vma=False,
    )
```

time: 77.3 us -> 78.2 us (1.012)
  the two profiles are of different devices: /device:TPU:72 before, /device:TPU:88 now
where the time goes in v4:
time: 78.2 us; the launch traced here: 77.7 us
  starting transfers between devices  32.8 us (42%)
  Pallas kernels  22 us (28%)
  waiting for transfers between devices  18.6 us (24%)
  local copies, waits for them, and re-layouts  3.47 us (4%)
  between operations  0.85 us (1%)
    ppermute x6, starting transfers between devices, along_x(): lax.ppermute(block, 'peer', [(i, i - i % ROW + (i + columns) % ROW) for i...  18.7 us
    ppermute x4, starting transfers between devices, along_z(): lax.ppermute(block, 'peer', [(i, i + far) for i in range(peers) if 0 <= i...  14.1 us
    ppermute x4, waiting for transfers between devices, along_z(): lax.ppermute(block, 'peer', [(i, i + far) for i in range(peers) if 0 <= i...  13.9 us
    pallas_call x1, Pallas kernels, body(): call(rest_kernel, (array((T, H * D), BF16), array((T, H * D), F32), array...  6.95 us
    pallas_call x1, Pallas kernels, body(): call(pair_kernel, (array(block, BF16),), [ANY] * 2, [pltpu.SemaphoreType....  5.09 us
    ppermute x6, waiting for transfers between devices, along_x(): lax.ppermute(block, 'peer', [(i, i - i % ROW + (i + columns) % ROW) for i...  4.72 us
    unnamed x14, local copies, waits for them, and re-layouts  3.47 us
    pallas_call x2, Pallas kernels, body(): call(functools.partial(far_scores, d), tiles + sums, [SM] + [VM] * 3, blo...  3.03 us
  transfers between devices with their start and end apart: 10, of which 6 were waited for; matrix products, arithmetic and copies ran while one was open for 0% of the time, Pallas kernels for 16%

profile of v4, /device:TPU:88, one launch (start us, length us, event | category | flops | bytes accessed | tf_op | source)
XLA Modules:
  0.0 77.7 jit_solution(6516629651559343723)
XLA Ops:
  0.6 0.0 copy-start.3
  0.7 5.1 %shard_map.84.own_ref = bf16[2,256,128]{2,1,0:T(8,128)(2,1)} custom-call(bf16[256,128]{1,0:T(8,128)(2,1)} %k_ref.1, bf16[256,128]{1,0:T(8,128)(2,1)} %v_ref.1), custom_call_target="tpu_custom_call" | custom-call | bytes 1048576 | tf_op jit(solution)/shard_map/pallas_call | solution.py:248
  5.8 6.4 %collective-permute-start.1 = (bf16[2,256,128]{2,1,0:T(8,128)(2,1)}, bf16[2,256,128]{2,1,0:T(8,128)(2,1)S(1)}, u32[]{:S(2)}, u32[]{:S(2)}) collective-permute-start(bf16[2,256,128]{2,1,0:T(8,128)(2,1)} %shard_map.84.own_ref), channel_id=1, source_target_pairs={{0,64},{8,72},{16,80},{24,88},{32,96},{40,104},{48,112},{56,120},{... | collective-permute-start | bytes 393224 | tf_op jit(solution)/shard_map/ppermute | solution.py:220
  12.2 3.8 %collective-permute-start = (bf16[2,256,128]{2,1,0:T(8,128)(2,1)}, bf16[2,256,128]{2,1,0:T(8,128)(2,1)S(1)}, u32[]{:S(2)}, u32[]{:S(2)}) collective-permute-start(bf16[2,256,128]{2,1,0:T(8,128)(2,1)} %shard_map.84.own_ref), channel_id=1, source_target_pairs={{0,32},{8,40},{16,48},{24,56},{32,64},{40,72},{48,80},{56,88},{64,... | collective-permute-start | bytes 393224 | tf_op jit(solution)/shard_map/ppermute | solution.py:220
  16.0 0.9 %copy-done.4 = bf16[2,256,128]{2,1,0:T(8,128)(2,1)S(1)} copy-done((bf16[2,256,128]{2,1,0:T(8,128)(2,1)S(1)}, bf16[2,256,128]{2,1,0:T(8,128)(2,1)}, u32[]{:S(2)}) %copy-start.4) | copy-done | bytes 131096
  16.9 1.9 %collective-permute-done.1.z2_ref = bf16[2,256,128]{2,1,0:T(8,128)(2,1)S(1)} collective-permute-done((bf16[2,256,128]{2,1,0:T(8,128)(2,1)}, bf16[2,256,128]{2,1,0:T(8,128)(2,1)S(1)}, u32[]{:S(2)}, u32[]{:S(2)}) %collective-permute-start.1) | collective-permute-done | bytes 131104 | tf_op jit(solution)/shard_map/ppermute | solution.py:220
  18.9 1.9 %collective-permute-done.z1_ref = bf16[2,256,128]{2,1,0:T(8,128)(2,1)S(1)} collective-permute-done((bf16[2,256,128]{2,1,0:T(8,128)(2,1)}, bf16[2,256,128]{2,1,0:T(8,128)(2,1)S(1)}, u32[]{:S(2)}, u32[]{:S(2)}) %collective-permute-start) | collective-permute-done | bytes 131104 | tf_op jit(solution)/shard_map/ppermute | solution.py:220
  20.8 0.1 shard_map.86
  20.8 4.7 %collective-permute-start.4 = (bf16[2,2,256,128]{3,2,1,0:T(8,128)(2,1)S(1)}, bf16[2,2,256,128]{3,2,1,0:T(8,128)(2,1)S(1)}, u32[]{:S(2)}, u32[]{:S(2)}) collective-permute-start(bf16[2,2,256,128]{3,2,1,0:T(8,128)(2,1)S(1)} %get-tuple-element.36), channel_id=1, source_target_pairs={{0,24},{8,0},{16,8},{24,16},{32,56},{40,32},{48,40},{56,48},{64,88... | collective-permute-start | bytes 786440 | tf_op jit(solution)/shard_map/ppermute | solution.py:224
  25.5 1.9 %collective-permute-start.2 = (bf16[2,2,256,128]{3,2,1,0:T(8,128)(2,1)S(1)}, bf16[2,2,256,128]{3,2,1,0:T(8,128)(2,1)S(1)}, u32[]{:S(2)}, u32[]{:S(2)}) collective-permute-start(bf16[2,2,256,128]{3,2,1,0:T(8,128)(2,1)S(1)} %get-tuple-element.34), channel_id=1, source_target_pairs={{0,8},{8,16},{16,24},{24,0},{32,40},{40,48},{48,56},{56,32},{64,72... | collective-permute-start | bytes 786440 | tf_op jit(solution)/shard_map/ppermute | solution.py:224
  27.4 4.2 %collective-permute-start.3 = (bf16[2,2,256,128]{3,2,1,0:T(8,128)(2,1)S(1)}, bf16[2,2,256,128]{3,2,1,0:T(8,128)(2,1)S(1)}, u32[]{:S(2)}, u32[]{:S(2)}) collective-permute-start(bf16[2,2,256,128]{3,2,1,0:T(8,128)(2,1)S(1)} %get-tuple-element.35), channel_id=1, source_target_pairs={{0,16},{8,24},{16,0},{24,8},{32,48},{40,56},{48,32},{56,40},{64,80... | collective-permute-start | bytes 786440 | tf_op jit(solution)/shard_map/ppermute | solution.py:224
  31.6 0.9 %copy-done = bf16[256,512]{1,0:T(8,128)(2,1)S(1)} copy-done((bf16[256,512]{1,0:T(8,128)(2,1)S(1)}, bf16[256,512]{1,0:T(8,128)(2,1)}, u32[]{:S(2)}) %copy-start) | copy-done | bytes 262168
  32.6 0.9 %copy-done.2 = bf16[256,512]{1,0:T(8,128)(2,1)S(1)} copy-done((bf16[256,512]{1,0:T(8,128)(2,1)S(1)}, bf16[256,512]{1,0:T(8,128)(2,1)}, u32[]{:S(2)}) %copy-start.2) | copy-done | bytes 262168
  33.5 0.7 copy-done.5
  34.2 1.8 %shard_map.87 = (f32[3,4,256]{2,1,0:T(4,128)S(1)}, f32[3,4,256]{2,1,0:T(4,128)S(1)}, f32[3,4,256]{2,1,0:T(4,128)S(1)}) custom-call(s32[32]{0:T(128)S(1)} %copy-done.5, bf16[256,512]{1,0:T(8,128)(2,1)S(1)} %copy-done, bf16[256,512]{1,0:T(8,128)(2,1)S(1)} %copy-done.2, bf16[2,256,128]{2,1,0:T(8,128)(2,1)S(1)} %shard_map.85.own_ref, ...), custom_call_target="tpu_custom_call" | custom-call | flops 402653184 | bytes 1048576 | tf_op jit(solution)/shard_map/pallas_call | solution.py:257
  36.1 1.5 %shard_map.89 = (f32[2,4,256,256]{3,2,1,0:T(8,128)S(1)}, f32[2,4,256,256]{3,2,1,0:T(8,128)S(1)}, f32[2,4,256]{2,1,0:T(4,128)S(1)}, f32[2,4,256]{2,1,0:T(4,128)S(1)}, f32[2,4,256]{2,1,0:T(4,128)S(1)}) custom-call(s32[32]{0:T(128)S(1)} %copy-done.6, bf16[256,512]{1,0:T(8,128)(2,1)S(1)} %copy-done.1, bf16[256,512]{1,0:T(8,128)(2,1)S(1)} %copy-done.3, ...), custom_call_target="tpu_custom_call" | custom-call | flops 268435456 | bytes 1048576 | tf_op jit(solution)/shard_map/pallas_call | solution.py:260
  37.6 3.8 %collective-permute-done.2.far_ref.f1_ref = bf16[2,2,256,128]{3,2,1,0:T(8,128)(2,1)S(1)} collective-permute-done((bf16[2,2,256,128]{3,2,1,0:T(8,128)(2,1)S(1)}, bf16[2,2,256,128]{3,2,1,0:T(8,128)(2,1)S(1)}, u32[]{:S(2)}, u32[]{:S(2)}) %collective-permute-start.2) | collective-permute-done | bytes 262176 | tf_op jit(solution)/shard_map/ppermute | solution.py:224
  41.4 1.5 %shard_map.88 = (f32[2,4,256,256]{3,2,1,0:T(8,128)S(1)}, f32[2,4,256,256]{3,2,1,0:T(8,128)S(1)}, f32[2,4,256]{2,1,0:T(4,128)S(1)}, f32[2,4,256]{2,1,0:T(4,128)S(1)}, f32[2,4,256]{2,1,0:T(4,128)S(1)}) custom-call(s32[32]{0:T(128)S(1)} %copy-done.6, bf16[256,512]{1,0:T(8,128)(2,1)S(1)} %copy-done.1, bf16[256,512]{1,0:T(8,128)(2,1)S(1)} %copy-done.3, ...), custom_call_target="tpu_custom_call" | custom-call | flops 268435456 | bytes 1048576 | tf_op jit(solution)/shard_map/pallas_call | solution.py:260
  42.9 2.6 %shard_map.90 = (bf16[2,2,256,128]{3,2,1,0:T(8,128)(2,1)S(1)}, f32[4,256]{1,0:T(4,128)S(1)}, f32[4,256]{1,0:T(4,128)S(1)}, f32[4,256]{1,0:T(4,128)S(1)}, f32[2,4...) custom-call(s32[32]{0:T(128)S(1)} %copy-done.6, bf16[256,512]{1,0:T(8,128)(2,1)S(1)} %copy-done.1, ...), custom_call_target="tpu_custom_call" | custom-call | flops 536870912 | bytes 1048576 | tf_op jit(solution)/shard_map/pallas_call | solution.py:263
  45.5 0.8 shard_map.92
  46.2 1.9 %collective-permute-start.5 = (bf16[2,2,256,128]{3,2,1,0:T(8,128)(2,1)S(1)}, bf16[2,2,256,128]{3,2,1,0:T(8,128)(2,1)S(1)}, u32[]{:S(2)}, u32[]{:S(2)}) collective-permute-start(bf16[2,2,256,128]{3,2,1,0:T(8,128)(2,1)S(1)} %shard_map.92), channel_id=1, source_target_pairs={{0,24},{8,0},{16,8},{24,16},{32,56},{40,32},{48,40},{56,48},{64,88... | collective-permute-start | bytes 786440 | tf_op jit(solution)/shard_map/ppermute | solution.py:224
  48.1 2.0 %collective-permute-start.6 = (bf16[2,2,256,128]{3,2,1,0:T(8,128)(2,1)S(1)}, bf16[2,2,256,128]{3,2,1,0:T(8,128)(2,1)S(1)}, u32[]{:S(2)}, u32[]{:S(2)}) collective-permute-start(bf16[2,2,256,128]{3,2,1,0:T(8,128)(2,1)S(1)} %get-tuple-element.55), channel_id=1, source_target_pairs={{0,16},{8,24},{16,0},{24,8},{32,48},{40,56},{48,32},{56,40},{64,80... | collective-permute-start | bytes 786440 | tf_op jit(solution)/shard_map/ppermute | solution.py:224
  50.2 0.8 shard_map.93
  50.9 4.0 %collective-permute-start.7 = (bf16[2,2,256,128]{3,2,1,0:T(8,128)(2,1)S(1)}, bf16[2,2,256,128]{3,2,1,0:T(8,128)(2,1)S(1)}, u32[]{:S(2)}, u32[]{:S(2)}) collective-permute-start(bf16[2,2,256,128]{3,2,1,0:T(8,128)(2,1)S(1)} %shard_map.93), channel_id=1, source_target_pairs={{0,8},{8,16},{16,24},{24,0},{32,40},{40,48},{48,56},{56,32},{64,72... | collective-permute-start | bytes 786440 | tf_op jit(solution)/shard_map/ppermute | solution.py:224
  55.0 7.0 %shard_map.91 = (bf16[256,512]{1,0:T(8,128)(2,1)}, f32[256,512]{1,0:T(8,128)}, f32[3,2,256,128]{3,2,1,0:T(8,128)S(1)}) custom-call(s32[32]{0:T(128)S(1)} %copy-done.6, bf16[256,512]{1,0:T(8,128)(2,1)S(1)} %copy-done.1, bf16[256,512]{1,0:T(8,128)(2,1)S(1)} %copy-done.3, bf16[2,256,128]{2,1,0:T(8,128)(2,1)S(1)} %shard_map.85.own_ref, ...), custom_call_target="tpu_custom_call" | custom-call | flops 1207959552 | bytes 1048576 | tf_op jit(solution)/shard_map/pallas_call | solution.py:277
  61.9 0.9 %collective-permute-done.7.g3_ref = bf16[2,2,256,128]{3,2,1,0:T(8,128)(2,1)S(1)} collective-permute-done((bf16[2,2,256,128]{3,2,1,0:T(8,128)(2,1)S(1)}, bf16[2,2,256,128]{3,2,1,0:T(8,128)(2,1)S(1)}, u32[]{:S(2)}, u32[]{:S(2)}) %collective-permute-start.7) | collective-permute-done | bytes 262176 | tf_op jit(solution)/shard_map/ppermute | solution.py:224
  62.8 0.2 shard_map.94
  63.1 1.9 %collective-permute-start.8 = (bf16[2,256,128]{2,1,0:T(8,128)(2,1)S(1)}, bf16[2,256,128]{2,1,0:T(8,128)(2,1)S(1)}, u32[]{:S(2)}, u32[]{:S(2)}) collective-permute-start(bf16[2,256,128]{2,1,0:T(8,128)(2,1)S(1)} %get-tuple-element.60), channel_id=1, source_target_pairs={{32,0},{40,8},{48,16},{56,24},{64,32},{72,40},{80,48},{88,56},{96,... | collective-permute-start | bytes 393224 | tf_op jit(solution)/shard_map/ppermute | solution.py:220
  65.0 1.9 %collective-permute-start.9 = (bf16[2,256,128]{2,1,0:T(8,128)(2,1)S(1)}, bf16[2,256,128]{2,1,0:T(8,128)(2,1)S(1)}, u32[]{:S(2)}, u32[]{:S(2)}) collective-permute-start(bf16[2,256,128]{2,1,0:T(8,128)(2,1)S(1)} %get-tuple-element.61), channel_id=1, source_target_pairs={{64,0},{72,8},{80,16},{88,24},{96,32},{104,40},{112,48},{120,56},{... | collective-permute-start | bytes 393224 | tf_op jit(solution)/shard_map/ppermute | solution.py:220
  66.9 4.6 %collective-permute-done.8.one_ref = bf16[2,256,128]{2,1,0:T(8,128)(2,1)S(1)} collective-permute-done((bf16[2,256,128]{2,1,0:T(8,128)(2,1)S(1)}, bf16[2,256,128]{2,1,0:T(8,128)(2,1)S(1)}, u32[]{:S(2)}, u32[]{:S(2)}) %collective-permute-start.8) | collective-permute-done | bytes 131104 | tf_op jit(solution)/shard_map/ppermute | solution.py:220
  71.6 5.4 %collective-permute-done.9.two_ref = bf16[2,256,128]{2,1,0:T(8,128)(2,1)S(1)} collective-permute-done((bf16[2,256,128]{2,1,0:T(8,128)(2,1)S(1)}, bf16[2,256,128]{2,1,0:T(8,128)(2,1)S(1)}, u32[]{:S(2)}, u32[]{:S(2)}) %collective-permute-start.9) | collective-permute-done | bytes 131104 | tf_op jit(solution)/shard_map/ppermute | solution.py:220
  77.0 0.7 shard_map.95
  (14 shorter events, 0.0 us)
Async XLA Ops:
  0.6 35.4 %copy-start.3 = (bf16[256,512]{1,0:T(8,128)(2,1)S(1)}, bf16[256,512]{1,0:T(8,128)(2,1)}, u32[]{:S(2)}) copy-start(bf16[256,512]{1,0:T(8,128)(2,1)} %g_ref.13) | copy-start | bytes 786436
  0.6 35.4 %copy-start.1 = (bf16[256,512]{1,0:T(8,128)(2,1)S(1)}, bf16[256,512]{1,0:T(8,128)(2,1)}, u32[]{:S(2)}) copy-start(bf16[256,512]{1,0:T(8,128)(2,1)} %q_ref.13) | copy-start | bytes 786436
  5.8 13.1 %collective-permute-start.1 = (bf16[2,256,128]{2,1,0:T(8,128)(2,1)}, bf16[2,256,128]{2,1,0:T(8,128)(2,1)S(1)}, u32[]{:S(2)}, u32[]{:S(2)}) collective-permute-start(bf16[2,256,128]{2,1,0:T(8,128)(2,1)} %shard_map.84.own_ref), channel_id=1, source_target_pairs={{0,64},{8,72},{16,80},{24,88},{32,96},{40,104},{48,112},{56,120},{... | collective-permute-start | bytes 393224 | tf_op jit(solution)/shard_map/ppermute | solution.py:220
  12.2 8.6 %collective-permute-start = (bf16[2,256,128]{2,1,0:T(8,128)(2,1)}, bf16[2,256,128]{2,1,0:T(8,128)(2,1)S(1)}, u32[]{:S(2)}, u32[]{:S(2)}) collective-permute-start(bf16[2,256,128]{2,1,0:T(8,128)(2,1)} %shard_map.84.own_ref), channel_id=1, source_target_pairs={{0,32},{8,40},{16,48},{24,56},{32,64},{40,72},{48,80},{56,88},{64,... | collective-permute-start | bytes 393224 | tf_op jit(solution)/shard_map/ppermute | solution.py:220
  16.0 0.9 %copy-start.4 = (bf16[2,256,128]{2,1,0:T(8,128)(2,1)S(1)}, bf16[2,256,128]{2,1,0:T(8,128)(2,1)}, u32[]{:S(2)}) copy-start(bf16[2,256,128]{2,1,0:T(8,128)(2,1)} %shard_map.84.own_ref) | copy-start | bytes 393220
  16.9 19.2 %copy-start.6 = (s32[32]{0:T(128)S(1)}, s32[32]{0:T(128)}, u32[]{:S(2)}) copy-start(s32[32]{0:T(128)} %lengths_ref.9) | copy-start | bytes 388
  20.8 15.2 %collective-permute-start.4 = (bf16[2,2,256,128]{3,2,1,0:T(8,128)(2,1)S(1)}, bf16[2,2,256,128]{3,2,1,0:T(8,128)(2,1)S(1)}, u32[]{:S(2)}, u32[]{:S(2)}) collective-permute-start(bf16[2,2,256,128]{3,2,1,0:T(8,128)(2,1)S(1)} %get-tuple-element.36), channel_id=1, source_target_pairs={{0,24},{8,0},{16,8},{24,16},{32,56},{40,32},{48,40},{56,48},{64,88... | collective-permute-start | bytes 786440 | tf_op jit(solution)/shard_map/ppermute | solution.py:224
  25.5 15.9 %collective-permute-start.2 = (bf16[2,2,256,128]{3,2,1,0:T(8,128)(2,1)S(1)}, bf16[2,2,256,128]{3,2,1,0:T(8,128)(2,1)S(1)}, u32[]{:S(2)}, u32[]{:S(2)}) collective-permute-start(bf16[2,2,256,128]{3,2,1,0:T(8,128)(2,1)S(1)} %get-tuple-element.34), channel_id=1, source_target_pairs={{0,8},{8,16},{16,24},{24,0},{32,40},{40,48},{48,56},{56,32},{64,72... | collective-permute-start | bytes 786440 | tf_op jit(solution)/shard_map/ppermute | solution.py:224
  27.4 15.5 %collective-permute-start.3 = (bf16[2,2,256,128]{3,2,1,0:T(8,128)(2,1)S(1)}, bf16[2,2,256,128]{3,2,1,0:T(8,128)(2,1)S(1)}, u32[]{:S(2)}, u32[]{:S(2)}) collective-permute-start(bf16[2,2,256,128]{3,2,1,0:T(8,128)(2,1)S(1)} %get-tuple-element.35), channel_id=1, source_target_pairs={{0,16},{8,24},{16,0},{24,8},{32,48},{40,56},{48,32},{56,40},{64,80... | collective-permute-start | bytes 786440 | tf_op jit(solution)/shard_map/ppermute | solution.py:224
  31.6 1.0 %copy-start = (bf16[256,512]{1,0:T(8,128)(2,1)S(1)}, bf16[256,512]{1,0:T(8,128)(2,1)}, u32[]{:S(2)}) copy-start(bf16[256,512]{1,0:T(8,128)(2,1)} %q_ref.13) | copy-start | bytes 786436
  32.6 0.9 %copy-start.2 = (bf16[256,512]{1,0:T(8,128)(2,1)S(1)}, bf16[256,512]{1,0:T(8,128)(2,1)}, u32[]{:S(2)}) copy-start(bf16[256,512]{1,0:T(8,128)(2,1)} %g_ref.13) | copy-start | bytes 786436
  33.5 0.7 copy-start.5
  46.2 15.7 %collective-permute-start.5 = (bf16[2,2,256,128]{3,2,1,0:T(8,128)(2,1)S(1)}, bf16[2,2,256,128]{3,2,1,0:T(8,128)(2,1)S(1)}, u32[]{:S(2)}, u32[]{:S(2)}) collective-permute-start(bf16[2,2,256,128]{3,2,1,0:T(8,128)(2,1)S(1)} %shard_map.92), channel_id=1, source_target_pairs={{0,24},{8,0},{16,8},{24,16},{32,56},{40,32},{48,40},{56,48},{64,88... | collective-permute-start | bytes 786440 | tf_op jit(solution)/shard_map/ppermute | solution.py:224
  48.1 13.8 %collective-permute-start.6 = (bf16[2,2,256,128]{3,2,1,0:T(8,128)(2,1)S(1)}, bf16[2,2,256,128]{3,2,1,0:T(8,128)(2,1)S(1)}, u32[]{:S(2)}, u32[]{:S(2)}) collective-permute-start(bf16[2,2,256,128]{3,2,1,0:T(8,128)(2,1)S(1)} %get-tuple-element.55), channel_id=1, source_target_pairs={{0,16},{8,24},{16,0},{24,8},{32,48},{40,56},{48,32},{56,40},{64,80... | collective-permute-start | bytes 786440 | tf_op jit(solution)/shard_map/ppermute | solution.py:224
  50.9 11.9 %collective-permute-start.7 = (bf16[2,2,256,128]{3,2,1,0:T(8,128)(2,1)S(1)}, bf16[2,2,256,128]{3,2,1,0:T(8,128)(2,1)S(1)}, u32[]{:S(2)}, u32[]{:S(2)}) collective-permute-start(bf16[2,2,256,128]{3,2,1,0:T(8,128)(2,1)S(1)} %shard_map.93), channel_id=1, source_target_pairs={{0,8},{8,16},{16,24},{24,0},{32,40},{40,48},{48,56},{56,32},{64,72... | collective-permute-start | bytes 786440 | tf_op jit(solution)/shard_map/ppermute | solution.py:224
  63.1 8.5 %collective-permute-start.8 = (bf16[2,256,128]{2,1,0:T(8,128)(2,1)S(1)}, bf16[2,256,128]{2,1,0:T(8,128)(2,1)S(1)}, u32[]{:S(2)}, u32[]{:S(2)}) collective-permute-start(bf16[2,256,128]{2,1,0:T(8,128)(2,1)S(1)} %get-tuple-element.60), channel_id=1, source_target_pairs={{32,0},{40,8},{48,16},{56,24},{64,32},{72,40},{80,48},{88,56},{96,... | collective-permute-start | bytes 393224 | tf_op jit(solution)/shard_map/ppermute | solution.py:220
  65.0 12.0 %collective-permute-start.9 = (bf16[2,256,128]{2,1,0:T(8,128)(2,1)S(1)}, bf16[2,256,128]{2,1,0:T(8,128)(2,1)S(1)}, u32[]{:S(2)}, u32[]{:S(2)}) collective-permute-start(bf16[2,256,128]{2,1,0:T(8,128)(2,1)S(1)} %get-tuple-element.61), channel_id=1, source_target_pairs={{64,0},{72,8},{80,16},{88,24},{96,32},{104,40},{112,48},{120,56},{... | collective-permute-start | bytes 393224 | tf_op jit(solution)/shard_map/ppermute | solution.py:220

commit v5 on v4

--- a/solution.py
+++ b/solution.py
@@ -57,15 +57,18 @@
         r_ref[index, h : h + 1] = jnp.sum(p * dp, axis=0, keepdims=True)
 
 
-def pair_kernel(k_ref, v_ref, out_ref, sem):
-    copies = [pltpu.make_async_copy(r, out_ref.at[i], sem.at[i]) for i, r in enumerate((k_ref, v_ref))]
-    for copy in copies:
-        copy.start()
-    for copy in copies:
-        copy.wait()
-
-
-def pack_kernel(own_ref, z1_ref, z2_ref, *out_refs):
+def pair_kernel(k_ref, v_ref, out_ref):
+    out_ref[0] = k_ref[...]
+    out_ref[1] = v_ref[...]
+
+
+def hold_kernel(lengths_ref, q_ref, g_ref, q_out, g_out, starts_ref):
+    q_out[...] = q_ref[...]
+    g_out[...] = g_ref[...]
+    starts_ref[...] = doc_starts(lengths_ref, lax.axis_index("peer") * T)
+
+
+def pack_kernel(_, own_ref, z1_ref, z2_ref, *out_refs):
     x = lax.rem(lax.axis_index("peer"), ROW)
     for d, ref in enumerate(out_refs, 1):
 
@@ -93,13 +96,9 @@
     return (rows + (first - behind * T)) < starts
 
 
-def hold_kernel(own_ref, held_ref):
-    held_ref[...] = own_ref[...]
-
-
-def near_kernel(lengths_ref, q_ref, g_ref, own_ref, z1_ref, z2_ref, m_ref, t_ref, r_ref):
+def near_kernel(starts_ref, q_ref, g_ref, own_ref, z1_ref, z2_ref, m_ref, t_ref, r_ref):
     first = lax.axis_index("peer") * T
-    starts = doc_starts(lengths_ref, first)
+    starts = starts_ref[...]
     for i, ref in enumerate((own_ref, z1_ref, z2_ref)):
         scores(q_ref, g_ref, ref[0], ref[1], near_hidden(first, starts, i), i, m_ref, t_ref, r_ref)
 
@@ -114,10 +113,10 @@
     return dk * SCALE, dv
 
 
-def far_scores(d, lengths_ref, q_ref, g_ref, far_ref, p_ref, dp_ref, m_ref, t_ref, r_ref):
+def far_scores(d, starts_ref, q_ref, g_ref, far_ref, p_ref, dp_ref, m_ref, t_ref, r_ref):
     peer = lax.axis_index("peer")
     first = peer * T
-    starts = doc_starts(lengths_ref, first)
+    starts = starts_ref[...]
     for i in range(2):
         hidden = far_hidden(first, starts, behind(d, i, lax.rem(peer, ROW)))
         scores(q_ref, g_ref, far_ref[i, 0], far_ref[i, 1], hidden, i, m_ref, t_ref, r_ref, p_ref, dp_ref)
@@ -135,36 +134,36 @@
 
 
 def last_kernel(
-    d, lengths_ref, q_ref, g_ref, far_ref, mn, tn, rn, m1, t1, r1, m3, t3, r3,
-    back_ref, peak_ref, over_ref, rd_ref, w1_ref, w3_ref,
-    p_ref, dp_ref, m_ref, t_ref, r_ref, w_ref, pb_ref, ds_ref,
+    starts_ref, q_ref, g_ref, far_ref, mn, tn, rn, m1, t1, r1, p2_ref, dp2_ref, m2, t2, r2,
+    back_ref, peak_ref, over_ref, rd_ref, w1_ref, w3_ref, p_ref, dp_ref,
+    m_ref, t_ref, r_ref, w2_ref, pb_ref, ds_ref,
 ):
-    far_scores(d, lengths_ref, q_ref, g_ref, far_ref, p_ref, dp_ref, m_ref, t_ref, r_ref)
+    far_scores(3, starts_ref, q_ref, g_ref, far_ref, p_ref, dp_ref, m_ref, t_ref, r_ref)
 
     def each(near, *pairs):
         return [near[b] for b in range(3)] + [ref[b] for ref in pairs for b in range(2)]
 
-    peaks, totals, dots = each(mn, m1, m3, m_ref), each(tn, t1, t3, t_ref), each(rn, r1, r3, r_ref)
+    peaks, totals, dots = each(mn, m1, m2, m_ref), each(tn, t1, t2, t_ref), each(rn, r1, r2, r_ref)
     peak = functools.reduce(jnp.maximum, peaks)
     factors = [jnp.exp2((m - peak) * TO_EXP2) for m in peaks]
     over = 1.0 / sum(f * t for f, t in zip(factors, totals))
     peak_ref[...] = peak
     over_ref[...] = over
     rd_ref[...] = sum(f * r for f, r in zip(factors, dots)) * over
-    for n, ref in enumerate((w1_ref, w3_ref, w_ref)):
+    for n, ref in enumerate((w1_ref, w2_ref, w3_ref)):
         for b in range(2):
             ref[b] = factors[3 + 2 * n + b] * over
-    far_back(p_ref, dp_ref, w_ref, rd_ref, q_ref, g_ref, back_ref, pb_ref, ds_ref)
+    far_back(p2_ref, dp2_ref, w2_ref, rd_ref, q_ref, g_ref, back_ref, pb_ref, ds_ref)
 
 
 def rest_kernel(
-    lengths_ref, q_ref, g_ref, own_ref, z1_ref, z2_ref, f1_ref, f2_ref, f3_ref, peak_ref, over_ref, rd_ref,
+    starts_ref, q_ref, g_ref, own_ref, z1_ref, z2_ref, f1_ref, f2_ref, f3_ref, peak_ref, over_ref, rd_ref,
     out_ref, dq_ref, near_ref, o_acc, dq_acc, pb_ref, ds_ref,
 ):
     peer = lax.axis_index("peer")
     x = lax.rem(peer, ROW)
     first = peer * T
-    starts = doc_starts(lengths_ref, first)
+    starts = starts_ref[...]
     near = (own_ref, z1_ref, z2_ref)
     for b in range(9):
         if b < 3:
@@ -196,23 +195,31 @@
         dq_ref[:, h * D : (h + 1) * D] = dq_acc[h].T * SCALE
 
 
-def gather_kernel(near_ref, g1_ref, g2_ref, g3_ref, own_ref, one_ref, two_ref):
-    x = lax.rem(lax.axis_index("peer"), ROW)
-    own, one, two = near_ref[0], near_ref[1], near_ref[2]
-    for d, ref in enumerate((g1_ref, g2_ref, g3_ref), 1):
-        a, b = ref[0].astype(F32), ref[1].astype(F32)
-        same = x + d < ROW
-        own += jnp.where(same, a, 0.0)
-        two += jnp.where(same, 0.0, a)
-        one += b
+def add_back(d, ref, own, one, two):
+    same = lax.rem(lax.axis_index("peer"), ROW) + d < ROW
+    a, b = ref[0].astype(F32), ref[1].astype(F32)
+    return own + jnp.where(same, a, 0.0), one + b, two + jnp.where(same, 0.0, a)
+
+
+def gather_first_kernel(mine_ref, r2_ref, out_ref):
+    for i, total in enumerate(add_back(2, r2_ref, mine_ref[0], mine_ref[1], mine_ref[2])):
+        out_ref[i] = total
+
+
+def gather_kernel(mine_ref, r1_ref, r3_ref, own_ref, one_ref, two_ref):
+    own, one, two = add_back(3, r3_ref, *add_back(1, r1_ref, mine_ref[0], mine_ref[1], mine_ref[2]))
     own_ref[...] = own
     one_ref[...] = one.astype(BF16)
     two_ref[...] = two.astype(BF16)
 
 
-def final_kernel(own_ref, one_ref, two_ref, dk_ref, dv_ref):
-    dk_ref[...] = own_ref[0] + one_ref[0].astype(F32) + two_ref[0].astype(F32)
-    dv_ref[...] = own_ref[1] + one_ref[1].astype(F32) + two_ref[1].astype(F32)
+def add_two_kernel(own_ref, two_ref, out_ref):
+    out_ref[...] = own_ref[...] + two_ref[...].astype(F32)
+
+
+def final_kernel(own_ref, one_ref, dk_ref, dv_ref):
+    dk_ref[...] = own_ref[0] + one_ref[0].astype(F32)
+    dv_ref[...] = own_ref[1] + one_ref[1].astype(F32)
 
 
 def along_z(block, rows, peers):
@@ -245,49 +252,52 @@
     pair = array((2, *block), BF16)
     tiles, sums = (array((2, H, T, T), F32),) * 2, (array((2, *stats), F32),) * 3
     staged = [pltpu.VMEM((2, H, T, T), BF16)] * 2
-    (own,) = call(
-        pair_kernel, (array(block, BF16),), [ANY] * 2, [pltpu.SemaphoreType.DMA((2,))], limit=60, first=ANY
-    )(keys, values)
+    (own,) = call(pair_kernel, (array(block, BF16),), [VM] * 2, limit=4)(keys, values)
     z1 = along_z(own, 1, peers)
     z2 = along_z(own, 2, peers)
-    wanted = (doc_lengths, queries, grad_out)
-    (own,) = call(hold_kernel, (array(block, BF16),), [VM], limit=4)(own)
-    packed = call(pack_kernel, (pair,) * 3, [VM] * 3, limit=4)(own, z1, z2)
+    queries, grad_out, starts = call(
+        hold_kernel,
+        (array((T, H * D), BF16), array((T, H * D), BF16), array((1, T), jnp.int32)),
+        [SM] + [VM] * 2,
+        blocks=1,
+        limit=4,
+    )(doc_lengths, queries, grad_out)
+    wanted = (starts, queries, grad_out)
+    packed = call(pack_kernel, (pair,) * 3, [VM] * 4, limit=4)(starts, own, z1, z2)
     f1, f2, f3 = (along_x(p, d, peers) for d, p in enumerate(packed, 1))
-    near = call(near_kernel, (array((3, *stats), F32),) * 3, [SM] + [VM] * 5, blocks=3, limit=8)(*wanted, own, z1, z2)
-    tiles1, sums1, tiles3, sums3 = [], [], [], []
-    for d, f, t, u in ((1, f1, tiles1, sums1), (3, f3, tiles3, sums3)):
-        got = call(functools.partial(far_scores, d), tiles + sums, [SM] + [VM] * 3, blocks=2, limit=8)(*wanted, f)
-        t.extend(got[:2])
-        u.extend(got[2:])
-    b2, peak, over, rd, w1, w3 = call(
-        functools.partial(last_kernel, 2),
-        (pair,) + (array(stats, F32),) * 3 + (array((2, *stats), F32),) * 2,
-        [SM] + [VM] * 12,
-        [pltpu.VMEM((2, H, T, T), F32)] * 2 + [pltpu.VMEM((2, *stats), F32)] * 4 + staged,
+    near = call(near_kernel, (array((3, *stats), F32),) * 3, [VM] * 6, blocks=3, limit=8)(*wanted, own, z1, z2)
+    arrive = {d: call(functools.partial(far_scores, d), tiles + sums, [VM] * 4, blocks=2, limit=8) for d in (1, 2)}
+    p2, dp2, *sums2 = arrive[2](*wanted, f2)
+    p1, dp1, *sums1 = arrive[1](*wanted, f1)
+    b2, peak, over, rd, w1, w3, p3, dp3 = call(
+        last_kernel,
+        (pair,) + (array(stats, F32),) * 3 + (array((2, *stats), F32),) * 2 + tiles,
+        [VM] * 15,
+        [pltpu.VMEM((2, *stats), F32)] * 4 + staged,
         blocks=4,
-        limit=16,
-    )(*wanted, f2, *near, *sums1, *sums3)
+        limit=8,
+    )(*wanted, f3, *near, *sums1, p2, dp2, *sums2)
     r2 = along_x(b2, -2, peers)
     back = functools.partial(call, far_back, (pair,), [VM] * 6, staged, blocks=2, limit=8)
-    (b3,) = back()(*tiles3, w3, rd, queries, grad_out)
+    (b3,) = back()(p3, dp3, w3, rd, queries, grad_out)
     r3 = along_x(b3, -3, peers)
-    (b1,) = back()(*tiles1, w1, rd, queries, grad_out)
+    (b1,) = back()(p1, dp1, w1, rd, queries, grad_out)
     r1 = along_x(b1, -1, peers)
     attended, query_grad, mine = call(
         rest_kernel,
         (array((T, H * D), BF16), array((T, H * D), F32), array((3, *block), F32)),
-        [SM] + [VM] * 11,
+        [VM] * 12,
         [pltpu.VMEM((H, D, T), F32)] * 2 + staged,
         blocks=9,
         limit=16,
     )(*wanted, own, z1, z2, f1, f2, f3, peak, over, rd)
+    (mine,) = call(gather_first_kernel, (array((3, *block), F32),), [VM] * 2, limit=4)(mine, r2)
     mine, one, two = call(
-        gather_kernel, (array(block, F32), array(block, BF16), array(block, BF16)), [VM] * 4, limit=8
-    )(mine, r1, r2, r3)
-    key_grad, value_grad = call(final_kernel, (array((T, D), F32),) * 2, [VM] * 3, limit=4)(
-        mine, along_z(one, -1, peers), along_z(two, -2, peers)
-    )
+        gather_kernel, (array(block, F32), array(block, BF16), array(block, BF16)), [VM] * 3, limit=4
+    )(mine, r1, r3)
+    two, one = along_z(two, -2, peers), along_z(one, -1, peers)
+    (mine,) = call(add_two_kernel, (array(block, F32),), [VM] * 2, limit=4)(mine, two)
+    key_grad, value_grad = call(final_kernel, (array((T, D), F32),) * 2, [VM] * 2, limit=4)(mine, one)
     return attended, query_grad, key_grad, value_grad
 
 

time: 78.2 us -> 74.1 us (0.948)
  the two profiles are of different devices: /device:TPU:88 before, /device:TPU:98 now
where the time goes in v5:
time: 74.1 us; the launch traced here: 73.6 us
  starting transfers between devices  34.4 us (46%)
  waiting for transfers between devices  19.5 us (26%)
  Pallas kernels  14.7 us (20%)
  local copies, waits for them, and re-layouts  4.22 us (6%)
  between operations  0.83 us (1%)
    ppermute x6, starting transfers between devices, along_x(): lax.ppermute(block, 'peer', [(i, i - i % ROW + (i + columns) % ROW) for i...  20.3 us
    ppermute x4, starting transfers between devices, along_z(): lax.ppermute(block, 'peer', [(i, i + far) for i in range(peers) if 0 <= i...  14.1 us
    ppermute x4, waiting for transfers between devices, along_z(): lax.ppermute(block, 'peer', [(i, i + far) for i in range(peers) if 0 <= i...  12.6 us
    ppermute x6, waiting for transfers between devices, along_x(): lax.ppermute(block, 'peer', [(i, i - i % ROW + (i + columns) % ROW) for i...  6.92 us
    pallas_call x1, Pallas kernels, body(): call(rest_kernel, (array((T, H * D), BF16), array((T, H * D), F32), array...  6.4 us
    unnamed x10, local copies, waits for them, and re-layouts  4.22 us
    pallas_call x1, Pallas kernels, body(): call(last_kernel, (pair,) + (array(stats, F32),) * 3 + (array((2, *stats)...  1.86 us
  transfers between devices with their start and end apart: 10, of which 5 were waited for; matrix products, arithmetic and copies ran while one was open for 0% of the time, Pallas kernels for 15%

profile of v5, /device:TPU:98, one launch (start us, length us, event | category | flops | bytes accessed | tf_op | source)
XLA Modules:
  0.0 73.6 jit_solution(10705975345871632343)
XLA Ops:
  0.6 0.8 %copy-done.2 = bf16[256,128]{1,0:T(8,128)(2,1)S(1)} copy-done((bf16[256,128]{1,0:T(8,128)(2,1)S(1)}, bf16[256,128]{1,0:T(8,128)(2,1)}, u32[]{:S(2)}) %copy-start.2) | copy-done | bytes 65560
  1.5 0.8 %copy-done.3 = bf16[256,128]{1,0:T(8,128)(2,1)S(1)} copy-done((bf16[256,128]{1,0:T(8,128)(2,1)S(1)}, bf16[256,128]{1,0:T(8,128)(2,1)}, u32[]{:S(2)}) %copy-start.3) | copy-done | bytes 65560
  2.3 6.4 %collective-permute-start.1 = (bf16[2,256,128]{2,1,0:T(8,128)(2,1)S(1)}, bf16[2,256,128]{2,1,0:T(8,128)(2,1)S(1)}, u32[]{:S(2)}, u32[]{:S(2)}) collective-permute-start(bf16[2,256,128]{2,1,0:T(8,128)(2,1)S(1)} %shard_map.85.own_ref), channel_id=1, source_target_pairs={{0,64},{8,72},{16,80},{24,88},{32,96},{40,104},{48,112},{56,120},{... | collective-permute-start | bytes 393224 | tf_op jit(solution)/shard_map/ppermute | solution.py:227
  8.7 3.8 %collective-permute-start = (bf16[2,256,128]{2,1,0:T(8,128)(2,1)S(1)}, bf16[2,256,128]{2,1,0:T(8,128)(2,1)S(1)}, u32[]{:S(2)}, u32[]{:S(2)}) collective-permute-start(bf16[2,256,128]{2,1,0:T(8,128)(2,1)S(1)} %shard_map.85.own_ref), channel_id=1, source_target_pairs={{0,32},{8,40},{16,48},{24,56},{32,64},{40,72},{48,80},{56,88},{64,... | collective-permute-start | bytes 393224 | tf_op jit(solution)/shard_map/ppermute | solution.py:227
  12.6 0.9 %copy-done = bf16[256,512]{1,0:T(8,128)(2,1)S(1)} copy-done((bf16[256,512]{1,0:T(8,128)(2,1)S(1)}, bf16[256,512]{1,0:T(8,128)(2,1)}, u32[]{:S(2)}) %copy-start) | copy-done | bytes 262168
  13.5 0.9 %copy-done.1 = bf16[256,512]{1,0:T(8,128)(2,1)S(1)} copy-done((bf16[256,512]{1,0:T(8,128)(2,1)S(1)}, bf16[256,512]{1,0:T(8,128)(2,1)}, u32[]{:S(2)}) %copy-start.1) | copy-done | bytes 262168
  14.5 0.7 copy-done.4
  15.1 0.6 shard_map.84
  15.7 1.9 %collective-permute-done.z1_ref = bf16[2,256,128]{2,1,0:T(8,128)(2,1)S(1)} collective-permute-done((bf16[2,256,128]{2,1,0:T(8,128)(2,1)S(1)}, bf16[2,256,128]{2,1,0:T(8,128)(2,1)S(1)}, u32[]{:S(2)}, u32[]{:S(2)}) %collective-permute-start) | collective-permute-done | bytes 131104 | tf_op jit(solution)/shard_map/ppermute | solution.py:227
  17.6 0.1 shard_map.86
  17.7 4.0 %collective-permute-start.3 = (bf16[2,2,256,128]{3,2,1,0:T(8,128)(2,1)S(1)}, bf16[2,2,256,128]{3,2,1,0:T(8,128)(2,1)S(1)}, u32[]{:S(2)}, u32[]{:S(2)}) collective-permute-start(bf16[2,2,256,128]{3,2,1,0:T(8,128)(2,1)S(1)} %get-tuple-element.43), channel_id=1, source_target_pairs={{0,16},{8,24},{16,0},{24,8},{32,48},{40,56},{48,32},{56,40},{64,80... | collective-permute-start | bytes 786440 | tf_op jit(solution)/shard_map/ppermute | solution.py:231
  21.7 1.9 %collective-permute-start.2 = (bf16[2,2,256,128]{3,2,1,0:T(8,128)(2,1)S(1)}, bf16[2,2,256,128]{3,2,1,0:T(8,128)(2,1)S(1)}, u32[]{:S(2)}, u32[]{:S(2)}) collective-permute-start(bf16[2,2,256,128]{3,2,1,0:T(8,128)(2,1)S(1)} %get-tuple-element.42), channel_id=1, source_target_pairs={{0,8},{8,16},{16,24},{24,0},{32,40},{40,48},{48,56},{56,32},{64,72... | collective-permute-start | bytes 786440 | tf_op jit(solution)/shard_map/ppermute | solution.py:231
  23.6 3.9 %collective-permute-start.4 = (bf16[2,2,256,128]{3,2,1,0:T(8,128)(2,1)S(1)}, bf16[2,2,256,128]{3,2,1,0:T(8,128)(2,1)S(1)}, u32[]{:S(2)}, u32[]{:S(2)}) collective-permute-start(bf16[2,2,256,128]{3,2,1,0:T(8,128)(2,1)S(1)} %get-tuple-element.44), channel_id=1, source_target_pairs={{0,24},{8,0},{16,8},{24,16},{32,56},{40,32},{48,40},{56,48},{64,88... | collective-permute-start | bytes 786440 | tf_op jit(solution)/shard_map/ppermute | solution.py:231
  27.5 1.3 %shard_map.87 = (f32[3,4,256]{2,1,0:T(4,128)S(1)}, f32[3,4,256]{2,1,0:T(4,128)S(1)}, f32[3,4,256]{2,1,0:T(4,128)S(1)}) custom-call(s32[1,256]{1,0:T(1,128)S(1)} %get-tuple-element.39._.starts_ref, bf16[256,512]{1,0:T(8,128)(2,1)S(1)} %get-tuple-element.40.q_ref, bf16[256,512]{1,0:T(8,128)(2,1)S(1)} %get-tuple-element.41.g_ref, ...), custom_call_target="tpu_custom_call" | custom-call | flops 402653184 | bytes 1048576 | tf_op jit(solution)/shard_map/pallas_call | solution.py:268
  28.8 1.0 %shard_map.89 = (f32[2,4,256,256]{3,2,1,0:T(8,128)S(1)}, f32[2,4,256,256]{3,2,1,0:T(8,128)S(1)}, f32[2,4,256]{2,1,0:T(4,128)S(1)}, f32[2,4,256]{2,1,0:T(4,128)S(1)}, f32[2,4,256]{2,1,0:T(4,128)S(1)}) custom-call(s32[1,256]{1,0:T(1,128)S(1)} %get-tuple-element.39._.starts_ref, bf16[256,512]{1,0:T(8,128)(2,1)S(1)} %get-tuple-element.40.q_ref, ...), custom_call_target="tpu_custom_call" | custom-call | flops 268435456 | bytes 1048576 | tf_op jit(solution)/shard_map/pallas_call | solution.py:270
  29.8 4.3 %collective-permute-done.2.far_ref.f1_ref = bf16[2,2,256,128]{3,2,1,0:T(8,128)(2,1)S(1)} collective-permute-done((bf16[2,2,256,128]{3,2,1,0:T(8,128)(2,1)S(1)}, bf16[2,2,256,128]{3,2,1,0:T(8,128)(2,1)S(1)}, u32[]{:S(2)}, u32[]{:S(2)}) %collective-permute-start.2) | collective-permute-done | bytes 262176 | tf_op jit(solution)/shard_map/ppermute | solution.py:231
  34.2 1.0 %shard_map.88 = (f32[2,4,256,256]{3,2,1,0:T(8,128)S(1)}, f32[2,4,256,256]{3,2,1,0:T(8,128)S(1)}, f32[2,4,256]{2,1,0:T(4,128)S(1)}, f32[2,4,256]{2,1,0:T(4,128)S(1)}, f32[2,4,256]{2,1,0:T(4,128)S(1)}) custom-call(s32[1,256]{1,0:T(1,128)S(1)} %get-tuple-element.39._.starts_ref, bf16[256,512]{1,0:T(8,128)(2,1)S(1)} %get-tuple-element.40.q_ref, ...), custom_call_target="tpu_custom_call" | custom-call | flops 268435456 | bytes 1048576 | tf_op jit(solution)/shard_map/pallas_call | solution.py:271
  35.1 1.9 %shard_map.90 = (bf16[2,2,256,128]{3,2,1,0:T(8,128)(2,1)S(1)}, f32[4,256]{1,0:T(4,128)S(1)}, f32[4,256]{1,0:T(4,128)S(1)}, f32[4,256]{1,0:T(4,128)S(1)}, f32[2,4...) custom-call(s32[1,256]{1,0:T(1,128)S(1)} %get-tuple-element.39._.sta, ...), custom_call_target="tpu_custom_call" | custom-call | flops 536870912 | bytes 1048576 | tf_op jit(solution)/shard_map/pallas_call | solution.py:272
  37.0 0.8 %shard_map.94 = bf16[2,2,256,128]{3,2,1,0:T(8,128)(2,1)S(1)} custom-call(f32[2,4,256,256]{3,2,1,0:T(8,128)S(1)} %get-tuple-element.66.p_ref, f32[2,4,256,256]{3,2,1,0:T(8,128)S(1)} %get-tuple-element.67.dp_ref, f32[2,4,256]{2,1,0:T(4,128)S(1)} %get-tuple-element.68.w_ref, f32[4,256]{1,0:T(4,128)S(1)} %get-tuple-element.58.rd_ref, ...), custom_call_target="tpu_custom_call" | custom-call | flops 268435456 | bytes 1048576 | tf_op jit(solution)/shard_map/pallas_call | solution.py:282
  37.8 3.3 %collective-permute-start.7 = (bf16[2,2,256,128]{3,2,1,0:T(8,128)(2,1)S(1)}, bf16[2,2,256,128]{3,2,1,0:T(8,128)(2,1)S(1)}, u32[]{:S(2)}, u32[]{:S(2)}) collective-permute-start(bf16[2,2,256,128]{3,2,1,0:T(8,128)(2,1)S(1)} %shard_map.94), channel_id=1, source_target_pairs={{0,8},{8,16},{16,24},{24,0},{32,40},{40,48},{48,56},{56,32},{64,72... | collective-permute-start | bytes 786440 | tf_op jit(solution)/shard_map/ppermute | solution.py:231
  41.2 3.1 %collective-permute-start.5 = (bf16[2,2,256,128]{3,2,1,0:T(8,128)(2,1)S(1)}, bf16[2,2,256,128]{3,2,1,0:T(8,128)(2,1)S(1)}, u32[]{:S(2)}, u32[]{:S(2)}) collective-permute-start(bf16[2,2,256,128]{3,2,1,0:T(8,128)(2,1)S(1)} %get-tuple-element.62), channel_id=1, source_target_pairs={{0,16},{8,24},{16,0},{24,8},{32,48},{40,56},{48,32},{56,40},{64,80... | collective-permute-start | bytes 786440 | tf_op jit(solution)/shard_map/ppermute | solution.py:231
  44.2 0.7 shard_map.93
  45.0 4.0 %collective-permute-start.6 = (bf16[2,2,256,128]{3,2,1,0:T(8,128)(2,1)S(1)}, bf16[2,2,256,128]{3,2,1,0:T(8,128)(2,1)S(1)}, u32[]{:S(2)}, u32[]{:S(2)}) collective-permute-start(bf16[2,2,256,128]{3,2,1,0:T(8,128)(2,1)S(1)} %shard_map.93), channel_id=1, source_target_pairs={{0,24},{8,0},{16,8},{24,16},{32,56},{40,32},{48,40},{56,48},{64,88... | collective-permute-start | bytes 786440 | tf_op jit(solution)/shard_map/ppermute | solution.py:231
  49.0 6.4 %shard_map.91 = (bf16[256,512]{1,0:T(8,128)(2,1)}, f32[256,512]{1,0:T(8,128)}, f32[3,2,256,128]{3,2,1,0:T(8,128)S(1)}) custom-call(s32[1,256]{1,0:T(1,128)S(1)} %get-tuple-element.39._.starts_ref, bf16[256,512]{1,0:T(8,128)(2,1)S(1)} %get-tuple-element.40.q_ref, bf16[256,512]{1,0:T(8,128)(2,1)S(1)} %get-tuple-element.41.g_ref, ...), custom_call_target="tpu_custom_call" | custom-call | flops 1207959552 | bytes 1048576 | tf_op jit(solution)/shard_map/pallas_call | solution.py:286
  55.4 0.1 shard_map.92.mine_ref
  55.5 2.6 %collective-permute-done.6.r1_ref = bf16[2,2,256,128]{3,2,1,0:T(8,128)(2,1)S(1)} collective-permute-done((bf16[2,2,256,128]{3,2,1,0:T(8,128)(2,1)S(1)}, bf16[2,2,256,128]{3,2,1,0:T(8,128)(2,1)S(1)}, u32[]{:S(2)}, u32[]{:S(2)}) %collective-permute-start.6) | collective-permute-done | bytes 262176 | tf_op jit(solution)/shard_map/ppermute | solution.py:231
  58.1 0.2 shard_map.95
  58.3 1.9 %collective-permute-start.8 = (bf16[2,256,128]{2,1,0:T(8,128)(2,1)S(1)}, bf16[2,256,128]{2,1,0:T(8,128)(2,1)S(1)}, u32[]{:S(2)}, u32[]{:S(2)}) collective-permute-start(bf16[2,256,128]{2,1,0:T(8,128)(2,1)S(1)} %get-tuple-element.70), channel_id=1, source_target_pairs={{64,0},{72,8},{80,16},{88,24},{96,32},{104,40},{112,48},{120,56},{... | collective-permute-start | bytes 393224 | tf_op jit(solution)/shard_map/ppermute | solution.py:227
  60.2 1.9 %collective-permute-start.9 = (bf16[2,256,128]{2,1,0:T(8,128)(2,1)S(1)}, bf16[2,256,128]{2,1,0:T(8,128)(2,1)S(1)}, u32[]{:S(2)}, u32[]{:S(2)}) collective-permute-start(bf16[2,256,128]{2,1,0:T(8,128)(2,1)S(1)} %get-tuple-element.71), channel_id=1, source_target_pairs={{32,0},{40,8},{48,16},{56,24},{64,32},{72,40},{80,48},{88,56},{96,... | collective-permute-start | bytes 393224 | tf_op jit(solution)/shard_map/ppermute | solution.py:227
  62.1 8.4 %collective-permute-done.8.two_ref = bf16[2,256,128]{2,1,0:T(8,128)(2,1)S(1)} collective-permute-done((bf16[2,256,128]{2,1,0:T(8,128)(2,1)S(1)}, bf16[2,256,128]{2,1,0:T(8,128)(2,1)S(1)}, u32[]{:S(2)}, u32[]{:S(2)}) %collective-permute-start.8) | collective-permute-done | bytes 131104 | tf_op jit(solution)/shard_map/ppermute | solution.py:227
  70.6 2.3 %collective-permute-done.9.one_ref = bf16[2,256,128]{2,1,0:T(8,128)(2,1)S(1)} collective-permute-done((bf16[2,256,128]{2,1,0:T(8,128)(2,1)S(1)}, bf16[2,256,128]{2,1,0:T(8,128)(2,1)S(1)}, u32[]{:S(2)}, u32[]{:S(2)}) %collective-permute-start.9) | collective-permute-done | bytes 131104 | tf_op jit(solution)/shard_map/ppermute | solution.py:227
  72.9 0.7 shard_map.97
  (12 shorter events, 0.1 us)
Async XLA Ops:
  0.6 0.8 %copy-start.2 = (bf16[256,128]{1,0:T(8,128)(2,1)S(1)}, bf16[256,128]{1,0:T(8,128)(2,1)}, u32[]{:S(2)}) copy-start(bf16[256,128]{1,0:T(8,128)(2,1)} %k_ref.1) | copy-start | bytes 196612
  1.5 0.8 %copy-start.3 = (bf16[256,128]{1,0:T(8,128)(2,1)S(1)}, bf16[256,128]{1,0:T(8,128)(2,1)}, u32[]{:S(2)}) copy-start(bf16[256,128]{1,0:T(8,128)(2,1)} %v_ref.1) | copy-start | bytes 196612
  2.3 13.4 %collective-permute-start.1 = (bf16[2,256,128]{2,1,0:T(8,128)(2,1)S(1)}, bf16[2,256,128]{2,1,0:T(8,128)(2,1)S(1)}, u32[]{:S(2)}, u32[]{:S(2)}) collective-permute-start(bf16[2,256,128]{2,1,0:T(8,128)(2,1)S(1)} %shard_map.85.own_ref), channel_id=1, source_target_pairs={{0,64},{8,72},{16,80},{24,88},{32,96},{40,104},{48,112},{56,120},{... | collective-permute-start | bytes 393224 | tf_op jit(solution)/shard_map/ppermute | solution.py:227
  8.7 8.9 %collective-permute-start = (bf16[2,256,128]{2,1,0:T(8,128)(2,1)S(1)}, bf16[2,256,128]{2,1,0:T(8,128)(2,1)S(1)}, u32[]{:S(2)}, u32[]{:S(2)}) collective-permute-start(bf16[2,256,128]{2,1,0:T(8,128)(2,1)S(1)} %shard_map.85.own_ref), channel_id=1, source_target_pairs={{0,32},{8,40},{16,48},{24,56},{32,64},{40,72},{48,80},{56,88},{64,... | collective-permute-start | bytes 393224 | tf_op jit(solution)/shard_map/ppermute | solution.py:227
  12.6 1.0 %copy-start = (bf16[256,512]{1,0:T(8,128)(2,1)S(1)}, bf16[256,512]{1,0:T(8,128)(2,1)}, u32[]{:S(2)}) copy-start(bf16[256,512]{1,0:T(8,128)(2,1)} %q_ref.1) | copy-start | bytes 786436
  13.5 0.9 %copy-start.1 = (bf16[256,512]{1,0:T(8,128)(2,1)S(1)}, bf16[256,512]{1,0:T(8,128)(2,1)}, u32[]{:S(2)}) copy-start(bf16[256,512]{1,0:T(8,128)(2,1)} %g_ref.1) | copy-start | bytes 786436
  14.5 0.7 copy-start.4
  17.7 11.2 %collective-permute-start.3 = (bf16[2,2,256,128]{3,2,1,0:T(8,128)(2,1)S(1)}, bf16[2,2,256,128]{3,2,1,0:T(8,128)(2,1)S(1)}, u32[]{:S(2)}, u32[]{:S(2)}) collective-permute-start(bf16[2,2,256,128]{3,2,1,0:T(8,128)(2,1)S(1)} %get-tuple-element.43), channel_id=1, source_target_pairs={{0,16},{8,24},{16,0},{24,8},{32,48},{40,56},{48,32},{56,40},{64,80... | collective-permute-start | bytes 786440 | tf_op jit(solution)/shard_map/ppermute | solution.py:231
  21.7 12.5 %collective-permute-start.2 = (bf16[2,2,256,128]{3,2,1,0:T(8,128)(2,1)S(1)}, bf16[2,2,256,128]{3,2,1,0:T(8,128)(2,1)S(1)}, u32[]{:S(2)}, u32[]{:S(2)}) collective-permute-start(bf16[2,2,256,128]{3,2,1,0:T(8,128)(2,1)S(1)} %get-tuple-element.42), channel_id=1, source_target_pairs={{0,8},{8,16},{16,24},{24,0},{32,40},{40,48},{48,56},{56,32},{64,72... | collective-permute-start | bytes 786440 | tf_op jit(solution)/shard_map/ppermute | solution.py:231
  23.6 11.5 %collective-permute-start.4 = (bf16[2,2,256,128]{3,2,1,0:T(8,128)(2,1)S(1)}, bf16[2,2,256,128]{3,2,1,0:T(8,128)(2,1)S(1)}, u32[]{:S(2)}, u32[]{:S(2)}) collective-permute-start(bf16[2,2,256,128]{3,2,1,0:T(8,128)(2,1)S(1)} %get-tuple-element.44), channel_id=1, source_target_pairs={{0,24},{8,0},{16,8},{24,16},{32,56},{40,32},{48,40},{56,48},{64,88... | collective-permute-start | bytes 786440 | tf_op jit(solution)/shard_map/ppermute | solution.py:231
  37.8 17.7 %collective-permute-start.7 = (bf16[2,2,256,128]{3,2,1,0:T(8,128)(2,1)S(1)}, bf16[2,2,256,128]{3,2,1,0:T(8,128)(2,1)S(1)}, u32[]{:S(2)}, u32[]{:S(2)}) collective-permute-start(bf16[2,2,256,128]{3,2,1,0:T(8,128)(2,1)S(1)} %shard_map.94), channel_id=1, source_target_pairs={{0,8},{8,16},{16,24},{24,0},{32,40},{40,48},{48,56},{56,32},{64,72... | collective-permute-start | bytes 786440 | tf_op jit(solution)/shard_map/ppermute | solution.py:231
  41.2 14.3 %collective-permute-start.5 = (bf16[2,2,256,128]{3,2,1,0:T(8,128)(2,1)S(1)}, bf16[2,2,256,128]{3,2,1,0:T(8,128)(2,1)S(1)}, u32[]{:S(2)}, u32[]{:S(2)}) collective-permute-start(bf16[2,2,256,128]{3,2,1,0:T(8,128)(2,1)S(1)} %get-tuple-element.62), channel_id=1, source_target_pairs={{0,16},{8,24},{16,0},{24,8},{32,48},{40,56},{48,32},{56,40},{64,80... | collective-permute-start | bytes 786440 | tf_op jit(solution)/shard_map/ppermute | solution.py:231
  45.0 13.1 %collective-permute-start.6 = (bf16[2,2,256,128]{3,2,1,0:T(8,128)(2,1)S(1)}, bf16[2,2,256,128]{3,2,1,0:T(8,128)(2,1)S(1)}, u32[]{:S(2)}, u32[]{:S(2)}) collective-permute-start(bf16[2,2,256,128]{3,2,1,0:T(8,128)(2,1)S(1)} %shard_map.93), channel_id=1, source_target_pairs={{0,24},{8,0},{16,8},{24,16},{32,56},{40,32},{48,40},{56,48},{64,88... | collective-permute-start | bytes 786440 | tf_op jit(solution)/shard_map/ppermute | solution.py:231
  58.3 12.3 %collective-permute-start.8 = (bf16[2,256,128]{2,1,0:T(8,128)(2,1)S(1)}, bf16[2,256,128]{2,1,0:T(8,128)(2,1)S(1)}, u32[]{:S(2)}, u32[]{:S(2)}) collective-permute-start(bf16[2,256,128]{2,1,0:T(8,128)(2,1)S(1)} %get-tuple-element.70), channel_id=1, source_target_pairs={{64,0},{72,8},{80,16},{88,24},{96,32},{104,40},{112,48},{120,56},{... | collective-permute-start | bytes 393224 | tf_op jit(solution)/shard_map/ppermute | solution.py:227
  60.2 12.7 %collective-permute-start.9 = (bf16[2,256,128]{2,1,0:T(8,128)(2,1)S(1)}, bf16[2,256,128]{2,1,0:T(8,128)(2,1)S(1)}, u32[]{:S(2)}, u32[]{:S(2)}) collective-permute-start(bf16[2,256,128]{2,1,0:T(8,128)(2,1)S(1)} %get-tuple-element.71), channel_id=1, source_target_pairs={{32,0},{40,8},{48,16},{56,24},{64,32},{72,40},{80,48},{88,56},{96,... | collective-permute-start | bytes 393224 | tf_op jit(solution)/shard_map/ppermute | solution.py:227

commit v6 on v5

--- a/solution.py
+++ b/solution.py
@@ -134,11 +134,11 @@
 
 
 def last_kernel(
-    starts_ref, q_ref, g_ref, far_ref, mn, tn, rn, m1, t1, r1, p2_ref, dp2_ref, m2, t2, r2,
-    back_ref, peak_ref, over_ref, rd_ref, w1_ref, w3_ref, p_ref, dp_ref,
-    m_ref, t_ref, r_ref, w2_ref, pb_ref, ds_ref,
+    starts_ref, q_ref, g_ref, far_ref, mn, tn, rn, p1_ref, dp1_ref, m1, t1, r1, p2_ref, dp2_ref, m2, t2, r2,
+    b1_ref, b2_ref, b3_ref, peak_ref, over_ref, rd_ref,
+    p3_ref, dp3_ref, m_ref, t_ref, r_ref, w1_ref, w2_ref, w3_ref, pb_ref, ds_ref,
 ):
-    far_scores(3, starts_ref, q_ref, g_ref, far_ref, p_ref, dp_ref, m_ref, t_ref, r_ref)
+    far_scores(3, starts_ref, q_ref, g_ref, far_ref, p3_ref, dp3_ref, m_ref, t_ref, r_ref)
 
     def each(near, *pairs):
         return [near[b] for b in range(3)] + [ref[b] for ref in pairs for b in range(2)]
@@ -153,7 +153,9 @@
     for n, ref in enumerate((w1_ref, w2_ref, w3_ref)):
         for b in range(2):
             ref[b] = factors[3 + 2 * n + b] * over
-    far_back(p2_ref, dp2_ref, w2_ref, rd_ref, q_ref, g_ref, back_ref, pb_ref, ds_ref)
+    far_back(p2_ref, dp2_ref, w2_ref, rd_ref, q_ref, g_ref, b2_ref, pb_ref, ds_ref)
+    far_back(p1_ref, dp1_ref, w1_ref, rd_ref, q_ref, g_ref, b1_ref, pb_ref, ds_ref)
+    far_back(p3_ref, dp3_ref, w3_ref, rd_ref, q_ref, g_ref, b3_ref, pb_ref, ds_ref)
 
 
 def rest_kernel(
@@ -206,8 +208,13 @@
         out_ref[i] = total
 
 
-def gather_kernel(mine_ref, r1_ref, r3_ref, own_ref, one_ref, two_ref):
-    own, one, two = add_back(3, r3_ref, *add_back(1, r1_ref, mine_ref[0], mine_ref[1], mine_ref[2]))
+def gather_one_kernel(mine_ref, r1_ref, out_ref):
+    for i, total in enumerate(add_back(1, r1_ref, mine_ref[0], mine_ref[1], mine_ref[2])):
+        out_ref[i] = total
+
+
+def gather_kernel(mine_ref, r3_ref, own_ref, one_ref, two_ref):
+    own, one, two = add_back(3, r3_ref, mine_ref[0], mine_ref[1], mine_ref[2])
     own_ref[...] = own
     one_ref[...] = one.astype(BF16)
     two_ref[...] = two.astype(BF16)
@@ -269,20 +276,15 @@
     arrive = {d: call(functools.partial(far_scores, d), tiles + sums, [VM] * 4, blocks=2, limit=8) for d in (1, 2)}
     p2, dp2, *sums2 = arrive[2](*wanted, f2)
     p1, dp1, *sums1 = arrive[1](*wanted, f1)
-    b2, peak, over, rd, w1, w3, p3, dp3 = call(
+    *backs, peak, over, rd = call(
         last_kernel,
-        (pair,) + (array(stats, F32),) * 3 + (array((2, *stats), F32),) * 2 + tiles,
-        [VM] * 15,
-        [pltpu.VMEM((2, *stats), F32)] * 4 + staged,
-        blocks=4,
-        limit=8,
-    )(*wanted, f3, *near, *sums1, p2, dp2, *sums2)
-    r2 = along_x(b2, -2, peers)
-    back = functools.partial(call, far_back, (pair,), [VM] * 6, staged, blocks=2, limit=8)
-    (b3,) = back()(p3, dp3, w3, rd, queries, grad_out)
-    r3 = along_x(b3, -3, peers)
-    (b1,) = back()(p1, dp1, w1, rd, queries, grad_out)
-    r1 = along_x(b1, -1, peers)
+        (pair,) * 3 + (array(stats, F32),) * 3,
+        [VM] * 17,
+        [pltpu.VMEM((2, H, T, T), F32)] * 2 + [pltpu.VMEM((2, *stats), F32)] * 6 + staged,
+        blocks=8,
+        limit=16,
+    )(*wanted, f3, *near, p1, dp1, *sums1, p2, dp2, *sums2)
+    r1, r2, r3 = (along_x(b, -d, peers) for d, b in enumerate(backs, 1))
     attended, query_grad, mine = call(
         rest_kernel,
         (array((T, H * D), BF16), array((T, H * D), F32), array((3, *block), F32)),
@@ -292,9 +294,10 @@
         limit=16,
     )(*wanted, own, z1, z2, f1, f2, f3, peak, over, rd)
     (mine,) = call(gather_first_kernel, (array((3, *block), F32),), [VM] * 2, limit=4)(mine, r2)
+    (mine,) = call(gather_one_kernel, (array((3, *block), F32),), [VM] * 2, limit=4)(mine, r1)
     mine, one, two = call(
-        gather_kernel, (array(block, F32), array(block, BF16), array(block, BF16)), [VM] * 3, limit=4
-    )(mine, r1, r3)
+        gather_kernel, (array(block, F32), array(block, BF16), array(block, BF16)), [VM] * 2, limit=4
+    )(mine, r3)
     two, one = along_z(two, -2, peers), along_z(one, -1, peers)
     (mine,) = call(add_two_kernel, (array(block, F32),), [VM] * 2, limit=4)(mine, two)
     key_grad, value_grad = call(final_kernel, (array((T, D), F32),) * 2, [VM] * 2, limit=4)(mine, one)

time: 74.1 us -> 71.6 us (0.966)
  the two profiles are of different devices: /device:TPU:98 before, /device:TPU:116 now
where the time goes in v6:
time: 71.6 us; the launch traced here: 71.1 us
  starting transfers between devices  31.2 us (44%)
  waiting for transfers between devices  20 us (28%)
  Pallas kernels  14.9 us (21%)
  local copies, waits for them, and re-layouts  4.22 us (6%)
  between operations  0.82 us (1%)
    ppermute x6, starting transfers between devices, along_x(): lax.ppermute(block, 'peer', [(i, i - i % ROW + (i + columns) % ROW) for i...  17.1 us
    ppermute x4, starting transfers between devices, along_z(): lax.ppermute(block, 'peer', [(i, i + far) for i in range(peers) if 0 <= i...  14.1 us
    ppermute x4, waiting for transfers between devices, along_z(): lax.ppermute(block, 'peer', [(i, i + far) for i in range(peers) if 0 <= i...  12.5 us
    ppermute x6, waiting for transfers between devices, along_x(): lax.ppermute(block, 'peer', [(i, i - i % ROW + (i + columns) % ROW) for i...  7.55 us
    pallas_call x1, Pallas kernels, body(): call(rest_kernel, (array((T, H * D), BF16), array((T, H * D), F32), array...  6.45 us
    unnamed x10, local copies, waits for them, and re-layouts  4.22 us
    pallas_call x1, Pallas kernels, body(): call(last_kernel, (pair,) * 3 + (array(stats, F32),) * 3, [VM] * 17, [plt...  3.46 us
  transfers between devices with their start and end apart: 10, of which 7 were waited for; matrix products, arithmetic and copies ran while one was open for 0% of the time, Pallas kernels for 15%

profile of v6, /device:TPU:116, one launch (start us, length us, event | category | flops | bytes accessed | tf_op | source)
XLA Modules:
  0.0 71.1 jit_solution(897972109608385032)
XLA Ops:
  0.6 0.8 %copy-done.2 = bf16[256,128]{1,0:T(8,128)(2,1)S(1)} copy-done((bf16[256,128]{1,0:T(8,128)(2,1)S(1)}, bf16[256,128]{1,0:T(8,128)(2,1)}, u32[]{:S(2)}) %copy-start.2) | copy-done | bytes 65560
  1.5 0.8 %copy-done.3 = bf16[256,128]{1,0:T(8,128)(2,1)S(1)} copy-done((bf16[256,128]{1,0:T(8,128)(2,1)S(1)}, bf16[256,128]{1,0:T(8,128)(2,1)}, u32[]{:S(2)}) %copy-start.3) | copy-done | bytes 65560
  2.3 6.4 %collective-permute-start.1 = (bf16[2,256,128]{2,1,0:T(8,128)(2,1)S(1)}, bf16[2,256,128]{2,1,0:T(8,128)(2,1)S(1)}, u32[]{:S(2)}, u32[]{:S(2)}) collective-permute-start(bf16[2,256,128]{2,1,0:T(8,128)(2,1)S(1)} %shard_map.85.own_ref), channel_id=1, source_target_pairs={{0,64},{8,72},{16,80},{24,88},{32,96},{40,104},{48,112},{56,120},{... | collective-permute-start | bytes 393224 | tf_op jit(solution)/shard_map/ppermute | solution.py:234
  8.7 3.8 %collective-permute-start = (bf16[2,256,128]{2,1,0:T(8,128)(2,1)S(1)}, bf16[2,256,128]{2,1,0:T(8,128)(2,1)S(1)}, u32[]{:S(2)}, u32[]{:S(2)}) collective-permute-start(bf16[2,256,128]{2,1,0:T(8,128)(2,1)S(1)} %shard_map.85.own_ref), channel_id=1, source_target_pairs={{0,32},{8,40},{16,48},{24,56},{32,64},{40,72},{48,80},{56,88},{64,... | collective-permute-start | bytes 393224 | tf_op jit(solution)/shard_map/ppermute | solution.py:234
  12.6 0.9 %copy-done = bf16[256,512]{1,0:T(8,128)(2,1)S(1)} copy-done((bf16[256,512]{1,0:T(8,128)(2,1)S(1)}, bf16[256,512]{1,0:T(8,128)(2,1)}, u32[]{:S(2)}) %copy-start) | copy-done | bytes 262168
  13.5 0.9 %copy-done.1 = bf16[256,512]{1,0:T(8,128)(2,1)S(1)} copy-done((bf16[256,512]{1,0:T(8,128)(2,1)S(1)}, bf16[256,512]{1,0:T(8,128)(2,1)}, u32[]{:S(2)}) %copy-start.1) | copy-done | bytes 262168
  14.5 0.7 copy-done.4
  15.1 0.6 shard_map.84
  15.7 1.9 %collective-permute-done.z1_ref = bf16[2,256,128]{2,1,0:T(8,128)(2,1)S(1)} collective-permute-done((bf16[2,256,128]{2,1,0:T(8,128)(2,1)S(1)}, bf16[2,256,128]{2,1,0:T(8,128)(2,1)S(1)}, u32[]{:S(2)}, u32[]{:S(2)}) %collective-permute-start) | collective-permute-done | bytes 131104 | tf_op jit(solution)/shard_map/ppermute | solution.py:234
  17.6 2.4 %collective-permute-start.3 = (bf16[2,2,256,128]{3,2,1,0:T(8,128)(2,1)S(1)}, bf16[2,2,256,128]{3,2,1,0:T(8,128)(2,1)S(1)}, u32[]{:S(2)}, u32[]{:S(2)}) collective-permute-start(bf16[2,2,256,128]{3,2,1,0:T(8,128)(2,1)S(1)} %get-tuple-element.41), channel_id=1, source_target_pairs={{0,16},{8,24},{16,0},{24,8},{32,48},{40,56},{48,32},{56,40},{64,80... | collective-permute-start | bytes 786440 | tf_op jit(solution)/shard_map/ppermute | solution.py:238
  20.1 4.0 %collective-permute-start.2 = (bf16[2,2,256,128]{3,2,1,0:T(8,128)(2,1)S(1)}, bf16[2,2,256,128]{3,2,1,0:T(8,128)(2,1)S(1)}, u32[]{:S(2)}, u32[]{:S(2)}) collective-permute-start(bf16[2,2,256,128]{3,2,1,0:T(8,128)(2,1)S(1)} %get-tuple-element.40), channel_id=1, source_target_pairs={{0,8},{8,16},{16,24},{24,0},{32,40},{40,48},{48,56},{56,32},{64,72... | collective-permute-start | bytes 786440 | tf_op jit(solution)/shard_map/ppermute | solution.py:238
  24.1 2.0 %collective-permute-start.4 = (bf16[2,2,256,128]{3,2,1,0:T(8,128)(2,1)S(1)}, bf16[2,2,256,128]{3,2,1,0:T(8,128)(2,1)S(1)}, u32[]{:S(2)}, u32[]{:S(2)}) collective-permute-start(bf16[2,2,256,128]{3,2,1,0:T(8,128)(2,1)S(1)} %get-tuple-element.42), channel_id=1, source_target_pairs={{0,24},{8,0},{16,8},{24,16},{32,56},{40,32},{48,40},{56,48},{64,88... | collective-permute-start | bytes 786440 | tf_op jit(solution)/shard_map/ppermute | solution.py:238
  26.1 1.3 %shard_map.87 = (f32[3,4,256]{2,1,0:T(4,128)S(1)}, f32[3,4,256]{2,1,0:T(4,128)S(1)}, f32[3,4,256]{2,1,0:T(4,128)S(1)}) custom-call(s32[1,256]{1,0:T(1,128)S(1)} %get-tuple-element.37._.starts_ref, bf16[256,512]{1,0:T(8,128)(2,1)S(1)} %get-tuple-element.38.q_ref, bf16[256,512]{1,0:T(8,128)(2,1)S(1)} %get-tuple-element.39.g_ref, ...), custom_call_target="tpu_custom_call" | custom-call | flops 402653184 | bytes 1048576 | tf_op jit(solution)/shard_map/pallas_call | solution.py:275
  27.4 2.9 %collective-permute-done.3.far_ref.f2_ref = bf16[2,2,256,128]{3,2,1,0:T(8,128)(2,1)S(1)} collective-permute-done((bf16[2,2,256,128]{3,2,1,0:T(8,128)(2,1)S(1)}, bf16[2,2,256,128]{3,2,1,0:T(8,128)(2,1)S(1)}, u32[]{:S(2)}, u32[]{:S(2)}) %collective-permute-start.3) | collective-permute-done | bytes 262176 | tf_op jit(solution)/shard_map/ppermute | solution.py:238
  30.3 1.0 %shard_map.89 = (f32[2,4,256,256]{3,2,1,0:T(8,128)S(1)}, f32[2,4,256,256]{3,2,1,0:T(8,128)S(1)}, f32[2,4,256]{2,1,0:T(4,128)S(1)}, f32[2,4,256]{2,1,0:T(4,128)S(1)}, f32[2,4,256]{2,1,0:T(4,128)S(1)}) custom-call(s32[1,256]{1,0:T(1,128)S(1)} %get-tuple-element.37._.starts_ref, bf16[256,512]{1,0:T(8,128)(2,1)S(1)} %get-tuple-element.38.q_ref, ...), custom_call_target="tpu_custom_call" | custom-call | flops 268435456 | bytes 1048576 | tf_op jit(solution)/shard_map/pallas_call | solution.py:277
  31.3 2.8 %collective-permute-done.2.far_ref.f1_ref = bf16[2,2,256,128]{3,2,1,0:T(8,128)(2,1)S(1)} collective-permute-done((bf16[2,2,256,128]{3,2,1,0:T(8,128)(2,1)S(1)}, bf16[2,2,256,128]{3,2,1,0:T(8,128)(2,1)S(1)}, u32[]{:S(2)}, u32[]{:S(2)}) %collective-permute-start.2) | collective-permute-done | bytes 262176 | tf_op jit(solution)/shard_map/ppermute | solution.py:238
  34.1 1.0 %shard_map.88 = (f32[2,4,256,256]{3,2,1,0:T(8,128)S(1)}, f32[2,4,256,256]{3,2,1,0:T(8,128)S(1)}, f32[2,4,256]{2,1,0:T(4,128)S(1)}, f32[2,4,256]{2,1,0:T(4,128)S(1)}, f32[2,4,256]{2,1,0:T(4,128)S(1)}) custom-call(s32[1,256]{1,0:T(1,128)S(1)} %get-tuple-element.37._.starts_ref, bf16[256,512]{1,0:T(8,128)(2,1)S(1)} %get-tuple-element.38.q_ref, ...), custom_call_target="tpu_custom_call" | custom-call | flops 268435456 | bytes 1048576 | tf_op jit(solution)/shard_map/pallas_call | solution.py:278
  35.1 3.5 %shard_map.90 = (bf16[2,2,256,128]{3,2,1,0:T(8,128)(2,1)S(1)}, bf16[2,2,256,128]{3,2,1,0:T(8,128)(2,1)S(1)}, bf16[2,2,256,128]{3,2,1,0:T(8,128)(2,1)S(1)}, f32[4...) custom-call(s32[1,256]{1,0:T(1,128)S(1)} %get-tuple-element.37._.starts_ref, ...), custom_call_target="tpu_custom_call" | custom-call | flops 1073741824 | bytes 1048576 | tf_op jit(solution)/shard_map/pallas_call | solution.py:279
  38.6 2.7 %collective-permute-start.5 = (bf16[2,2,256,128]{3,2,1,0:T(8,128)(2,1)S(1)}, bf16[2,2,256,128]{3,2,1,0:T(8,128)(2,1)S(1)}, u32[]{:S(2)}, u32[]{:S(2)}) collective-permute-start(bf16[2,2,256,128]{3,2,1,0:T(8,128)(2,1)S(1)} %get-tuple-element.62), channel_id=1, source_target_pairs={{0,16},{8,24},{16,0},{24,8},{32,48},{40,56},{48,32},{56,40},{64,80... | collective-permute-start | bytes 786440 | tf_op jit(solution)/shard_map/ppermute | solution.py:238
  41.3 3.6 %collective-permute-start.6 = (bf16[2,2,256,128]{3,2,1,0:T(8,128)(2,1)S(1)}, bf16[2,2,256,128]{3,2,1,0:T(8,128)(2,1)S(1)}, u32[]{:S(2)}, u32[]{:S(2)}) collective-permute-start(bf16[2,2,256,128]{3,2,1,0:T(8,128)(2,1)S(1)} %get-tuple-element.63), channel_id=1, source_target_pairs={{0,24},{8,0},{16,8},{24,16},{32,56},{40,32},{48,40},{56,48},{64,88... | collective-permute-start | bytes 786440 | tf_op jit(solution)/shard_map/ppermute | solution.py:238
  44.9 2.4 %collective-permute-start.7 = (bf16[2,2,256,128]{3,2,1,0:T(8,128)(2,1)S(1)}, bf16[2,2,256,128]{3,2,1,0:T(8,128)(2,1)S(1)}, u32[]{:S(2)}, u32[]{:S(2)}) collective-permute-start(bf16[2,2,256,128]{3,2,1,0:T(8,128)(2,1)S(1)} %get-tuple-element.64), channel_id=1, source_target_pairs={{0,8},{8,16},{16,24},{24,0},{32,40},{40,48},{48,56},{56,32},{64,72... | collective-permute-start | bytes 786440 | tf_op jit(solution)/shard_map/ppermute | solution.py:238
  47.3 6.5 %shard_map.91 = (bf16[256,512]{1,0:T(8,128)(2,1)}, f32[256,512]{1,0:T(8,128)}, f32[3,2,256,128]{3,2,1,0:T(8,128)S(1)}) custom-call(s32[1,256]{1,0:T(1,128)S(1)} %get-tuple-element.37._.starts_ref, bf16[256,512]{1,0:T(8,128)(2,1)S(1)} %get-tuple-element.38.q_ref, bf16[256,512]{1,0:T(8,128)(2,1)S(1)} %get-tuple-element.39.g_ref, ...), custom_call_target="tpu_custom_call" | custom-call | flops 1207959552 | bytes 1048576 | tf_op jit(solution)/shard_map/pallas_call | solution.py:288
  53.8 0.1 shard_map.92.mine_ref
  53.9 0.1 collective-permute-done.6.r1_ref
  53.9 0.1 shard_map.93.mine_ref
  54.0 1.8 %collective-permute-done.7.r3_ref = bf16[2,2,256,128]{3,2,1,0:T(8,128)(2,1)S(1)} collective-permute-done((bf16[2,2,256,128]{3,2,1,0:T(8,128)(2,1)S(1)}, bf16[2,2,256,128]{3,2,1,0:T(8,128)(2,1)S(1)}, u32[]{:S(2)}, u32[]{:S(2)}) %collective-permute-start.7) | collective-permute-done | bytes 262176 | tf_op jit(solution)/shard_map/ppermute | solution.py:238
  55.8 0.1 shard_map.94
  55.9 1.9 %collective-permute-start.8 = (bf16[2,256,128]{2,1,0:T(8,128)(2,1)S(1)}, bf16[2,256,128]{2,1,0:T(8,128)(2,1)S(1)}, u32[]{:S(2)}, u32[]{:S(2)}) collective-permute-start(bf16[2,256,128]{2,1,0:T(8,128)(2,1)S(1)} %get-tuple-element.66), channel_id=1, source_target_pairs={{64,0},{72,8},{80,16},{88,24},{96,32},{104,40},{112,48},{120,56},{... | collective-permute-start | bytes 393224 | tf_op jit(solution)/shard_map/ppermute | solution.py:234
  57.8 1.9 %collective-permute-start.9 = (bf16[2,256,128]{2,1,0:T(8,128)(2,1)S(1)}, bf16[2,256,128]{2,1,0:T(8,128)(2,1)S(1)}, u32[]{:S(2)}, u32[]{:S(2)}) collective-permute-start(bf16[2,256,128]{2,1,0:T(8,128)(2,1)S(1)} %get-tuple-element.67), channel_id=1, source_target_pairs={{32,0},{40,8},{48,16},{56,24},{64,32},{72,40},{80,48},{88,56},{96,... | collective-permute-start | bytes 393224 | tf_op jit(solution)/shard_map/ppermute | solution.py:234
  59.8 8.4 %collective-permute-done.8.two_ref = bf16[2,256,128]{2,1,0:T(8,128)(2,1)S(1)} collective-permute-done((bf16[2,256,128]{2,1,0:T(8,128)(2,1)S(1)}, bf16[2,256,128]{2,1,0:T(8,128)(2,1)S(1)}, u32[]{:S(2)}, u32[]{:S(2)}) %collective-permute-start.8) | collective-permute-done | bytes 131104 | tf_op jit(solution)/shard_map/ppermute | solution.py:234
  68.2 2.2 %collective-permute-done.9.one_ref = bf16[2,256,128]{2,1,0:T(8,128)(2,1)S(1)} collective-permute-done((bf16[2,256,128]{2,1,0:T(8,128)(2,1)S(1)}, bf16[2,256,128]{2,1,0:T(8,128)(2,1)S(1)}, u32[]{:S(2)}, u32[]{:S(2)}) %collective-permute-start.9) | collective-permute-done | bytes 131104 | tf_op jit(solution)/shard_map/ppermute | solution.py:234
  70.4 0.7 %shard_map.96 = (f32[256,128]{1,0:T(8,128)}, f32[256,128]{1,0:T(8,128)}) custom-call(f32[2,256,128]{2,1,0:T(8,128)S(1)} %shard_map.95.own_ref, bf16[2,256,128]{2,1,0:T(8,128)(2,1)S(1)} %collective-permute-done.9.one_ref), custom_call_target="tpu_custom_call" | custom-call | bytes 1048576 | tf_op jit(solution)/shard_map/pallas_call | solution.py:303
  (11 shorter events, 0.1 us)
Async XLA Ops:
  0.6 0.8 %copy-start.2 = (bf16[256,128]{1,0:T(8,128)(2,1)S(1)}, bf16[256,128]{1,0:T(8,128)(2,1)}, u32[]{:S(2)}) copy-start(bf16[256,128]{1,0:T(8,128)(2,1)} %k_ref.1) | copy-start | bytes 196612
  1.5 0.8 %copy-start.3 = (bf16[256,128]{1,0:T(8,128)(2,1)S(1)}, bf16[256,128]{1,0:T(8,128)(2,1)}, u32[]{:S(2)}) copy-start(bf16[256,128]{1,0:T(8,128)(2,1)} %v_ref.1) | copy-start | bytes 196612
  2.3 13.4 %collective-permute-start.1 = (bf16[2,256,128]{2,1,0:T(8,128)(2,1)S(1)}, bf16[2,256,128]{2,1,0:T(8,128)(2,1)S(1)}, u32[]{:S(2)}, u32[]{:S(2)}) collective-permute-start(bf16[2,256,128]{2,1,0:T(8,128)(2,1)S(1)} %shard_map.85.own_ref), channel_id=1, source_target_pairs={{0,64},{8,72},{16,80},{24,88},{32,96},{40,104},{48,112},{56,120},{... | collective-permute-start | bytes 393224 | tf_op jit(solution)/shard_map/ppermute | solution.py:234
  8.7 8.9 %collective-permute-start = (bf16[2,256,128]{2,1,0:T(8,128)(2,1)S(1)}, bf16[2,256,128]{2,1,0:T(8,128)(2,1)S(1)}, u32[]{:S(2)}, u32[]{:S(2)}) collective-permute-start(bf16[2,256,128]{2,1,0:T(8,128)(2,1)S(1)} %shard_map.85.own_ref), channel_id=1, source_target_pairs={{0,32},{8,40},{16,48},{24,56},{32,64},{40,72},{48,80},{56,88},{64,... | collective-permute-start | bytes 393224 | tf_op jit(solution)/shard_map/ppermute | solution.py:234
  12.6 1.0 %copy-start = (bf16[256,512]{1,0:T(8,128)(2,1)S(1)}, bf16[256,512]{1,0:T(8,128)(2,1)}, u32[]{:S(2)}) copy-start(bf16[256,512]{1,0:T(8,128)(2,1)} %q_ref.1) | copy-start | bytes 786436
  13.5 0.9 %copy-start.1 = (bf16[256,512]{1,0:T(8,128)(2,1)S(1)}, bf16[256,512]{1,0:T(8,128)(2,1)}, u32[]{:S(2)}) copy-start(bf16[256,512]{1,0:T(8,128)(2,1)} %g_ref.1) | copy-start | bytes 786436
  14.5 0.7 copy-start.4
  17.6 12.7 %collective-permute-start.3 = (bf16[2,2,256,128]{3,2,1,0:T(8,128)(2,1)S(1)}, bf16[2,2,256,128]{3,2,1,0:T(8,128)(2,1)S(1)}, u32[]{:S(2)}, u32[]{:S(2)}) collective-permute-start(bf16[2,2,256,128]{3,2,1,0:T(8,128)(2,1)S(1)} %get-tuple-element.41), channel_id=1, source_target_pairs={{0,16},{8,24},{16,0},{24,8},{32,48},{40,56},{48,32},{56,40},{64,80... | collective-permute-start | bytes 786440 | tf_op jit(solution)/shard_map/ppermute | solution.py:238
  20.1 14.0 %collective-permute-start.2 = (bf16[2,2,256,128]{3,2,1,0:T(8,128)(2,1)S(1)}, bf16[2,2,256,128]{3,2,1,0:T(8,128)(2,1)S(1)}, u32[]{:S(2)}, u32[]{:S(2)}) collective-permute-start(bf16[2,2,256,128]{3,2,1,0:T(8,128)(2,1)S(1)} %get-tuple-element.40), channel_id=1, source_target_pairs={{0,8},{8,16},{16,24},{24,0},{32,40},{40,48},{48,56},{56,32},{64,72... | collective-permute-start | bytes 786440 | tf_op jit(solution)/shard_map/ppermute | solution.py:238
  24.1 11.0 %collective-permute-start.4 = (bf16[2,2,256,128]{3,2,1,0:T(8,128)(2,1)S(1)}, bf16[2,2,256,128]{3,2,1,0:T(8,128)(2,1)S(1)}, u32[]{:S(2)}, u32[]{:S(2)}) collective-permute-start(bf16[2,2,256,128]{3,2,1,0:T(8,128)(2,1)S(1)} %get-tuple-element.42), channel_id=1, source_target_pairs={{0,24},{8,0},{16,8},{24,16},{32,56},{40,32},{48,40},{56,48},{64,88... | collective-permute-start | bytes 786440 | tf_op jit(solution)/shard_map/ppermute | solution.py:238
  38.6 15.2 %collective-permute-start.5 = (bf16[2,2,256,128]{3,2,1,0:T(8,128)(2,1)S(1)}, bf16[2,2,256,128]{3,2,1,0:T(8,128)(2,1)S(1)}, u32[]{:S(2)}, u32[]{:S(2)}) collective-permute-start(bf16[2,2,256,128]{3,2,1,0:T(8,128)(2,1)S(1)} %get-tuple-element.62), channel_id=1, source_target_pairs={{0,16},{8,24},{16,0},{24,8},{32,48},{40,56},{48,32},{56,40},{64,80... | collective-permute-start | bytes 786440 | tf_op jit(solution)/shard_map/ppermute | solution.py:238
  41.3 12.7 %collective-permute-start.6 = (bf16[2,2,256,128]{3,2,1,0:T(8,128)(2,1)S(1)}, bf16[2,2,256,128]{3,2,1,0:T(8,128)(2,1)S(1)}, u32[]{:S(2)}, u32[]{:S(2)}) collective-permute-start(bf16[2,2,256,128]{3,2,1,0:T(8,128)(2,1)S(1)} %get-tuple-element.63), channel_id=1, source_target_pairs={{0,24},{8,0},{16,8},{24,16},{32,56},{40,32},{48,40},{56,48},{64,88... | collective-permute-start | bytes 786440 | tf_op jit(solution)/shard_map/ppermute | solution.py:238
  44.9 10.9 %collective-permute-start.7 = (bf16[2,2,256,128]{3,2,1,0:T(8,128)(2,1)S(1)}, bf16[2,2,256,128]{3,2,1,0:T(8,128)(2,1)S(1)}, u32[]{:S(2)}, u32[]{:S(2)}) collective-permute-start(bf16[2,2,256,128]{3,2,1,0:T(8,128)(2,1)S(1)} %get-tuple-element.64), channel_id=1, source_target_pairs={{0,8},{8,16},{16,24},{24,0},{32,40},{40,48},{48,56},{56,32},{64,72... | collective-permute-start | bytes 786440 | tf_op jit(solution)/shard_map/ppermute | solution.py:238
  55.9 12.3 %collective-permute-start.8 = (bf16[2,256,128]{2,1,0:T(8,128)(2,1)S(1)}, bf16[2,256,128]{2,1,0:T(8,128)(2,1)S(1)}, u32[]{:S(2)}, u32[]{:S(2)}) collective-permute-start(bf16[2,256,128]{2,1,0:T(8,128)(2,1)S(1)} %get-tuple-element.66), channel_id=1, source_target_pairs={{64,0},{72,8},{80,16},{88,24},{96,32},{104,40},{112,48},{120,56},{... | collective-permute-start | bytes 393224 | tf_op jit(solution)/shard_map/ppermute | solution.py:234
  57.8 12.5 %collective-permute-start.9 = (bf16[2,256,128]{2,1,0:T(8,128)(2,1)S(1)}, bf16[2,256,128]{2,1,0:T(8,128)(2,1)S(1)}, u32[]{:S(2)}, u32[]{:S(2)}) collective-permute-start(bf16[2,256,128]{2,1,0:T(8,128)(2,1)S(1)} %get-tuple-element.67), channel_id=1, source_target_pairs={{32,0},{40,8},{48,16},{56,24},{64,32},{72,40},{80,48},{88,56},{96,... | collective-permute-start | bytes 393224 | tf_op jit(solution)/shard_map/ppermute | solution.py:234

commit v7 on v6

--- a/solution.py
+++ b/solution.py
@@ -158,9 +158,28 @@
     far_back(p3_ref, dp3_ref, w3_ref, rd_ref, q_ref, g_ref, b3_ref, pb_ref, ds_ref)
 
 
-def rest_kernel(
-    starts_ref, q_ref, g_ref, own_ref, z1_ref, z2_ref, f1_ref, f2_ref, f3_ref, peak_ref, over_ref, rd_ref,
-    out_ref, dq_ref, near_ref, o_acc, dq_acc, pb_ref, ds_ref,
+def weights(q_ref, g_ref, key, value, hidden, peak_ref, over_ref, rd_ref, pb_ref, ds_ref):
+    for h in range(H):
+        s = dot(key, head(q_ref, h), LONG)
+        dp = dot(value, head(g_ref, h), LONG)
+        s = jnp.where(hidden, NEG, s)
+        pn = jnp.exp2((s - peak_ref[h : h + 1]) * TO_EXP2) * over_ref[h : h + 1]
+        pb_ref[h] = pn.astype(BF16)
+        ds_ref[h] = (pn * (dp - rd_ref[h : h + 1])).astype(BF16)
+
+
+def near_back_kernel(starts_ref, q_ref, g_ref, own_ref, z1_ref, z2_ref, peak_ref, over_ref, rd_ref, near_ref, pb_ref, ds_ref):
+    first = lax.axis_index("peer") * T
+    for b, ref in enumerate((own_ref, z1_ref, z2_ref)):
+        pb, ds = pb_ref.at[b % 2], ds_ref.at[b % 2]
+        hidden = near_hidden(first, starts_ref[...], b)
+        weights(q_ref, g_ref, ref[0], ref[1], hidden, peak_ref, over_ref, rd_ref, pb, ds)
+        near_ref[b, 0], near_ref[b, 1] = key_side(q_ref, g_ref, pb, ds)
+
+
+def query_side_kernel(
+    starts_ref, q_ref, g_ref, own_ref, z1_ref, z2_ref, f1_ref, f2_ref, f3_ref, peak_ref, over_ref, rd_ref, _,
+    out_ref, dq_ref, o_acc, dq_acc, pb_ref, ds_ref,
 ):
     peer = lax.axis_index("peer")
     x = lax.rem(peer, ROW)
@@ -177,20 +196,12 @@
             key, value = ref[kind, 0], ref[kind, 1]
             hidden = far_hidden(first, starts, behind(d, kind, x))
         pb, ds = pb_ref.at[b % 2], ds_ref.at[b % 2]
-        for h in range(H):
-            s = dot(key, head(q_ref, h), LONG)
-            dp = dot(value, head(g_ref, h), LONG)
-            s = jnp.where(hidden, NEG, s)
-            pn = jnp.exp2((s - peak_ref[h : h + 1]) * TO_EXP2) * over_ref[h : h + 1]
-            pb[h] = pn.astype(BF16)
-            ds[h] = (pn * (dp - rd_ref[h : h + 1])).astype(BF16)
+        weights(q_ref, g_ref, key, value, hidden, peak_ref, over_ref, rd_ref, pb, ds)
         kt, vt = key.T, value.T
         for h in range(H):
             o, dq = dot(vt, pb[h], PLAIN), dot(kt, ds[h], PLAIN)
             o_acc[h] = o if b == 0 else o_acc[h] + o
             dq_acc[h] = dq if b == 0 else dq_acc[h] + dq
-        if b < 3:
-            near_ref[b, 0], near_ref[b, 1] = key_side(q_ref, g_ref, pb, ds)
 
     for h in range(H):
         out_ref[:, h * D : (h + 1) * D] = o_acc[h].T.astype(BF16)
@@ -285,19 +296,22 @@
         limit=16,
     )(*wanted, f3, *near, p1, dp1, *sums1, p2, dp2, *sums2)
     r1, r2, r3 = (along_x(b, -d, peers) for d, b in enumerate(backs, 1))
-    attended, query_grad, mine = call(
-        rest_kernel,
-        (array((T, H * D), BF16), array((T, H * D), F32), array((3, *block), F32)),
-        [VM] * 12,
-        [pltpu.VMEM((H, D, T), F32)] * 2 + staged,
-        blocks=9,
-        limit=16,
-    )(*wanted, own, z1, z2, f1, f2, f3, peak, over, rd)
+    (mine,) = call(near_back_kernel, (array((3, *block), F32),), [VM] * 9, staged, blocks=3, limit=8)(
+        *wanted, own, z1, z2, peak, over, rd
+    )
     (mine,) = call(gather_first_kernel, (array((3, *block), F32),), [VM] * 2, limit=4)(mine, r2)
     (mine,) = call(gather_one_kernel, (array((3, *block), F32),), [VM] * 2, limit=4)(mine, r1)
     mine, one, two = call(
         gather_kernel, (array(block, F32), array(block, BF16), array(block, BF16)), [VM] * 2, limit=4
     )(mine, r3)
+    attended, query_grad = call(
+        query_side_kernel,
+        (array((T, H * D), BF16), array((T, H * D), F32)),
+        [VM] * 13,
+        [pltpu.VMEM((H, D, T), F32)] * 2 + staged,
+        blocks=9,
+        limit=16,
+    )(*wanted, own, z1, z2, f1, f2, f3, peak, over, rd, one)
     two, one = along_z(two, -2, peers), along_z(one, -1, peers)
     (mine,) = call(add_two_kernel, (array(block, F32),), [VM] * 2, limit=4)(mine, two)
     key_grad, value_grad = call(final_kernel, (array((T, D), F32),) * 2, [VM] * 2, limit=4)(mine, one)

time: 71.6 us -> 71.6 us (level)
  the two profiles are of different devices: /device:TPU:116 before, /device:TPU:124 now
where the time goes in v7:
time: 71.6 us; the launch traced here: 71.1 us
  starting transfers between devices  31.2 us (44%)
  waiting for transfers between devices  19 us (27%)
  Pallas kernels  15.9 us (22%)
  local copies, waits for them, and re-layouts  4.22 us (6%)
  between operations  0.82 us (1%)
    ppermute x6, starting transfers between devices, along_x(): lax.ppermute(block, 'peer', [(i, i - i % ROW + (i + columns) % ROW) for i...  16.9 us
    ppermute x4, starting transfers between devices, along_z(): lax.ppermute(block, 'peer', [(i, i + far) for i in range(peers) if 0 <= i...  14.2 us
    ppermute x6, waiting for transfers between devices, along_x(): lax.ppermute(block, 'peer', [(i, i - i % ROW + (i + columns) % ROW) for i...  12.3 us
    ppermute x4, waiting for transfers between devices, along_z(): lax.ppermute(block, 'peer', [(i, i + far) for i in range(peers) if 0 <= i...  6.64 us
    pallas_call x1, Pallas kernels, body(): call(query_side_kernel, (array((T, H * D), BF16), array((T, H * D), F32))...  5.63 us
    unnamed x10, local copies, waits for them, and re-layouts  4.22 us
    pallas_call x1, Pallas kernels, body(): call(last_kernel, (pair,) * 3 + (array(stats, F32),) * 3, [VM] * 17, [plt...  3.47 us
    pallas_call x1, Pallas kernels, body(): call(near_back_kernel, (array((3, *block), F32),), [VM] * 9, staged, bloc...  1.9 us
  transfers between devices with their start and end apart: 10, of which 8 were waited for; matrix products, arithmetic and copies ran while one was open for 0% of the time, Pallas kernels for 16%

profile of v7, /device:TPU:124, one launch (start us, length us, event | category | flops | bytes accessed | tf_op | source)
XLA Modules:
  0.0 71.1 jit_solution(16926327645724795875)
XLA Ops:
  0.6 0.8 %copy-done.2 = bf16[256,128]{1,0:T(8,128)(2,1)S(1)} copy-done((bf16[256,128]{1,0:T(8,128)(2,1)S(1)}, bf16[256,128]{1,0:T(8,128)(2,1)}, u32[]{:S(2)}) %copy-start.2) | copy-done | bytes 65560
  1.5 0.8 %copy-done.3 = bf16[256,128]{1,0:T(8,128)(2,1)S(1)} copy-done((bf16[256,128]{1,0:T(8,128)(2,1)S(1)}, bf16[256,128]{1,0:T(8,128)(2,1)}, u32[]{:S(2)}) %copy-start.3) | copy-done | bytes 65560
  2.3 6.4 %collective-permute-start.1 = (bf16[2,256,128]{2,1,0:T(8,128)(2,1)S(1)}, bf16[2,256,128]{2,1,0:T(8,128)(2,1)S(1)}, u32[]{:S(2)}, u32[]{:S(2)}) collective-permute-start(bf16[2,256,128]{2,1,0:T(8,128)(2,1)S(1)} %shard_map.85.own_ref), channel_id=1, source_target_pairs={{0,64},{8,72},{16,80},{24,88},{32,96},{40,104},{48,112},{56,120},{... | collective-permute-start | bytes 393224 | tf_op jit(solution)/shard_map/ppermute | solution.py:245
  8.7 3.8 %collective-permute-start = (bf16[2,256,128]{2,1,0:T(8,128)(2,1)S(1)}, bf16[2,256,128]{2,1,0:T(8,128)(2,1)S(1)}, u32[]{:S(2)}, u32[]{:S(2)}) collective-permute-start(bf16[2,256,128]{2,1,0:T(8,128)(2,1)S(1)} %shard_map.85.own_ref), channel_id=1, source_target_pairs={{0,32},{8,40},{16,48},{24,56},{32,64},{40,72},{48,80},{56,88},{64,... | collective-permute-start | bytes 393224 | tf_op jit(solution)/shard_map/ppermute | solution.py:245
  12.6 0.9 %copy-done = bf16[256,512]{1,0:T(8,128)(2,1)S(1)} copy-done((bf16[256,512]{1,0:T(8,128)(2,1)S(1)}, bf16[256,512]{1,0:T(8,128)(2,1)}, u32[]{:S(2)}) %copy-start) | copy-done | bytes 262168
  13.5 0.9 %copy-done.1 = bf16[256,512]{1,0:T(8,128)(2,1)S(1)} copy-done((bf16[256,512]{1,0:T(8,128)(2,1)S(1)}, bf16[256,512]{1,0:T(8,128)(2,1)}, u32[]{:S(2)}) %copy-start.1) | copy-done | bytes 262168
  14.5 0.7 copy-done.4
  15.1 0.6 shard_map.84
  15.7 1.9 %collective-permute-done.z1_ref = bf16[2,256,128]{2,1,0:T(8,128)(2,1)S(1)} collective-permute-done((bf16[2,256,128]{2,1,0:T(8,128)(2,1)S(1)}, bf16[2,256,128]{2,1,0:T(8,128)(2,1)S(1)}, u32[]{:S(2)}, u32[]{:S(2)}) %collective-permute-start) | collective-permute-done | bytes 131104 | tf_op jit(solution)/shard_map/ppermute | solution.py:245
  17.6 2.4 %collective-permute-start.3 = (bf16[2,2,256,128]{3,2,1,0:T(8,128)(2,1)S(1)}, bf16[2,2,256,128]{3,2,1,0:T(8,128)(2,1)S(1)}, u32[]{:S(2)}, u32[]{:S(2)}) collective-permute-start(bf16[2,2,256,128]{3,2,1,0:T(8,128)(2,1)S(1)} %get-tuple-element.40), channel_id=1, source_target_pairs={{0,16},{8,24},{16,0},{24,8},{32,48},{40,56},{48,32},{56,40},{64,80... | collective-permute-start | bytes 786440 | tf_op jit(solution)/shard_map/ppermute | solution.py:249
  20.1 4.0 %collective-permute-start.2 = (bf16[2,2,256,128]{3,2,1,0:T(8,128)(2,1)S(1)}, bf16[2,2,256,128]{3,2,1,0:T(8,128)(2,1)S(1)}, u32[]{:S(2)}, u32[]{:S(2)}) collective-permute-start(bf16[2,2,256,128]{3,2,1,0:T(8,128)(2,1)S(1)} %get-tuple-element.39), channel_id=1, source_target_pairs={{0,8},{8,16},{16,24},{24,0},{32,40},{40,48},{48,56},{56,32},{64,72... | collective-permute-start | bytes 786440 | tf_op jit(solution)/shard_map/ppermute | solution.py:249
  24.1 2.0 %collective-permute-start.4 = (bf16[2,2,256,128]{3,2,1,0:T(8,128)(2,1)S(1)}, bf16[2,2,256,128]{3,2,1,0:T(8,128)(2,1)S(1)}, u32[]{:S(2)}, u32[]{:S(2)}) collective-permute-start(bf16[2,2,256,128]{3,2,1,0:T(8,128)(2,1)S(1)} %get-tuple-element.41), channel_id=1, source_target_pairs={{0,24},{8,0},{16,8},{24,16},{32,56},{40,32},{48,40},{56,48},{64,88... | collective-permute-start | bytes 786440 | tf_op jit(solution)/shard_map/ppermute | solution.py:249
  26.1 1.3 %shard_map.87 = (f32[3,4,256]{2,1,0:T(4,128)S(1)}, f32[3,4,256]{2,1,0:T(4,128)S(1)}, f32[3,4,256]{2,1,0:T(4,128)S(1)}) custom-call(s32[1,256]{1,0:T(1,128)S(1)} %get-tuple-element.36._.starts_ref, bf16[256,512]{1,0:T(8,128)(2,1)S(1)} %get-tuple-element.37.q_ref, bf16[256,512]{1,0:T(8,128)(2,1)S(1)} %get-tuple-element.38.g_ref, ...), custom_call_target="tpu_custom_call" | custom-call | flops 402653184 | bytes 1048576 | tf_op jit(solution)/shard_map/pallas_call | solution.py:286
  27.4 3.0 %collective-permute-done.3.far_ref.f2_ref = bf16[2,2,256,128]{3,2,1,0:T(8,128)(2,1)S(1)} collective-permute-done((bf16[2,2,256,128]{3,2,1,0:T(8,128)(2,1)S(1)}, bf16[2,2,256,128]{3,2,1,0:T(8,128)(2,1)S(1)}, u32[]{:S(2)}, u32[]{:S(2)}) %collective-permute-start.3) | collective-permute-done | bytes 262176 | tf_op jit(solution)/shard_map/ppermute | solution.py:249
  30.3 1.0 %shard_map.89 = (f32[2,4,256,256]{3,2,1,0:T(8,128)S(1)}, f32[2,4,256,256]{3,2,1,0:T(8,128)S(1)}, f32[2,4,256]{2,1,0:T(4,128)S(1)}, f32[2,4,256]{2,1,0:T(4,128)S(1)}, f32[2,4,256]{2,1,0:T(4,128)S(1)}) custom-call(s32[1,256]{1,0:T(1,128)S(1)} %get-tuple-element.36._.starts_ref, bf16[256,512]{1,0:T(8,128)(2,1)S(1)} %get-tuple-element.37.q_ref, ...), custom_call_target="tpu_custom_call" | custom-call | flops 268435456 | bytes 1048576 | tf_op jit(solution)/shard_map/pallas_call | solution.py:288
  31.3 2.8 %collective-permute-done.2.far_ref.f1_ref = bf16[2,2,256,128]{3,2,1,0:T(8,128)(2,1)S(1)} collective-permute-done((bf16[2,2,256,128]{3,2,1,0:T(8,128)(2,1)S(1)}, bf16[2,2,256,128]{3,2,1,0:T(8,128)(2,1)S(1)}, u32[]{:S(2)}, u32[]{:S(2)}) %collective-permute-start.2) | collective-permute-done | bytes 262176 | tf_op jit(solution)/shard_map/ppermute | solution.py:249
  34.1 1.0 %shard_map.88 = (f32[2,4,256,256]{3,2,1,0:T(8,128)S(1)}, f32[2,4,256,256]{3,2,1,0:T(8,128)S(1)}, f32[2,4,256]{2,1,0:T(4,128)S(1)}, f32[2,4,256]{2,1,0:T(4,128)S(1)}, f32[2,4,256]{2,1,0:T(4,128)S(1)}) custom-call(s32[1,256]{1,0:T(1,128)S(1)} %get-tuple-element.36._.starts_ref, bf16[256,512]{1,0:T(8,128)(2,1)S(1)} %get-tuple-element.37.q_ref, ...), custom_call_target="tpu_custom_call" | custom-call | flops 268435456 | bytes 1048576 | tf_op jit(solution)/shard_map/pallas_call | solution.py:289
  35.1 3.5 %shard_map.90 = (bf16[2,2,256,128]{3,2,1,0:T(8,128)(2,1)S(1)}, bf16[2,2,256,128]{3,2,1,0:T(8,128)(2,1)S(1)}, bf16[2,2,256,128]{3,2,1,0:T(8,128)(2,1)S(1)}, f32[4...) custom-call(s32[1,256]{1,0:T(1,128)S(1)} %get-tuple-element.36._.starts_ref, ...), custom_call_target="tpu_custom_call" | custom-call | flops 1073741824 | bytes 1048576 | tf_op jit(solution)/shard_map/pallas_call | solution.py:290
  38.6 2.7 %collective-permute-start.5 = (bf16[2,2,256,128]{3,2,1,0:T(8,128)(2,1)S(1)}, bf16[2,2,256,128]{3,2,1,0:T(8,128)(2,1)S(1)}, u32[]{:S(2)}, u32[]{:S(2)}) collective-permute-start(bf16[2,2,256,128]{3,2,1,0:T(8,128)(2,1)S(1)} %get-tuple-element.58), channel_id=1, source_target_pairs={{0,16},{8,24},{16,0},{24,8},{32,48},{40,56},{48,32},{56,40},{64,80... | collective-permute-start | bytes 786440 | tf_op jit(solution)/shard_map/ppermute | solution.py:249
  41.3 3.6 %collective-permute-start.6 = (bf16[2,2,256,128]{3,2,1,0:T(8,128)(2,1)S(1)}, bf16[2,2,256,128]{3,2,1,0:T(8,128)(2,1)S(1)}, u32[]{:S(2)}, u32[]{:S(2)}) collective-permute-start(bf16[2,2,256,128]{3,2,1,0:T(8,128)(2,1)S(1)} %get-tuple-element.59), channel_id=1, source_target_pairs={{0,24},{8,0},{16,8},{24,16},{32,56},{40,32},{48,40},{56,48},{64,88... | collective-permute-start | bytes 786440 | tf_op jit(solution)/shard_map/ppermute | solution.py:249
  44.9 2.2 %collective-permute-start.7 = (bf16[2,2,256,128]{3,2,1,0:T(8,128)(2,1)S(1)}, bf16[2,2,256,128]{3,2,1,0:T(8,128)(2,1)S(1)}, u32[]{:S(2)}, u32[]{:S(2)}) collective-permute-start(bf16[2,2,256,128]{3,2,1,0:T(8,128)(2,1)S(1)} %get-tuple-element.60), channel_id=1, source_target_pairs={{0,8},{8,16},{16,24},{24,0},{32,40},{40,48},{48,56},{56,32},{64,72... | collective-permute-start | bytes 786440 | tf_op jit(solution)/shard_map/ppermute | solution.py:249
  47.1 1.9 %shard_map.91.mine_ref = f32[3,2,256,128]{3,2,1,0:T(8,128)S(1)} custom-call(s32[1,256]{1,0:T(1,128)S(1)} %get-tuple-element.36._.starts_ref, bf16[256,512]{1,0:T(8,128)(2,1)S(1)} %get-tuple-element.37.q_ref, bf16[256,512]{1,0:T(8,128)(2,1)S(1)} %get-tuple-element.38.g_ref, bf16[2,256,128]{2,1,0:T(8,128)(2,1)S(1)} %shard_map.85.own_ref, ...), custom_call_target="tpu_custom_call" | custom-call | flops 402653184 | bytes 1048576 | tf_op jit(solution)/shard_map/pallas_call | solution.py:299
  49.1 1.4 %collective-permute-done.5.r2_ref = bf16[2,2,256,128]{3,2,1,0:T(8,128)(2,1)S(1)} collective-permute-done((bf16[2,2,256,128]{3,2,1,0:T(8,128)(2,1)S(1)}, bf16[2,2,256,128]{3,2,1,0:T(8,128)(2,1)S(1)}, u32[]{:S(2)}, u32[]{:S(2)}) %collective-permute-start.5) | collective-permute-done | bytes 262176 | tf_op jit(solution)/shard_map/ppermute | solution.py:249
  50.5 3.4 %collective-permute-done.6.r1_ref = bf16[2,2,256,128]{3,2,1,0:T(8,128)(2,1)S(1)} collective-permute-done((bf16[2,2,256,128]{3,2,1,0:T(8,128)(2,1)S(1)}, bf16[2,2,256,128]{3,2,1,0:T(8,128)(2,1)S(1)}, u32[]{:S(2)}, u32[]{:S(2)}) %collective-permute-start.6) | collective-permute-done | bytes 262176 | tf_op jit(solution)/shard_map/ppermute | solution.py:249
  53.9 0.1 shard_map.93.mine_ref
  54.0 1.8 %collective-permute-done.7.r3_ref = bf16[2,2,256,128]{3,2,1,0:T(8,128)(2,1)S(1)} collective-permute-done((bf16[2,2,256,128]{3,2,1,0:T(8,128)(2,1)S(1)}, bf16[2,2,256,128]{3,2,1,0:T(8,128)(2,1)S(1)}, u32[]{:S(2)}, u32[]{:S(2)}) %collective-permute-start.7) | collective-permute-done | bytes 262176 | tf_op jit(solution)/shard_map/ppermute | solution.py:249
  55.9 1.9 %collective-permute-start.8 = (bf16[2,256,128]{2,1,0:T(8,128)(2,1)S(1)}, bf16[2,256,128]{2,1,0:T(8,128)(2,1)S(1)}, u32[]{:S(2)}, u32[]{:S(2)}) collective-permute-start(bf16[2,256,128]{2,1,0:T(8,128)(2,1)S(1)} %get-tuple-element.65), channel_id=1, source_target_pairs={{64,0},{72,8},{80,16},{88,24},{96,32},{104,40},{112,48},{120,56},{... | collective-permute-start | bytes 393224 | tf_op jit(solution)/shard_map/ppermute | solution.py:245
  57.8 2.1 %collective-permute-start.9 = (bf16[2,256,128]{2,1,0:T(8,128)(2,1)S(1)}, bf16[2,256,128]{2,1,0:T(8,128)(2,1)S(1)}, u32[]{:S(2)}, u32[]{:S(2)}) collective-permute-start(bf16[2,256,128]{2,1,0:T(8,128)(2,1)S(1)} %get-tuple-element.61._), channel_id=1, source_target_pairs={{32,0},{40,8},{48,16},{56,24},{64,32},{72,40},{80,48},{88,56},{96,... | collective-permute-start | bytes 393224 | tf_op jit(solution)/shard_map/ppermute | solution.py:245
  60.0 5.6 %shard_map.95 = (bf16[256,512]{1,0:T(8,128)(2,1)}, f32[256,512]{1,0:T(8,128)}) custom-call(s32[1,256]{1,0:T(1,128)S(1)} %get-tuple-element.36._.starts_ref, bf16[256,512]{1,0:T(8,128)(2,1)S(1)} %get-tuple-element.37.q_ref, bf16[256,512]{1,0:T(8,128)(2,1)S(1)} %get-tuple-element.38.g_ref, bf16[2,256,128]{2,1,0:T(8,128)(2,1)S(1)} %shard_map.85.own_ref, ...), custom_call_target="tpu_custom_call" | custom-call | flops 1207959552 | bytes 1048576 | tf_op jit(solution)/shard_map/pallas_call | solution.py:307
  65.6 2.6 %collective-permute-done.8.two_ref = bf16[2,256,128]{2,1,0:T(8,128)(2,1)S(1)} collective-permute-done((bf16[2,256,128]{2,1,0:T(8,128)(2,1)S(1)}, bf16[2,256,128]{2,1,0:T(8,128)(2,1)S(1)}, u32[]{:S(2)}, u32[]{:S(2)}) %collective-permute-start.8) | collective-permute-done | bytes 131104 | tf_op jit(solution)/shard_map/ppermute | solution.py:245
  68.2 2.2 %collective-permute-done.9.one_ref = bf16[2,256,128]{2,1,0:T(8,128)(2,1)S(1)} collective-permute-done((bf16[2,256,128]{2,1,0:T(8,128)(2,1)S(1)}, bf16[2,256,128]{2,1,0:T(8,128)(2,1)S(1)}, u32[]{:S(2)}, u32[]{:S(2)}) %collective-permute-start.9) | collective-permute-done | bytes 131104 | tf_op jit(solution)/shard_map/ppermute | solution.py:245
  70.4 0.7 %shard_map.97 = (f32[256,128]{1,0:T(8,128)}, f32[256,128]{1,0:T(8,128)}) custom-call(f32[2,256,128]{2,1,0:T(8,128)S(1)} %shard_map.96.own_ref, bf16[2,256,128]{2,1,0:T(8,128)(2,1)S(1)} %collective-permute-done.9.one_ref), custom_call_target="tpu_custom_call" | custom-call | bytes 1048576 | tf_op jit(solution)/shard_map/pallas_call | solution.py:317
  (12 shorter events, 0.3 us)
Async XLA Ops:
  0.6 0.8 %copy-start.2 = (bf16[256,128]{1,0:T(8,128)(2,1)S(1)}, bf16[256,128]{1,0:T(8,128)(2,1)}, u32[]{:S(2)}) copy-start(bf16[256,128]{1,0:T(8,128)(2,1)} %k_ref.1) | copy-start | bytes 196612
  1.5 0.8 %copy-start.3 = (bf16[256,128]{1,0:T(8,128)(2,1)S(1)}, bf16[256,128]{1,0:T(8,128)(2,1)}, u32[]{:S(2)}) copy-start(bf16[256,128]{1,0:T(8,128)(2,1)} %v_ref.1) | copy-start | bytes 196612
  2.3 13.4 %collective-permute-start.1 = (bf16[2,256,128]{2,1,0:T(8,128)(2,1)S(1)}, bf16[2,256,128]{2,1,0:T(8,128)(2,1)S(1)}, u32[]{:S(2)}, u32[]{:S(2)}) collective-permute-start(bf16[2,256,128]{2,1,0:T(8,128)(2,1)S(1)} %shard_map.85.own_ref), channel_id=1, source_target_pairs={{0,64},{8,72},{16,80},{24,88},{32,96},{40,104},{48,112},{56,120},{... | collective-permute-start | bytes 393224 | tf_op jit(solution)/shard_map/ppermute | solution.py:245
  8.7 8.9 %collective-permute-start = (bf16[2,256,128]{2,1,0:T(8,128)(2,1)S(1)}, bf16[2,256,128]{2,1,0:T(8,128)(2,1)S(1)}, u32[]{:S(2)}, u32[]{:S(2)}) collective-permute-start(bf16[2,256,128]{2,1,0:T(8,128)(2,1)S(1)} %shard_map.85.own_ref), channel_id=1, source_target_pairs={{0,32},{8,40},{16,48},{24,56},{32,64},{40,72},{48,80},{56,88},{64,... | collective-permute-start | bytes 393224 | tf_op jit(solution)/shard_map/ppermute | solution.py:245
  12.6 1.0 %copy-start = (bf16[256,512]{1,0:T(8,128)(2,1)S(1)}, bf16[256,512]{1,0:T(8,128)(2,1)}, u32[]{:S(2)}) copy-start(bf16[256,512]{1,0:T(8,128)(2,1)} %q_ref.1) | copy-start | bytes 786436
  13.5 0.9 %copy-start.1 = (bf16[256,512]{1,0:T(8,128)(2,1)S(1)}, bf16[256,512]{1,0:T(8,128)(2,1)}, u32[]{:S(2)}) copy-start(bf16[256,512]{1,0:T(8,128)(2,1)} %g_ref.1) | copy-start | bytes 786436
  14.5 0.7 copy-start.4
  17.6 12.7 %collective-permute-start.3 = (bf16[2,2,256,128]{3,2,1,0:T(8,128)(2,1)S(1)}, bf16[2,2,256,128]{3,2,1,0:T(8,128)(2,1)S(1)}, u32[]{:S(2)}, u32[]{:S(2)}) collective-permute-start(bf16[2,2,256,128]{3,2,1,0:T(8,128)(2,1)S(1)} %get-tuple-element.40), channel_id=1, source_target_pairs={{0,16},{8,24},{16,0},{24,8},{32,48},{40,56},{48,32},{56,40},{64,80... | collective-permute-start | bytes 786440 | tf_op jit(solution)/shard_map/ppermute | solution.py:249
  20.1 14.0 %collective-permute-start.2 = (bf16[2,2,256,128]{3,2,1,0:T(8,128)(2,1)S(1)}, bf16[2,2,256,128]{3,2,1,0:T(8,128)(2,1)S(1)}, u32[]{:S(2)}, u32[]{:S(2)}) collective-permute-start(bf16[2,2,256,128]{3,2,1,0:T(8,128)(2,1)S(1)} %get-tuple-element.39), channel_id=1, source_target_pairs={{0,8},{8,16},{16,24},{24,0},{32,40},{40,48},{48,56},{56,32},{64,72... | collective-permute-start | bytes 786440 | tf_op jit(solution)/shard_map/ppermute | solution.py:249
  24.1 11.0 %collective-permute-start.4 = (bf16[2,2,256,128]{3,2,1,0:T(8,128)(2,1)S(1)}, bf16[2,2,256,128]{3,2,1,0:T(8,128)(2,1)S(1)}, u32[]{:S(2)}, u32[]{:S(2)}) collective-permute-start(bf16[2,2,256,128]{3,2,1,0:T(8,128)(2,1)S(1)} %get-tuple-element.41), channel_id=1, source_target_pairs={{0,24},{8,0},{16,8},{24,16},{32,56},{40,32},{48,40},{56,48},{64,88... | collective-permute-start | bytes 786440 | tf_op jit(solution)/shard_map/ppermute | solution.py:249
  38.6 11.9 %collective-permute-start.5 = (bf16[2,2,256,128]{3,2,1,0:T(8,128)(2,1)S(1)}, bf16[2,2,256,128]{3,2,1,0:T(8,128)(2,1)S(1)}, u32[]{:S(2)}, u32[]{:S(2)}) collective-permute-start(bf16[2,2,256,128]{3,2,1,0:T(8,128)(2,1)S(1)} %get-tuple-element.58), channel_id=1, source_target_pairs={{0,16},{8,24},{16,0},{24,8},{32,48},{40,56},{48,32},{56,40},{64,80... | collective-permute-start | bytes 786440 | tf_op jit(solution)/shard_map/ppermute | solution.py:249
  41.3 12.6 %collective-permute-start.6 = (bf16[2,2,256,128]{3,2,1,0:T(8,128)(2,1)S(1)}, bf16[2,2,256,128]{3,2,1,0:T(8,128)(2,1)S(1)}, u32[]{:S(2)}, u32[]{:S(2)}) collective-permute-start(bf16[2,2,256,128]{3,2,1,0:T(8,128)(2,1)S(1)} %get-tuple-element.59), channel_id=1, source_target_pairs={{0,24},{8,0},{16,8},{24,16},{32,56},{40,32},{48,40},{56,48},{64,88... | collective-permute-start | bytes 786440 | tf_op jit(solution)/shard_map/ppermute | solution.py:249
  44.9 10.9 %collective-permute-start.7 = (bf16[2,2,256,128]{3,2,1,0:T(8,128)(2,1)S(1)}, bf16[2,2,256,128]{3,2,1,0:T(8,128)(2,1)S(1)}, u32[]{:S(2)}, u32[]{:S(2)}) collective-permute-start(bf16[2,2,256,128]{3,2,1,0:T(8,128)(2,1)S(1)} %get-tuple-element.60), channel_id=1, source_target_pairs={{0,8},{8,16},{16,24},{24,0},{32,40},{40,48},{48,56},{56,32},{64,72... | collective-permute-start | bytes 786440 | tf_op jit(solution)/shard_map/ppermute | solution.py:249
  55.9 12.3 %collective-permute-start.8 = (bf16[2,256,128]{2,1,0:T(8,128)(2,1)S(1)}, bf16[2,256,128]{2,1,0:T(8,128)(2,1)S(1)}, u32[]{:S(2)}, u32[]{:S(2)}) collective-permute-start(bf16[2,256,128]{2,1,0:T(8,128)(2,1)S(1)} %get-tuple-element.65), channel_id=1, source_target_pairs={{64,0},{72,8},{80,16},{88,24},{96,32},{104,40},{112,48},{120,56},{... | collective-permute-start | bytes 393224 | tf_op jit(solution)/shard_map/ppermute | solution.py:245
  57.8 12.5 %collective-permute-start.9 = (bf16[2,256,128]{2,1,0:T(8,128)(2,1)S(1)}, bf16[2,256,128]{2,1,0:T(8,128)(2,1)S(1)}, u32[]{:S(2)}, u32[]{:S(2)}) collective-permute-start(bf16[2,256,128]{2,1,0:T(8,128)(2,1)S(1)} %get-tuple-element.61._), channel_id=1, source_target_pairs={{32,0},{40,8},{48,16},{56,24},{64,32},{72,40},{80,48},{88,56},{96,... | collective-permute-start | bytes 393224 | tf_op jit(solution)/shard_map/ppermute | solution.py:245

commit v8 on v6

--- a/solution.py
+++ b/solution.py
@@ -134,9 +134,9 @@
 
 
 def last_kernel(
-    starts_ref, q_ref, g_ref, far_ref, mn, tn, rn, p1_ref, dp1_ref, m1, t1, r1, p2_ref, dp2_ref, m2, t2, r2,
-    b1_ref, b2_ref, b3_ref, peak_ref, over_ref, rd_ref,
-    p3_ref, dp3_ref, m_ref, t_ref, r_ref, w1_ref, w2_ref, w3_ref, pb_ref, ds_ref,
+    starts_ref, q_ref, g_ref, far_ref, mn, tn, rn, m1, t1, r1, p2_ref, dp2_ref, m2, t2, r2,
+    b2_ref, peak_ref, over_ref, rd_ref, w1_ref, w3_ref, p3_ref, dp3_ref,
+    m_ref, t_ref, r_ref, w2_ref, pb_ref, ds_ref,
 ):
     far_scores(3, starts_ref, q_ref, g_ref, far_ref, p3_ref, dp3_ref, m_ref, t_ref, r_ref)
 
@@ -154,6 +154,9 @@
         for b in range(2):
             ref[b] = factors[3 + 2 * n + b] * over
     far_back(p2_ref, dp2_ref, w2_ref, rd_ref, q_ref, g_ref, b2_ref, pb_ref, ds_ref)
+
+
+def sides_kernel(q_ref, g_ref, rd_ref, p1_ref, dp1_ref, w1_ref, p3_ref, dp3_ref, w3_ref, b1_ref, b3_ref, pb_ref, ds_ref):
     far_back(p1_ref, dp1_ref, w1_ref, rd_ref, q_ref, g_ref, b1_ref, pb_ref, ds_ref)
     far_back(p3_ref, dp3_ref, w3_ref, rd_ref, q_ref, g_ref, b3_ref, pb_ref, ds_ref)
 
@@ -276,15 +279,19 @@
     arrive = {d: call(functools.partial(far_scores, d), tiles + sums, [VM] * 4, blocks=2, limit=8) for d in (1, 2)}
     p2, dp2, *sums2 = arrive[2](*wanted, f2)
     p1, dp1, *sums1 = arrive[1](*wanted, f1)
-    *backs, peak, over, rd = call(
+    b2, peak, over, rd, w1, w3, p3, dp3 = call(
         last_kernel,
-        (pair,) * 3 + (array(stats, F32),) * 3,
-        [VM] * 17,
-        [pltpu.VMEM((2, H, T, T), F32)] * 2 + [pltpu.VMEM((2, *stats), F32)] * 6 + staged,
-        blocks=8,
-        limit=16,
-    )(*wanted, f3, *near, p1, dp1, *sums1, p2, dp2, *sums2)
-    r1, r2, r3 = (along_x(b, -d, peers) for d, b in enumerate(backs, 1))
+        (pair,) + (array(stats, F32),) * 3 + (array((2, *stats), F32),) * 2 + tiles,
+        [VM] * 15,
+        [pltpu.VMEM((2, *stats), F32)] * 4 + staged,
+        blocks=4,
+        limit=8,
+    )(*wanted, f3, *near, *sums1, p2, dp2, *sums2)
+    r2 = along_x(b2, -2, peers)
+    b1, b3 = call(sides_kernel, (pair,) * 2, [VM] * 9, staged, blocks=4, limit=8)(
+        queries, grad_out, rd, p1, dp1, w1, p3, dp3, w3
+    )
+    r1, r3 = along_x(b1, -1, peers), along_x(b3, -3, peers)
     attended, query_grad, mine = call(
         rest_kernel,
         (array((T, H * D), BF16), array((T, H * D), F32), array((3, *block), F32)),

time: 71.6 us -> 71.2 us (level)
  the two profiles are of different devices: /device:TPU:116 before, /device:TPU:112 now
where the time goes in v8:
time: 71.2 us; the launch traced here: 70.6 us
  starting transfers between devices  36.7 us (52%)
  Pallas kernels  14.8 us (21%)
  waiting for transfers between devices  14.1 us (20%)
  local copies, waits for them, and re-layouts  4.22 us (6%)
  between operations  0.84 us (1%)
    ppermute x6, starting transfers between devices, along_x(): lax.ppermute(block, 'peer', [(i, i - i % ROW + (i + columns) % ROW) for i...  22.6 us
    ppermute x4, starting transfers between devices, along_z(): lax.ppermute(block, 'peer', [(i, i + far) for i in range(peers) if 0 <= i...  14.1 us
    ppermute x4, waiting for transfers between devices, along_z(): lax.ppermute(block, 'peer', [(i, i + far) for i in range(peers) if 0 <= i...  11.4 us
    pallas_call x1, Pallas kernels, body(): call(rest_kernel, (array((T, H * D), BF16), array((T, H * D), F32), array...  6.44 us
    unnamed x10, local copies, waits for them, and re-layouts  4.22 us
    ppermute x6, waiting for transfers between devices, along_x(): lax.ppermute(block, 'peer', [(i, i - i % ROW + (i + columns) % ROW) for i...  2.69 us
    pallas_call x1, Pallas kernels, body(): call(last_kernel, (pair,) + (array(stats, F32),) * 3 + (array((2, *stats)...  1.88 us
    pallas_call x1, Pallas kernels, body(): call(sides_kernel, (pair,) * 2, [VM] * 9, staged, blocks=4, limit=8)  1.48 us
  transfers between devices with their start and end apart: 10, of which 5 were waited for; matrix products, arithmetic and copies ran while one was open for 0% of the time, Pallas kernels for 17%

profile of v8, /device:TPU:112, one launch (start us, length us, event | category | flops | bytes accessed | tf_op | source)
XLA Modules:
  0.0 70.6 jit_solution(3866897574658309343)
XLA Ops:
  0.6 0.8 %copy-done.2 = bf16[256,128]{1,0:T(8,128)(2,1)S(1)} copy-done((bf16[256,128]{1,0:T(8,128)(2,1)S(1)}, bf16[256,128]{1,0:T(8,128)(2,1)}, u32[]{:S(2)}) %copy-start.2) | copy-done | bytes 65560
  1.5 0.8 %copy-done.3 = bf16[256,128]{1,0:T(8,128)(2,1)S(1)} copy-done((bf16[256,128]{1,0:T(8,128)(2,1)S(1)}, bf16[256,128]{1,0:T(8,128)(2,1)}, u32[]{:S(2)}) %copy-start.3) | copy-done | bytes 65560
  2.3 6.4 %collective-permute-start.1 = (bf16[2,256,128]{2,1,0:T(8,128)(2,1)S(1)}, bf16[2,256,128]{2,1,0:T(8,128)(2,1)S(1)}, u32[]{:S(2)}, u32[]{:S(2)}) collective-permute-start(bf16[2,256,128]{2,1,0:T(8,128)(2,1)S(1)} %shard_map.85.own_ref), channel_id=1, source_target_pairs={{0,64},{8,72},{16,80},{24,88},{32,96},{40,104},{48,112},{56,120},{... | collective-permute-start | bytes 393224 | tf_op jit(solution)/shard_map/ppermute | solution.py:237
  8.7 3.8 %collective-permute-start = (bf16[2,256,128]{2,1,0:T(8,128)(2,1)S(1)}, bf16[2,256,128]{2,1,0:T(8,128)(2,1)S(1)}, u32[]{:S(2)}, u32[]{:S(2)}) collective-permute-start(bf16[2,256,128]{2,1,0:T(8,128)(2,1)S(1)} %shard_map.85.own_ref), channel_id=1, source_target_pairs={{0,32},{8,40},{16,48},{24,56},{32,64},{40,72},{48,80},{56,88},{64,... | collective-permute-start | bytes 393224 | tf_op jit(solution)/shard_map/ppermute | solution.py:237
  12.6 0.9 %copy-done = bf16[256,512]{1,0:T(8,128)(2,1)S(1)} copy-done((bf16[256,512]{1,0:T(8,128)(2,1)S(1)}, bf16[256,512]{1,0:T(8,128)(2,1)}, u32[]{:S(2)}) %copy-start) | copy-done | bytes 262168
  13.5 0.9 %copy-done.1 = bf16[256,512]{1,0:T(8,128)(2,1)S(1)} copy-done((bf16[256,512]{1,0:T(8,128)(2,1)S(1)}, bf16[256,512]{1,0:T(8,128)(2,1)}, u32[]{:S(2)}) %copy-start.1) | copy-done | bytes 262168
  14.5 0.7 copy-done.4
  15.1 0.6 shard_map.84
  15.7 1.9 %collective-permute-done.z1_ref = bf16[2,256,128]{2,1,0:T(8,128)(2,1)S(1)} collective-permute-done((bf16[2,256,128]{2,1,0:T(8,128)(2,1)S(1)}, bf16[2,256,128]{2,1,0:T(8,128)(2,1)S(1)}, u32[]{:S(2)}, u32[]{:S(2)}) %collective-permute-start) | collective-permute-done | bytes 131104 | tf_op jit(solution)/shard_map/ppermute | solution.py:237
  17.6 0.1 shard_map.86
  17.7 4.9 %collective-permute-start.3 = (bf16[2,2,256,128]{3,2,1,0:T(8,128)(2,1)S(1)}, bf16[2,2,256,128]{3,2,1,0:T(8,128)(2,1)S(1)}, u32[]{:S(2)}, u32[]{:S(2)}) collective-permute-start(bf16[2,2,256,128]{3,2,1,0:T(8,128)(2,1)S(1)} %get-tuple-element.45), channel_id=1, source_target_pairs={{0,16},{8,24},{16,0},{24,8},{32,48},{40,56},{48,32},{56,40},{64,80... | collective-permute-start | bytes 786440 | tf_op jit(solution)/shard_map/ppermute | solution.py:241
  22.6 2.5 %collective-permute-start.2 = (bf16[2,2,256,128]{3,2,1,0:T(8,128)(2,1)S(1)}, bf16[2,2,256,128]{3,2,1,0:T(8,128)(2,1)S(1)}, u32[]{:S(2)}, u32[]{:S(2)}) collective-permute-start(bf16[2,2,256,128]{3,2,1,0:T(8,128)(2,1)S(1)} %get-tuple-element.44), channel_id=1, source_target_pairs={{0,8},{8,16},{16,24},{24,0},{32,40},{40,48},{48,56},{56,32},{64,72... | collective-permute-start | bytes 786440 | tf_op jit(solution)/shard_map/ppermute | solution.py:241
  25.1 4.6 %collective-permute-start.4 = (bf16[2,2,256,128]{3,2,1,0:T(8,128)(2,1)S(1)}, bf16[2,2,256,128]{3,2,1,0:T(8,128)(2,1)S(1)}, u32[]{:S(2)}, u32[]{:S(2)}) collective-permute-start(bf16[2,2,256,128]{3,2,1,0:T(8,128)(2,1)S(1)} %get-tuple-element.46), channel_id=1, source_target_pairs={{0,24},{8,0},{16,8},{24,16},{32,56},{40,32},{48,40},{56,48},{64,88... | collective-permute-start | bytes 786440 | tf_op jit(solution)/shard_map/ppermute | solution.py:241
  29.7 1.3 %shard_map.87 = (f32[3,4,256]{2,1,0:T(4,128)S(1)}, f32[3,4,256]{2,1,0:T(4,128)S(1)}, f32[3,4,256]{2,1,0:T(4,128)S(1)}) custom-call(s32[1,256]{1,0:T(1,128)S(1)} %get-tuple-element.41._.starts_ref, bf16[256,512]{1,0:T(8,128)(2,1)S(1)} %get-tuple-element.42.q_ref, bf16[256,512]{1,0:T(8,128)(2,1)S(1)} %get-tuple-element.43.g_ref, ...), custom_call_target="tpu_custom_call" | custom-call | flops 402653184 | bytes 1048576 | tf_op jit(solution)/shard_map/pallas_call | solution.py:278
  31.0 1.0 %shard_map.89 = (f32[2,4,256,256]{3,2,1,0:T(8,128)S(1)}, f32[2,4,256,256]{3,2,1,0:T(8,128)S(1)}, f32[2,4,256]{2,1,0:T(4,128)S(1)}, f32[2,4,256]{2,1,0:T(4,128)S(1)}, f32[2,4,256]{2,1,0:T(4,128)S(1)}) custom-call(s32[1,256]{1,0:T(1,128)S(1)} %get-tuple-element.41._.starts_ref, bf16[256,512]{1,0:T(8,128)(2,1)S(1)} %get-tuple-element.42.q_ref, ...), custom_call_target="tpu_custom_call" | custom-call | flops 268435456 | bytes 1048576 | tf_op jit(solution)/shard_map/pallas_call | solution.py:280
  32.0 2.4 %collective-permute-done.2.far_ref.f1_ref = bf16[2,2,256,128]{3,2,1,0:T(8,128)(2,1)S(1)} collective-permute-done((bf16[2,2,256,128]{3,2,1,0:T(8,128)(2,1)S(1)}, bf16[2,2,256,128]{3,2,1,0:T(8,128)(2,1)S(1)}, u32[]{:S(2)}, u32[]{:S(2)}) %collective-permute-start.2) | collective-permute-done | bytes 262176 | tf_op jit(solution)/shard_map/ppermute | solution.py:241
  34.4 1.0 %shard_map.88 = (f32[2,4,256,256]{3,2,1,0:T(8,128)S(1)}, f32[2,4,256,256]{3,2,1,0:T(8,128)S(1)}, f32[2,4,256]{2,1,0:T(4,128)S(1)}, f32[2,4,256]{2,1,0:T(4,128)S(1)}, f32[2,4,256]{2,1,0:T(4,128)S(1)}) custom-call(s32[1,256]{1,0:T(1,128)S(1)} %get-tuple-element.41._.starts_ref, bf16[256,512]{1,0:T(8,128)(2,1)S(1)} %get-tuple-element.42.q_ref, ...), custom_call_target="tpu_custom_call" | custom-call | flops 268435456 | bytes 1048576 | tf_op jit(solution)/shard_map/pallas_call | solution.py:281
  35.4 1.9 %shard_map.90 = (bf16[2,2,256,128]{3,2,1,0:T(8,128)(2,1)S(1)}, f32[4,256]{1,0:T(4,128)S(1)}, f32[4,256]{1,0:T(4,128)S(1)}, f32[4,256]{1,0:T(4,128)S(1)}, f32[2,4...) custom-call(s32[1,256]{1,0:T(1,128)S(1)} %get-tuple-element.41._.sta, ...), custom_call_target="tpu_custom_call" | custom-call | flops 536870912 | bytes 1048576 | tf_op jit(solution)/shard_map/pallas_call | solution.py:282
  37.3 4.6 %collective-permute-start.5 = (bf16[2,2,256,128]{3,2,1,0:T(8,128)(2,1)S(1)}, bf16[2,2,256,128]{3,2,1,0:T(8,128)(2,1)S(1)}, u32[]{:S(2)}, u32[]{:S(2)}) collective-permute-start(bf16[2,2,256,128]{3,2,1,0:T(8,128)(2,1)S(1)} %get-tuple-element.64), channel_id=1, source_target_pairs={{0,16},{8,24},{16,0},{24,8},{32,48},{40,56},{48,32},{56,40},{64,80... | collective-permute-start | bytes 786440 | tf_op jit(solution)/shard_map/ppermute | solution.py:241
  41.9 1.5 %shard_map.93 = (bf16[2,2,256,128]{3,2,1,0:T(8,128)(2,1)S(1)}, bf16[2,2,256,128]{3,2,1,0:T(8,128)(2,1)S(1)}) custom-call(bf16[256,512]{1,0:T(8,128)(2,1)S(1)} %get-tuple-element.42.q_ref, bf16[256,512]{1,0:T(8,128)(2,1)S(1)} %get-tuple-element.43.g_ref, f32[4,256]{1,0:T(4,128)S(1)} %get-tuple-element.60.rd_ref, ...), custom_call_target="tpu_custom_call" | custom-call | flops 536870912 | bytes 1048576 | tf_op jit(solution)/shard_map/pallas_call | solution.py:291
  43.4 3.1 %collective-permute-start.6 = (bf16[2,2,256,128]{3,2,1,0:T(8,128)(2,1)S(1)}, bf16[2,2,256,128]{3,2,1,0:T(8,128)(2,1)S(1)}, u32[]{:S(2)}, u32[]{:S(2)}) collective-permute-start(bf16[2,2,256,128]{3,2,1,0:T(8,128)(2,1)S(1)} %get-tuple-element.71), channel_id=1, source_target_pairs={{0,24},{8,0},{16,8},{24,16},{32,56},{40,32},{48,40},{56,48},{64,88... | collective-permute-start | bytes 786440 | tf_op jit(solution)/shard_map/ppermute | solution.py:241
  46.5 2.9 %collective-permute-start.7 = (bf16[2,2,256,128]{3,2,1,0:T(8,128)(2,1)S(1)}, bf16[2,2,256,128]{3,2,1,0:T(8,128)(2,1)S(1)}, u32[]{:S(2)}, u32[]{:S(2)}) collective-permute-start(bf16[2,2,256,128]{3,2,1,0:T(8,128)(2,1)S(1)} %get-tuple-element.72), channel_id=1, source_target_pairs={{0,8},{8,16},{16,24},{24,0},{32,40},{40,48},{48,56},{56,32},{64,72... | collective-permute-start | bytes 786440 | tf_op jit(solution)/shard_map/ppermute | solution.py:241
  49.4 6.4 %shard_map.91 = (bf16[256,512]{1,0:T(8,128)(2,1)}, f32[256,512]{1,0:T(8,128)}, f32[3,2,256,128]{3,2,1,0:T(8,128)S(1)}) custom-call(s32[1,256]{1,0:T(1,128)S(1)} %get-tuple-element.41._.starts_ref, bf16[256,512]{1,0:T(8,128)(2,1)S(1)} %get-tuple-element.42.q_ref, bf16[256,512]{1,0:T(8,128)(2,1)S(1)} %get-tuple-element.43.g_ref, ...), custom_call_target="tpu_custom_call" | custom-call | flops 1207959552 | bytes 1048576 | tf_op jit(solution)/shard_map/pallas_call | solution.py:295
  55.9 0.1 shard_map.92.mine_ref
  56.0 0.1 shard_map.94.mine_ref
  56.1 0.3 collective-permute-done.7.r3_ref
  56.4 0.1 shard_map.95
  56.5 1.9 %collective-permute-start.8 = (bf16[2,256,128]{2,1,0:T(8,128)(2,1)S(1)}, bf16[2,256,128]{2,1,0:T(8,128)(2,1)S(1)}, u32[]{:S(2)}, u32[]{:S(2)}) collective-permute-start(bf16[2,256,128]{2,1,0:T(8,128)(2,1)S(1)} %get-tuple-element.74), channel_id=1, source_target_pairs={{64,0},{72,8},{80,16},{88,24},{96,32},{104,40},{112,48},{120,56},{... | collective-permute-start | bytes 393224 | tf_op jit(solution)/shard_map/ppermute | solution.py:237
  58.4 1.9 %collective-permute-start.9 = (bf16[2,256,128]{2,1,0:T(8,128)(2,1)S(1)}, bf16[2,256,128]{2,1,0:T(8,128)(2,1)S(1)}, u32[]{:S(2)}, u32[]{:S(2)}) collective-permute-start(bf16[2,256,128]{2,1,0:T(8,128)(2,1)S(1)} %get-tuple-element.75), channel_id=1, source_target_pairs={{32,0},{40,8},{48,16},{56,24},{64,32},{72,40},{80,48},{88,56},{96,... | collective-permute-start | bytes 393224 | tf_op jit(solution)/shard_map/ppermute | solution.py:237
  60.3 8.0 %collective-permute-done.8.two_ref = bf16[2,256,128]{2,1,0:T(8,128)(2,1)S(1)} collective-permute-done((bf16[2,256,128]{2,1,0:T(8,128)(2,1)S(1)}, bf16[2,256,128]{2,1,0:T(8,128)(2,1)S(1)}, u32[]{:S(2)}, u32[]{:S(2)}) %collective-permute-start.8) | collective-permute-done | bytes 131104 | tf_op jit(solution)/shard_map/ppermute | solution.py:237
  68.4 1.5 %collective-permute-done.9.one_ref = bf16[2,256,128]{2,1,0:T(8,128)(2,1)S(1)} collective-permute-done((bf16[2,256,128]{2,1,0:T(8,128)(2,1)S(1)}, bf16[2,256,128]{2,1,0:T(8,128)(2,1)S(1)}, u32[]{:S(2)}, u32[]{:S(2)}) %collective-permute-start.9) | collective-permute-done | bytes 131104 | tf_op jit(solution)/shard_map/ppermute | solution.py:237
  69.9 0.7 %shard_map.97 = (f32[256,128]{1,0:T(8,128)}, f32[256,128]{1,0:T(8,128)}) custom-call(f32[2,256,128]{2,1,0:T(8,128)S(1)} %shard_map.96.own_ref, bf16[2,256,128]{2,1,0:T(8,128)(2,1)S(1)} %collective-permute-done.9.one_ref), custom_call_target="tpu_custom_call" | custom-call | bytes 1048576 | tf_op jit(solution)/shard_map/pallas_call | solution.py:310
  (12 shorter events, 0.1 us)
Async XLA Ops:
  0.6 0.8 %copy-start.2 = (bf16[256,128]{1,0:T(8,128)(2,1)S(1)}, bf16[256,128]{1,0:T(8,128)(2,1)}, u32[]{:S(2)}) copy-start(bf16[256,128]{1,0:T(8,128)(2,1)} %k_ref.1) | copy-start | bytes 196612
  1.5 0.8 %copy-start.3 = (bf16[256,128]{1,0:T(8,128)(2,1)S(1)}, bf16[256,128]{1,0:T(8,128)(2,1)}, u32[]{:S(2)}) copy-start(bf16[256,128]{1,0:T(8,128)(2,1)} %v_ref.1) | copy-start | bytes 196612
  2.3 13.4 %collective-permute-start.1 = (bf16[2,256,128]{2,1,0:T(8,128)(2,1)S(1)}, bf16[2,256,128]{2,1,0:T(8,128)(2,1)S(1)}, u32[]{:S(2)}, u32[]{:S(2)}) collective-permute-start(bf16[2,256,128]{2,1,0:T(8,128)(2,1)S(1)} %shard_map.85.own_ref), channel_id=1, source_target_pairs={{0,64},{8,72},{16,80},{24,88},{32,96},{40,104},{48,112},{56,120},{... | collective-permute-start | bytes 393224 | tf_op jit(solution)/shard_map/ppermute | solution.py:237
  8.7 8.9 %collective-permute-start = (bf16[2,256,128]{2,1,0:T(8,128)(2,1)S(1)}, bf16[2,256,128]{2,1,0:T(8,128)(2,1)S(1)}, u32[]{:S(2)}, u32[]{:S(2)}) collective-permute-start(bf16[2,256,128]{2,1,0:T(8,128)(2,1)S(1)} %shard_map.85.own_ref), channel_id=1, source_target_pairs={{0,32},{8,40},{16,48},{24,56},{32,64},{40,72},{48,80},{56,88},{64,... | collective-permute-start | bytes 393224 | tf_op jit(solution)/shard_map/ppermute | solution.py:237
  12.6 1.0 %copy-start = (bf16[256,512]{1,0:T(8,128)(2,1)S(1)}, bf16[256,512]{1,0:T(8,128)(2,1)}, u32[]{:S(2)}) copy-start(bf16[256,512]{1,0:T(8,128)(2,1)} %q_ref.1) | copy-start | bytes 786436
  13.5 0.9 %copy-start.1 = (bf16[256,512]{1,0:T(8,128)(2,1)S(1)}, bf16[256,512]{1,0:T(8,128)(2,1)}, u32[]{:S(2)}) copy-start(bf16[256,512]{1,0:T(8,128)(2,1)} %g_ref.1) | copy-start | bytes 786436
  14.5 0.7 copy-start.4
  17.7 13.3 %collective-permute-start.3 = (bf16[2,2,256,128]{3,2,1,0:T(8,128)(2,1)S(1)}, bf16[2,2,256,128]{3,2,1,0:T(8,128)(2,1)S(1)}, u32[]{:S(2)}, u32[]{:S(2)}) collective-permute-start(bf16[2,2,256,128]{3,2,1,0:T(8,128)(2,1)S(1)} %get-tuple-element.45), channel_id=1, source_target_pairs={{0,16},{8,24},{16,0},{24,8},{32,48},{40,56},{48,32},{56,40},{64,80... | collective-permute-start | bytes 786440 | tf_op jit(solution)/shard_map/ppermute | solution.py:241
  22.6 11.8 %collective-permute-start.2 = (bf16[2,2,256,128]{3,2,1,0:T(8,128)(2,1)S(1)}, bf16[2,2,256,128]{3,2,1,0:T(8,128)(2,1)S(1)}, u32[]{:S(2)}, u32[]{:S(2)}) collective-permute-start(bf16[2,2,256,128]{3,2,1,0:T(8,128)(2,1)S(1)} %get-tuple-element.44), channel_id=1, source_target_pairs={{0,8},{8,16},{16,24},{24,0},{32,40},{40,48},{48,56},{56,32},{64,72... | collective-permute-start | bytes 786440 | tf_op jit(solution)/shard_map/ppermute | solution.py:241
  25.1 10.3 %collective-permute-start.4 = (bf16[2,2,256,128]{3,2,1,0:T(8,128)(2,1)S(1)}, bf16[2,2,256,128]{3,2,1,0:T(8,128)(2,1)S(1)}, u32[]{:S(2)}, u32[]{:S(2)}) collective-permute-start(bf16[2,2,256,128]{3,2,1,0:T(8,128)(2,1)S(1)} %get-tuple-element.46), channel_id=1, source_target_pairs={{0,24},{8,0},{16,8},{24,16},{32,56},{40,32},{48,40},{56,48},{64,88... | collective-permute-start | bytes 786440 | tf_op jit(solution)/shard_map/ppermute | solution.py:241
  37.3 18.6 %collective-permute-start.5 = (bf16[2,2,256,128]{3,2,1,0:T(8,128)(2,1)S(1)}, bf16[2,2,256,128]{3,2,1,0:T(8,128)(2,1)S(1)}, u32[]{:S(2)}, u32[]{:S(2)}) collective-permute-start(bf16[2,2,256,128]{3,2,1,0:T(8,128)(2,1)S(1)} %get-tuple-element.64), channel_id=1, source_target_pairs={{0,16},{8,24},{16,0},{24,8},{32,48},{40,56},{48,32},{56,40},{64,80... | collective-permute-start | bytes 786440 | tf_op jit(solution)/shard_map/ppermute | solution.py:241
  43.4 12.6 %collective-permute-start.6 = (bf16[2,2,256,128]{3,2,1,0:T(8,128)(2,1)S(1)}, bf16[2,2,256,128]{3,2,1,0:T(8,128)(2,1)S(1)}, u32[]{:S(2)}, u32[]{:S(2)}) collective-permute-start(bf16[2,2,256,128]{3,2,1,0:T(8,128)(2,1)S(1)} %get-tuple-element.71), channel_id=1, source_target_pairs={{0,24},{8,0},{16,8},{24,16},{32,56},{40,32},{48,40},{56,48},{64,88... | collective-permute-start | bytes 786440 | tf_op jit(solution)/shard_map/ppermute | solution.py:241
  46.5 9.9 %collective-permute-start.7 = (bf16[2,2,256,128]{3,2,1,0:T(8,128)(2,1)S(1)}, bf16[2,2,256,128]{3,2,1,0:T(8,128)(2,1)S(1)}, u32[]{:S(2)}, u32[]{:S(2)}) collective-permute-start(bf16[2,2,256,128]{3,2,1,0:T(8,128)(2,1)S(1)} %get-tuple-element.72), channel_id=1, source_target_pairs={{0,8},{8,16},{16,24},{24,0},{32,40},{40,48},{48,56},{56,32},{64,72... | collective-permute-start | bytes 786440 | tf_op jit(solution)/shard_map/ppermute | solution.py:241
  56.5 11.9 %collective-permute-start.8 = (bf16[2,256,128]{2,1,0:T(8,128)(2,1)S(1)}, bf16[2,256,128]{2,1,0:T(8,128)(2,1)S(1)}, u32[]{:S(2)}, u32[]{:S(2)}) collective-permute-start(bf16[2,256,128]{2,1,0:T(8,128)(2,1)S(1)} %get-tuple-element.74), channel_id=1, source_target_pairs={{64,0},{72,8},{80,16},{88,24},{96,32},{104,40},{112,48},{120,56},{... | collective-permute-start | bytes 393224 | tf_op jit(solution)/shard_map/ppermute | solution.py:237
  58.4 11.5 %collective-permute-start.9 = (bf16[2,256,128]{2,1,0:T(8,128)(2,1)S(1)}, bf16[2,256,128]{2,1,0:T(8,128)(2,1)S(1)}, u32[]{:S(2)}, u32[]{:S(2)}) collective-permute-start(bf16[2,256,128]{2,1,0:T(8,128)(2,1)S(1)} %get-tuple-element.75), channel_id=1, source_target_pairs={{32,0},{40,8},{48,16},{56,24},{64,32},{72,40},{80,48},{88,56},{96,... | collective-permute-start | bytes 393224 | tf_op jit(solution)/shard_map/ppermute | solution.py:237

commit v9 on v7

--- a/solution.py
+++ b/solution.py
@@ -134,9 +134,9 @@
 
 
 def last_kernel(
-    starts_ref, q_ref, g_ref, far_ref, mn, tn, rn, p1_ref, dp1_ref, m1, t1, r1, p2_ref, dp2_ref, m2, t2, r2,
-    b1_ref, b2_ref, b3_ref, peak_ref, over_ref, rd_ref,
-    p3_ref, dp3_ref, m_ref, t_ref, r_ref, w1_ref, w2_ref, w3_ref, pb_ref, ds_ref,
+    starts_ref, q_ref, g_ref, far_ref, mn, tn, rn, m1, t1, r1, p2_ref, dp2_ref, m2, t2, r2,
+    b2_ref, peak_ref, over_ref, rd_ref, w1_ref, w3_ref, p3_ref, dp3_ref,
+    m_ref, t_ref, r_ref, w2_ref, pb_ref, ds_ref,
 ):
     far_scores(3, starts_ref, q_ref, g_ref, far_ref, p3_ref, dp3_ref, m_ref, t_ref, r_ref)
 
@@ -154,6 +154,9 @@
         for b in range(2):
             ref[b] = factors[3 + 2 * n + b] * over
     far_back(p2_ref, dp2_ref, w2_ref, rd_ref, q_ref, g_ref, b2_ref, pb_ref, ds_ref)
+
+
+def sides_kernel(q_ref, g_ref, rd_ref, p1_ref, dp1_ref, w1_ref, p3_ref, dp3_ref, w3_ref, b1_ref, b3_ref, pb_ref, ds_ref):
     far_back(p1_ref, dp1_ref, w1_ref, rd_ref, q_ref, g_ref, b1_ref, pb_ref, ds_ref)
     far_back(p3_ref, dp3_ref, w3_ref, rd_ref, q_ref, g_ref, b3_ref, pb_ref, ds_ref)
 
@@ -287,15 +290,19 @@
     arrive = {d: call(functools.partial(far_scores, d), tiles + sums, [VM] * 4, blocks=2, limit=8) for d in (1, 2)}
     p2, dp2, *sums2 = arrive[2](*wanted, f2)
     p1, dp1, *sums1 = arrive[1](*wanted, f1)
-    *backs, peak, over, rd = call(
+    b2, peak, over, rd, w1, w3, p3, dp3 = call(
         last_kernel,
-        (pair,) * 3 + (array(stats, F32),) * 3,
-        [VM] * 17,
-        [pltpu.VMEM((2, H, T, T), F32)] * 2 + [pltpu.VMEM((2, *stats), F32)] * 6 + staged,
-        blocks=8,
-        limit=16,
-    )(*wanted, f3, *near, p1, dp1, *sums1, p2, dp2, *sums2)
-    r1, r2, r3 = (along_x(b, -d, peers) for d, b in enumerate(backs, 1))
+        (pair,) + (array(stats, F32),) * 3 + (array((2, *stats), F32),) * 2 + tiles,
+        [VM] * 15,
+        [pltpu.VMEM((2, *stats), F32)] * 4 + staged,
+        blocks=4,
+        limit=8,
+    )(*wanted, f3, *near, *sums1, p2, dp2, *sums2)
+    r2 = along_x(b2, -2, peers)
+    b1, b3 = call(sides_kernel, (pair,) * 2, [VM] * 9, staged, blocks=4, limit=8)(
+        queries, grad_out, rd, p1, dp1, w1, p3, dp3, w3
+    )
+    r1, r3 = along_x(b1, -1, peers), along_x(b3, -3, peers)
     (mine,) = call(near_back_kernel, (array((3, *block), F32),), [VM] * 9, staged, blocks=3, limit=8)(
         *wanted, own, z1, z2, peak, over, rd
     )

time: 71.6 us -> 69.8 us (0.975)
  the two profiles are of different devices: /device:TPU:124 before, /device:TPU:104 now
where the time goes in v9:
time: 69.8 us; the launch traced here: 69.3 us
  starting transfers between devices  36.7 us (53%)
  Pallas kernels  15.6 us (22%)
  waiting for transfers between devices  11.9 us (17%)
  local copies, waits for them, and re-layouts  4.22 us (6%)
  between operations  0.84 us (1%)
    ppermute x6, starting transfers between devices, along_x(): lax.ppermute(block, 'peer', [(i, i - i % ROW + (i + columns) % ROW) for i...  22.5 us
    ppermute x4, starting transfers between devices, along_z(): lax.ppermute(block, 'peer', [(i, i + far) for i in range(peers) if 0 <= i...  14.2 us
    ppermute x6, waiting for transfers between devices, along_x(): lax.ppermute(block, 'peer', [(i, i - i % ROW + (i + columns) % ROW) for i...  7.53 us
    pallas_call x1, Pallas kernels, body(): call(query_side_kernel, (array((T, H * D), BF16), array((T, H * D), F32))...  5.58 us
    ppermute x4, waiting for transfers between devices, along_z(): lax.ppermute(block, 'peer', [(i, i + far) for i in range(peers) if 0 <= i...  4.4 us
    unnamed x10, local copies, waits for them, and re-layouts  4.22 us
    pallas_call x1, Pallas kernels, body(): call(near_back_kernel, (array((3, *block), F32),), [VM] * 9, staged, bloc...  1.86 us
    pallas_call x1, Pallas kernels, body(): call(last_kernel, (pair,) + (array(stats, F32),) * 3 + (array((2, *stats)...  1.79 us
  transfers between devices with their start and end apart: 10, of which 6 were waited for; matrix products, arithmetic and copies ran while one was open for 0% of the time, Pallas kernels for 19%

profile of v9, /device:TPU:104, one launch (start us, length us, event | category | flops | bytes accessed | tf_op | source)
XLA Modules:
  0.0 69.3 jit_solution(11998421050607950395)
XLA Ops:
  0.6 0.8 %copy-done.2 = bf16[256,128]{1,0:T(8,128)(2,1)S(1)} copy-done((bf16[256,128]{1,0:T(8,128)(2,1)S(1)}, bf16[256,128]{1,0:T(8,128)(2,1)}, u32[]{:S(2)}) %copy-start.2) | copy-done | bytes 65560
  1.5 0.8 %copy-done.3 = bf16[256,128]{1,0:T(8,128)(2,1)S(1)} copy-done((bf16[256,128]{1,0:T(8,128)(2,1)S(1)}, bf16[256,128]{1,0:T(8,128)(2,1)}, u32[]{:S(2)}) %copy-start.3) | copy-done | bytes 65560
  2.3 6.4 %collective-permute-start.1 = (bf16[2,256,128]{2,1,0:T(8,128)(2,1)S(1)}, bf16[2,256,128]{2,1,0:T(8,128)(2,1)S(1)}, u32[]{:S(2)}, u32[]{:S(2)}) collective-permute-start(bf16[2,256,128]{2,1,0:T(8,128)(2,1)S(1)} %shard_map.85.own_ref), channel_id=1, source_target_pairs={{0,64},{8,72},{16,80},{24,88},{32,96},{40,104},{48,112},{56,120},{... | collective-permute-start | bytes 393224 | tf_op jit(solution)/shard_map/ppermute | solution.py:248
  8.7 3.8 %collective-permute-start = (bf16[2,256,128]{2,1,0:T(8,128)(2,1)S(1)}, bf16[2,256,128]{2,1,0:T(8,128)(2,1)S(1)}, u32[]{:S(2)}, u32[]{:S(2)}) collective-permute-start(bf16[2,256,128]{2,1,0:T(8,128)(2,1)S(1)} %shard_map.85.own_ref), channel_id=1, source_target_pairs={{0,32},{8,40},{16,48},{24,56},{32,64},{40,72},{48,80},{56,88},{64,... | collective-permute-start | bytes 393224 | tf_op jit(solution)/shard_map/ppermute | solution.py:248
  12.6 0.9 %copy-done = bf16[256,512]{1,0:T(8,128)(2,1)S(1)} copy-done((bf16[256,512]{1,0:T(8,128)(2,1)S(1)}, bf16[256,512]{1,0:T(8,128)(2,1)}, u32[]{:S(2)}) %copy-start) | copy-done | bytes 262168
  13.5 0.9 %copy-done.1 = bf16[256,512]{1,0:T(8,128)(2,1)S(1)} copy-done((bf16[256,512]{1,0:T(8,128)(2,1)S(1)}, bf16[256,512]{1,0:T(8,128)(2,1)}, u32[]{:S(2)}) %copy-start.1) | copy-done | bytes 262168
  14.5 0.7 copy-done.4
  15.1 0.6 shard_map.84
  15.7 1.9 %collective-permute-done.z1_ref = bf16[2,256,128]{2,1,0:T(8,128)(2,1)S(1)} collective-permute-done((bf16[2,256,128]{2,1,0:T(8,128)(2,1)S(1)}, bf16[2,256,128]{2,1,0:T(8,128)(2,1)S(1)}, u32[]{:S(2)}, u32[]{:S(2)}) %collective-permute-start) | collective-permute-done | bytes 131104 | tf_op jit(solution)/shard_map/ppermute | solution.py:248
  17.7 4.9 %collective-permute-start.3 = (bf16[2,2,256,128]{3,2,1,0:T(8,128)(2,1)S(1)}, bf16[2,2,256,128]{3,2,1,0:T(8,128)(2,1)S(1)}, u32[]{:S(2)}, u32[]{:S(2)}) collective-permute-start(bf16[2,2,256,128]{3,2,1,0:T(8,128)(2,1)S(1)} %get-tuple-element.44), channel_id=1, source_target_pairs={{0,16},{8,24},{16,0},{24,8},{32,48},{40,56},{48,32},{56,40},{64,80... | collective-permute-start | bytes 786440 | tf_op jit(solution)/shard_map/ppermute | solution.py:252
  22.6 2.5 %collective-permute-start.2 = (bf16[2,2,256,128]{3,2,1,0:T(8,128)(2,1)S(1)}, bf16[2,2,256,128]{3,2,1,0:T(8,128)(2,1)S(1)}, u32[]{:S(2)}, u32[]{:S(2)}) collective-permute-start(bf16[2,2,256,128]{3,2,1,0:T(8,128)(2,1)S(1)} %get-tuple-element.43), channel_id=1, source_target_pairs={{0,8},{8,16},{16,24},{24,0},{32,40},{40,48},{48,56},{56,32},{64,72... | collective-permute-start | bytes 786440 | tf_op jit(solution)/shard_map/ppermute | solution.py:252
  25.1 4.6 %collective-permute-start.4 = (bf16[2,2,256,128]{3,2,1,0:T(8,128)(2,1)S(1)}, bf16[2,2,256,128]{3,2,1,0:T(8,128)(2,1)S(1)}, u32[]{:S(2)}, u32[]{:S(2)}) collective-permute-start(bf16[2,2,256,128]{3,2,1,0:T(8,128)(2,1)S(1)} %get-tuple-element.45), channel_id=1, source_target_pairs={{0,24},{8,0},{16,8},{24,16},{32,56},{40,32},{48,40},{56,48},{64,88... | collective-permute-start | bytes 786440 | tf_op jit(solution)/shard_map/ppermute | solution.py:252
  29.7 1.3 %shard_map.87 = (f32[3,4,256]{2,1,0:T(4,128)S(1)}, f32[3,4,256]{2,1,0:T(4,128)S(1)}, f32[3,4,256]{2,1,0:T(4,128)S(1)}) custom-call(s32[1,256]{1,0:T(1,128)S(1)} %get-tuple-element.40._.starts_ref, bf16[256,512]{1,0:T(8,128)(2,1)S(1)} %get-tuple-element.41.q_ref, bf16[256,512]{1,0:T(8,128)(2,1)S(1)} %get-tuple-element.42.g_ref, ...), custom_call_target="tpu_custom_call" | custom-call | flops 402653184 | bytes 1048576 | tf_op jit(solution)/shard_map/pallas_call | solution.py:289
  30.9 1.0 %shard_map.89 = (f32[2,4,256,256]{3,2,1,0:T(8,128)S(1)}, f32[2,4,256,256]{3,2,1,0:T(8,128)S(1)}, f32[2,4,256]{2,1,0:T(4,128)S(1)}, f32[2,4,256]{2,1,0:T(4,128)S(1)}, f32[2,4,256]{2,1,0:T(4,128)S(1)}) custom-call(s32[1,256]{1,0:T(1,128)S(1)} %get-tuple-element.40._.starts_ref, bf16[256,512]{1,0:T(8,128)(2,1)S(1)} %get-tuple-element.41.q_ref, ...), custom_call_target="tpu_custom_call" | custom-call | flops 268435456 | bytes 1048576 | tf_op jit(solution)/shard_map/pallas_call | solution.py:291
  31.9 2.5 %collective-permute-done.2.far_ref.f1_ref = bf16[2,2,256,128]{3,2,1,0:T(8,128)(2,1)S(1)} collective-permute-done((bf16[2,2,256,128]{3,2,1,0:T(8,128)(2,1)S(1)}, bf16[2,2,256,128]{3,2,1,0:T(8,128)(2,1)S(1)}, u32[]{:S(2)}, u32[]{:S(2)}) %collective-permute-start.2) | collective-permute-done | bytes 262176 | tf_op jit(solution)/shard_map/ppermute | solution.py:252
  34.4 1.0 %shard_map.88 = (f32[2,4,256,256]{3,2,1,0:T(8,128)S(1)}, f32[2,4,256,256]{3,2,1,0:T(8,128)S(1)}, f32[2,4,256]{2,1,0:T(4,128)S(1)}, f32[2,4,256]{2,1,0:T(4,128)S(1)}, f32[2,4,256]{2,1,0:T(4,128)S(1)}) custom-call(s32[1,256]{1,0:T(1,128)S(1)} %get-tuple-element.40._.starts_ref, bf16[256,512]{1,0:T(8,128)(2,1)S(1)} %get-tuple-element.41.q_ref, ...), custom_call_target="tpu_custom_call" | custom-call | flops 268435456 | bytes 1048576 | tf_op jit(solution)/shard_map/pallas_call | solution.py:292
  35.4 1.8 %shard_map.90 = (bf16[2,2,256,128]{3,2,1,0:T(8,128)(2,1)S(1)}, f32[4,256]{1,0:T(4,128)S(1)}, f32[4,256]{1,0:T(4,128)S(1)}, f32[4,256]{1,0:T(4,128)S(1)}, f32[2,4...) custom-call(s32[1,256]{1,0:T(1,128)S(1)} %get-tuple-element.40._.sta, ...), custom_call_target="tpu_custom_call" | custom-call | flops 536870912 | bytes 1048576 | tf_op jit(solution)/shard_map/pallas_call | solution.py:293
  37.2 4.6 %collective-permute-start.5 = (bf16[2,2,256,128]{3,2,1,0:T(8,128)(2,1)S(1)}, bf16[2,2,256,128]{3,2,1,0:T(8,128)(2,1)S(1)}, u32[]{:S(2)}, u32[]{:S(2)}) collective-permute-start(bf16[2,2,256,128]{3,2,1,0:T(8,128)(2,1)S(1)} %get-tuple-element.60), channel_id=1, source_target_pairs={{0,16},{8,24},{16,0},{24,8},{32,48},{40,56},{48,32},{56,40},{64,80... | collective-permute-start | bytes 786440 | tf_op jit(solution)/shard_map/ppermute | solution.py:252
  41.8 1.5 %shard_map.93 = (bf16[2,2,256,128]{3,2,1,0:T(8,128)(2,1)S(1)}, bf16[2,2,256,128]{3,2,1,0:T(8,128)(2,1)S(1)}) custom-call(bf16[256,512]{1,0:T(8,128)(2,1)S(1)} %get-tuple-element.41.q_ref, bf16[256,512]{1,0:T(8,128)(2,1)S(1)} %get-tuple-element.42.g_ref, f32[4,256]{1,0:T(4,128)S(1)} %get-tuple-element.59.rd_ref, ...), custom_call_target="tpu_custom_call" | custom-call | flops 536870912 | bytes 1048576 | tf_op jit(solution)/shard_map/pallas_call | solution.py:302
  43.3 3.1 %collective-permute-start.6 = (bf16[2,2,256,128]{3,2,1,0:T(8,128)(2,1)S(1)}, bf16[2,2,256,128]{3,2,1,0:T(8,128)(2,1)S(1)}, u32[]{:S(2)}, u32[]{:S(2)}) collective-permute-start(bf16[2,2,256,128]{3,2,1,0:T(8,128)(2,1)S(1)} %get-tuple-element.67), channel_id=1, source_target_pairs={{0,24},{8,0},{16,8},{24,16},{32,56},{40,32},{48,40},{56,48},{64,88... | collective-permute-start | bytes 786440 | tf_op jit(solution)/shard_map/ppermute | solution.py:252
  46.5 2.7 %collective-permute-start.7 = (bf16[2,2,256,128]{3,2,1,0:T(8,128)(2,1)S(1)}, bf16[2,2,256,128]{3,2,1,0:T(8,128)(2,1)S(1)}, u32[]{:S(2)}, u32[]{:S(2)}) collective-permute-start(bf16[2,2,256,128]{3,2,1,0:T(8,128)(2,1)S(1)} %get-tuple-element.68), channel_id=1, source_target_pairs={{0,8},{8,16},{16,24},{24,0},{32,40},{40,48},{48,56},{56,32},{64,72... | collective-permute-start | bytes 786440 | tf_op jit(solution)/shard_map/ppermute | solution.py:252
  49.2 1.9 %shard_map.91.mine_ref = f32[3,2,256,128]{3,2,1,0:T(8,128)S(1)} custom-call(s32[1,256]{1,0:T(1,128)S(1)} %get-tuple-element.40._.starts_ref, bf16[256,512]{1,0:T(8,128)(2,1)S(1)} %get-tuple-element.41.q_ref, bf16[256,512]{1,0:T(8,128)(2,1)S(1)} %get-tuple-element.42.g_ref, bf16[2,256,128]{2,1,0:T(8,128)(2,1)S(1)} %shard_map.85.own_ref, ...), custom_call_target="tpu_custom_call" | custom-call | flops 402653184 | bytes 1048576 | tf_op jit(solution)/shard_map/pallas_call | solution.py:306
  51.1 0.1 shard_map.92.mine_ref
  51.2 2.0 %collective-permute-done.6.r1_ref = bf16[2,2,256,128]{3,2,1,0:T(8,128)(2,1)S(1)} collective-permute-done((bf16[2,2,256,128]{3,2,1,0:T(8,128)(2,1)S(1)}, bf16[2,2,256,128]{3,2,1,0:T(8,128)(2,1)S(1)}, u32[]{:S(2)}, u32[]{:S(2)}) %collective-permute-start.6) | collective-permute-done | bytes 262176 | tf_op jit(solution)/shard_map/ppermute | solution.py:252
  53.3 3.1 %collective-permute-done.7.r3_ref = bf16[2,2,256,128]{3,2,1,0:T(8,128)(2,1)S(1)} collective-permute-done((bf16[2,2,256,128]{3,2,1,0:T(8,128)(2,1)S(1)}, bf16[2,2,256,128]{3,2,1,0:T(8,128)(2,1)S(1)}, u32[]{:S(2)}, u32[]{:S(2)}) %collective-permute-start.7) | collective-permute-done | bytes 262176 | tf_op jit(solution)/shard_map/ppermute | solution.py:252
  56.3 0.1 shard_map.95
  56.4 1.9 %collective-permute-start.8 = (bf16[2,256,128]{2,1,0:T(8,128)(2,1)S(1)}, bf16[2,256,128]{2,1,0:T(8,128)(2,1)S(1)}, u32[]{:S(2)}, u32[]{:S(2)}) collective-permute-start(bf16[2,256,128]{2,1,0:T(8,128)(2,1)S(1)} %get-tuple-element.73), channel_id=1, source_target_pairs={{64,0},{72,8},{80,16},{88,24},{96,32},{104,40},{112,48},{120,56},{... | collective-permute-start | bytes 393224 | tf_op jit(solution)/shard_map/ppermute | solution.py:248
  58.3 2.1 %collective-permute-start.9 = (bf16[2,256,128]{2,1,0:T(8,128)(2,1)S(1)}, bf16[2,256,128]{2,1,0:T(8,128)(2,1)S(1)}, u32[]{:S(2)}, u32[]{:S(2)}) collective-permute-start(bf16[2,256,128]{2,1,0:T(8,128)(2,1)S(1)} %get-tuple-element.69._), channel_id=1, source_target_pairs={{32,0},{40,8},{48,16},{56,24},{64,32},{72,40},{80,48},{88,56},{96,... | collective-permute-start | bytes 393224 | tf_op jit(solution)/shard_map/ppermute | solution.py:248
  60.5 5.6 %shard_map.96 = (bf16[256,512]{1,0:T(8,128)(2,1)}, f32[256,512]{1,0:T(8,128)}) custom-call(s32[1,256]{1,0:T(1,128)S(1)} %get-tuple-element.40._.starts_ref, bf16[256,512]{1,0:T(8,128)(2,1)S(1)} %get-tuple-element.41.q_ref, bf16[256,512]{1,0:T(8,128)(2,1)S(1)} %get-tuple-element.42.g_ref, bf16[2,256,128]{2,1,0:T(8,128)(2,1)S(1)} %shard_map.85.own_ref, ...), custom_call_target="tpu_custom_call" | custom-call | flops 1207959552 | bytes 1048576 | tf_op jit(solution)/shard_map/pallas_call | solution.py:314
  66.0 1.2 %collective-permute-done.8.two_ref = bf16[2,256,128]{2,1,0:T(8,128)(2,1)S(1)} collective-permute-done((bf16[2,256,128]{2,1,0:T(8,128)(2,1)S(1)}, bf16[2,256,128]{2,1,0:T(8,128)(2,1)S(1)}, u32[]{:S(2)}, u32[]{:S(2)}) %collective-permute-start.8) | collective-permute-done | bytes 131104 | tf_op jit(solution)/shard_map/ppermute | solution.py:248
  67.2 1.4 %collective-permute-done.9.one_ref = bf16[2,256,128]{2,1,0:T(8,128)(2,1)S(1)} collective-permute-done((bf16[2,256,128]{2,1,0:T(8,128)(2,1)S(1)}, bf16[2,256,128]{2,1,0:T(8,128)(2,1)S(1)}, u32[]{:S(2)}, u32[]{:S(2)}) %collective-permute-start.9) | collective-permute-done | bytes 131104 | tf_op jit(solution)/shard_map/ppermute | solution.py:248
  68.6 0.7 %shard_map.98 = (f32[256,128]{1,0:T(8,128)}, f32[256,128]{1,0:T(8,128)}) custom-call(f32[2,256,128]{2,1,0:T(8,128)S(1)} %shard_map.97.own_ref, bf16[2,256,128]{2,1,0:T(8,128)(2,1)S(1)} %collective-permute-done.9.one_ref), custom_call_target="tpu_custom_call" | custom-call | bytes 1048576 | tf_op jit(solution)/shard_map/pallas_call | solution.py:324
  (13 shorter events, 0.2 us)
Async XLA Ops:
  0.6 0.8 %copy-start.2 = (bf16[256,128]{1,0:T(8,128)(2,1)S(1)}, bf16[256,128]{1,0:T(8,128)(2,1)}, u32[]{:S(2)}) copy-start(bf16[256,128]{1,0:T(8,128)(2,1)} %k_ref.1) | copy-start | bytes 196612
  1.5 0.8 %copy-start.3 = (bf16[256,128]{1,0:T(8,128)(2,1)S(1)}, bf16[256,128]{1,0:T(8,128)(2,1)}, u32[]{:S(2)}) copy-start(bf16[256,128]{1,0:T(8,128)(2,1)} %v_ref.1) | copy-start | bytes 196612
  2.3 13.4 %collective-permute-start.1 = (bf16[2,256,128]{2,1,0:T(8,128)(2,1)S(1)}, bf16[2,256,128]{2,1,0:T(8,128)(2,1)S(1)}, u32[]{:S(2)}, u32[]{:S(2)}) collective-permute-start(bf16[2,256,128]{2,1,0:T(8,128)(2,1)S(1)} %shard_map.85.own_ref), channel_id=1, source_target_pairs={{0,64},{8,72},{16,80},{24,88},{32,96},{40,104},{48,112},{56,120},{... | collective-permute-start | bytes 393224 | tf_op jit(solution)/shard_map/ppermute | solution.py:248
  8.7 8.9 %collective-permute-start = (bf16[2,256,128]{2,1,0:T(8,128)(2,1)S(1)}, bf16[2,256,128]{2,1,0:T(8,128)(2,1)S(1)}, u32[]{:S(2)}, u32[]{:S(2)}) collective-permute-start(bf16[2,256,128]{2,1,0:T(8,128)(2,1)S(1)} %shard_map.85.own_ref), channel_id=1, source_target_pairs={{0,32},{8,40},{16,48},{24,56},{32,64},{40,72},{48,80},{56,88},{64,... | collective-permute-start | bytes 393224 | tf_op jit(solution)/shard_map/ppermute | solution.py:248
  12.6 1.0 %copy-start = (bf16[256,512]{1,0:T(8,128)(2,1)S(1)}, bf16[256,512]{1,0:T(8,128)(2,1)}, u32[]{:S(2)}) copy-start(bf16[256,512]{1,0:T(8,128)(2,1)} %q_ref.1) | copy-start | bytes 786436
  13.5 0.9 %copy-start.1 = (bf16[256,512]{1,0:T(8,128)(2,1)S(1)}, bf16[256,512]{1,0:T(8,128)(2,1)}, u32[]{:S(2)}) copy-start(bf16[256,512]{1,0:T(8,128)(2,1)} %g_ref.1) | copy-start | bytes 786436
  14.5 0.7 copy-start.4
  17.7 13.3 %collective-permute-start.3 = (bf16[2,2,256,128]{3,2,1,0:T(8,128)(2,1)S(1)}, bf16[2,2,256,128]{3,2,1,0:T(8,128)(2,1)S(1)}, u32[]{:S(2)}, u32[]{:S(2)}) collective-permute-start(bf16[2,2,256,128]{3,2,1,0:T(8,128)(2,1)S(1)} %get-tuple-element.44), channel_id=1, source_target_pairs={{0,16},{8,24},{16,0},{24,8},{32,48},{40,56},{48,32},{56,40},{64,80... | collective-permute-start | bytes 786440 | tf_op jit(solution)/shard_map/ppermute | solution.py:252
  22.6 11.8 %collective-permute-start.2 = (bf16[2,2,256,128]{3,2,1,0:T(8,128)(2,1)S(1)}, bf16[2,2,256,128]{3,2,1,0:T(8,128)(2,1)S(1)}, u32[]{:S(2)}, u32[]{:S(2)}) collective-permute-start(bf16[2,2,256,128]{3,2,1,0:T(8,128)(2,1)S(1)} %get-tuple-element.43), channel_id=1, source_target_pairs={{0,8},{8,16},{16,24},{24,0},{32,40},{40,48},{48,56},{56,32},{64,72... | collective-permute-start | bytes 786440 | tf_op jit(solution)/shard_map/ppermute | solution.py:252
  25.1 10.3 %collective-permute-start.4 = (bf16[2,2,256,128]{3,2,1,0:T(8,128)(2,1)S(1)}, bf16[2,2,256,128]{3,2,1,0:T(8,128)(2,1)S(1)}, u32[]{:S(2)}, u32[]{:S(2)}) collective-permute-start(bf16[2,2,256,128]{3,2,1,0:T(8,128)(2,1)S(1)} %get-tuple-element.45), channel_id=1, source_target_pairs={{0,24},{8,0},{16,8},{24,16},{32,56},{40,32},{48,40},{56,48},{64,88... | collective-permute-start | bytes 786440 | tf_op jit(solution)/shard_map/ppermute | solution.py:252
  37.2 13.9 %collective-permute-start.5 = (bf16[2,2,256,128]{3,2,1,0:T(8,128)(2,1)S(1)}, bf16[2,2,256,128]{3,2,1,0:T(8,128)(2,1)S(1)}, u32[]{:S(2)}, u32[]{:S(2)}) collective-permute-start(bf16[2,2,256,128]{3,2,1,0:T(8,128)(2,1)S(1)} %get-tuple-element.60), channel_id=1, source_target_pairs={{0,16},{8,24},{16,0},{24,8},{32,48},{40,56},{48,32},{56,40},{64,80... | collective-permute-start | bytes 786440 | tf_op jit(solution)/shard_map/ppermute | solution.py:252
  43.3 9.8 %collective-permute-start.6 = (bf16[2,2,256,128]{3,2,1,0:T(8,128)(2,1)S(1)}, bf16[2,2,256,128]{3,2,1,0:T(8,128)(2,1)S(1)}, u32[]{:S(2)}, u32[]{:S(2)}) collective-permute-start(bf16[2,2,256,128]{3,2,1,0:T(8,128)(2,1)S(1)} %get-tuple-element.67), channel_id=1, source_target_pairs={{0,24},{8,0},{16,8},{24,16},{32,56},{40,32},{48,40},{56,48},{64,88... | collective-permute-start | bytes 786440 | tf_op jit(solution)/shard_map/ppermute | solution.py:252
  46.5 9.9 %collective-permute-start.7 = (bf16[2,2,256,128]{3,2,1,0:T(8,128)(2,1)S(1)}, bf16[2,2,256,128]{3,2,1,0:T(8,128)(2,1)S(1)}, u32[]{:S(2)}, u32[]{:S(2)}) collective-permute-start(bf16[2,2,256,128]{3,2,1,0:T(8,128)(2,1)S(1)} %get-tuple-element.68), channel_id=1, source_target_pairs={{0,8},{8,16},{16,24},{24,0},{32,40},{40,48},{48,56},{56,32},{64,72... | collective-permute-start | bytes 786440 | tf_op jit(solution)/shard_map/ppermute | solution.py:252
  56.4 10.8 %collective-permute-start.8 = (bf16[2,256,128]{2,1,0:T(8,128)(2,1)S(1)}, bf16[2,256,128]{2,1,0:T(8,128)(2,1)S(1)}, u32[]{:S(2)}, u32[]{:S(2)}) collective-permute-start(bf16[2,256,128]{2,1,0:T(8,128)(2,1)S(1)} %get-tuple-element.73), channel_id=1, source_target_pairs={{64,0},{72,8},{80,16},{88,24},{96,32},{104,40},{112,48},{120,56},{... | collective-permute-start | bytes 393224 | tf_op jit(solution)/shard_map/ppermute | solution.py:248
  58.3 10.3 %collective-permute-start.9 = (bf16[2,256,128]{2,1,0:T(8,128)(2,1)S(1)}, bf16[2,256,128]{2,1,0:T(8,128)(2,1)S(1)}, u32[]{:S(2)}, u32[]{:S(2)}) collective-permute-start(bf16[2,256,128]{2,1,0:T(8,128)(2,1)S(1)} %get-tuple-element.69._), channel_id=1, source_target_pairs={{32,0},{40,8},{48,16},{56,24},{64,32},{72,40},{80,48},{88,56},{96,... | collective-permute-start | bytes 393224 | tf_op jit(solution)/shard_map/ppermute | solution.py:248

commit v10 on v9

--- a/solution.py
+++ b/solution.py
@@ -57,9 +57,12 @@
         r_ref[index, h : h + 1] = jnp.sum(p * dp, axis=0, keepdims=True)
 
 
-def pair_kernel(k_ref, v_ref, out_ref):
-    out_ref[0] = k_ref[...]
-    out_ref[1] = v_ref[...]
+def pair_kernel(k_ref, v_ref, out_ref, sem):
+    copies = [pltpu.make_async_copy(r, out_ref.at[i], sem.at[i]) for i, r in enumerate((k_ref, v_ref))]
+    for copy in copies:
+        copy.start()
+    for copy in copies:
+        copy.wait()
 
 
 def hold_kernel(lengths_ref, q_ref, g_ref, q_out, g_out, starts_ref):
@@ -273,7 +276,9 @@
     pair = array((2, *block), BF16)
     tiles, sums = (array((2, H, T, T), F32),) * 2, (array((2, *stats), F32),) * 3
     staged = [pltpu.VMEM((2, H, T, T), BF16)] * 2
-    (own,) = call(pair_kernel, (array(block, BF16),), [VM] * 2, limit=4)(keys, values)
+    (own,) = call(pair_kernel, (pltpu.VMEM(block, BF16),), [ANY] * 2, [pltpu.SemaphoreType.DMA((2,))], limit=54)(
+        keys, values
+    )
     z1 = along_z(own, 1, peers)
     z2 = along_z(own, 2, peers)
     queries, grad_out, starts = call(

time: 69.8 us -> 69 us (0.989)
  the two profiles are of different devices: /device:TPU:104 before, /device:TPU:120 now
where the time goes in v10:
time: 69 us; the launch traced here: 68.5 us
  starting transfers between devices  36.7 us (53%)
  Pallas kernels  16.5 us (24%)
  waiting for transfers between devices  11.9 us (17%)
  local copies, waits for them, and re-layouts  2.55 us (4%)
  between operations  0.83 us (1%)
    ppermute x6, starting transfers between devices, along_x(): lax.ppermute(block, 'peer', [(i, i - i % ROW + (i + columns) % ROW) for i...  22.5 us
    ppermute x4, starting transfers between devices, along_z(): lax.ppermute(block, 'peer', [(i, i + far) for i in range(peers) if 0 <= i...  14.2 us
    ppermute x6, waiting for transfers between devices, along_x(): lax.ppermute(block, 'peer', [(i, i - i % ROW + (i + columns) % ROW) for i...  7.53 us
    pallas_call x1, Pallas kernels, body(): call(query_side_kernel, (array((T, H * D), BF16), array((T, H * D), F32))...  5.58 us
    ppermute x4, waiting for transfers between devices, along_z(): lax.ppermute(block, 'peer', [(i, i + far) for i in range(peers) if 0 <= i...  4.39 us
    unnamed x6, local copies, waits for them, and re-layouts  2.55 us
    pallas_call x1, Pallas kernels, body(): call(near_back_kernel, (array((3, *block), F32),), [VM] * 9, staged, bloc...  1.87 us
    pallas_call x1, Pallas kernels, body(): call(last_kernel, (pair,) + (array(stats, F32),) * 3 + (array((2, *stats)...  1.79 us
  transfers between devices with their start and end apart: 10, of which 6 were waited for; matrix products, arithmetic and copies ran while one was open for 0% of the time, Pallas kernels for 19%

profile of v10, /device:TPU:120, one launch (start us, length us, event | category | flops | bytes accessed | tf_op | source)
XLA Modules:
  0.0 68.5 jit_solution(14107665888836295259)
XLA Ops:
  0.6 0.9 %shard_map.85.own_ref = bf16[2,256,128]{2,1,0:T(8,128)(2,1)S(1)} custom-call(bf16[256,128]{1,0:T(8,128)(2,1)} %k_ref.1, bf16[256,128]{1,0:T(8,128)(2,1)} %v_ref.1), custom_call_target="tpu_custom_call" | custom-call | bytes 1048576 | tf_op jit(solution)/shard_map/pallas_call | solution.py:279
  1.5 6.4 %collective-permute-start.1 = (bf16[2,256,128]{2,1,0:T(8,128)(2,1)S(1)}, bf16[2,256,128]{2,1,0:T(8,128)(2,1)S(1)}, u32[]{:S(2)}, u32[]{:S(2)}) collective-permute-start(bf16[2,256,128]{2,1,0:T(8,128)(2,1)S(1)} %shard_map.85.own_ref), channel_id=1, source_target_pairs={{0,64},{8,72},{16,80},{24,88},{32,96},{40,104},{48,112},{56,120},{... | collective-permute-start | bytes 393224 | tf_op jit(solution)/shard_map/ppermute | solution.py:251
  7.9 3.8 %collective-permute-start = (bf16[2,256,128]{2,1,0:T(8,128)(2,1)S(1)}, bf16[2,256,128]{2,1,0:T(8,128)(2,1)S(1)}, u32[]{:S(2)}, u32[]{:S(2)}) collective-permute-start(bf16[2,256,128]{2,1,0:T(8,128)(2,1)S(1)} %shard_map.85.own_ref), channel_id=1, source_target_pairs={{0,32},{8,40},{16,48},{24,56},{32,64},{40,72},{48,80},{56,88},{64,... | collective-permute-start | bytes 393224 | tf_op jit(solution)/shard_map/ppermute | solution.py:251
  11.8 0.9 %copy-done = bf16[256,512]{1,0:T(8,128)(2,1)S(1)} copy-done((bf16[256,512]{1,0:T(8,128)(2,1)S(1)}, bf16[256,512]{1,0:T(8,128)(2,1)}, u32[]{:S(2)}) %copy-start) | copy-done | bytes 262168
  12.7 0.9 %copy-done.1 = bf16[256,512]{1,0:T(8,128)(2,1)S(1)} copy-done((bf16[256,512]{1,0:T(8,128)(2,1)S(1)}, bf16[256,512]{1,0:T(8,128)(2,1)}, u32[]{:S(2)}) %copy-start.1) | copy-done | bytes 262168
  13.7 0.7 copy-done.2
  14.3 0.6 shard_map.84
  14.9 1.9 %collective-permute-done.z1_ref = bf16[2,256,128]{2,1,0:T(8,128)(2,1)S(1)} collective-permute-done((bf16[2,256,128]{2,1,0:T(8,128)(2,1)S(1)}, bf16[2,256,128]{2,1,0:T(8,128)(2,1)S(1)}, u32[]{:S(2)}, u32[]{:S(2)}) %collective-permute-start) | collective-permute-done | bytes 131104 | tf_op jit(solution)/shard_map/ppermute | solution.py:251
  16.9 4.9 %collective-permute-start.3 = (bf16[2,2,256,128]{3,2,1,0:T(8,128)(2,1)S(1)}, bf16[2,2,256,128]{3,2,1,0:T(8,128)(2,1)S(1)}, u32[]{:S(2)}, u32[]{:S(2)}) collective-permute-start(bf16[2,2,256,128]{3,2,1,0:T(8,128)(2,1)S(1)} %get-tuple-element.44), channel_id=1, source_target_pairs={{0,16},{8,24},{16,0},{24,8},{32,48},{40,56},{48,32},{56,40},{64,80... | collective-permute-start | bytes 786440 | tf_op jit(solution)/shard_map/ppermute | solution.py:255
  21.8 2.5 %collective-permute-start.2 = (bf16[2,2,256,128]{3,2,1,0:T(8,128)(2,1)S(1)}, bf16[2,2,256,128]{3,2,1,0:T(8,128)(2,1)S(1)}, u32[]{:S(2)}, u32[]{:S(2)}) collective-permute-start(bf16[2,2,256,128]{3,2,1,0:T(8,128)(2,1)S(1)} %get-tuple-element.43), channel_id=1, source_target_pairs={{0,8},{8,16},{16,24},{24,0},{32,40},{40,48},{48,56},{56,32},{64,72... | collective-permute-start | bytes 786440 | tf_op jit(solution)/shard_map/ppermute | solution.py:255
  24.3 4.6 %collective-permute-start.4 = (bf16[2,2,256,128]{3,2,1,0:T(8,128)(2,1)S(1)}, bf16[2,2,256,128]{3,2,1,0:T(8,128)(2,1)S(1)}, u32[]{:S(2)}, u32[]{:S(2)}) collective-permute-start(bf16[2,2,256,128]{3,2,1,0:T(8,128)(2,1)S(1)} %get-tuple-element.45), channel_id=1, source_target_pairs={{0,24},{8,0},{16,8},{24,16},{32,56},{40,32},{48,40},{56,48},{64,88... | collective-permute-start | bytes 786440 | tf_op jit(solution)/shard_map/ppermute | solution.py:255
  28.9 1.3 %shard_map.87 = (f32[3,4,256]{2,1,0:T(4,128)S(1)}, f32[3,4,256]{2,1,0:T(4,128)S(1)}, f32[3,4,256]{2,1,0:T(4,128)S(1)}) custom-call(s32[1,256]{1,0:T(1,128)S(1)} %get-tuple-element.40._.starts_ref, bf16[256,512]{1,0:T(8,128)(2,1)S(1)} %get-tuple-element.41.q_ref, bf16[256,512]{1,0:T(8,128)(2,1)S(1)} %get-tuple-element.42.g_ref, ...), custom_call_target="tpu_custom_call" | custom-call | flops 402653184 | bytes 1048576 | tf_op jit(solution)/shard_map/pallas_call | solution.py:294
  30.1 1.0 %shard_map.89 = (f32[2,4,256,256]{3,2,1,0:T(8,128)S(1)}, f32[2,4,256,256]{3,2,1,0:T(8,128)S(1)}, f32[2,4,256]{2,1,0:T(4,128)S(1)}, f32[2,4,256]{2,1,0:T(4,128)S(1)}, f32[2,4,256]{2,1,0:T(4,128)S(1)}) custom-call(s32[1,256]{1,0:T(1,128)S(1)} %get-tuple-element.40._.starts_ref, bf16[256,512]{1,0:T(8,128)(2,1)S(1)} %get-tuple-element.41.q_ref, ...), custom_call_target="tpu_custom_call" | custom-call | flops 268435456 | bytes 1048576 | tf_op jit(solution)/shard_map/pallas_call | solution.py:296
  31.1 2.5 %collective-permute-done.2.far_ref.f1_ref = bf16[2,2,256,128]{3,2,1,0:T(8,128)(2,1)S(1)} collective-permute-done((bf16[2,2,256,128]{3,2,1,0:T(8,128)(2,1)S(1)}, bf16[2,2,256,128]{3,2,1,0:T(8,128)(2,1)S(1)}, u32[]{:S(2)}, u32[]{:S(2)}) %collective-permute-start.2) | collective-permute-done | bytes 262176 | tf_op jit(solution)/shard_map/ppermute | solution.py:255
  33.6 1.0 %shard_map.88 = (f32[2,4,256,256]{3,2,1,0:T(8,128)S(1)}, f32[2,4,256,256]{3,2,1,0:T(8,128)S(1)}, f32[2,4,256]{2,1,0:T(4,128)S(1)}, f32[2,4,256]{2,1,0:T(4,128)S(1)}, f32[2,4,256]{2,1,0:T(4,128)S(1)}) custom-call(s32[1,256]{1,0:T(1,128)S(1)} %get-tuple-element.40._.starts_ref, bf16[256,512]{1,0:T(8,128)(2,1)S(1)} %get-tuple-element.41.q_ref, ...), custom_call_target="tpu_custom_call" | custom-call | flops 268435456 | bytes 1048576 | tf_op jit(solution)/shard_map/pallas_call | solution.py:297
  34.6 1.8 %shard_map.90 = (bf16[2,2,256,128]{3,2,1,0:T(8,128)(2,1)S(1)}, f32[4,256]{1,0:T(4,128)S(1)}, f32[4,256]{1,0:T(4,128)S(1)}, f32[4,256]{1,0:T(4,128)S(1)}, f32[2,4...) custom-call(s32[1,256]{1,0:T(1,128)S(1)} %get-tuple-element.40._.sta, ...), custom_call_target="tpu_custom_call" | custom-call | flops 536870912 | bytes 1048576 | tf_op jit(solution)/shard_map/pallas_call | solution.py:298
  36.4 4.6 %collective-permute-start.5 = (bf16[2,2,256,128]{3,2,1,0:T(8,128)(2,1)S(1)}, bf16[2,2,256,128]{3,2,1,0:T(8,128)(2,1)S(1)}, u32[]{:S(2)}, u32[]{:S(2)}) collective-permute-start(bf16[2,2,256,128]{3,2,1,0:T(8,128)(2,1)S(1)} %get-tuple-element.60), channel_id=1, source_target_pairs={{0,16},{8,24},{16,0},{24,8},{32,48},{40,56},{48,32},{56,40},{64,80... | collective-permute-start | bytes 786440 | tf_op jit(solution)/shard_map/ppermute | solution.py:255
  41.0 1.5 %shard_map.93 = (bf16[2,2,256,128]{3,2,1,0:T(8,128)(2,1)S(1)}, bf16[2,2,256,128]{3,2,1,0:T(8,128)(2,1)S(1)}) custom-call(bf16[256,512]{1,0:T(8,128)(2,1)S(1)} %get-tuple-element.41.q_ref, bf16[256,512]{1,0:T(8,128)(2,1)S(1)} %get-tuple-element.42.g_ref, f32[4,256]{1,0:T(4,128)S(1)} %get-tuple-element.59.rd_ref, ...), custom_call_target="tpu_custom_call" | custom-call | flops 536870912 | bytes 1048576 | tf_op jit(solution)/shard_map/pallas_call | solution.py:307
  42.5 3.1 %collective-permute-start.6 = (bf16[2,2,256,128]{3,2,1,0:T(8,128)(2,1)S(1)}, bf16[2,2,256,128]{3,2,1,0:T(8,128)(2,1)S(1)}, u32[]{:S(2)}, u32[]{:S(2)}) collective-permute-start(bf16[2,2,256,128]{3,2,1,0:T(8,128)(2,1)S(1)} %get-tuple-element.67), channel_id=1, source_target_pairs={{0,24},{8,0},{16,8},{24,16},{32,56},{40,32},{48,40},{56,48},{64,88... | collective-permute-start | bytes 786440 | tf_op jit(solution)/shard_map/ppermute | solution.py:255
  45.7 2.7 %collective-permute-start.7 = (bf16[2,2,256,128]{3,2,1,0:T(8,128)(2,1)S(1)}, bf16[2,2,256,128]{3,2,1,0:T(8,128)(2,1)S(1)}, u32[]{:S(2)}, u32[]{:S(2)}) collective-permute-start(bf16[2,2,256,128]{3,2,1,0:T(8,128)(2,1)S(1)} %get-tuple-element.68), channel_id=1, source_target_pairs={{0,8},{8,16},{16,24},{24,0},{32,40},{40,48},{48,56},{56,32},{64,72... | collective-permute-start | bytes 786440 | tf_op jit(solution)/shard_map/ppermute | solution.py:255
  48.4 1.9 %shard_map.91.mine_ref = f32[3,2,256,128]{3,2,1,0:T(8,128)S(1)} custom-call(s32[1,256]{1,0:T(1,128)S(1)} %get-tuple-element.40._.starts_ref, bf16[256,512]{1,0:T(8,128)(2,1)S(1)} %get-tuple-element.41.q_ref, bf16[256,512]{1,0:T(8,128)(2,1)S(1)} %get-tuple-element.42.g_ref, bf16[2,256,128]{2,1,0:T(8,128)(2,1)S(1)} %shard_map.85.own_ref, ...), custom_call_target="tpu_custom_call" | custom-call | flops 402653184 | bytes 1048576 | tf_op jit(solution)/shard_map/pallas_call | solution.py:311
  50.3 0.1 shard_map.92.mine_ref
  50.4 2.0 %collective-permute-done.6.r1_ref = bf16[2,2,256,128]{3,2,1,0:T(8,128)(2,1)S(1)} collective-permute-done((bf16[2,2,256,128]{3,2,1,0:T(8,128)(2,1)S(1)}, bf16[2,2,256,128]{3,2,1,0:T(8,128)(2,1)S(1)}, u32[]{:S(2)}, u32[]{:S(2)}) %collective-permute-start.6) | collective-permute-done | bytes 262176 | tf_op jit(solution)/shard_map/ppermute | solution.py:255
  52.4 0.1 shard_map.94.mine_ref
  52.5 3.1 %collective-permute-done.7.r3_ref = bf16[2,2,256,128]{3,2,1,0:T(8,128)(2,1)S(1)} collective-permute-done((bf16[2,2,256,128]{3,2,1,0:T(8,128)(2,1)S(1)}, bf16[2,2,256,128]{3,2,1,0:T(8,128)(2,1)S(1)}, u32[]{:S(2)}, u32[]{:S(2)}) %collective-permute-start.7) | collective-permute-done | bytes 262176 | tf_op jit(solution)/shard_map/ppermute | solution.py:255
  55.5 0.1 shard_map.95
  55.6 1.9 %collective-permute-start.8 = (bf16[2,256,128]{2,1,0:T(8,128)(2,1)S(1)}, bf16[2,256,128]{2,1,0:T(8,128)(2,1)S(1)}, u32[]{:S(2)}, u32[]{:S(2)}) collective-permute-start(bf16[2,256,128]{2,1,0:T(8,128)(2,1)S(1)} %get-tuple-element.73), channel_id=1, source_target_pairs={{64,0},{72,8},{80,16},{88,24},{96,32},{104,40},{112,48},{120,56},{... | collective-permute-start | bytes 393224 | tf_op jit(solution)/shard_map/ppermute | solution.py:251
  57.6 2.1 %collective-permute-start.9 = (bf16[2,256,128]{2,1,0:T(8,128)(2,1)S(1)}, bf16[2,256,128]{2,1,0:T(8,128)(2,1)S(1)}, u32[]{:S(2)}, u32[]{:S(2)}) collective-permute-start(bf16[2,256,128]{2,1,0:T(8,128)(2,1)S(1)} %get-tuple-element.69._), channel_id=1, source_target_pairs={{32,0},{40,8},{48,16},{56,24},{64,32},{72,40},{80,48},{88,56},{96,... | collective-permute-start | bytes 393224 | tf_op jit(solution)/shard_map/ppermute | solution.py:251
  59.7 5.6 %shard_map.96 = (bf16[256,512]{1,0:T(8,128)(2,1)}, f32[256,512]{1,0:T(8,128)}) custom-call(s32[1,256]{1,0:T(1,128)S(1)} %get-tuple-element.40._.starts_ref, bf16[256,512]{1,0:T(8,128)(2,1)S(1)} %get-tuple-element.41.q_ref, bf16[256,512]{1,0:T(8,128)(2,1)S(1)} %get-tuple-element.42.g_ref, bf16[2,256,128]{2,1,0:T(8,128)(2,1)S(1)} %shard_map.85.own_ref, ...), custom_call_target="tpu_custom_call" | custom-call | flops 1207959552 | bytes 1048576 | tf_op jit(solution)/shard_map/pallas_call | solution.py:319
  65.2 1.2 %collective-permute-done.8.two_ref = bf16[2,256,128]{2,1,0:T(8,128)(2,1)S(1)} collective-permute-done((bf16[2,256,128]{2,1,0:T(8,128)(2,1)S(1)}, bf16[2,256,128]{2,1,0:T(8,128)(2,1)S(1)}, u32[]{:S(2)}, u32[]{:S(2)}) %collective-permute-start.8) | collective-permute-done | bytes 131104 | tf_op jit(solution)/shard_map/ppermute | solution.py:251
  66.4 1.4 %collective-permute-done.9.one_ref = bf16[2,256,128]{2,1,0:T(8,128)(2,1)S(1)} collective-permute-done((bf16[2,256,128]{2,1,0:T(8,128)(2,1)S(1)}, bf16[2,256,128]{2,1,0:T(8,128)(2,1)S(1)}, u32[]{:S(2)}, u32[]{:S(2)}) %collective-permute-start.9) | collective-permute-done | bytes 131104 | tf_op jit(solution)/shard_map/ppermute | solution.py:251
  67.8 0.7 %shard_map.98 = (f32[256,128]{1,0:T(8,128)}, f32[256,128]{1,0:T(8,128)}) custom-call(f32[2,256,128]{2,1,0:T(8,128)S(1)} %shard_map.97.own_ref, bf16[2,256,128]{2,1,0:T(8,128)(2,1)S(1)} %collective-permute-done.9.one_ref), custom_call_target="tpu_custom_call" | custom-call | bytes 1048576 | tf_op jit(solution)/shard_map/pallas_call | solution.py:329
  (9 shorter events, 0.1 us)
Async XLA Ops:
  1.5 13.4 %collective-permute-start.1 = (bf16[2,256,128]{2,1,0:T(8,128)(2,1)S(1)}, bf16[2,256,128]{2,1,0:T(8,128)(2,1)S(1)}, u32[]{:S(2)}, u32[]{:S(2)}) collective-permute-start(bf16[2,256,128]{2,1,0:T(8,128)(2,1)S(1)} %shard_map.85.own_ref), channel_id=1, source_target_pairs={{0,64},{8,72},{16,80},{24,88},{32,96},{40,104},{48,112},{56,120},{... | collective-permute-start | bytes 393224 | tf_op jit(solution)/shard_map/ppermute | solution.py:251
  7.9 8.9 %collective-permute-start = (bf16[2,256,128]{2,1,0:T(8,128)(2,1)S(1)}, bf16[2,256,128]{2,1,0:T(8,128)(2,1)S(1)}, u32[]{:S(2)}, u32[]{:S(2)}) collective-permute-start(bf16[2,256,128]{2,1,0:T(8,128)(2,1)S(1)} %shard_map.85.own_ref), channel_id=1, source_target_pairs={{0,32},{8,40},{16,48},{24,56},{32,64},{40,72},{48,80},{56,88},{64,... | collective-permute-start | bytes 393224 | tf_op jit(solution)/shard_map/ppermute | solution.py:251
  11.8 1.0 %copy-start = (bf16[256,512]{1,0:T(8,128)(2,1)S(1)}, bf16[256,512]{1,0:T(8,128)(2,1)}, u32[]{:S(2)}) copy-start(bf16[256,512]{1,0:T(8,128)(2,1)} %q_ref.1) | copy-start | bytes 786436
  12.7 0.9 %copy-start.1 = (bf16[256,512]{1,0:T(8,128)(2,1)S(1)}, bf16[256,512]{1,0:T(8,128)(2,1)}, u32[]{:S(2)}) copy-start(bf16[256,512]{1,0:T(8,128)(2,1)} %g_ref.1) | copy-start | bytes 786436
  13.7 0.7 copy-start.2
  16.9 13.3 %collective-permute-start.3 = (bf16[2,2,256,128]{3,2,1,0:T(8,128)(2,1)S(1)}, bf16[2,2,256,128]{3,2,1,0:T(8,128)(2,1)S(1)}, u32[]{:S(2)}, u32[]{:S(2)}) collective-permute-start(bf16[2,2,256,128]{3,2,1,0:T(8,128)(2,1)S(1)} %get-tuple-element.44), channel_id=1, source_target_pairs={{0,16},{8,24},{16,0},{24,8},{32,48},{40,56},{48,32},{56,40},{64,80... | collective-permute-start | bytes 786440 | tf_op jit(solution)/shard_map/ppermute | solution.py:255
  21.8 11.8 %collective-permute-start.2 = (bf16[2,2,256,128]{3,2,1,0:T(8,128)(2,1)S(1)}, bf16[2,2,256,128]{3,2,1,0:T(8,128)(2,1)S(1)}, u32[]{:S(2)}, u32[]{:S(2)}) collective-permute-start(bf16[2,2,256,128]{3,2,1,0:T(8,128)(2,1)S(1)} %get-tuple-element.43), channel_id=1, source_target_pairs={{0,8},{8,16},{16,24},{24,0},{32,40},{40,48},{48,56},{56,32},{64,72... | collective-permute-start | bytes 786440 | tf_op jit(solution)/shard_map/ppermute | solution.py:255
  24.3 10.3 %collective-permute-start.4 = (bf16[2,2,256,128]{3,2,1,0:T(8,128)(2,1)S(1)}, bf16[2,2,256,128]{3,2,1,0:T(8,128)(2,1)S(1)}, u32[]{:S(2)}, u32[]{:S(2)}) collective-permute-start(bf16[2,2,256,128]{3,2,1,0:T(8,128)(2,1)S(1)} %get-tuple-element.45), channel_id=1, source_target_pairs={{0,24},{8,0},{16,8},{24,16},{32,56},{40,32},{48,40},{56,48},{64,88... | collective-permute-start | bytes 786440 | tf_op jit(solution)/shard_map/ppermute | solution.py:255
  36.4 13.9 %collective-permute-start.5 = (bf16[2,2,256,128]{3,2,1,0:T(8,128)(2,1)S(1)}, bf16[2,2,256,128]{3,2,1,0:T(8,128)(2,1)S(1)}, u32[]{:S(2)}, u32[]{:S(2)}) collective-permute-start(bf16[2,2,256,128]{3,2,1,0:T(8,128)(2,1)S(1)} %get-tuple-element.60), channel_id=1, source_target_pairs={{0,16},{8,24},{16,0},{24,8},{32,48},{40,56},{48,32},{56,40},{64,80... | collective-permute-start | bytes 786440 | tf_op jit(solution)/shard_map/ppermute | solution.py:255
  42.5 9.8 %collective-permute-start.6 = (bf16[2,2,256,128]{3,2,1,0:T(8,128)(2,1)S(1)}, bf16[2,2,256,128]{3,2,1,0:T(8,128)(2,1)S(1)}, u32[]{:S(2)}, u32[]{:S(2)}) collective-permute-start(bf16[2,2,256,128]{3,2,1,0:T(8,128)(2,1)S(1)} %get-tuple-element.67), channel_id=1, source_target_pairs={{0,24},{8,0},{16,8},{24,16},{32,56},{40,32},{48,40},{56,48},{64,88... | collective-permute-start | bytes 786440 | tf_op jit(solution)/shard_map/ppermute | solution.py:255
  45.7 9.9 %collective-permute-start.7 = (bf16[2,2,256,128]{3,2,1,0:T(8,128)(2,1)S(1)}, bf16[2,2,256,128]{3,2,1,0:T(8,128)(2,1)S(1)}, u32[]{:S(2)}, u32[]{:S(2)}) collective-permute-start(bf16[2,2,256,128]{3,2,1,0:T(8,128)(2,1)S(1)} %get-tuple-element.68), channel_id=1, source_target_pairs={{0,8},{8,16},{16,24},{24,0},{32,40},{40,48},{48,56},{56,32},{64,72... | collective-permute-start | bytes 786440 | tf_op jit(solution)/shard_map/ppermute | solution.py:255
  55.6 10.8 %collective-permute-start.8 = (bf16[2,256,128]{2,1,0:T(8,128)(2,1)S(1)}, bf16[2,256,128]{2,1,0:T(8,128)(2,1)S(1)}, u32[]{:S(2)}, u32[]{:S(2)}) collective-permute-start(bf16[2,256,128]{2,1,0:T(8,128)(2,1)S(1)} %get-tuple-element.73), channel_id=1, source_target_pairs={{64,0},{72,8},{80,16},{88,24},{96,32},{104,40},{112,48},{120,56},{... | collective-permute-start | bytes 393224 | tf_op jit(solution)/shard_map/ppermute | solution.py:251
  57.6 10.3 %collective-permute-start.9 = (bf16[2,256,128]{2,1,0:T(8,128)(2,1)S(1)}, bf16[2,256,128]{2,1,0:T(8,128)(2,1)S(1)}, u32[]{:S(2)}, u32[]{:S(2)}) collective-permute-start(bf16[2,256,128]{2,1,0:T(8,128)(2,1)S(1)} %get-tuple-element.69._), channel_id=1, source_target_pairs={{32,0},{40,8},{48,16},{56,24},{64,32},{72,40},{80,48},{88,56},{96,... | collective-permute-start | bytes 393224 | tf_op jit(solution)/shard_map/ppermute | solution.py:251

commit v11 on v10

--- a/solution.py
+++ b/solution.py
@@ -174,44 +174,45 @@
         ds_ref[h] = (pn * (dp - rd_ref[h : h + 1])).astype(BF16)
 
 
-def near_back_kernel(starts_ref, q_ref, g_ref, own_ref, z1_ref, z2_ref, peak_ref, over_ref, rd_ref, near_ref, pb_ref, ds_ref):
+def query_side(key, value, pb_ref, ds_ref, o_ref, dq_ref, fresh):
+    kt, vt = key.T, value.T
+    for h in range(H):
+        o, dq = dot(vt, pb_ref[h], PLAIN), dot(kt, ds_ref[h], PLAIN)
+        o_ref[h] = o if fresh else o_ref[h] + o
+        dq_ref[h] = dq if fresh else dq_ref[h] + dq
+
+
+def near_back_kernel(
+    starts_ref, q_ref, g_ref, own_ref, z1_ref, z2_ref, peak_ref, over_ref, rd_ref,
+    near_ref, o_ref, dq_ref, pb_ref, ds_ref,
+):
     first = lax.axis_index("peer") * T
     for b, ref in enumerate((own_ref, z1_ref, z2_ref)):
         pb, ds = pb_ref.at[b % 2], ds_ref.at[b % 2]
         hidden = near_hidden(first, starts_ref[...], b)
         weights(q_ref, g_ref, ref[0], ref[1], hidden, peak_ref, over_ref, rd_ref, pb, ds)
         near_ref[b, 0], near_ref[b, 1] = key_side(q_ref, g_ref, pb, ds)
+        query_side(ref[0], ref[1], pb, ds, o_ref, dq_ref, b == 0)
 
 
 def query_side_kernel(
-    starts_ref, q_ref, g_ref, own_ref, z1_ref, z2_ref, f1_ref, f2_ref, f3_ref, peak_ref, over_ref, rd_ref, _,
+    starts_ref, q_ref, g_ref, f1_ref, f2_ref, f3_ref, peak_ref, over_ref, rd_ref, o_ref, dq_in_ref, _,
     out_ref, dq_ref, o_acc, dq_acc, pb_ref, ds_ref,
 ):
     peer = lax.axis_index("peer")
     x = lax.rem(peer, ROW)
     first = peer * T
-    starts = starts_ref[...]
-    near = (own_ref, z1_ref, z2_ref)
-    for b in range(9):
-        if b < 3:
-            key, value = near[b][0], near[b][1]
-            hidden = near_hidden(first, starts, b)
-        else:
-            d, kind = (b - 3) // 2 + 1, (b - 3) % 2
-            ref = (f1_ref, f2_ref, f3_ref)[d - 1]
-            key, value = ref[kind, 0], ref[kind, 1]
-            hidden = far_hidden(first, starts, behind(d, kind, x))
+    for b in range(6):
+        d, kind = b // 2 + 1, b % 2
+        ref = (f1_ref, f2_ref, f3_ref)[d - 1]
+        hidden = far_hidden(first, starts_ref[...], behind(d, kind, x))
         pb, ds = pb_ref.at[b % 2], ds_ref.at[b % 2]
-        weights(q_ref, g_ref, key, value, hidden, peak_ref, over_ref, rd_ref, pb, ds)
-        kt, vt = key.T, value.T
-        for h in range(H):
-            o, dq = dot(vt, pb[h], PLAIN), dot(kt, ds[h], PLAIN)
-            o_acc[h] = o if b == 0 else o_acc[h] + o
-            dq_acc[h] = dq if b == 0 else dq_acc[h] + dq
+        weights(q_ref, g_ref, ref[kind, 0], ref[kind, 1], hidden, peak_ref, over_ref, rd_ref, pb, ds)
+        query_side(ref[kind, 0], ref[kind, 1], pb, ds, o_acc, dq_acc, b == 0)
 
     for h in range(H):
-        out_ref[:, h * D : (h + 1) * D] = o_acc[h].T.astype(BF16)
-        dq_ref[:, h * D : (h + 1) * D] = dq_acc[h].T * SCALE
+        out_ref[:, h * D : (h + 1) * D] = (o_acc[h] + o_ref[h]).T.astype(BF16)
+        dq_ref[:, h * D : (h + 1) * D] = (dq_acc[h] + dq_in_ref[h]).T * SCALE
 
 
 def add_back(d, ref, own, one, two):
@@ -308,9 +309,14 @@
         queries, grad_out, rd, p1, dp1, w1, p3, dp3, w3
     )
     r1, r3 = along_x(b1, -1, peers), along_x(b3, -3, peers)
-    (mine,) = call(near_back_kernel, (array((3, *block), F32),), [VM] * 9, staged, blocks=3, limit=8)(
-        *wanted, own, z1, z2, peak, over, rd
-    )
+    mine, near_o, near_dq = call(
+        near_back_kernel,
+        (array((3, *block), F32),) + (array((H, D, T), F32),) * 2,
+        [VM] * 9,
+        staged,
+        blocks=3,
+        limit=8,
+    )(*wanted, own, z1, z2, peak, over, rd)
     (mine,) = call(gather_first_kernel, (array((3, *block), F32),), [VM] * 2, limit=4)(mine, r2)
     (mine,) = call(gather_one_kernel, (array((3, *block), F32),), [VM] * 2, limit=4)(mine, r1)
     mine, one, two = call(
@@ -319,11 +325,11 @@
     attended, query_grad = call(
         query_side_kernel,
         (array((T, H * D), BF16), array((T, H * D), F32)),
-        [VM] * 13,
+        [VM] * 12,
         [pltpu.VMEM((H, D, T), F32)] * 2 + staged,
         blocks=9,
         limit=16,
-    )(*wanted, own, z1, z2, f1, f2, f3, peak, over, rd, one)
+    )(*wanted, f1, f2, f3, peak, over, rd, near_o, near_dq, one)
     two, one = along_z(two, -2, peers), along_z(one, -1, peers)
     (mine,) = call(add_two_kernel, (array(block, F32),), [VM] * 2, limit=4)(mine, two)
     key_grad, value_grad = call(final_kernel, (array((T, D), F32),) * 2, [VM] * 2, limit=4)(mine, one)

time: 69 us -> 69.1 us (level)
  waiting for transfers between devices: 11.9 us -> 12.8 us
  Pallas kernels: 16.5 us -> 15.7 us
    pallas_call x1, Pallas kernels: 5.58 us -> 4.13 us  [body(): call(query_side_kernel, (array((T, H * D), BF16), array((T, H * D), F32))...]
    ppermute x4, waiting for transfers between devices: 4.39 us -> 5.85 us  [along_z(): lax.ppermute(block, 'peer', [(i, i + far) for i in range(peers) if 0 <= i...]
  transfers between devices with their start and end apart: 10 -> 10, of which waited for: 6 -> 6; matrix products, arithmetic and copies ran while one was open for 0% -> 0% of each run, Pallas kernels for 19% -> 18%
where the time goes in v11:
time: 69.1 us; the launch traced here: 68.6 us
  starting transfers between devices  36.7 us (53%)
  Pallas kernels  15.7 us (23%)
  waiting for transfers between devices  12.8 us (19%)
  local copies, waits for them, and re-layouts  2.55 us (4%)
  between operations  0.83 us (1%)
    ppermute x6, starting transfers between devices, along_x(): lax.ppermute(block, 'peer', [(i, i - i % ROW + (i + columns) % ROW) for i...  22.5 us
    ppermute x4, starting transfers between devices, along_z(): lax.ppermute(block, 'peer', [(i, i + far) for i in range(peers) if 0 <= i...  14.2 us
    ppermute x6, waiting for transfers between devices, along_x(): lax.ppermute(block, 'peer', [(i, i - i % ROW + (i + columns) % ROW) for i...  6.97 us
    ppermute x4, waiting for transfers between devices, along_z(): lax.ppermute(block, 'peer', [(i, i + far) for i in range(peers) if 0 <= i...  5.85 us
    pallas_call x1, Pallas kernels, body(): call(query_side_kernel, (array((T, H * D), BF16), array((T, H * D), F32))...  4.13 us
    unnamed x6, local copies, waits for them, and re-layouts  2.55 us
    pallas_call x1, Pallas kernels, body(): call(near_back_kernel, (array((3, *block), F32),) + (array((H, D, T), F32...  2.32 us
    pallas_call x1, Pallas kernels, body(): call(last_kernel, (pair,) + (array(stats, F32),) * 3 + (array((2, *stats)...  1.88 us
  transfers between devices with their start and end apart: 10, of which 6 were waited for; matrix products, arithmetic and copies ran while one was open for 0% of the time, Pallas kernels for 18%

profile of v11, /device:TPU:120, one launch (start us, length us, event | category | flops | bytes accessed | tf_op | source)
XLA Modules:
  0.0 68.6 jit_solution(8721136200856674381)
XLA Ops:
  0.6 0.9 %shard_map.85.own_ref = bf16[2,256,128]{2,1,0:T(8,128)(2,1)S(1)} custom-call(bf16[256,128]{1,0:T(8,128)(2,1)} %k_ref.1, bf16[256,128]{1,0:T(8,128)(2,1)} %v_ref.1), custom_call_target="tpu_custom_call" | custom-call | bytes 1048576 | tf_op jit(solution)/shard_map/pallas_call | solution.py:280
  1.5 6.4 %collective-permute-start.1 = (bf16[2,256,128]{2,1,0:T(8,128)(2,1)S(1)}, bf16[2,256,128]{2,1,0:T(8,128)(2,1)S(1)}, u32[]{:S(2)}, u32[]{:S(2)}) collective-permute-start(bf16[2,256,128]{2,1,0:T(8,128)(2,1)S(1)} %shard_map.85.own_ref), channel_id=1, source_target_pairs={{0,64},{8,72},{16,80},{24,88},{32,96},{40,104},{48,112},{56,120},{... | collective-permute-start | bytes 393224 | tf_op jit(solution)/shard_map/ppermute | solution.py:252
  7.9 3.8 %collective-permute-start = (bf16[2,256,128]{2,1,0:T(8,128)(2,1)S(1)}, bf16[2,256,128]{2,1,0:T(8,128)(2,1)S(1)}, u32[]{:S(2)}, u32[]{:S(2)}) collective-permute-start(bf16[2,256,128]{2,1,0:T(8,128)(2,1)S(1)} %shard_map.85.own_ref), channel_id=1, source_target_pairs={{0,32},{8,40},{16,48},{24,56},{32,64},{40,72},{48,80},{56,88},{64,... | collective-permute-start | bytes 393224 | tf_op jit(solution)/shard_map/ppermute | solution.py:252
  11.8 0.9 %copy-done = bf16[256,512]{1,0:T(8,128)(2,1)S(1)} copy-done((bf16[256,512]{1,0:T(8,128)(2,1)S(1)}, bf16[256,512]{1,0:T(8,128)(2,1)}, u32[]{:S(2)}) %copy-start) | copy-done | bytes 262168
  12.7 0.9 %copy-done.1 = bf16[256,512]{1,0:T(8,128)(2,1)S(1)} copy-done((bf16[256,512]{1,0:T(8,128)(2,1)S(1)}, bf16[256,512]{1,0:T(8,128)(2,1)}, u32[]{:S(2)}) %copy-start.1) | copy-done | bytes 262168
  13.7 0.7 copy-done.2
  14.3 0.6 shard_map.84
  14.9 1.9 %collective-permute-done.z1_ref = bf16[2,256,128]{2,1,0:T(8,128)(2,1)S(1)} collective-permute-done((bf16[2,256,128]{2,1,0:T(8,128)(2,1)S(1)}, bf16[2,256,128]{2,1,0:T(8,128)(2,1)S(1)}, u32[]{:S(2)}, u32[]{:S(2)}) %collective-permute-start) | collective-permute-done | bytes 131104 | tf_op jit(solution)/shard_map/ppermute | solution.py:252
  16.9 4.9 %collective-permute-start.3 = (bf16[2,2,256,128]{3,2,1,0:T(8,128)(2,1)S(1)}, bf16[2,2,256,128]{3,2,1,0:T(8,128)(2,1)S(1)}, u32[]{:S(2)}, u32[]{:S(2)}) collective-permute-start(bf16[2,2,256,128]{3,2,1,0:T(8,128)(2,1)S(1)} %get-tuple-element.47), channel_id=1, source_target_pairs={{0,16},{8,24},{16,0},{24,8},{32,48},{40,56},{48,32},{56,40},{64,80... | collective-permute-start | bytes 786440 | tf_op jit(solution)/shard_map/ppermute | solution.py:256
  21.8 2.5 %collective-permute-start.2 = (bf16[2,2,256,128]{3,2,1,0:T(8,128)(2,1)S(1)}, bf16[2,2,256,128]{3,2,1,0:T(8,128)(2,1)S(1)}, u32[]{:S(2)}, u32[]{:S(2)}) collective-permute-start(bf16[2,2,256,128]{3,2,1,0:T(8,128)(2,1)S(1)} %get-tuple-element.46), channel_id=1, source_target_pairs={{0,8},{8,16},{16,24},{24,0},{32,40},{40,48},{48,56},{56,32},{64,72... | collective-permute-start | bytes 786440 | tf_op jit(solution)/shard_map/ppermute | solution.py:256
  24.3 4.6 %collective-permute-start.4 = (bf16[2,2,256,128]{3,2,1,0:T(8,128)(2,1)S(1)}, bf16[2,2,256,128]{3,2,1,0:T(8,128)(2,1)S(1)}, u32[]{:S(2)}, u32[]{:S(2)}) collective-permute-start(bf16[2,2,256,128]{3,2,1,0:T(8,128)(2,1)S(1)} %get-tuple-element.48), channel_id=1, source_target_pairs={{0,24},{8,0},{16,8},{24,16},{32,56},{40,32},{48,40},{56,48},{64,88... | collective-permute-start | bytes 786440 | tf_op jit(solution)/shard_map/ppermute | solution.py:256
  28.9 1.3 %shard_map.87 = (f32[3,4,256]{2,1,0:T(4,128)S(1)}, f32[3,4,256]{2,1,0:T(4,128)S(1)}, f32[3,4,256]{2,1,0:T(4,128)S(1)}) custom-call(s32[1,256]{1,0:T(1,128)S(1)} %get-tuple-element.43._.starts_ref, bf16[256,512]{1,0:T(8,128)(2,1)S(1)} %get-tuple-element.44.q_ref, bf16[256,512]{1,0:T(8,128)(2,1)S(1)} %get-tuple-element.45.g_ref, ...), custom_call_target="tpu_custom_call" | custom-call | flops 402653184 | bytes 1048576 | tf_op jit(solution)/shard_map/pallas_call | solution.py:295
  30.2 1.0 %shard_map.89 = (f32[2,4,256,256]{3,2,1,0:T(8,128)S(1)}, f32[2,4,256,256]{3,2,1,0:T(8,128)S(1)}, f32[2,4,256]{2,1,0:T(4,128)S(1)}, f32[2,4,256]{2,1,0:T(4,128)S(1)}, f32[2,4,256]{2,1,0:T(4,128)S(1)}) custom-call(s32[1,256]{1,0:T(1,128)S(1)} %get-tuple-element.43._.starts_ref, bf16[256,512]{1,0:T(8,128)(2,1)S(1)} %get-tuple-element.44.q_ref, ...), custom_call_target="tpu_custom_call" | custom-call | flops 268435456 | bytes 1048576 | tf_op jit(solution)/shard_map/pallas_call | solution.py:297
  31.2 2.4 %collective-permute-done.2.far_ref.f1_ref = bf16[2,2,256,128]{3,2,1,0:T(8,128)(2,1)S(1)} collective-permute-done((bf16[2,2,256,128]{3,2,1,0:T(8,128)(2,1)S(1)}, bf16[2,2,256,128]{3,2,1,0:T(8,128)(2,1)S(1)}, u32[]{:S(2)}, u32[]{:S(2)}) %collective-permute-start.2) | collective-permute-done | bytes 262176 | tf_op jit(solution)/shard_map/ppermute | solution.py:256
  33.6 1.0 %shard_map.88 = (f32[2,4,256,256]{3,2,1,0:T(8,128)S(1)}, f32[2,4,256,256]{3,2,1,0:T(8,128)S(1)}, f32[2,4,256]{2,1,0:T(4,128)S(1)}, f32[2,4,256]{2,1,0:T(4,128)S(1)}, f32[2,4,256]{2,1,0:T(4,128)S(1)}) custom-call(s32[1,256]{1,0:T(1,128)S(1)} %get-tuple-element.43._.starts_ref, bf16[256,512]{1,0:T(8,128)(2,1)S(1)} %get-tuple-element.44.q_ref, ...), custom_call_target="tpu_custom_call" | custom-call | flops 268435456 | bytes 1048576 | tf_op jit(solution)/shard_map/pallas_call | solution.py:298
  34.6 1.9 %shard_map.90 = (bf16[2,2,256,128]{3,2,1,0:T(8,128)(2,1)S(1)}, f32[4,256]{1,0:T(4,128)S(1)}, f32[4,256]{1,0:T(4,128)S(1)}, f32[4,256]{1,0:T(4,128)S(1)}, f32[2,4...) custom-call(s32[1,256]{1,0:T(1,128)S(1)} %get-tuple-element.43._.sta, ...), custom_call_target="tpu_custom_call" | custom-call | flops 536870912 | bytes 1048576 | tf_op jit(solution)/shard_map/pallas_call | solution.py:299
  36.5 4.6 %collective-permute-start.5 = (bf16[2,2,256,128]{3,2,1,0:T(8,128)(2,1)S(1)}, bf16[2,2,256,128]{3,2,1,0:T(8,128)(2,1)S(1)}, u32[]{:S(2)}, u32[]{:S(2)}) collective-permute-start(bf16[2,2,256,128]{3,2,1,0:T(8,128)(2,1)S(1)} %get-tuple-element.66), channel_id=1, source_target_pairs={{0,16},{8,24},{16,0},{24,8},{32,48},{40,56},{48,32},{56,40},{64,80... | collective-permute-start | bytes 786440 | tf_op jit(solution)/shard_map/ppermute | solution.py:256
  41.1 1.5 %shard_map.93 = (bf16[2,2,256,128]{3,2,1,0:T(8,128)(2,1)S(1)}, bf16[2,2,256,128]{3,2,1,0:T(8,128)(2,1)S(1)}) custom-call(bf16[256,512]{1,0:T(8,128)(2,1)S(1)} %get-tuple-element.44.q_ref, bf16[256,512]{1,0:T(8,128)(2,1)S(1)} %get-tuple-element.45.g_ref, f32[4,256]{1,0:T(4,128)S(1)} %get-tuple-element.62.rd_ref, ...), custom_call_target="tpu_custom_call" | custom-call | flops 536870912 | bytes 1048576 | tf_op jit(solution)/shard_map/pallas_call | solution.py:308
  42.6 3.1 %collective-permute-start.6 = (bf16[2,2,256,128]{3,2,1,0:T(8,128)(2,1)S(1)}, bf16[2,2,256,128]{3,2,1,0:T(8,128)(2,1)S(1)}, u32[]{:S(2)}, u32[]{:S(2)}) collective-permute-start(bf16[2,2,256,128]{3,2,1,0:T(8,128)(2,1)S(1)} %get-tuple-element.73), channel_id=1, source_target_pairs={{0,24},{8,0},{16,8},{24,16},{32,56},{40,32},{48,40},{56,48},{64,88... | collective-permute-start | bytes 786440 | tf_op jit(solution)/shard_map/ppermute | solution.py:256
  45.7 2.7 %collective-permute-start.7 = (bf16[2,2,256,128]{3,2,1,0:T(8,128)(2,1)S(1)}, bf16[2,2,256,128]{3,2,1,0:T(8,128)(2,1)S(1)}, u32[]{:S(2)}, u32[]{:S(2)}) collective-permute-start(bf16[2,2,256,128]{3,2,1,0:T(8,128)(2,1)S(1)} %get-tuple-element.74), channel_id=1, source_target_pairs={{0,8},{8,16},{16,24},{24,0},{32,40},{40,48},{48,56},{56,32},{64,72... | collective-permute-start | bytes 786440 | tf_op jit(solution)/shard_map/ppermute | solution.py:256
  48.5 2.3 %shard_map.91 = (f32[3,2,256,128]{3,2,1,0:T(8,128)S(1)}, f32[4,128,256]{2,1,0:T(8,128)S(1)}, f32[4,128,256]{2,1,0:T(8,128)S(1)}) custom-call(s32[1,256]{1,0:T(1,128)S(1)} %get-tuple-element.43._.starts_ref, bf16[256,512]{1,0:T(8,128)(2,1)S(1)} %get-tuple-element.44.q_ref, bf16[256,512]{1,0:T(8,128)(2,1)S(1)} %get-tuple-element.45.g_ref, ...), custom_call_target="tpu_custom_call" | custom-call | flops 402653184 | bytes 1048576 | tf_op jit(solution)/shard_map/pallas_call | solution.py:312
  50.8 0.1 shard_map.92.mine_ref
  50.9 1.5 %collective-permute-done.6.r1_ref = bf16[2,2,256,128]{3,2,1,0:T(8,128)(2,1)S(1)} collective-permute-done((bf16[2,2,256,128]{3,2,1,0:T(8,128)(2,1)S(1)}, bf16[2,2,256,128]{3,2,1,0:T(8,128)(2,1)S(1)}, u32[]{:S(2)}, u32[]{:S(2)}) %collective-permute-start.6) | collective-permute-done | bytes 262176 | tf_op jit(solution)/shard_map/ppermute | solution.py:256
  52.5 0.1 shard_map.94.mine_ref
  52.5 3.1 %collective-permute-done.7.r3_ref = bf16[2,2,256,128]{3,2,1,0:T(8,128)(2,1)S(1)} collective-permute-done((bf16[2,2,256,128]{3,2,1,0:T(8,128)(2,1)S(1)}, bf16[2,2,256,128]{3,2,1,0:T(8,128)(2,1)S(1)}, u32[]{:S(2)}, u32[]{:S(2)}) %collective-permute-start.7) | collective-permute-done | bytes 262176 | tf_op jit(solution)/shard_map/ppermute | solution.py:256
  55.6 0.1 shard_map.95
  55.7 1.9 %collective-permute-start.8 = (bf16[2,256,128]{2,1,0:T(8,128)(2,1)S(1)}, bf16[2,256,128]{2,1,0:T(8,128)(2,1)S(1)}, u32[]{:S(2)}, u32[]{:S(2)}) collective-permute-start(bf16[2,256,128]{2,1,0:T(8,128)(2,1)S(1)} %get-tuple-element.79), channel_id=1, source_target_pairs={{64,0},{72,8},{80,16},{88,24},{96,32},{104,40},{112,48},{120,56},{... | collective-permute-start | bytes 393224 | tf_op jit(solution)/shard_map/ppermute | solution.py:252
  57.6 2.1 %collective-permute-start.9 = (bf16[2,256,128]{2,1,0:T(8,128)(2,1)S(1)}, bf16[2,256,128]{2,1,0:T(8,128)(2,1)S(1)}, u32[]{:S(2)}, u32[]{:S(2)}) collective-permute-start(bf16[2,256,128]{2,1,0:T(8,128)(2,1)S(1)} %get-tuple-element.75._), channel_id=1, source_target_pairs={{32,0},{40,8},{48,16},{56,24},{64,32},{72,40},{80,48},{88,56},{96,... | collective-permute-start | bytes 393224 | tf_op jit(solution)/shard_map/ppermute | solution.py:252
  59.7 4.1 %shard_map.96 = (bf16[256,512]{1,0:T(8,128)(2,1)}, f32[256,512]{1,0:T(8,128)}) custom-call(s32[1,256]{1,0:T(1,128)S(1)} %get-tuple-element.43._.starts_ref, bf16[256,512]{1,0:T(8,128)(2,1)S(1)} %get-tuple-element.44.q_ref, bf16[256,512]{1,0:T(8,128)(2,1)S(1)} %get-tuple-element.45.g_ref, bf16[2,2,256,128]{3,2,1,0:T(8,128)(2,1)S(1)} %collective-permute-done.2.far_ref.f1_ref, ...), custom_call_target="tpu_custom_call" | custom-call | flops 1207959552 | bytes 1048576 | tf_op jit(solution)/shard_map/pallas_call | solution.py:325
  63.9 2.6 %collective-permute-done.8.two_ref = bf16[2,256,128]{2,1,0:T(8,128)(2,1)S(1)} collective-permute-done((bf16[2,256,128]{2,1,0:T(8,128)(2,1)S(1)}, bf16[2,256,128]{2,1,0:T(8,128)(2,1)S(1)}, u32[]{:S(2)}, u32[]{:S(2)}) %collective-permute-start.8) | collective-permute-done | bytes 131104 | tf_op jit(solution)/shard_map/ppermute | solution.py:252
  66.5 1.3 %collective-permute-done.9.one_ref = bf16[2,256,128]{2,1,0:T(8,128)(2,1)S(1)} collective-permute-done((bf16[2,256,128]{2,1,0:T(8,128)(2,1)S(1)}, bf16[2,256,128]{2,1,0:T(8,128)(2,1)S(1)}, u32[]{:S(2)}, u32[]{:S(2)}) %collective-permute-start.9) | collective-permute-done | bytes 131104 | tf_op jit(solution)/shard_map/ppermute | solution.py:252
  67.9 0.7 %shard_map.98 = (f32[256,128]{1,0:T(8,128)}, f32[256,128]{1,0:T(8,128)}) custom-call(f32[2,256,128]{2,1,0:T(8,128)S(1)} %shard_map.97.own_ref, bf16[2,256,128]{2,1,0:T(8,128)(2,1)S(1)} %collective-permute-done.9.one_ref), custom_call_target="tpu_custom_call" | custom-call | bytes 1048576 | tf_op jit(solution)/shard_map/pallas_call | solution.py:335
  (9 shorter events, 0.1 us)
Async XLA Ops:
  1.5 13.4 %collective-permute-start.1 = (bf16[2,256,128]{2,1,0:T(8,128)(2,1)S(1)}, bf16[2,256,128]{2,1,0:T(8,128)(2,1)S(1)}, u32[]{:S(2)}, u32[]{:S(2)}) collective-permute-start(bf16[2,256,128]{2,1,0:T(8,128)(2,1)S(1)} %shard_map.85.own_ref), channel_id=1, source_target_pairs={{0,64},{8,72},{16,80},{24,88},{32,96},{40,104},{48,112},{56,120},{... | collective-permute-start | bytes 393224 | tf_op jit(solution)/shard_map/ppermute | solution.py:252
  7.9 8.9 %collective-permute-start = (bf16[2,256,128]{2,1,0:T(8,128)(2,1)S(1)}, bf16[2,256,128]{2,1,0:T(8,128)(2,1)S(1)}, u32[]{:S(2)}, u32[]{:S(2)}) collective-permute-start(bf16[2,256,128]{2,1,0:T(8,128)(2,1)S(1)} %shard_map.85.own_ref), channel_id=1, source_target_pairs={{0,32},{8,40},{16,48},{24,56},{32,64},{40,72},{48,80},{56,88},{64,... | collective-permute-start | bytes 393224 | tf_op jit(solution)/shard_map/ppermute | solution.py:252
  11.8 1.0 %copy-start = (bf16[256,512]{1,0:T(8,128)(2,1)S(1)}, bf16[256,512]{1,0:T(8,128)(2,1)}, u32[]{:S(2)}) copy-start(bf16[256,512]{1,0:T(8,128)(2,1)} %q_ref.1) | copy-start | bytes 786436
  12.7 0.9 %copy-start.1 = (bf16[256,512]{1,0:T(8,128)(2,1)S(1)}, bf16[256,512]{1,0:T(8,128)(2,1)}, u32[]{:S(2)}) copy-start(bf16[256,512]{1,0:T(8,128)(2,1)} %g_ref.1) | copy-start | bytes 786436
  13.7 0.7 copy-start.2
  16.9 13.3 %collective-permute-start.3 = (bf16[2,2,256,128]{3,2,1,0:T(8,128)(2,1)S(1)}, bf16[2,2,256,128]{3,2,1,0:T(8,128)(2,1)S(1)}, u32[]{:S(2)}, u32[]{:S(2)}) collective-permute-start(bf16[2,2,256,128]{3,2,1,0:T(8,128)(2,1)S(1)} %get-tuple-element.47), channel_id=1, source_target_pairs={{0,16},{8,24},{16,0},{24,8},{32,48},{40,56},{48,32},{56,40},{64,80... | collective-permute-start | bytes 786440 | tf_op jit(solution)/shard_map/ppermute | solution.py:256
  21.8 11.8 %collective-permute-start.2 = (bf16[2,2,256,128]{3,2,1,0:T(8,128)(2,1)S(1)}, bf16[2,2,256,128]{3,2,1,0:T(8,128)(2,1)S(1)}, u32[]{:S(2)}, u32[]{:S(2)}) collective-permute-start(bf16[2,2,256,128]{3,2,1,0:T(8,128)(2,1)S(1)} %get-tuple-element.46), channel_id=1, source_target_pairs={{0,8},{8,16},{16,24},{24,0},{32,40},{40,48},{48,56},{56,32},{64,72... | collective-permute-start | bytes 786440 | tf_op jit(solution)/shard_map/ppermute | solution.py:256
  24.3 10.3 %collective-permute-start.4 = (bf16[2,2,256,128]{3,2,1,0:T(8,128)(2,1)S(1)}, bf16[2,2,256,128]{3,2,1,0:T(8,128)(2,1)S(1)}, u32[]{:S(2)}, u32[]{:S(2)}) collective-permute-start(bf16[2,2,256,128]{3,2,1,0:T(8,128)(2,1)S(1)} %get-tuple-element.48), channel_id=1, source_target_pairs={{0,24},{8,0},{16,8},{24,16},{32,56},{40,32},{48,40},{56,48},{64,88... | collective-permute-start | bytes 786440 | tf_op jit(solution)/shard_map/ppermute | solution.py:256
  36.5 14.3 %collective-permute-start.5 = (bf16[2,2,256,128]{3,2,1,0:T(8,128)(2,1)S(1)}, bf16[2,2,256,128]{3,2,1,0:T(8,128)(2,1)S(1)}, u32[]{:S(2)}, u32[]{:S(2)}) collective-permute-start(bf16[2,2,256,128]{3,2,1,0:T(8,128)(2,1)S(1)} %get-tuple-element.66), channel_id=1, source_target_pairs={{0,16},{8,24},{16,0},{24,8},{32,48},{40,56},{48,32},{56,40},{64,80... | collective-permute-start | bytes 786440 | tf_op jit(solution)/shard_map/ppermute | solution.py:256
  42.6 9.8 %collective-permute-start.6 = (bf16[2,2,256,128]{3,2,1,0:T(8,128)(2,1)S(1)}, bf16[2,2,256,128]{3,2,1,0:T(8,128)(2,1)S(1)}, u32[]{:S(2)}, u32[]{:S(2)}) collective-permute-start(bf16[2,2,256,128]{3,2,1,0:T(8,128)(2,1)S(1)} %get-tuple-element.73), channel_id=1, source_target_pairs={{0,24},{8,0},{16,8},{24,16},{32,56},{40,32},{48,40},{56,48},{64,88... | collective-permute-start | bytes 786440 | tf_op jit(solution)/shard_map/ppermute | solution.py:256
  45.7 9.9 %collective-permute-start.7 = (bf16[2,2,256,128]{3,2,1,0:T(8,128)(2,1)S(1)}, bf16[2,2,256,128]{3,2,1,0:T(8,128)(2,1)S(1)}, u32[]{:S(2)}, u32[]{:S(2)}) collective-permute-start(bf16[2,2,256,128]{3,2,1,0:T(8,128)(2,1)S(1)} %get-tuple-element.74), channel_id=1, source_target_pairs={{0,8},{8,16},{16,24},{24,0},{32,40},{40,48},{48,56},{56,32},{64,72... | collective-permute-start | bytes 786440 | tf_op jit(solution)/shard_map/ppermute | solution.py:256
  55.7 10.8 %collective-permute-start.8 = (bf16[2,256,128]{2,1,0:T(8,128)(2,1)S(1)}, bf16[2,256,128]{2,1,0:T(8,128)(2,1)S(1)}, u32[]{:S(2)}, u32[]{:S(2)}) collective-permute-start(bf16[2,256,128]{2,1,0:T(8,128)(2,1)S(1)} %get-tuple-element.79), channel_id=1, source_target_pairs={{64,0},{72,8},{80,16},{88,24},{96,32},{104,40},{112,48},{120,56},{... | collective-permute-start | bytes 393224 | tf_op jit(solution)/shard_map/ppermute | solution.py:252
  57.6 10.3 %collective-permute-start.9 = (bf16[2,256,128]{2,1,0:T(8,128)(2,1)S(1)}, bf16[2,256,128]{2,1,0:T(8,128)(2,1)S(1)}, u32[]{:S(2)}, u32[]{:S(2)}) collective-permute-start(bf16[2,256,128]{2,1,0:T(8,128)(2,1)S(1)} %get-tuple-element.75._), channel_id=1, source_target_pairs={{32,0},{40,8},{48,16},{56,24},{64,32},{72,40},{80,48},{88,56},{96,... | collective-permute-start | bytes 393224 | tf_op jit(solution)/shard_map/ppermute | solution.py:252

commit v12 on v11

--- a/solution.py
+++ b/solution.py
@@ -238,13 +238,13 @@
     two_ref[...] = two.astype(BF16)
 
 
-def add_two_kernel(own_ref, two_ref, out_ref):
-    out_ref[...] = own_ref[...] + two_ref[...].astype(F32)
-
-
-def final_kernel(own_ref, one_ref, dk_ref, dv_ref):
-    dk_ref[...] = own_ref[0] + one_ref[0].astype(F32)
-    dv_ref[...] = own_ref[1] + one_ref[1].astype(F32)
+def add_kernel(own_ref, one_ref, out_ref):
+    out_ref[...] = own_ref[...] + one_ref[...].astype(F32)
+
+
+def final_kernel(own_ref, two_ref, dk_ref, dv_ref):
+    dk_ref[...] = own_ref[0] + two_ref[0].astype(F32)
+    dv_ref[...] = own_ref[1] + two_ref[1].astype(F32)
 
 
 def along_z(block, rows, peers):
@@ -331,8 +331,8 @@
         limit=16,
     )(*wanted, f1, f2, f3, peak, over, rd, near_o, near_dq, one)
     two, one = along_z(two, -2, peers), along_z(one, -1, peers)
-    (mine,) = call(add_two_kernel, (array(block, F32),), [VM] * 2, limit=4)(mine, two)
-    key_grad, value_grad = call(final_kernel, (array((T, D), F32),) * 2, [VM] * 2, limit=4)(mine, one)
+    (mine,) = call(add_kernel, (array(block, F32),), [VM] * 2, limit=4)(mine, one)
+    key_grad, value_grad = call(final_kernel, (array((T, D), F32),) * 2, [VM] * 2, limit=4)(mine, two)
     return attended, query_grad, key_grad, value_grad
 
 

time: 69.1 us -> 70.8 us (1.025)
  waiting for transfers between devices: 12.8 us -> 14.5 us
    ppermute x4, waiting for transfers between devices: 5.85 us -> 7.53 us  [along_z(): lax.ppermute(block, 'peer', [(i, i + far) for i in range(peers) if 0 <= i...]
  transfers between devices with their start and end apart: 10 -> 10, of which waited for: 6 -> 6; matrix products, arithmetic and copies ran while one was open for 0% -> 0% of each run, Pallas kernels for 18% -> 17%
where the time goes in v12:
time: 70.8 us; the launch traced here: 70.3 us
  starting transfers between devices  36.7 us (52%)
  Pallas kernels  15.7 us (22%)
  waiting for transfers between devices  14.5 us (20%)
  local copies, waits for them, and re-layouts  2.55 us (4%)
  between operations  0.83 us (1%)
    ppermute x6, starting transfers between devices, along_x(): lax.ppermute(block, 'peer', [(i, i - i % ROW + (i + columns) % ROW) for i...  22.5 us
    ppermute x4, starting transfers between devices, along_z(): lax.ppermute(block, 'peer', [(i, i + far) for i in range(peers) if 0 <= i...  14.2 us
    ppermute x4, waiting for transfers between devices, along_z(): lax.ppermute(block, 'peer', [(i, i + far) for i in range(peers) if 0 <= i...  7.53 us
    ppermute x6, waiting for transfers between devices, along_x(): lax.ppermute(block, 'peer', [(i, i - i % ROW + (i + columns) % ROW) for i...  6.97 us
    pallas_call x1, Pallas kernels, body(): call(query_side_kernel, (array((T, H * D), BF16), array((T, H * D), F32))...  4.14 us
    unnamed x6, local copies, waits for them, and re-layouts  2.55 us
    pallas_call x1, Pallas kernels, body(): call(near_back_kernel, (array((3, *block), F32),) + (array((H, D, T), F32...  2.32 us
    pallas_call x1, Pallas kernels, body(): call(last_kernel, (pair,) + (array(stats, F32),) * 3 + (array((2, *stats)...  1.88 us
  transfers between devices with their start and end apart: 10, of which 6 were waited for; matrix products, arithmetic and copies ran while one was open for 0% of the time, Pallas kernels for 17%

profile of v12, /device:TPU:120, one launch (start us, length us, event | category | flops | bytes accessed | tf_op | source)
XLA Modules:
  0.0 70.3 jit_solution(14863281422800401414)
XLA Ops:
  0.6 0.9 %shard_map.85.own_ref = bf16[2,256,128]{2,1,0:T(8,128)(2,1)S(1)} custom-call(bf16[256,128]{1,0:T(8,128)(2,1)} %k_ref.1, bf16[256,128]{1,0:T(8,128)(2,1)} %v_ref.1), custom_call_target="tpu_custom_call" | custom-call | bytes 1048576 | tf_op jit(solution)/shard_map/pallas_call | solution.py:280
  1.5 6.4 %collective-permute-start.1 = (bf16[2,256,128]{2,1,0:T(8,128)(2,1)S(1)}, bf16[2,256,128]{2,1,0:T(8,128)(2,1)S(1)}, u32[]{:S(2)}, u32[]{:S(2)}) collective-permute-start(bf16[2,256,128]{2,1,0:T(8,128)(2,1)S(1)} %shard_map.85.own_ref), channel_id=1, source_target_pairs={{0,64},{8,72},{16,80},{24,88},{32,96},{40,104},{48,112},{56,120},{... | collective-permute-start | bytes 393224 | tf_op jit(solution)/shard_map/ppermute | solution.py:252
  7.9 3.8 %collective-permute-start = (bf16[2,256,128]{2,1,0:T(8,128)(2,1)S(1)}, bf16[2,256,128]{2,1,0:T(8,128)(2,1)S(1)}, u32[]{:S(2)}, u32[]{:S(2)}) collective-permute-start(bf16[2,256,128]{2,1,0:T(8,128)(2,1)S(1)} %shard_map.85.own_ref), channel_id=1, source_target_pairs={{0,32},{8,40},{16,48},{24,56},{32,64},{40,72},{48,80},{56,88},{64,... | collective-permute-start | bytes 393224 | tf_op jit(solution)/shard_map/ppermute | solution.py:252
  11.8 0.9 %copy-done = bf16[256,512]{1,0:T(8,128)(2,1)S(1)} copy-done((bf16[256,512]{1,0:T(8,128)(2,1)S(1)}, bf16[256,512]{1,0:T(8,128)(2,1)}, u32[]{:S(2)}) %copy-start) | copy-done | bytes 262168
  12.7 0.9 %copy-done.1 = bf16[256,512]{1,0:T(8,128)(2,1)S(1)} copy-done((bf16[256,512]{1,0:T(8,128)(2,1)S(1)}, bf16[256,512]{1,0:T(8,128)(2,1)}, u32[]{:S(2)}) %copy-start.1) | copy-done | bytes 262168
  13.7 0.7 copy-done.2
  14.3 0.6 shard_map.84
  14.9 1.9 %collective-permute-done.z1_ref = bf16[2,256,128]{2,1,0:T(8,128)(2,1)S(1)} collective-permute-done((bf16[2,256,128]{2,1,0:T(8,128)(2,1)S(1)}, bf16[2,256,128]{2,1,0:T(8,128)(2,1)S(1)}, u32[]{:S(2)}, u32[]{:S(2)}) %collective-permute-start) | collective-permute-done | bytes 131104 | tf_op jit(solution)/shard_map/ppermute | solution.py:252
  16.9 4.9 %collective-permute-start.3 = (bf16[2,2,256,128]{3,2,1,0:T(8,128)(2,1)S(1)}, bf16[2,2,256,128]{3,2,1,0:T(8,128)(2,1)S(1)}, u32[]{:S(2)}, u32[]{:S(2)}) collective-permute-start(bf16[2,2,256,128]{3,2,1,0:T(8,128)(2,1)S(1)} %get-tuple-element.47), channel_id=1, source_target_pairs={{0,16},{8,24},{16,0},{24,8},{32,48},{40,56},{48,32},{56,40},{64,80... | collective-permute-start | bytes 786440 | tf_op jit(solution)/shard_map/ppermute | solution.py:256
  21.8 2.5 %collective-permute-start.2 = (bf16[2,2,256,128]{3,2,1,0:T(8,128)(2,1)S(1)}, bf16[2,2,256,128]{3,2,1,0:T(8,128)(2,1)S(1)}, u32[]{:S(2)}, u32[]{:S(2)}) collective-permute-start(bf16[2,2,256,128]{3,2,1,0:T(8,128)(2,1)S(1)} %get-tuple-element.46), channel_id=1, source_target_pairs={{0,8},{8,16},{16,24},{24,0},{32,40},{40,48},{48,56},{56,32},{64,72... | collective-permute-start | bytes 786440 | tf_op jit(solution)/shard_map/ppermute | solution.py:256
  24.3 4.6 %collective-permute-start.4 = (bf16[2,2,256,128]{3,2,1,0:T(8,128)(2,1)S(1)}, bf16[2,2,256,128]{3,2,1,0:T(8,128)(2,1)S(1)}, u32[]{:S(2)}, u32[]{:S(2)}) collective-permute-start(bf16[2,2,256,128]{3,2,1,0:T(8,128)(2,1)S(1)} %get-tuple-element.48), channel_id=1, source_target_pairs={{0,24},{8,0},{16,8},{24,16},{32,56},{40,32},{48,40},{56,48},{64,88... | collective-permute-start | bytes 786440 | tf_op jit(solution)/shard_map/ppermute | solution.py:256
  28.9 1.3 %shard_map.87 = (f32[3,4,256]{2,1,0:T(4,128)S(1)}, f32[3,4,256]{2,1,0:T(4,128)S(1)}, f32[3,4,256]{2,1,0:T(4,128)S(1)}) custom-call(s32[1,256]{1,0:T(1,128)S(1)} %get-tuple-element.43._.starts_ref, bf16[256,512]{1,0:T(8,128)(2,1)S(1)} %get-tuple-element.44.q_ref, bf16[256,512]{1,0:T(8,128)(2,1)S(1)} %get-tuple-element.45.g_ref, ...), custom_call_target="tpu_custom_call" | custom-call | flops 402653184 | bytes 1048576 | tf_op jit(solution)/shard_map/pallas_call | solution.py:295
  30.2 1.0 %shard_map.89 = (f32[2,4,256,256]{3,2,1,0:T(8,128)S(1)}, f32[2,4,256,256]{3,2,1,0:T(8,128)S(1)}, f32[2,4,256]{2,1,0:T(4,128)S(1)}, f32[2,4,256]{2,1,0:T(4,128)S(1)}, f32[2,4,256]{2,1,0:T(4,128)S(1)}) custom-call(s32[1,256]{1,0:T(1,128)S(1)} %get-tuple-element.43._.starts_ref, bf16[256,512]{1,0:T(8,128)(2,1)S(1)} %get-tuple-element.44.q_ref, ...), custom_call_target="tpu_custom_call" | custom-call | flops 268435456 | bytes 1048576 | tf_op jit(solution)/shard_map/pallas_call | solution.py:297
  31.2 2.4 %collective-permute-done.2.far_ref.f1_ref = bf16[2,2,256,128]{3,2,1,0:T(8,128)(2,1)S(1)} collective-permute-done((bf16[2,2,256,128]{3,2,1,0:T(8,128)(2,1)S(1)}, bf16[2,2,256,128]{3,2,1,0:T(8,128)(2,1)S(1)}, u32[]{:S(2)}, u32[]{:S(2)}) %collective-permute-start.2) | collective-permute-done | bytes 262176 | tf_op jit(solution)/shard_map/ppermute | solution.py:256
  33.6 1.0 %shard_map.88 = (f32[2,4,256,256]{3,2,1,0:T(8,128)S(1)}, f32[2,4,256,256]{3,2,1,0:T(8,128)S(1)}, f32[2,4,256]{2,1,0:T(4,128)S(1)}, f32[2,4,256]{2,1,0:T(4,128)S(1)}, f32[2,4,256]{2,1,0:T(4,128)S(1)}) custom-call(s32[1,256]{1,0:T(1,128)S(1)} %get-tuple-element.43._.starts_ref, bf16[256,512]{1,0:T(8,128)(2,1)S(1)} %get-tuple-element.44.q_ref, ...), custom_call_target="tpu_custom_call" | custom-call | flops 268435456 | bytes 1048576 | tf_op jit(solution)/shard_map/pallas_call | solution.py:298
  34.6 1.9 %shard_map.90 = (bf16[2,2,256,128]{3,2,1,0:T(8,128)(2,1)S(1)}, f32[4,256]{1,0:T(4,128)S(1)}, f32[4,256]{1,0:T(4,128)S(1)}, f32[4,256]{1,0:T(4,128)S(1)}, f32[2,4...) custom-call(s32[1,256]{1,0:T(1,128)S(1)} %get-tuple-element.43._.sta, ...), custom_call_target="tpu_custom_call" | custom-call | flops 536870912 | bytes 1048576 | tf_op jit(solution)/shard_map/pallas_call | solution.py:299
  36.5 4.6 %collective-permute-start.5 = (bf16[2,2,256,128]{3,2,1,0:T(8,128)(2,1)S(1)}, bf16[2,2,256,128]{3,2,1,0:T(8,128)(2,1)S(1)}, u32[]{:S(2)}, u32[]{:S(2)}) collective-permute-start(bf16[2,2,256,128]{3,2,1,0:T(8,128)(2,1)S(1)} %get-tuple-element.66), channel_id=1, source_target_pairs={{0,16},{8,24},{16,0},{24,8},{32,48},{40,56},{48,32},{56,40},{64,80... | collective-permute-start | bytes 786440 | tf_op jit(solution)/shard_map/ppermute | solution.py:256
  41.1 1.5 %shard_map.93 = (bf16[2,2,256,128]{3,2,1,0:T(8,128)(2,1)S(1)}, bf16[2,2,256,128]{3,2,1,0:T(8,128)(2,1)S(1)}) custom-call(bf16[256,512]{1,0:T(8,128)(2,1)S(1)} %get-tuple-element.44.q_ref, bf16[256,512]{1,0:T(8,128)(2,1)S(1)} %get-tuple-element.45.g_ref, f32[4,256]{1,0:T(4,128)S(1)} %get-tuple-element.62.rd_ref, ...), custom_call_target="tpu_custom_call" | custom-call | flops 536870912 | bytes 1048576 | tf_op jit(solution)/shard_map/pallas_call | solution.py:308
  42.6 3.1 %collective-permute-start.6 = (bf16[2,2,256,128]{3,2,1,0:T(8,128)(2,1)S(1)}, bf16[2,2,256,128]{3,2,1,0:T(8,128)(2,1)S(1)}, u32[]{:S(2)}, u32[]{:S(2)}) collective-permute-start(bf16[2,2,256,128]{3,2,1,0:T(8,128)(2,1)S(1)} %get-tuple-element.73), channel_id=1, source_target_pairs={{0,24},{8,0},{16,8},{24,16},{32,56},{40,32},{48,40},{56,48},{64,88... | collective-permute-start | bytes 786440 | tf_op jit(solution)/shard_map/ppermute | solution.py:256
  45.7 2.7 %collective-permute-start.7 = (bf16[2,2,256,128]{3,2,1,0:T(8,128)(2,1)S(1)}, bf16[2,2,256,128]{3,2,1,0:T(8,128)(2,1)S(1)}, u32[]{:S(2)}, u32[]{:S(2)}) collective-permute-start(bf16[2,2,256,128]{3,2,1,0:T(8,128)(2,1)S(1)} %get-tuple-element.74), channel_id=1, source_target_pairs={{0,8},{8,16},{16,24},{24,0},{32,40},{40,48},{48,56},{56,32},{64,72... | collective-permute-start | bytes 786440 | tf_op jit(solution)/shard_map/ppermute | solution.py:256
  48.5 2.3 %shard_map.91 = (f32[3,2,256,128]{3,2,1,0:T(8,128)S(1)}, f32[4,128,256]{2,1,0:T(8,128)S(1)}, f32[4,128,256]{2,1,0:T(8,128)S(1)}) custom-call(s32[1,256]{1,0:T(1,128)S(1)} %get-tuple-element.43._.starts_ref, bf16[256,512]{1,0:T(8,128)(2,1)S(1)} %get-tuple-element.44.q_ref, bf16[256,512]{1,0:T(8,128)(2,1)S(1)} %get-tuple-element.45.g_ref, ...), custom_call_target="tpu_custom_call" | custom-call | flops 402653184 | bytes 1048576 | tf_op jit(solution)/shard_map/pallas_call | solution.py:312
  50.8 0.1 shard_map.92.mine_ref
  50.9 1.5 %collective-permute-done.6.r1_ref = bf16[2,2,256,128]{3,2,1,0:T(8,128)(2,1)S(1)} collective-permute-done((bf16[2,2,256,128]{3,2,1,0:T(8,128)(2,1)S(1)}, bf16[2,2,256,128]{3,2,1,0:T(8,128)(2,1)S(1)}, u32[]{:S(2)}, u32[]{:S(2)}) %collective-permute-start.6) | collective-permute-done | bytes 262176 | tf_op jit(solution)/shard_map/ppermute | solution.py:256
  52.5 0.1 shard_map.94.mine_ref
  52.5 3.1 %collective-permute-done.7.r3_ref = bf16[2,2,256,128]{3,2,1,0:T(8,128)(2,1)S(1)} collective-permute-done((bf16[2,2,256,128]{3,2,1,0:T(8,128)(2,1)S(1)}, bf16[2,2,256,128]{3,2,1,0:T(8,128)(2,1)S(1)}, u32[]{:S(2)}, u32[]{:S(2)}) %collective-permute-start.7) | collective-permute-done | bytes 262176 | tf_op jit(solution)/shard_map/ppermute | solution.py:256
  55.6 0.1 shard_map.95
  55.7 1.9 %collective-permute-start.8 = (bf16[2,256,128]{2,1,0:T(8,128)(2,1)S(1)}, bf16[2,256,128]{2,1,0:T(8,128)(2,1)S(1)}, u32[]{:S(2)}, u32[]{:S(2)}) collective-permute-start(bf16[2,256,128]{2,1,0:T(8,128)(2,1)S(1)} %get-tuple-element.75._), channel_id=1, source_target_pairs={{32,0},{40,8},{48,16},{56,24},{64,32},{72,40},{80,48},{88,56},{96,... | collective-permute-start | bytes 393224 | tf_op jit(solution)/shard_map/ppermute | solution.py:252
  57.6 2.1 %collective-permute-start.9 = (bf16[2,256,128]{2,1,0:T(8,128)(2,1)S(1)}, bf16[2,256,128]{2,1,0:T(8,128)(2,1)S(1)}, u32[]{:S(2)}, u32[]{:S(2)}) collective-permute-start(bf16[2,256,128]{2,1,0:T(8,128)(2,1)S(1)} %get-tuple-element.79), channel_id=1, source_target_pairs={{64,0},{72,8},{80,16},{88,24},{96,32},{104,40},{112,48},{120,56},{... | collective-permute-start | bytes 393224 | tf_op jit(solution)/shard_map/ppermute | solution.py:252
  59.7 4.1 %shard_map.96 = (bf16[256,512]{1,0:T(8,128)(2,1)}, f32[256,512]{1,0:T(8,128)}) custom-call(s32[1,256]{1,0:T(1,128)S(1)} %get-tuple-element.43._.starts_ref, bf16[256,512]{1,0:T(8,128)(2,1)S(1)} %get-tuple-element.44.q_ref, bf16[256,512]{1,0:T(8,128)(2,1)S(1)} %get-tuple-element.45.g_ref, bf16[2,2,256,128]{3,2,1,0:T(8,128)(2,1)S(1)} %collective-permute-done.2.far_ref.f1_ref, ...), custom_call_target="tpu_custom_call" | custom-call | flops 1207959552 | bytes 1048576 | tf_op jit(solution)/shard_map/pallas_call | solution.py:325
  63.9 1.6 %collective-permute-done.8.one_ref = bf16[2,256,128]{2,1,0:T(8,128)(2,1)S(1)} collective-permute-done((bf16[2,256,128]{2,1,0:T(8,128)(2,1)S(1)}, bf16[2,256,128]{2,1,0:T(8,128)(2,1)S(1)}, u32[]{:S(2)}, u32[]{:S(2)}) %collective-permute-start.8) | collective-permute-done | bytes 131104 | tf_op jit(solution)/shard_map/ppermute | solution.py:252
  65.5 4.1 %collective-permute-done.9.two_ref = bf16[2,256,128]{2,1,0:T(8,128)(2,1)S(1)} collective-permute-done((bf16[2,256,128]{2,1,0:T(8,128)(2,1)S(1)}, bf16[2,256,128]{2,1,0:T(8,128)(2,1)S(1)}, u32[]{:S(2)}, u32[]{:S(2)}) %collective-permute-start.9) | collective-permute-done | bytes 131104 | tf_op jit(solution)/shard_map/ppermute | solution.py:252
  69.6 0.7 %shard_map.98 = (f32[256,128]{1,0:T(8,128)}, f32[256,128]{1,0:T(8,128)}) custom-call(f32[2,256,128]{2,1,0:T(8,128)S(1)} %shard_map.97.own_ref, bf16[2,256,128]{2,1,0:T(8,128)(2,1)S(1)} %collective-permute-done.9.two_ref), custom_call_target="tpu_custom_call" | custom-call | bytes 1048576 | tf_op jit(solution)/shard_map/pallas_call | solution.py:335
  (9 shorter events, 0.1 us)
Async XLA Ops:
  1.5 13.4 %collective-permute-start.1 = (bf16[2,256,128]{2,1,0:T(8,128)(2,1)S(1)}, bf16[2,256,128]{2,1,0:T(8,128)(2,1)S(1)}, u32[]{:S(2)}, u32[]{:S(2)}) collective-permute-start(bf16[2,256,128]{2,1,0:T(8,128)(2,1)S(1)} %shard_map.85.own_ref), channel_id=1, source_target_pairs={{0,64},{8,72},{16,80},{24,88},{32,96},{40,104},{48,112},{56,120},{... | collective-permute-start | bytes 393224 | tf_op jit(solution)/shard_map/ppermute | solution.py:252
  7.9 8.9 %collective-permute-start = (bf16[2,256,128]{2,1,0:T(8,128)(2,1)S(1)}, bf16[2,256,128]{2,1,0:T(8,128)(2,1)S(1)}, u32[]{:S(2)}, u32[]{:S(2)}) collective-permute-start(bf16[2,256,128]{2,1,0:T(8,128)(2,1)S(1)} %shard_map.85.own_ref), channel_id=1, source_target_pairs={{0,32},{8,40},{16,48},{24,56},{32,64},{40,72},{48,80},{56,88},{64,... | collective-permute-start | bytes 393224 | tf_op jit(solution)/shard_map/ppermute | solution.py:252
  11.8 1.0 %copy-start = (bf16[256,512]{1,0:T(8,128)(2,1)S(1)}, bf16[256,512]{1,0:T(8,128)(2,1)}, u32[]{:S(2)}) copy-start(bf16[256,512]{1,0:T(8,128)(2,1)} %q_ref.1) | copy-start | bytes 786436
  12.7 0.9 %copy-start.1 = (bf16[256,512]{1,0:T(8,128)(2,1)S(1)}, bf16[256,512]{1,0:T(8,128)(2,1)}, u32[]{:S(2)}) copy-start(bf16[256,512]{1,0:T(8,128)(2,1)} %g_ref.1) | copy-start | bytes 786436
  13.7 0.7 copy-start.2
  16.9 13.3 %collective-permute-start.3 = (bf16[2,2,256,128]{3,2,1,0:T(8,128)(2,1)S(1)}, bf16[2,2,256,128]{3,2,1,0:T(8,128)(2,1)S(1)}, u32[]{:S(2)}, u32[]{:S(2)}) collective-permute-start(bf16[2,2,256,128]{3,2,1,0:T(8,128)(2,1)S(1)} %get-tuple-element.47), channel_id=1, source_target_pairs={{0,16},{8,24},{16,0},{24,8},{32,48},{40,56},{48,32},{56,40},{64,80... | collective-permute-start | bytes 786440 | tf_op jit(solution)/shard_map/ppermute | solution.py:256
  21.8 11.8 %collective-permute-start.2 = (bf16[2,2,256,128]{3,2,1,0:T(8,128)(2,1)S(1)}, bf16[2,2,256,128]{3,2,1,0:T(8,128)(2,1)S(1)}, u32[]{:S(2)}, u32[]{:S(2)}) collective-permute-start(bf16[2,2,256,128]{3,2,1,0:T(8,128)(2,1)S(1)} %get-tuple-element.46), channel_id=1, source_target_pairs={{0,8},{8,16},{16,24},{24,0},{32,40},{40,48},{48,56},{56,32},{64,72... | collective-permute-start | bytes 786440 | tf_op jit(solution)/shard_map/ppermute | solution.py:256
  24.3 10.3 %collective-permute-start.4 = (bf16[2,2,256,128]{3,2,1,0:T(8,128)(2,1)S(1)}, bf16[2,2,256,128]{3,2,1,0:T(8,128)(2,1)S(1)}, u32[]{:S(2)}, u32[]{:S(2)}) collective-permute-start(bf16[2,2,256,128]{3,2,1,0:T(8,128)(2,1)S(1)} %get-tuple-element.48), channel_id=1, source_target_pairs={{0,24},{8,0},{16,8},{24,16},{32,56},{40,32},{48,40},{56,48},{64,88... | collective-permute-start | bytes 786440 | tf_op jit(solution)/shard_map/ppermute | solution.py:256
  36.5 14.3 %collective-permute-start.5 = (bf16[2,2,256,128]{3,2,1,0:T(8,128)(2,1)S(1)}, bf16[2,2,256,128]{3,2,1,0:T(8,128)(2,1)S(1)}, u32[]{:S(2)}, u32[]{:S(2)}) collective-permute-start(bf16[2,2,256,128]{3,2,1,0:T(8,128)(2,1)S(1)} %get-tuple-element.66), channel_id=1, source_target_pairs={{0,16},{8,24},{16,0},{24,8},{32,48},{40,56},{48,32},{56,40},{64,80... | collective-permute-start | bytes 786440 | tf_op jit(solution)/shard_map/ppermute | solution.py:256
  42.6 9.8 %collective-permute-start.6 = (bf16[2,2,256,128]{3,2,1,0:T(8,128)(2,1)S(1)}, bf16[2,2,256,128]{3,2,1,0:T(8,128)(2,1)S(1)}, u32[]{:S(2)}, u32[]{:S(2)}) collective-permute-start(bf16[2,2,256,128]{3,2,1,0:T(8,128)(2,1)S(1)} %get-tuple-element.73), channel_id=1, source_target_pairs={{0,24},{8,0},{16,8},{24,16},{32,56},{40,32},{48,40},{56,48},{64,88... | collective-permute-start | bytes 786440 | tf_op jit(solution)/shard_map/ppermute | solution.py:256
  45.7 9.9 %collective-permute-start.7 = (bf16[2,2,256,128]{3,2,1,0:T(8,128)(2,1)S(1)}, bf16[2,2,256,128]{3,2,1,0:T(8,128)(2,1)S(1)}, u32[]{:S(2)}, u32[]{:S(2)}) collective-permute-start(bf16[2,2,256,128]{3,2,1,0:T(8,128)(2,1)S(1)} %get-tuple-element.74), channel_id=1, source_target_pairs={{0,8},{8,16},{16,24},{24,0},{32,40},{40,48},{48,56},{56,32},{64,72... | collective-permute-start | bytes 786440 | tf_op jit(solution)/shard_map/ppermute | solution.py:256
  55.7 9.8 %collective-permute-start.8 = (bf16[2,256,128]{2,1,0:T(8,128)(2,1)S(1)}, bf16[2,256,128]{2,1,0:T(8,128)(2,1)S(1)}, u32[]{:S(2)}, u32[]{:S(2)}) collective-permute-start(bf16[2,256,128]{2,1,0:T(8,128)(2,1)S(1)} %get-tuple-element.75._), channel_id=1, source_target_pairs={{32,0},{40,8},{48,16},{56,24},{64,32},{72,40},{80,48},{88,56},{96,... | collective-permute-start | bytes 393224 | tf_op jit(solution)/shard_map/ppermute | solution.py:252
  57.6 11.9 %collective-permute-start.9 = (bf16[2,256,128]{2,1,0:T(8,128)(2,1)S(1)}, bf16[2,256,128]{2,1,0:T(8,128)(2,1)S(1)}, u32[]{:S(2)}, u32[]{:S(2)}) collective-permute-start(bf16[2,256,128]{2,1,0:T(8,128)(2,1)S(1)} %get-tuple-element.79), channel_id=1, source_target_pairs={{64,0},{72,8},{80,16},{88,24},{96,32},{104,40},{112,48},{120,56},{... | collective-permute-start | bytes 393224 | tf_op jit(solution)/shard_map/ppermute | solution.py:252
